TPU v7x, 256 devices: a whole 4x4x8 slice. The times are simulated.
256 devices in a mesh: aux: 8 (over y, core), tile: 32 (over z, x).
Axes of the slice: x: 4, y: 4, z: 8, core: 2. Of those that a mesh axis runs over, the one named last changes fastest.
Arguments:
- integrals: bfloat16 [32, 4, 128, 32, 128], P('tile', None, None, 'aux'), may hold values from -6 to 6
- orbitals: bfloat16 [4096, 1024], P('tile'), may hold values from -0.25 to 0.25
- pair_tiles: int32 [32, 4], replicated, may hold values from 0 to 31, as said below
- pair_live: int32 [32, 4], replicated, may hold values from 0 to 1, as said below
- occ_live: int32 [32, 8], replicated, may hold values from 0 to 1, as said below
Outputs:
- exchange_blocks: float32 [32, 4, 128, 128], P('tile', None, 'aux')
Inputs may be any that keep to these rules, and one draw needn't show every extreme that they name: `pair_tiles`: row t holds 4 distinct tiles, none equal to t. `pair_live`: in each row the live slots come first; each tile has 1 to 4 live slots, and some tile has all 4. `occ_live`: each row has exactly 4 ones.
All inputs are finite; a program needn't handle non-finite values.
Results may differ from a plain program's by a relative error of at most 0.0038.
Values may be sent and summed in bfloat16 or wider, within the bound.
No kernel may reach another device: no remote copies, remote signals or barrier semaphores. Data moves between devices by JAX's collectives and lax.ppermute only.
A program may use at most 64 MiB of HBM per device.

v0:
```python
import math

import jax
import jax.numpy as jnp
from jax import lax
from jax.sharding import PartitionSpec as P


def shards(integrals, orbitals, pair_tiles, pair_live, occ_live):
    group_count = lax.axis_size("aux")
    own_tile = lax.axis_index("tile")
    slot_count = integrals.shape[1]
    tile_width = integrals.shape[2]
    aux_rows = integrals.shape[3]
    occ_count = orbitals.shape[1]
    tile_total = pair_tiles.shape[0]
    own_flags = lax.dynamic_index_in_dim(occ_live, own_tile, 0, keepdims=False)
    own_partners = lax.dynamic_index_in_dim(pair_tiles, own_tile, 0, keepdims=False)
    own_live = lax.dynamic_index_in_dim(pair_live, own_tile, 0, keepdims=False)
    integral_blocks = integrals[0].reshape(slot_count, tile_width, aux_rows * tile_width)
    contract_rows = (((0,), (0,)), ((), ()))
    masked = orbitals * jnp.repeat(own_flags, tile_width).astype(orbitals.dtype)[None, :]
    gathered = lax.all_gather(masked, "tile", axis=0, tiled=True)
    totals = jnp.zeros((occ_count, aux_rows * tile_width), jnp.float32)
    for slot in range(slot_count):
        partner_rows = lax.dynamic_slice_in_dim(
            gathered, own_partners[slot] * tile_width, tile_width, 0
        )
        totals = totals + lax.dot_general(
            partner_rows, integral_blocks[slot], contract_rows, preferred_element_type=jnp.float32
        ) * own_live[slot].astype(jnp.float32)
    half_field = totals.astype(jnp.bfloat16).reshape(occ_count, aux_rows, tile_width)
    regrouped = lax.all_to_all(half_field, "tile", split_axis=0, concat_axis=2, tiled=True)
    gram_rows = regrouped.reshape(-1, tile_total, tile_width)
    split_rows = gram_rows.reshape(
        gram_rows.shape[0], tile_total, group_count, tile_width // group_count
    )
    norm_scale = 1.0 / math.sqrt(aux_rows * group_count * occ_count)
    slot_flags = pair_live.astype(jnp.float32) * norm_scale
    gram_terms = []
    for slot in range(slot_count):
        partner_cols = jnp.take(gram_rows, pair_tiles[:, slot], axis=1)
        block = jnp.einsum(
            "rmgc,rmb->gmcb", split_rows, partner_cols, preferred_element_type=jnp.float32
        )
        gram_terms.append(block * slot_flags[:, slot][None, :, None, None])
    partial_sums = jnp.stack(gram_terms, axis=2)
    flat_sums = partial_sums.reshape(
        group_count * tile_total, slot_count, tile_width // group_count, tile_width
    )
    summed = lax.psum_scatter(flat_sums, ("aux", "tile"), scatter_dimension=0, tiled=True)
    return summed


def solution(mesh):
    return jax.shard_map(
        shards,
        mesh=mesh,
        in_specs=(P("tile", None, None, "aux", None), P("tile", None), P(), P(), P()),
        out_specs=P("tile", None, "aux", None),
        check_vma=False,
    )
```

profile of v0, /device:TPU:32, one launch (start us, length us, event | category | flops | bytes accessed | tf_op | source)
XLA Modules:
  0.0 461.8 jit_solution(9836019799548410840)
XLA Ops:
  6.5 0.9 fusion.35
  7.4 0.1 broadcast_bitcast_fusion
  7.5 1.7 broadcast_multiply_fusion
  9.2 0.0 all-gather.2.cloned.1.call-update
  9.2 0.8 constant_dynamic-slice_fusion
  10.0 0.6 fusion.45
  13.0 0.6 fusion.46
  16.2 1.3 fusion.44
  17.5 91.7 %all-gather.2.cloned.1.call-done = bf16[4096,1024]{1,0:T(8,128)(2,1)} async-done(((bf16[128,1024]{1,0:T(8,128)(2,1)}), bf16[4096,1024]{1,0:T(8,128)(2,1)}) %all-gather.2.cloned.1.call-update) | async-done | bytes 8388624 | tf_op jit(solution)/shard_map/all_gather | solution.py:23
  109.1 1.4 fusion.23
  110.6 1.4 fusion.25
  112.0 1.4 fusion.21
  113.4 1.7 add_convert_fusion
  115.1 0.0 copy-start.3
  115.1 0.0 copy-start.4
  115.1 1.4 copy.23
  116.6 7.6 %all-to-all-start = ((bf16[1024,4,128]{2,1,0:T(4,128)(2,1)}), bf16[1024,4,128]{2,1,0:T(4,128)(2,1)S(1)}, u32[]{:S(2)}, u32[]{:S(2)}) async-start(bf16[1024,4,128]{2,1,0:T(4,128)(2,1)} %copy.23), calls=%async_computation | async-start | bytes 2097152 | tf_op jit(solution)/shard_map/all_to_all | solution.py:33
  124.2 0.0 all-reduce.3.cloned.1.call-start
  124.4 26.8 %all-to-all-done = bf16[1024,4,128]{2,1,0:T(4,128)(2,1)S(1)} async-done(((bf16[1024,4,128]{2,1,0:T(4,128)(2,1)}), bf16[1024,4,128]{2,1,0:T(4,128)(2,1)S(1)}, u32[]{:S(2)}, u32[]{:S(2)}) %all-to-all-start) | async-done | bytes 1048608 | tf_op jit(solution)/shard_map/all_to_all | solution.py:33
  151.2 0.1 copy.24
  151.3 3.3 copy.27
  154.6 0.4 copy.25
  155.0 6.9 %copy.28 = bf16[128,32,8,16]{0,3,2,1:T(8,128)(2,1)S(1)} copy(bf16[128,32,8,16]{1,3,2,0:T(8,128)(2,1)} %bitcast.105) | data formatting | bytes 2097152 | tf_op jit(solution)/shard_map/reshape;reshape | solution.py:35
  162.0 0.4 copy.26
  162.4 0.7 gather_fusion
  163.2 0.5 fusion.6
  163.7 0.2 multiply_bitcast_fusion.3
  163.9 1.5 copy.29
  165.4 0.7 gather_fusion.1
  166.1 0.5 fusion.4
  166.7 0.2 multiply_bitcast_fusion.2
  166.9 1.5 copy.32
  168.4 0.7 gather_fusion.2
  169.1 0.5 fusion.2
  169.6 0.2 multiply_bitcast_fusion.1
  169.9 1.5 copy.35
  171.4 0.7 gather_fusion.3
  172.1 0.5 fusion
  172.6 0.0 copy-start.2
  172.7 0.2 multiply_bitcast_fusion
  172.9 0.2 copy.38
  173.1 1.2 copy-done.2
  174.2 0.7 copy-done
  174.9 0.6 copy-done.1
  175.6 3.5 pad_maximum_fusion
  179.1 0.0 all-reduce.3.cloned.1.call-update
  179.1 274.5 %all-reduce.3.cloned.1.call-done = f32[256,4,16,128]{3,2,0,1:T(8,128)} async-done(((f32[256,4,16,128]{3,2,0,1:T(8,128)}), f32[256,4,16,128]{3,2,0,1:T(8,128)}) %all-reduce.3.cloned.1.call-update) | async-done | bytes 8388624
  453.6 1.4 dynamic-slice_bitcast_fusion
  (10 shorter events, 0.0 us)
Async XLA Ops:
  6.5 102.6 %all-gather.2.cloned.1.call-start = ((), (), s32[]{:S(2)}) async-start(), calls=%async_computation.1 | async-start | bytes 8650752 | tf_op jit(solution)/shard_map/all_gather | solution.py:23
  115.1 9.2 %copy-start.3 = (s32[32,4]{0,1:T(4,128)S(1)}, s32[32,4]{0,1:T(4,128)}, u32[]{:S(2)}) copy-start(s32[32,4]{0,1:T(4,128)} %param.9) | copy-start | bytes 1540
  115.1 9.2 %copy-start.4 = (s32[32,4]{0,1:T(4,128)S(1)}, s32[32,4]{0,1:T(4,128)}, u32[]{:S(2)}) copy-start(s32[32,4]{0,1:T(4,128)} %param.10) | copy-start | bytes 1540
  116.6 34.6 %all-to-all-start = ((bf16[1024,4,128]{2,1,0:T(4,128)(2,1)}), bf16[1024,4,128]{2,1,0:T(4,128)(2,1)S(1)}, u32[]{:S(2)}, u32[]{:S(2)}) async-start(bf16[1024,4,128]{2,1,0:T(4,128)(2,1)} %copy.23), calls=%async_computation | async-start | bytes 2097152 | tf_op jit(solution)/shard_map/all_to_all | solution.py:33
  124.2 329.4 %all-reduce.3.cloned.1.call-start = ((), (), s32[]{:S(2)}) async-start(), calls=%async_computation.2 | async-start | bytes 16777216
  172.6 1.6 copy-start.2
  172.9 2.1 copy-start
  172.9 2.7 copy-start.1
Sparse Core Ops, SparseCore 0:
  9.9 99.1 all-gather.1
  179.3 274.2 all-reduce.2
where the time goes:
time: 465 us; the launch traced here: 462 us
  waiting for transfers between devices  393 us (85%)
  local copies, waits for them, and re-layouts  27.6 us (6%)
  between operations  18.7 us (4%)
  matrix products  7.99 us (2%)
  starting transfers between devices  7.67 us (2%)
  other arithmetic  6.93 us (1%)
    unnamed x3, waiting for transfers between devices  274 us
    all_gather x1, waiting for transfers between devices, shards(): gathered = lax.all_gather(masked, 'tile', axis=0, tiled=True)  91.7 us
    all_to_all x1, waiting for transfers between devices, shards(): lax.all_to_all(half_field, 'tile', split_axis=0, concat_axis=2, tiled=True)  26.8 us
  transfers between devices with their start and end apart: 3, of which 3 were waited for; matrix products, arithmetic and copies ran while one was open for 1% of the time, Pallas kernels for 0%

commit v1 on v0

v1 whole, which is shorter than its diff:
```python
import functools
import math

import jax
import jax.numpy as jnp
from jax import lax
from jax.experimental import pallas as pl
from jax.experimental.pallas import tpu as pltpu
from jax.sharding import Mesh, PartitionSpec as P

NY, NC, NZ, NX = 4, 2, 8, 4
TILES, SLOTS, TS = 32, 4, 128
OCC, LIVE = 8, 4
AUXROWS = 4
HALF = TS // 2
ROWS = TS // (NY * NC)
SCALE = 1.0 / math.sqrt(32768.0)
BF = jnp.bfloat16
F32 = jnp.float32
VMEM = pl.BlockSpec(memory_space=pltpu.VMEM)
SMEM = pl.BlockSpec(memory_space=pltpu.SMEM)


def prep_kernel(pos, occ_live, eri, orb, chunks, coeffs, split):
    core, z, tile = pos[1], pos[2], pos[2] * NX + pos[3]
    row = lax.broadcasted_iota(jnp.int32, (TS, TS), 0)
    col = lax.broadcasted_iota(jnp.int32, (TS, TS), 1)
    block_nu = TS // AUXROWS
    perm = (col == (row % block_nu) * AUXROWS + row // block_nu).astype(BF)
    for slot in range(SLOTS):
        for part in range(AUXROWS):
            start = (slot * AUXROWS + part) * TS
            mixed = jnp.dot(perm, eri[pl.ds(start, TS), :], preferred_element_type=F32).astype(BF)
            for aux in range(AUXROWS):
                split[aux, slot, pl.ds(part * block_nu, block_nu), :] = mixed[aux * block_nu:(aux + 1) * block_nu]
    for step in range(NZ):
        target = (z + step) % NZ
        hop = jnp.where(core == target // 4, 0, 1)
        for j in range(2):
            chunks[step, j] = split[target % 4, hop * 2 + j]
    count = jnp.int32(0)
    for occ in range(OCC):
        live = occ_live[tile, occ]

        @pl.when(live != 0)
        def _():
            flipped = orb[:, occ * TS:(occ + 1) * TS].astype(F32).T.astype(BF)
            coeffs[count] = jnp.where(core == 0, flipped[:HALF], flipped[HALF:])

        count = count + jnp.where(live != 0, 1, 0)


def prep(pos, occ_live, eri, orb):
    return pl.pallas_call(
        prep_kernel,
        out_shape=(
            jax.ShapeDtypeStruct((NZ, 2, TS, TS), BF),
            jax.ShapeDtypeStruct((LIVE, HALF, TS), BF),
        ),
        in_specs=[SMEM, SMEM, VMEM, VMEM],
        out_specs=(VMEM, VMEM),
        scratch_shapes=[pltpu.VMEM((AUXROWS, SLOTS, TS, TS), BF)],
        compiler_params=pltpu.CompilerParams(vmem_limit_bytes=16 * 2**20),
        name="prep",
    )(pos, occ_live, eri, orb)


def main_kernel(pos, pair_tiles, pair_live, occ_live,
                own0, own_r, own_l, own_r2, own_l2,
                oth0, oth_r, oth_l, oth_r2, oth_l2,
                c0, cr1, cl1, cr2, cl2, cr3, cl3, cr4, cl4,
                keep, send, dense, field, block):
    core, z, x = pos[1], pos[2], pos[3]

    def place(piece, zp, lo, hi):
        def body(entry, carry):
            tile = zp * NX + (x - entry) % NX
            count = jnp.int32(0)
            for occ in range(OCC):
                live = occ_live[tile, occ] != 0
                data = piece[entry - lo, jnp.minimum(count, LIVE - 1)]
                dense[tile, pl.ds(occ * HALF, HALF), :] = jnp.where(live, data, jnp.zeros_like(data))
                count = count + jnp.where(live, 1, 0)
            return carry

        lax.fori_loop(lo, hi, body, 0)

    for piece, shift, lo, hi in (
        (c0, 0, 0, 4), (cr1, -1, 0, 4), (cl1, 1, 0, 4), (cr2, -2, 0, 4), (cl2, 2, 0, 4),
        (cr3, -3, 0, 4), (cl3, 3, 0, 4), (cr4, 4, 0, 2), (cl4, 4, 2, 4),
    ):
        place(piece, (z + shift) % NZ, lo, hi)

    def transform(xp, own, oth, lo, hi, own_lo, oth_lo):
        def body(step, carry):
            zp = (z - step - 4 * core) % NZ
            tile = zp * NX + xp
            coeffs, eris = [], []
            for part, ref, index in (
                (core, own, step - own_lo),
                (1 - core, oth, (step + 4) % NZ - oth_lo),
            ):
                for j in range(2):
                    slot = part * 2 + j
                    live = pair_live[tile, slot] != 0
                    eri = ref[index, j]
                    eris.append(jnp.where(live, eri, jnp.zeros_like(eri)))
                    coeffs.append(dense[pair_tiles[tile, slot]])
            half = jnp.dot(
                jnp.concatenate(coeffs, axis=1), jnp.concatenate(eris, axis=0), preferred_element_type=F32
            )
            field[tile] = half.astype(BF)
            return carry

        lax.fori_loop(lo, hi, body, 0)

    transform(x, own0, oth0, 0, 8, 0, 0)
    transform((x - 1) % NX, own_r, oth_r, 0, 8, 0, 0)
    transform((x + 1) % NX, own_l, oth_l, 0, 8, 0, 0)
    transform((x + 2) % NX, own_r2, oth_l2, 0, 4, 0, 4)
    transform((x + 2) % NX, own_l2, oth_r2, 4, 8, 4, 0)

    def gram(zp, carry):
        tile = zp * NX + x
        partners = jnp.concatenate([field[pair_tiles[tile, slot]] for slot in range(SLOTS)], axis=1)
        block[...] = lax.dot_general(
            field[tile], partners, (((0,), (0,)), ((), ())), preferred_element_type=F32
        )
        for y in range(NY):
            near = pl.multiple_of(y * 2 * ROWS + core * ROWS, ROWS)
            far = pl.multiple_of(y * 2 * ROWS + (1 - core) * ROWS, ROWS)
            for slot in range(SLOTS):
                keep[y, zp, slot] = block[pl.ds(near, ROWS), slot * TS:(slot + 1) * TS]
                send[y, zp, slot] = block[pl.ds(far, ROWS), slot * TS:(slot + 1) * TS]
        return carry

    lax.fori_loop(0, NZ, gram, 0)


def exchange(*operands):
    shape = jax.ShapeDtypeStruct((NY, NZ, SLOTS, ROWS, TS), F32)
    return pl.pallas_call(
        main_kernel,
        out_shape=(shape, shape),
        in_specs=[SMEM] * 4 + [VMEM] * (len(operands) - 4),
        out_specs=(VMEM, VMEM),
        scratch_shapes=[
            pltpu.VMEM((TILES, OCC * HALF, TS), BF),
            pltpu.VMEM((TILES, OCC * HALF, TS), BF),
            pltpu.VMEM((TS, SLOTS * TS), F32),
        ],
        compiler_params=pltpu.CompilerParams(vmem_limit_bytes=40 * 2**20),
        name="exchange",
    )(*operands)


def shift(value, axis, size, by):
    return lax.ppermute(value, axis, [(i, (i + by) % size) for i in range(size)])


def spread(value, step):
    pairs = []
    for z in range(NZ):
        target = (z + step) % NZ
        core = target // 4
        pairs.append((core * NZ + z, target))
        pairs.append(((1 - core) * NZ + z, NZ + (target + 4) % NZ))
    return lax.ppermute(value, ("c", "z"), pairs)


def swap(value):
    return lax.ppermute(value, "c", [(0, 1), (1, 0)])


def shards(integrals, orbitals, pair_tiles, pair_live, occ_live):
    pos = jnp.stack([lax.axis_index(name).astype(jnp.int32) for name in ("y", "c", "z", "x")])
    tile = pos[2] * NX + pos[3]
    eri = integrals.reshape(SLOTS * TS * AUXROWS, TS)
    chunks, coeffs = prep(pos, occ_live, eri, orbitals)

    own0 = jnp.stack([spread(chunks[step], step) for step in range(NZ)])
    c0 = jnp.stack([coeffs] + [shift(coeffs, "x", NX, by) for by in (1, 2, 3)])

    own_r, own_l = shift(own0, "x", NX, 1), shift(own0, "x", NX, -1)
    cr1, cl1 = shift(c0, "z", NZ, 1), shift(c0, "z", NZ, -1)
    oth0 = swap(own0)
    own_r2, own_l2 = shift(own_r[:4], "x", NX, 1), shift(own_l[4:], "x", NX, -1)
    cr2, cl2 = shift(cr1, "z", NZ, 1), shift(cl1, "z", NZ, -1)
    oth_r, oth_l = swap(own_r), swap(own_l)
    cr3, cl3 = shift(cr2, "z", NZ, 1), shift(cl2, "z", NZ, -1)
    oth_r2, oth_l2 = swap(own_r2), swap(own_l2)
    cr4, cl4 = shift(cr3[:2], "z", NZ, 1), shift(cl3[2:], "z", NZ, -1)

    keep, send = exchange(
        pos, pair_tiles, pair_live, occ_live,
        own0, own_r, own_l, own_r2, own_l2, oth0, oth_r, oth_l, oth_r2, oth_l2,
        c0, cr1, cl1, cr2, cl2, cr3, cl3, cr4, cl4,
    )
    partial = (keep + swap(send)).reshape(NY * NZ, SLOTS, ROWS, TS)
    parts = lax.all_to_all(partial, ("y", "z"), split_axis=0, concat_axis=0, tiled=True)
    flags = lax.dynamic_index_in_dim(pair_live, tile, 0, keepdims=False).astype(F32) * SCALE
    return (jnp.sum(parts, axis=0) * flags[:, None, None])[None]


def solution(mesh):
    grid = Mesh(mesh.devices.reshape(NY, NC, NZ, NX), ("y", "c", "z", "x"))
    return jax.shard_map(
        shards,
        mesh=grid,
        in_specs=(
            P(("z", "x"), None, None, ("y", "c"), None),
            P(("z", "x"), None),
            P(),
            P(),
            P(),
        ),
        out_specs=P(("z", "x"), None, ("y", "c"), None),
        check_vma=False,
    )
```

time: 465 us -> 149 us (0.32)
  waiting for transfers between devices: 393 us -> 71.5 us
  starting transfers between devices: 7.67 us -> 42.9 us
  between operations: 18.7 us -> 0.25 us
  Pallas kernels: 0 us -> 16.7 us
  local copies, waits for them, and re-layouts: 27.6 us -> 14.5 us
  matrix products: 7.99 us -> 0 us
  other arithmetic: 6.93 us -> 2.19 us
    unnamed x3 -> x0, waiting for transfers between devices: 274 us -> none
    all_gather x1 -> x0, waiting for transfers between devices: 91.7 us -> none  [shards(): gathered = lax.all_gather(masked, 'tile', axis=0, tiled=True)]
    ppermute x0 -> x29, waiting for transfers between devices: none -> 43.6 us  [the longest x15 20.8 us: shift(): lax.ppermute(value, axis, [(i, (i + by) % size) for i in range(size)])]
    ppermute x0 -> x29, starting transfers between devices: none -> 35 us  [the longest x15 19.8 us: shift(): lax.ppermute(value, axis, [(i, (i + by) % size) for i in range(size)])]
    pallas_call x0 -> x2, Pallas kernels: none -> 16.7 us  [the longest x1 15.1 us: exchange(): pl.pallas_call(main_kernel, out_shape=(shape, shape), in_specs=[SMEM] * 4...]
    unnamed x10 -> x42, local copies, waits for them, and re-layouts: 2.51 us -> 13.7 us
    another operation x1, local copies, waits for them, and re-layouts: 6.93 us -> 0.01 us  [shards(): own0 = jnp.stack([spread(chunks[step], step) for step in range(NZ)])]
    dot_general x4 -> x0, matrix products: 5.95 us -> none  [shards(): lax.dot_general(partner_rows, integral_blocks[slot], contract_rows, prefe...]
  transfers between devices with their start and end apart: 3 -> 30, of which waited for: 3 -> 12; matrix products, arithmetic and copies ran while one was open for 1% -> 3% of each run, Pallas kernels for 0% -> 0%
where the time goes in v1:
time: 149 us; the launch traced here: 148 us
  waiting for transfers between devices  71.5 us (48%)
  starting transfers between devices  42.9 us (29%)
  Pallas kernels  16.7 us (11%)
  local copies, waits for them, and re-layouts  14.5 us (10%)
  other arithmetic  2.19 us (1%)
    all_to_all x1, waiting for transfers between devices, shards(): lax.all_to_all(partial, ('y', 'z'), split_axis=0, concat_axis=0, tiled=True)  27.9 us
    ppermute x15, waiting for transfers between devices, shift(): lax.ppermute(value, axis, [(i, (i + by) % size) for i in range(size)])  20.8 us
    ppermute x8, waiting for transfers between devices, spread(): return lax.ppermute(value, ('c', 'z'), pairs)  20.1 us
    ppermute x15, starting transfers between devices, shift(): lax.ppermute(value, axis, [(i, (i + by) % size) for i in range(size)])  19.8 us
    pallas_call x1, Pallas kernels, exchange(): pl.pallas_call(main_kernel, out_shape=(shape, shape), in_specs=[SMEM] * 4...  15.1 us
    ppermute x8, starting transfers between devices, spread(): return lax.ppermute(value, ('c', 'z'), pairs)  14.6 us
    unnamed x42, local copies, waits for them, and re-layouts  13.7 us
    all_to_all x1, starting transfers between devices, shards(): lax.all_to_all(partial, ('y', 'z'), split_axis=0, concat_axis=0, tiled=True)  7.89 us
  transfers between devices with their start and end apart: 30, of which 12 were waited for; matrix products, arithmetic and copies ran while one was open for 3% of the time, Pallas kernels for 0%

profile of v1, /device:TPU:32, one launch (start us, length us, event | category | flops | bytes accessed | tf_op | source)
XLA Modules:
  0.0 148.0 jit_solution(9423761818679622334)
XLA Ops:
  0.0 0.7 copy-done.15
  0.8 0.5 copy-done.12
  1.4 1.0 copy-done
  2.4 0.9 copy-done.9
  3.3 1.6 %prep.1 = (bf16[8,2,128,128]{3,2,1,0:T(8,128)(2,1)S(1)}, bf16[4,64,128]{2,1,0:T(8,128)(2,1)S(1)}) custom-call(s32[4]{0:T(128)S(1)} %pad_add_fusion.pos, s32[32,8]{1,0:T(8,128)S(1)} %copy.9.occ_live, bf16[2048,128]{1,0:T(8,128)(2,1)S(1)} %bitcast.44, bf16[128,1024]{1,0:T(8,128)(2,1)S(1)} %copy-done.9), custom_call_target="tpu_custom_call" | custom-call | tf_op jit(solution)/shard_map/prep/pallas_call | solution.py:54
  5.0 0.7 collective-permute-start
  5.6 2.8 %collective-permute-start.19 = (bf16[4,64,128]{2,1,0:T(8,128)(2,1)S(1)}, bf16[4,64,128]{2,1,0:T(8,128)(2,1)S(1)}, u32[]{:S(2)}, u32[]{:S(2)}) collective-permute-start(bf16[4,64,128]{2,1,0:T(8,128)(2,1)S(1)} %get-tuple-element.10), channel_id=1, source_target_pairs={{0,3},{1,0},{2,1},{3,2},{4,7},{5,4},{6,5},{7,6},{8,11},{9,8},{10,9... | collective-permute-start | bytes 196616 | tf_op jit(solution)/shard_map/ppermute | solution.py:158
  8.5 0.8 collective-permute-start.18
  9.3 0.9 collective-permute-start.17
  10.3 1.9 %collective-permute-start.1 = (bf16[2,128,128]{2,1,0:T(8,128)(2,1)S(1)}, bf16[2,128,128]{2,1,0:T(8,128)(2,1)S(1)}, u32[]{:S(2)}, u32[]{:S(2)}) collective-permute-start(bf16[2,128,128]{2,1,0:T(8,128)(2,1)S(1)} %get-tuple-element.19), channel_id=1, source_target_pairs={{0,4},{32,52},{4,8},{36,56},{8,12},{40,60},{44,16},{12,32},{48,20}... | collective-permute-start | bytes 196616 | tf_op jit(solution)/shard_map/ppermute | solution.py:168
  12.2 9.7 %collective-permute-done.1 = bf16[2,128,128]{2,1,0:T(8,128)(2,1)S(1)} collective-permute-done((bf16[2,128,128]{2,1,0:T(8,128)(2,1)S(1)}, bf16[2,128,128]{2,1,0:T(8,128)(2,1)S(1)}, u32[]{:S(2)}, u32[]{:S(2)}) %collective-permute-start.1) | collective-permute-done | bytes 65568 | tf_op jit(solution)/shard_map/ppermute | solution.py:168
  22.3 6.1 %collective-permute-done.2 = bf16[2,128,128]{2,1,0:T(8,128)(2,1)S(1)} collective-permute-done((bf16[2,128,128]{2,1,0:T(8,128)(2,1)S(1)}, bf16[2,128,128]{2,1,0:T(8,128)(2,1)S(1)}, u32[]{:S(2)}, u32[]{:S(2)}) %collective-permute-start.2) | collective-permute-done | bytes 65568 | tf_op jit(solution)/shard_map/ppermute | solution.py:168
  28.4 3.2 %collective-permute-start.6 = (bf16[2,128,128]{2,1,0:T(8,128)(2,1)S(1)}, bf16[2,128,128]{2,1,0:T(8,128)(2,1)S(1)}, u32[]{:S(2)}, u32[]{:S(2)}) collective-permute-start(bf16[2,128,128]{2,1,0:T(8,128)(2,1)S(1)} %get-tuple-element.14), channel_id=1, source_target_pairs={{32,24},{0,40},{36,28},{4,44},{8,0},{40,48},{12,4},{44,52},{16,8},... | collective-permute-start | bytes 196616 | tf_op jit(solution)/shard_map/ppermute | solution.py:168
  31.9 1.9 %collective-permute-start.4 = (bf16[2,128,128]{2,1,0:T(8,128)(2,1)S(1)}, bf16[2,128,128]{2,1,0:T(8,128)(2,1)S(1)}, u32[]{:S(2)}, u32[]{:S(2)}) collective-permute-start(bf16[2,128,128]{2,1,0:T(8,128)(2,1)S(1)} %get-tuple-element.16), channel_id=1, source_target_pairs={{32,16},{0,32},{36,20},{4,36},{40,24},{8,40},{44,28},{12,44},{16,0... | collective-permute-start | bytes 196616 | tf_op jit(solution)/shard_map/ppermute | solution.py:168
  33.8 6.1 %collective-permute-start.3 = (bf16[2,128,128]{2,1,0:T(8,128)(2,1)S(1)}, bf16[2,128,128]{2,1,0:T(8,128)(2,1)S(1)}, u32[]{:S(2)}, u32[]{:S(2)}) collective-permute-start(bf16[2,128,128]{2,1,0:T(8,128)(2,1)S(1)} %get-tuple-element.17), channel_id=1, source_target_pairs={{0,12},{32,60},{36,16},{4,32},{40,20},{8,36},{44,24},{12,40},{48,2... | collective-permute-start | bytes 196616 | tf_op jit(solution)/shard_map/ppermute | solution.py:168
  40.0 4.3 %collective-permute-done.3 = bf16[2,128,128]{2,1,0:T(8,128)(2,1)S(1)} collective-permute-done((bf16[2,128,128]{2,1,0:T(8,128)(2,1)S(1)}, bf16[2,128,128]{2,1,0:T(8,128)(2,1)S(1)}, u32[]{:S(2)}, u32[]{:S(2)}) %collective-permute-start.3) | collective-permute-done | bytes 65568 | tf_op jit(solution)/shard_map/ppermute | solution.py:168
  44.4 2.4 %collective-permute-start.9 = (bf16[8,2,128,128]{3,2,1,0:T(8,128)(2,1)S(1)}, bf16[8,2,128,128]{3,2,1,0:T(8,128)(2,1)S(1)}, u32[]{:S(2)}, u32[]{:S(2)}) collective-permute-start(bf16[8,2,128,128]{3,2,1,0:T(8,128)(2,1)S(1)} %bitcast_dynamic-update-slice_fusion.own0), channel_id=1, source_target_pairs={{0,3},{1,0},{2,1},{3,2},{4,7},{5,4},{6,5},{7,6},{8,11},{9,8},{10,9... | collective-permute-start | bytes 1572872 | tf_op jit(solution)/shard_map/ppermute | solution.py:158
  46.9 2.1 %collective-permute-start.20 = (bf16[4,4,64,128]{3,2,1,0:T(8,128)(2,1)S(1)}, bf16[4,4,64,128]{3,2,1,0:T(8,128)(2,1)S(1)}, u32[]{:S(2)}, u32[]{:S(2)}) collective-permute-start(bf16[4,4,64,128]{3,2,1,0:T(8,128)(2,1)S(1)} %pad_maximum_fusion.c0), channel_id=1, source_target_pairs={{0,4},{4,8},{8,12},{12,16},{16,20},{20,24},{24,28},{28,0},{1,5},{5... | collective-permute-start | bytes 786440 | tf_op jit(solution)/shard_map/ppermute | solution.py:158
  48.9 3.3 %collective-permute-done.21.cl1 = bf16[4,4,64,128]{3,2,1,0:T(8,128)(2,1)S(1)} collective-permute-done((bf16[4,4,64,128]{3,2,1,0:T(8,128)(2,1)S(1)}, bf16[4,4,64,128]{3,2,1,0:T(8,128)(2,1)S(1)}, u32[]{:S(2)}, u32[]{:S(2)}) %collective-permute-start.21) | collective-permute-done | bytes 262176 | tf_op jit(solution)/shard_map/ppermute | solution.py:158
  52.5 0.7 copy-done.1
  53.2 1.9 %collective-permute-done.20.cr1 = bf16[4,4,64,128]{3,2,1,0:T(8,128)(2,1)S(1)} collective-permute-done((bf16[4,4,64,128]{3,2,1,0:T(8,128)(2,1)S(1)}, bf16[4,4,64,128]{3,2,1,0:T(8,128)(2,1)S(1)}, u32[]{:S(2)}, u32[]{:S(2)}) %collective-permute-start.20) | collective-permute-done | bytes 262176 | tf_op jit(solution)/shard_map/ppermute | solution.py:158
  55.1 1.2 collective-permute-start.22
  56.3 3.0 %collective-permute-done.23.cl2 = bf16[4,4,64,128]{3,2,1,0:T(8,128)(2,1)S(1)} collective-permute-done((bf16[4,4,64,128]{3,2,1,0:T(8,128)(2,1)S(1)}, bf16[4,4,64,128]{3,2,1,0:T(8,128)(2,1)S(1)}, u32[]{:S(2)}, u32[]{:S(2)}) %collective-permute-start.23) | collective-permute-done | bytes 262176 | tf_op jit(solution)/shard_map/ppermute | solution.py:158
  59.3 1.0 collective-permute-start.25
  60.3 3.3 %collective-permute-start.11 = (bf16[4,2,128,128]{3,2,1,0:T(8,128)(2,1)S(1)}, bf16[4,2,128,128]{3,2,1,0:T(8,128)(2,1)}, u32[]{:S(2)}, u32[]{:S(2)}) collective-permute-start(bf16[4,2,128,128]{3,2,1,0:T(8,128)(2,1)S(1)} %slice.49), channel_id=1, source_target_pairs={{0,3},{1,0},{2,1},{3,2},{4,7},{5,4},{6,5},{7,6},{8,11},{9,8},{10,9... | collective-permute-start | bytes 786440 | tf_op jit(solution)/shard_map/ppermute | solution.py:158
  64.3 1.3 collective-permute-done.25.cl3
  65.6 1.8 %collective-permute-start.10 = (bf16[4,2,128,128]{3,2,1,0:T(8,128)(2,1)S(1)}, bf16[4,2,128,128]{3,2,1,0:T(8,128)(2,1)}, u32[]{:S(2)}, u32[]{:S(2)}) collective-permute-start(bf16[4,2,128,128]{3,2,1,0:T(8,128)(2,1)S(1)} %slice.48), channel_id=1, source_target_pairs={{0,1},{1,2},{2,3},{3,0},{4,5},{5,6},{6,7},{7,4},{8,9},{9,10},{10,1... | collective-permute-start | bytes 786440 | tf_op jit(solution)/shard_map/ppermute | solution.py:158
  67.5 6.8 %collective-permute-done.24.cr3 = bf16[4,4,64,128]{3,2,1,0:T(8,128)(2,1)S(1)} collective-permute-done((bf16[4,4,64,128]{3,2,1,0:T(8,128)(2,1)S(1)}, bf16[4,4,64,128]{3,2,1,0:T(8,128)(2,1)S(1)}, u32[]{:S(2)}, u32[]{:S(2)}) %collective-permute-start.24) | collective-permute-done | bytes 262176 | tf_op jit(solution)/shard_map/ppermute | solution.py:158
  74.3 3.0 %collective-permute-start.27 = (bf16[2,4,64,128]{3,2,1,0:T(8,128)(2,1)S(1)}, bf16[2,4,64,128]{3,2,1,0:T(8,128)(2,1)S(1)}, u32[]{:S(2)}, u32[]{:S(2)}) collective-permute-start(bf16[2,4,64,128]{3,2,1,0:T(8,128)(2,1)S(1)} %slice.51), channel_id=1, source_target_pairs={{0,28},{4,0},{8,4},{12,8},{16,12},{20,16},{24,20},{28,24},{1,29},{... | collective-permute-start | bytes 393224 | tf_op jit(solution)/shard_map/ppermute | solution.py:158
  77.8 0.7 slice.50
  78.4 1.5 %collective-permute-done.27.cl4 = bf16[2,4,64,128]{3,2,1,0:T(8,128)(2,1)S(1)} collective-permute-done((bf16[2,4,64,128]{3,2,1,0:T(8,128)(2,1)S(1)}, bf16[2,4,64,128]{3,2,1,0:T(8,128)(2,1)S(1)}, u32[]{:S(2)}, u32[]{:S(2)}) %collective-permute-start.27) | collective-permute-done | bytes 131104 | tf_op jit(solution)/shard_map/ppermute | solution.py:158
  79.9 1.4 copy.7.pair_tiles
  81.3 1.4 copy.8.pair_live
  82.6 3.0 %collective-permute-done.26.cr4 = bf16[2,4,64,128]{3,2,1,0:T(8,128)(2,1)} collective-permute-done((bf16[2,4,64,128]{3,2,1,0:T(8,128)(2,1)}, bf16[2,4,64,128]{3,2,1,0:T(8,128)(2,1)}, u32[]{:S(2)}, u32[]{:S(2)}) %collective-permute-start.26) | collective-permute-done | bytes 131104 | tf_op jit(solution)/shard_map/ppermute | solution.py:158
  85.7 0.9 copy-done.2
  86.6 0.9 copy-done.4
  87.6 0.9 copy-done.6
  88.5 0.9 copy-done.8
  89.5 0.7 copy-done.10
  90.2 0.7 copy-done.11
  90.9 0.6 copy-done.13
  91.5 15.1 %exchange.1 = (f32[4,8,4,16,128]{4,3,2,1,0:T(8,128)S(1)}, f32[4,8,4,16,128]{4,3,2,1,0:T(8,128)S(1)}) custom-call(s32[4]{0:T(128)S(1)} %copy-done.13, s32[32,4]{1,0:T(8,128)S(1)} %copy-done.10, s32[32,4]{1,0:T(8,128)S(1)} %copy-done.11, s32[32,8]{1,0:T(8,128)S(1)} %copy.9.occ_live, bf16[8,2,128,128]{3,2,1,0:T(8,128)(2,1)S(1)} %bitcast_dynamic-update-slice_fusion.own0, ...), custom_call_target="tpu_custom_call" | custom-call | tf_op jit(solution)/shard_map/exchange/pallas_call | solution.py:142
  106.8 2.6 %collective-permute-done.28 = f32[4,8,4,16,128]{4,3,2,1,0:T(8,128)S(1)} collective-permute-done((f32[4,8,4,16,128]{4,3,2,1,0:T(8,128)S(1)}, f32[4,8,4,16,128]{4,3,2,1,0:T(8,128)S(1)}, u32[]{:S(2)}, u32[]{:S(2)}) %collective-permute-start.28) | collective-permute-done | bytes 1048608 | tf_op jit(solution)/shard_map/ppermute | solution.py:172
  109.4 1.1 add.10
  110.5 7.9 %all-to-all-start = ((f32[32,4,16,128]{3,2,1,0:T(8,128)}), f32[32,4,16,128]{3,2,1,0:T(8,128)S(1)}, u32[]{:S(2)}, u32[]{:S(2)}) async-start(f32[32,4,16,128]{3,2,1,0:T(8,128)} %bitcast.25), calls=%async_computation | async-start | bytes 2097152 | tf_op jit(solution)/shard_map/all_to_all | solution.py:200
  118.5 0.7 copy-done.14
  119.3 27.9 %all-to-all-done = f32[32,4,16,128]{3,2,1,0:T(8,128)S(1)} async-done(((f32[32,4,16,128]{3,2,1,0:T(8,128)}), f32[32,4,16,128]{3,2,1,0:T(8,128)S(1)}, u32[]{:S(2)}, u32[]{:S(2)}) %all-to-all-start) | async-done | bytes 1048608 | tf_op jit(solution)/shard_map/all_to_all | solution.py:200
  147.3 0.7 bitcast_multiply_fusion
  (68 shorter events, 3.0 us)
Async XLA Ops:
  0.0 0.7 copy-start.15
  0.8 0.5 copy-start.12
  1.4 1.0 copy-start
  2.4 0.9 copy-start.9
  5.0 5.3 %collective-permute-start = (bf16[2,128,128]{2,1,0:T(8,128)(2,1)S(1)}, bf16[2,128,128]{2,1,0:T(8,128)(2,1)S(1)}, u32[]{:S(2)}, u32[]{:S(2)}) collective-permute-start(bf16[2,128,128]{2,1,0:T(8,128)(2,1)S(1)} %get-tuple-element.20), channel_id=1, source_target_pairs={{0,0},{32,48},{4,4},{36,52},{8,8},{40,56},{12,12},{44,60},{48,16},... | collective-permute-start | bytes 196616 | tf_op jit(solution)/shard_map/ppermute | solution.py:168
  5.6 26.0 %collective-permute-start.19 = (bf16[4,64,128]{2,1,0:T(8,128)(2,1)S(1)}, bf16[4,64,128]{2,1,0:T(8,128)(2,1)S(1)}, u32[]{:S(2)}, u32[]{:S(2)}) collective-permute-start(bf16[4,64,128]{2,1,0:T(8,128)(2,1)S(1)} %get-tuple-element.10), channel_id=1, source_target_pairs={{0,3},{1,0},{2,1},{3,2},{4,7},{5,4},{6,5},{7,6},{8,11},{9,8},{10,9... | collective-permute-start | bytes 196616 | tf_op jit(solution)/shard_map/ppermute | solution.py:158
  8.5 23.4 %collective-permute-start.18 = (bf16[4,64,128]{2,1,0:T(8,128)(2,1)S(1)}, bf16[4,64,128]{2,1,0:T(8,128)(2,1)S(1)}, u32[]{:S(2)}, u32[]{:S(2)}) collective-permute-start(bf16[4,64,128]{2,1,0:T(8,128)(2,1)S(1)} %get-tuple-element.10), channel_id=1, source_target_pairs={{0,2},{1,3},{2,0},{3,1},{4,6},{5,7},{6,4},{7,5},{8,10},{9,11},{10,... | collective-permute-start | bytes 196616 | tf_op jit(solution)/shard_map/ppermute | solution.py:158
  9.3 24.5 %collective-permute-start.17 = (bf16[4,64,128]{2,1,0:T(8,128)(2,1)S(1)}, bf16[4,64,128]{2,1,0:T(8,128)(2,1)S(1)}, u32[]{:S(2)}, u32[]{:S(2)}) collective-permute-start(bf16[4,64,128]{2,1,0:T(8,128)(2,1)S(1)} %get-tuple-element.10), channel_id=1, source_target_pairs={{0,1},{1,2},{2,3},{3,0},{4,5},{5,6},{6,7},{7,4},{8,9},{9,10},{10,1... | collective-permute-start | bytes 196616 | tf_op jit(solution)/shard_map/ppermute | solution.py:158
  10.2 34.2 %collective-permute-start.7 = (bf16[2,128,128]{2,1,0:T(8,128)(2,1)S(1)}, bf16[2,128,128]{2,1,0:T(8,128)(2,1)S(1)}, u32[]{:S(2)}, u32[]{:S(2)}) collective-permute-start(bf16[2,128,128]{2,1,0:T(8,128)(2,1)S(1)} %get-tuple-element.13), channel_id=1, source_target_pairs={{32,28},{0,44},{4,0},{36,48},{8,4},{40,52},{12,8},{44,56},{16,12},... | collective-permute-start | bytes 196616 | tf_op jit(solution)/shard_map/ppermute | solution.py:168
  10.3 11.6 %collective-permute-start.1 = (bf16[2,128,128]{2,1,0:T(8,128)(2,1)S(1)}, bf16[2,128,128]{2,1,0:T(8,128)(2,1)S(1)}, u32[]{:S(2)}, u32[]{:S(2)}) collective-permute-start(bf16[2,128,128]{2,1,0:T(8,128)(2,1)S(1)} %get-tuple-element.19), channel_id=1, source_target_pairs={{0,4},{32,52},{4,8},{36,56},{8,12},{40,60},{44,16},{12,32},{48,20}... | collective-permute-start | bytes 196616 | tf_op jit(solution)/shard_map/ppermute | solution.py:168
  21.9 6.5 %collective-permute-start.2 = (bf16[2,128,128]{2,1,0:T(8,128)(2,1)S(1)}, bf16[2,128,128]{2,1,0:T(8,128)(2,1)S(1)}, u32[]{:S(2)}, u32[]{:S(2)}) collective-permute-start(bf16[2,128,128]{2,1,0:T(8,128)(2,1)S(1)} %get-tuple-element.18), channel_id=1, source_target_pairs={{0,8},{32,56},{4,12},{36,60},{40,16},{8,32},{44,20},{12,36},{48,24... | collective-permute-start | bytes 196616 | tf_op jit(solution)/shard_map/ppermute | solution.py:168
  28.4 16.0 %collective-permute-start.6 = (bf16[2,128,128]{2,1,0:T(8,128)(2,1)S(1)}, bf16[2,128,128]{2,1,0:T(8,128)(2,1)S(1)}, u32[]{:S(2)}, u32[]{:S(2)}) collective-permute-start(bf16[2,128,128]{2,1,0:T(8,128)(2,1)S(1)} %get-tuple-element.14), channel_id=1, source_target_pairs={{32,24},{0,40},{36,28},{4,44},{8,0},{40,48},{12,4},{44,52},{16,8},... | collective-permute-start | bytes 196616 | tf_op jit(solution)/shard_map/ppermute | solution.py:168
  31.6 12.7 %collective-permute-start.5 = (bf16[2,128,128]{2,1,0:T(8,128)(2,1)S(1)}, bf16[2,128,128]{2,1,0:T(8,128)(2,1)S(1)}, u32[]{:S(2)}, u32[]{:S(2)}) collective-permute-start(bf16[2,128,128]{2,1,0:T(8,128)(2,1)S(1)} %get-tuple-element.15), channel_id=1, source_target_pairs={{32,20},{0,36},{36,24},{4,40},{40,28},{8,44},{12,0},{44,48},{16,4}... | collective-permute-start | bytes 196616 | tf_op jit(solution)/shard_map/ppermute | solution.py:168
  31.9 12.4 %collective-permute-start.4 = (bf16[2,128,128]{2,1,0:T(8,128)(2,1)S(1)}, bf16[2,128,128]{2,1,0:T(8,128)(2,1)S(1)}, u32[]{:S(2)}, u32[]{:S(2)}) collective-permute-start(bf16[2,128,128]{2,1,0:T(8,128)(2,1)S(1)} %get-tuple-element.16), channel_id=1, source_target_pairs={{32,16},{0,32},{36,20},{4,36},{40,24},{8,40},{44,28},{12,44},{16,0... | collective-permute-start | bytes 196616 | tf_op jit(solution)/shard_map/ppermute | solution.py:168
  33.8 10.5 %collective-permute-start.3 = (bf16[2,128,128]{2,1,0:T(8,128)(2,1)S(1)}, bf16[2,128,128]{2,1,0:T(8,128)(2,1)S(1)}, u32[]{:S(2)}, u32[]{:S(2)}) collective-permute-start(bf16[2,128,128]{2,1,0:T(8,128)(2,1)S(1)} %get-tuple-element.17), channel_id=1, source_target_pairs={{0,12},{32,60},{36,16},{4,32},{40,20},{8,36},{44,24},{12,40},{48,2... | collective-permute-start | bytes 196616 | tf_op jit(solution)/shard_map/ppermute | solution.py:168
  44.3 8.0 %collective-permute-start.21 = (bf16[4,4,64,128]{3,2,1,0:T(8,128)(2,1)S(1)}, bf16[4,4,64,128]{3,2,1,0:T(8,128)(2,1)S(1)}, u32[]{:S(2)}, u32[]{:S(2)}) collective-permute-start(bf16[4,4,64,128]{3,2,1,0:T(8,128)(2,1)S(1)} %pad_maximum_fusion.c0), channel_id=1, source_target_pairs={{0,28},{4,0},{8,4},{12,8},{16,12},{20,16},{24,20},{28,24},{1,29},{... | collective-permute-start | bytes 786440 | tf_op jit(solution)/shard_map/ppermute | solution.py:158
  44.4 15.8 %collective-permute-start.9 = (bf16[8,2,128,128]{3,2,1,0:T(8,128)(2,1)S(1)}, bf16[8,2,128,128]{3,2,1,0:T(8,128)(2,1)S(1)}, u32[]{:S(2)}, u32[]{:S(2)}) collective-permute-start(bf16[8,2,128,128]{3,2,1,0:T(8,128)(2,1)S(1)} %bitcast_dynamic-update-slice_fusion.own0), channel_id=1, source_target_pairs={{0,3},{1,0},{2,1},{3,2},{4,7},{5,4},{6,5},{7,6},{8,11},{9,8},{10,9... | collective-permute-start | bytes 1572872 | tf_op jit(solution)/shard_map/ppermute | solution.py:158
  46.9 8.2 %collective-permute-start.20 = (bf16[4,4,64,128]{3,2,1,0:T(8,128)(2,1)S(1)}, bf16[4,4,64,128]{3,2,1,0:T(8,128)(2,1)S(1)}, u32[]{:S(2)}, u32[]{:S(2)}) collective-permute-start(bf16[4,4,64,128]{3,2,1,0:T(8,128)(2,1)S(1)} %pad_maximum_fusion.c0), channel_id=1, source_target_pairs={{0,4},{4,8},{8,12},{12,16},{16,20},{20,24},{24,28},{28,0},{1,5},{5... | collective-permute-start | bytes 786440 | tf_op jit(solution)/shard_map/ppermute | solution.py:158
  48.9 14.7 %collective-permute-start.8 = (bf16[8,2,128,128]{3,2,1,0:T(8,128)(2,1)S(1)}, bf16[8,2,128,128]{3,2,1,0:T(8,128)(2,1)S(1)}, u32[]{:S(2)}, u32[]{:S(2)}) collective-permute-start(bf16[8,2,128,128]{3,2,1,0:T(8,128)(2,1)S(1)} %bitcast_dynamic-update-slice_fusion.own0), channel_id=1, source_target_pairs={{0,1},{1,2},{2,3},{3,0},{4,5},{5,6},{6,7},{7,4},{8,9},{9,10},{10,1... | collective-permute-start | bytes 1572872 | tf_op jit(solution)/shard_map/ppermute | solution.py:158
  48.9 15.4 %collective-permute-start.12 = (bf16[8,2,128,128]{3,2,1,0:T(8,128)(2,1)S(1)}, bf16[8,2,128,128]{3,2,1,0:T(8,128)(2,1)S(1)}, u32[]{:S(2)}, u32[]{:S(2)}) collective-permute-start(bf16[8,2,128,128]{3,2,1,0:T(8,128)(2,1)S(1)} %bitcast_dynamic-update-slice_fusion.own0), channel_id=1, source_target_pairs={{0,32},{32,0},{1,33},{33,1},{2,34},{34,2},{3,35},{35,3},{4,36},{36... | collective-permute-start | bytes 1572872 | tf_op jit(solution)/shard_map/ppermute | solution.py:172
  52.2 7.0 %collective-permute-start.23 = (bf16[4,4,64,128]{3,2,1,0:T(8,128)(2,1)S(1)}, bf16[4,4,64,128]{3,2,1,0:T(8,128)(2,1)S(1)}, u32[]{:S(2)}, u32[]{:S(2)}) collective-permute-start(bf16[4,4,64,128]{3,2,1,0:T(8,128)(2,1)S(1)} %collective-permute-done.21.cl1), channel_id=1, source_target_pairs={{0,28},{4,0},{8,4},{12,8},{16,12},{20,16},{24,20},{28,24},{1,29},{... | collective-permute-start | bytes 786440 | tf_op jit(solution)/shard_map/ppermute | solution.py:158
  52.5 0.7 copy-start.1
  55.1 5.2 %copy-start.3 = (bf16[4,4,64,128]{3,2,1,0:T(8,128)(2,1)}, bf16[4,4,64,128]{3,2,1,0:T(8,128)(2,1)S(1)}, u32[]{:S(2)}) copy-start(bf16[4,4,64,128]{3,2,1,0:T(8,128)(2,1)S(1)} %collective-permute-done.20.cr1) | copy-start | bytes 786436
  55.1 8.5 %collective-permute-start.22 = (bf16[4,4,64,128]{3,2,1,0:T(8,128)(2,1)S(1)}, bf16[4,4,64,128]{3,2,1,0:T(8,128)(2,1)S(1)}, u32[]{:S(2)}, u32[]{:S(2)}) collective-permute-start(bf16[4,4,64,128]{3,2,1,0:T(8,128)(2,1)S(1)} %collective-permute-done.20.cr1), channel_id=1, source_target_pairs={{0,4},{4,8},{8,12},{12,16},{16,20},{20,24},{24,28},{28,0},{1,5},{5... | collective-permute-start | bytes 786440 | tf_op jit(solution)/shard_map/ppermute | solution.py:158
  59.3 1.0 copy-start.5
  59.3 6.4 %collective-permute-start.25 = (bf16[4,4,64,128]{3,2,1,0:T(8,128)(2,1)S(1)}, bf16[4,4,64,128]{3,2,1,0:T(8,128)(2,1)S(1)}, u32[]{:S(2)}, u32[]{:S(2)}) collective-permute-start(bf16[4,4,64,128]{3,2,1,0:T(8,128)(2,1)S(1)} %collective-permute-done.23.cl2), channel_id=1, source_target_pairs={{0,28},{4,0},{8,4},{12,8},{16,12},{20,16},{24,20},{28,24},{1,29},{... | collective-permute-start | bytes 786440 | tf_op jit(solution)/shard_map/ppermute | solution.py:158
  60.3 17.0 %collective-permute-start.11 = (bf16[4,2,128,128]{3,2,1,0:T(8,128)(2,1)S(1)}, bf16[4,2,128,128]{3,2,1,0:T(8,128)(2,1)}, u32[]{:S(2)}, u32[]{:S(2)}) collective-permute-start(bf16[4,2,128,128]{3,2,1,0:T(8,128)(2,1)S(1)} %slice.49), channel_id=1, source_target_pairs={{0,3},{1,0},{2,1},{3,2},{4,7},{5,4},{6,5},{7,6},{8,11},{9,8},{10,9... | collective-permute-start | bytes 786440 | tf_op jit(solution)/shard_map/ppermute | solution.py:158
  63.6 0.7 copy-start.7
  63.6 22.1 %collective-permute-start.14 = (bf16[8,2,128,128]{3,2,1,0:T(8,128)(2,1)S(1)}, bf16[8,2,128,128]{3,2,1,0:T(8,128)(2,1)S(1)}, u32[]{:S(2)}, u32[]{:S(2)}) collective-permute-start(bf16[8,2,128,128]{3,2,1,0:T(8,128)(2,1)S(1)} %collective-permute-done.9.own_l), channel_id=1, source_target_pairs={{0,32},{32,0},{1,33},{33,1},{2,34},{34,2},{3,35},{35,3},{4,36},{36... | collective-permute-start | bytes 1572872 | tf_op jit(solution)/shard_map/ppermute | solution.py:172
  63.6 10.7 %collective-permute-start.24 = (bf16[4,4,64,128]{3,2,1,0:T(8,128)(2,1)S(1)}, bf16[4,4,64,128]{3,2,1,0:T(8,128)(2,1)S(1)}, u32[]{:S(2)}, u32[]{:S(2)}) collective-permute-start(bf16[4,4,64,128]{3,2,1,0:T(8,128)(2,1)S(1)} %collective-permute-done.22.cr2), channel_id=1, source_target_pairs={{0,4},{4,8},{8,12},{12,16},{16,20},{20,24},{24,28},{28,0},{1,5},{5... | collective-permute-start | bytes 786440 | tf_op jit(solution)/shard_map/ppermute | solution.py:158
  64.3 21.3 %collective-permute-start.13 = (bf16[8,2,128,128]{3,2,1,0:T(8,128)(2,1)S(1)}, bf16[8,2,128,128]{3,2,1,0:T(8,128)(2,1)}, u32[]{:S(2)}, u32[]{:S(2)}) collective-permute-start(bf16[8,2,128,128]{3,2,1,0:T(8,128)(2,1)S(1)} %collective-permute-done.8.own_r), channel_id=1, source_target_pairs={{0,32},{32,0},{1,33},{33,1},{2,34},{34,2},{3,35},{35,3},{4,36},{36... | collective-permute-start | bytes 1572872 | tf_op jit(solution)/shard_map/ppermute | solution.py:172
  65.6 11.6 %collective-permute-start.10 = (bf16[4,2,128,128]{3,2,1,0:T(8,128)(2,1)S(1)}, bf16[4,2,128,128]{3,2,1,0:T(8,128)(2,1)}, u32[]{:S(2)}, u32[]{:S(2)}) collective-permute-start(bf16[4,2,128,128]{3,2,1,0:T(8,128)(2,1)S(1)} %slice.48), channel_id=1, source_target_pairs={{0,1},{1,2},{2,3},{3,0},{4,5},{5,6},{6,7},{7,4},{8,9},{9,10},{10,1... | collective-permute-start | bytes 786440 | tf_op jit(solution)/shard_map/ppermute | solution.py:158
  74.3 5.6 %collective-permute-start.27 = (bf16[2,4,64,128]{3,2,1,0:T(8,128)(2,1)S(1)}, bf16[2,4,64,128]{3,2,1,0:T(8,128)(2,1)S(1)}, u32[]{:S(2)}, u32[]{:S(2)}) collective-permute-start(bf16[2,4,64,128]{3,2,1,0:T(8,128)(2,1)S(1)} %slice.51), channel_id=1, source_target_pairs={{0,28},{4,0},{8,4},{12,8},{16,12},{20,16},{24,20},{28,24},{1,29},{... | collective-permute-start | bytes 393224 | tf_op jit(solution)/shard_map/ppermute | solution.py:158
  77.3 8.4 %collective-permute-start.16 = (bf16[4,2,128,128]{3,2,1,0:T(8,128)(2,1)}, bf16[4,2,128,128]{3,2,1,0:T(8,128)(2,1)}, u32[]{:S(2)}, u32[]{:S(2)}) collective-permute-start(bf16[4,2,128,128]{3,2,1,0:T(8,128)(2,1)} %collective-permute-done.11.own_l2), channel_id=1, source_target_pairs={{0,32},{32,0},{1,33},{33,1},{2,34},{34,2},{3,35},{35,3},{4,36},{36... | collective-permute-start | bytes 786440 | tf_op jit(solution)/shard_map/ppermute | solution.py:172
  77.3 8.4 %collective-permute-start.15 = (bf16[4,2,128,128]{3,2,1,0:T(8,128)(2,1)}, bf16[4,2,128,128]{3,2,1,0:T(8,128)(2,1)}, u32[]{:S(2)}, u32[]{:S(2)}) collective-permute-start(bf16[4,2,128,128]{3,2,1,0:T(8,128)(2,1)} %collective-permute-done.10.own_r2), channel_id=1, source_target_pairs={{0,32},{32,0},{1,33},{33,1},{2,34},{34,2},{3,35},{35,3},{4,36},{36... | collective-permute-start | bytes 786440 | tf_op jit(solution)/shard_map/ppermute | solution.py:172
  79.9 5.7 %collective-permute-start.26 = (bf16[2,4,64,128]{3,2,1,0:T(8,128)(2,1)}, bf16[2,4,64,128]{3,2,1,0:T(8,128)(2,1)}, u32[]{:S(2)}, u32[]{:S(2)}) collective-permute-start(bf16[2,4,64,128]{3,2,1,0:T(8,128)(2,1)} %slice.50), channel_id=1, source_target_pairs={{0,4},{4,8},{8,12},{12,16},{16,20},{20,24},{24,28},{28,0},{1,5},{5... | collective-permute-start | bytes 393224 | tf_op jit(solution)/shard_map/ppermute | solution.py:158
  85.7 1.0 copy-start.2
  86.6 0.9 copy-start.4
  87.6 0.9 copy-start.6
  88.5 0.9 copy-start.8
  89.5 0.7 copy-start.10
  90.2 0.7 copy-start.11
  90.9 0.6 copy-start.13
  106.7 2.7 %collective-permute-start.28 = (f32[4,8,4,16,128]{4,3,2,1,0:T(8,128)S(1)}, f32[4,8,4,16,128]{4,3,2,1,0:T(8,128)S(1)}, u32[]{:S(2)}, u32[]{:S(2)}) collective-permute-start(f32[4,8,4,16,128]{4,3,2,1,0:T(8,128)S(1)} %get-tuple-element.12), channel_id=1, source_target_pairs={{0,32},{32,0},{1,33},{33,1},{2,34},{34,2},{3,35},{35,3},{4,36},{36... | collective-permute-start | bytes 3145736 | tf_op jit(solution)/shard_map/ppermute | solution.py:172
  110.5 36.7 %all-to-all-start = ((f32[32,4,16,128]{3,2,1,0:T(8,128)}), f32[32,4,16,128]{3,2,1,0:T(8,128)S(1)}, u32[]{:S(2)}, u32[]{:S(2)}) async-start(f32[32,4,16,128]{3,2,1,0:T(8,128)} %bitcast.25), calls=%async_computation | async-start | bytes 2097152 | tf_op jit(solution)/shard_map/all_to_all | solution.py:200
  118.4 0.7 copy-start.14

commit v2 on v1

v2 whole, which is shorter than its diff:
```python
import functools
import math

import jax
import jax.numpy as jnp
from jax import lax
from jax.experimental import pallas as pl
from jax.experimental.pallas import tpu as pltpu
from jax.sharding import Mesh, PartitionSpec as P

NY, NC, NZ, NX = 4, 2, 8, 4
TILES, SLOTS, TS = 32, 4, 128
OCC, LIVE = 8, 4
AUXROWS = 4
HALF = TS // 2
ROWS = TS // (NY * NC)
SCALE = 1.0 / math.sqrt(32768.0)
BF = jnp.bfloat16
F32 = jnp.float32
VMEM = pl.BlockSpec(memory_space=pltpu.VMEM)
SMEM = pl.BlockSpec(memory_space=pltpu.SMEM)
ANY = pl.BlockSpec(memory_space=pl.ANY)


def prep_kernel(pos, occ_live, eri, orb, keep, give, coeffs, rows, cols, sems):
    core, tile = pos[1], pos[2] * NX + pos[3]
    load_cols = pltpu.make_async_copy(orb, cols, sems.at[0])
    load_rows = pltpu.make_async_copy(eri, rows, sems.at[1])
    load_cols.start()
    load_rows.start()
    load_cols.wait()
    count = jnp.int32(0)
    for occ in range(OCC):
        live = occ_live[tile, occ]

        @pl.when(live != 0)
        def _():
            flipped = cols[:, occ * TS:(occ + 1) * TS].astype(F32).T.astype(BF)
            coeffs[jnp.minimum(count, LIVE - 1)] = jnp.where(core == 0, flipped[:HALF], flipped[HALF:])

        count = count + jnp.where(live != 0, 1, 0)
    row = lax.broadcasted_iota(jnp.int32, (TS, TS), 0)
    col = lax.broadcasted_iota(jnp.int32, (TS, TS), 1)
    block_nu = TS // AUXROWS
    perm = (col == (row % block_nu) * AUXROWS + row // block_nu).astype(BF)
    load_rows.wait()
    for out, part in ((give, 1 - core), (keep, core)):
        for j in range(2):
            for quarter in range(AUXROWS):
                start = pl.multiple_of(((part * 2 + j) * AUXROWS + quarter) * TS, TS)
                mixed = jnp.dot(perm, rows[pl.ds(start, TS), :], preferred_element_type=F32).astype(BF)
                for aux in range(AUXROWS):
                    out[aux, j, pl.ds(quarter * block_nu, block_nu), :] = mixed[aux * block_nu:(aux + 1) * block_nu]


def prep(pos, occ_live, eri, orb):
    piece = jax.ShapeDtypeStruct((AUXROWS, 2, TS, TS), BF)
    return pl.pallas_call(
        prep_kernel,
        out_shape=(piece, piece, jax.ShapeDtypeStruct((LIVE, HALF, TS), BF)),
        in_specs=[SMEM, SMEM, ANY, ANY],
        out_specs=(VMEM, VMEM, VMEM),
        scratch_shapes=[
            pltpu.VMEM(eri.shape, BF),
            pltpu.VMEM(orb.shape, BF),
            pltpu.SemaphoreType.DMA((2,)),
        ],
        compiler_params=pltpu.CompilerParams(vmem_limit_bytes=16 * 2**20),
        name="prep",
    )(pos, occ_live, eri, orb)


def main_kernel(pos, pair_tiles, pair_live, occ_index, *refs):
    inputs, (keep, send), scratch = refs[:11], refs[11:13], refs[13:]
    held, (dense, field, block, sems) = scratch[:11], scratch[11:]
    core, x = pos[1], pos[3]
    loads = [pltpu.make_async_copy(src, dst, sems.at[i]) for i, (src, dst) in enumerate(zip(inputs, held))]
    for load in loads:
        load.start()
    coeffs, own0, own_r, own_l, own_r2, own_l2, oth0, oth_r, oth_l, oth_r2, oth_l2 = held

    def clear(tile, carry):
        dense[tile] = jnp.zeros(dense.shape[1:], BF)
        return carry

    lax.fori_loop(0, TILES, clear, 0, unroll=4)
    loads[0].wait()

    def place(tile, carry):
        for k in range(LIVE):
            start = pl.multiple_of(occ_index[tile, k] * HALF, HALF)
            dense[tile, pl.ds(start, HALF), :] = coeffs[tile // NX, tile % NX, k]
        return carry

    lax.fori_loop(0, TILES, place, 0, unroll=4)

    def transform(xp, own, oth, lo, count):
        def body(step, carry):
            tile = (lo + step) * NX + xp
            lhs, rhs = [], []
            for part, ref in ((core, own), (1 - core, oth)):
                for j in range(2):
                    slot = part * 2 + j
                    eri = ref[step, j]
                    rhs.append(jnp.where(pair_live[tile, slot] != 0, eri, jnp.zeros_like(eri)))
                    lhs.append(dense[pair_tiles[tile, slot]])
            half = jnp.dot(
                jnp.concatenate(lhs, axis=1), jnp.concatenate(rhs, axis=0), preferred_element_type=F32
            )
            field[tile] = half.astype(BF)
            return carry

        lax.fori_loop(0, count, body, 0, unroll=4)

    for own, oth, xp, lo, count, first in (
        (own0, oth0, x, 0, 8, 1),
        (own_r, oth_r, (x + 3) % NX, 0, 8, 2),
        (own_l, oth_l, (x + 1) % NX, 0, 8, 3),
        (own_r2, oth_r2, (x + 2) % NX, 0, 4, 4),
        (own_l2, oth_l2, (x + 2) % NX, 4, 4, 5),
    ):
        loads[first].wait()
        loads[first + 5].wait()
        transform(xp, own, oth, lo, count)

    def gram(zp, carry):
        tile = zp * NX + x
        partners = jnp.concatenate([field[pair_tiles[tile, slot]] for slot in range(SLOTS)], axis=1)
        block[...] = lax.dot_general(
            field[tile], partners, (((0,), (0,)), ((), ())), preferred_element_type=F32
        )
        for y in range(NY):
            near = pl.multiple_of(y * 2 * ROWS + core * ROWS, ROWS)
            far = pl.multiple_of(y * 2 * ROWS + (1 - core) * ROWS, ROWS)
            for slot in range(SLOTS):
                keep[y, zp, slot] = block[pl.ds(near, ROWS), slot * TS:(slot + 1) * TS]
                send[y, zp, slot] = block[pl.ds(far, ROWS), slot * TS:(slot + 1) * TS]
        return carry

    lax.fori_loop(0, NZ, gram, 0)


def exchange(pos, pair_tiles, pair_live, occ_index, *pieces):
    shape = jax.ShapeDtypeStruct((NY, NZ, SLOTS, ROWS, TS), F32)
    return pl.pallas_call(
        main_kernel,
        out_shape=(shape, shape),
        in_specs=[SMEM] * 4 + [ANY] * len(pieces),
        out_specs=(VMEM, VMEM),
        scratch_shapes=[pltpu.VMEM(piece.shape, BF) for piece in pieces] + [
            pltpu.VMEM((TILES, OCC * HALF, TS), BF),
            pltpu.VMEM((TILES, OCC * HALF, TS), BF),
            pltpu.VMEM((TS, SLOTS * TS), F32),
            pltpu.SemaphoreType.DMA((len(pieces),)),
        ],
        compiler_params=pltpu.CompilerParams(vmem_limit_bytes=40 * 2**20),
        name="exchange",
    )(pos, pair_tiles, pair_live, occ_index, *pieces)


def shift(value, axis, size, by):
    return lax.ppermute(value, axis, [(i, (i + by) % size) for i in range(size)])


def swap(value):
    return lax.ppermute(value, "c", [(0, 1), (1, 0)])


def shards(integrals, orbitals, pair_tiles, pair_live, occ_live):
    pos = jnp.stack([lax.axis_index(name).astype(jnp.int32) for name in ("y", "c", "z", "x")])
    tile = pos[2] * NX + pos[3]
    eri = integrals.reshape(SLOTS * TS * AUXROWS, TS)
    keep_eri, give_eri, coeffs = prep(pos, occ_live, eri, orbitals)
    rank = jnp.cumsum(occ_live, axis=1) - 1
    hits = (occ_live[:, :, None] != 0) & (rank[:, :, None] == jnp.arange(LIVE)[None, None, :])
    occ_index = jnp.sum(jnp.where(hits, jnp.arange(OCC)[None, :, None], 0), axis=1).astype(jnp.int32)

    row_coeffs = lax.all_gather(coeffs, "x", axis=0)
    all_coeffs = lax.all_gather(row_coeffs, "z", axis=0)

    got_eri = swap(give_eri)
    by_aux = lax.dynamic_slice_in_dim(
        jnp.concatenate([keep_eri, got_eri, keep_eri]), pos[1] * AUXROWS, NZ, 0
    )
    own0 = lax.all_to_all(by_aux, "z", split_axis=0, concat_axis=0, tiled=True)
    own_r, own_l = shift(own0, "x", NX, 1), shift(own0, "x", NX, -1)
    oth0 = swap(own0)
    own_r2, own_l2 = shift(own_r[:4], "x", NX, 1), shift(own_l[4:], "x", NX, -1)
    oth_r, oth_l = swap(own_r), swap(own_l)
    oth_r2, oth_l2 = swap(own_r2), swap(own_l2)

    keep, send = exchange(
        pos, pair_tiles, pair_live, occ_index,
        all_coeffs, own0, own_r, own_l, own_r2, own_l2, oth0, oth_r, oth_l, oth_r2, oth_l2,
    )
    partial = (keep + swap(send)).astype(BF).reshape(NY * NZ, SLOTS, ROWS, TS)
    parts = lax.all_to_all(partial, ("y", "z"), split_axis=0, concat_axis=0, tiled=True).astype(F32)
    flags = lax.dynamic_index_in_dim(pair_live, tile, 0, keepdims=False).astype(F32) * SCALE
    return (jnp.sum(parts, axis=0) * flags[:, None, None])[None]


def solution(mesh):
    grid = Mesh(mesh.devices.reshape(NY, NC, NZ, NX), ("y", "c", "z", "x"))
    return jax.shard_map(
        shards,
        mesh=grid,
        in_specs=(
            P(("z", "x"), None, None, ("y", "c"), None),
            P(("z", "x"), None),
            P(),
            P(),
            P(),
        ),
        out_specs=P(("z", "x"), None, ("y", "c"), None),
        check_vma=False,
    )
```

time: 149 us -> 131 us (0.88)
  blocking collectives: 0 us -> 42.1 us
  waiting for transfers between devices: 71.5 us -> 38.9 us
  starting transfers between devices: 42.9 us -> 15.6 us
  between operations: 0.25 us -> 13.5 us
  local copies, waits for them, and re-layouts: 14.5 us -> 6.1 us
  Pallas kernels: 16.7 us -> 12.5 us
    all_to_all x0 -> x1, blocking collectives: none -> 28.8 us  [shards(): own0 = lax.all_to_all(by_aux, 'z', split_axis=0, concat_axis=0, tiled=True)]
    ppermute x8 -> x0, waiting for transfers between devices: 20.1 us -> none  [spread(): return lax.ppermute(value, ('c', 'z'), pairs)]
    ppermute x8 -> x0, starting transfers between devices: 14.6 us -> none  [spread(): return lax.ppermute(value, ('c', 'z'), pairs)]
    ppermute x15 -> x4, starting transfers between devices: 19.8 us -> 5.44 us  [shift(): lax.ppermute(value, axis, [(i, (i + by) % size) for i in range(size)])]
    all_gather x0 -> x1, blocking collectives: none -> 13.3 us  [shards(): row_coeffs = lax.all_gather(coeffs, 'x', axis=0)]
    all_to_all x1, waiting for transfers between devices: 27.9 us -> 17.7 us  [shards(): lax.all_to_all(partial, ('y', 'z'), split_axis=0, concat_axis=0, tiled=True)]
    unnamed x42 -> x15, local copies, waits for them, and re-layouts: 13.7 us -> 4.53 us
    ppermute x15 -> x4, waiting for transfers between devices: 20.8 us -> 15.6 us  [shift(): lax.ppermute(value, axis, [(i, (i + by) % size) for i in range(size)])]
  transfers between devices with their start and end apart: 30 -> 13, of which waited for: 12 -> 7; matrix products, arithmetic and copies ran while one was open for 3% -> 2% of each run, Pallas kernels for 0% -> 0%
where the time goes in v2:
time: 131 us
  blocking collectives  42.1 us (32%)
  waiting for transfers between devices  38.9 us (30%)
  starting transfers between devices  15.6 us (12%)
  between operations  13.5 us (10%)
  Pallas kernels  12.5 us (10%)
  local copies, waits for them, and re-layouts  6.1 us (5%)
  other arithmetic  2.33 us (2%)
    all_to_all x1, blocking collectives, shards(): own0 = lax.all_to_all(by_aux, 'z', split_axis=0, concat_axis=0, tiled=True)  28.8 us
    all_to_all x1, waiting for transfers between devices, shards(): lax.all_to_all(partial, ('y', 'z'), split_axis=0, concat_axis=0, tiled=True)  17.7 us
    ppermute x4, waiting for transfers between devices, shift(): lax.ppermute(value, axis, [(i, (i + by) % size) for i in range(size)])  15.6 us
    all_gather x1, blocking collectives, shards(): row_coeffs = lax.all_gather(coeffs, 'x', axis=0)  13.3 us
    pallas_call x1, Pallas kernels, exchange(): pl.pallas_call(main_kernel, out_shape=(shape, shape), in_specs=[SMEM] * 4...  10.9 us
    all_to_all x1, starting transfers between devices, shards(): lax.all_to_all(partial, ('y', 'z'), split_axis=0, concat_axis=0, tiled=True)  9.16 us
    ppermute x7, waiting for transfers between devices, swap(): return lax.ppermute(value, 'c', [(0, 1), (1, 0)])  5.63 us
    ppermute x4, starting transfers between devices, shift(): lax.ppermute(value, axis, [(i, (i + by) % size) for i in range(size)])  5.44 us
  transfers between devices with their start and end apart: 13, of which 7 were waited for; matrix products, arithmetic and copies ran while one was open for 2% of the time, Pallas kernels for 0%

profile of v2, /device:TPU:32, one launch (start us, length us, event | category | flops | bytes accessed | tf_op | source)
XLA Modules:
  0.0 131.1 jit_solution(5341549191699313442)
XLA Ops:
  6.5 0.0 all-gather.4.cloned.1.call-start
  6.5 0.8 copy.16.occ_live
  7.3 0.1 pad_add_fusion.pos
  7.4 1.0 copy-done.1
  8.4 0.9 copy-done.2
  9.4 1.6 %prep.1 = (bf16[4,2,128,128]{3,2,1,0:T(8,128)(2,1)S(1)}, bf16[4,2,128,128]{3,2,1,0:T(8,128)(2,1)S(1)}, bf16[4,64,128]{2,1,0:T(8,128)(2,1)S(1)}) custom-call(s32[4]{0:T(128)S(1)} %pad_add_fusion.pos, s32[32,8]{1,0:T(8,128)S(1)} %copy.16.occ_live, bf16[2048,128]{1,0:T(8,128)(2,1)S(1)} %bitcast.11, bf16[128,1024]{1,0:T(8,128)(2,1)S(1)} %copy-done.2), custom_call_target="tpu_custom_call" | custom-call | tf_op jit(solution)/shard_map/prep/pallas_call | solution.py:58
  11.0 0.0 copy-start.5
  11.0 0.0 copy-start.4
  11.0 13.3 %all-gather = bf16[16,64,128]{2,1,0:T(8,128)(2,1)} all-gather(bf16[4,64,128]{2,1,0:T(8,128)(2,1)S(1)} %get-tuple-element.10), channel_id=2, replica_groups=mesh['y'=4,'c'=2,'z'=8,'x'=4] {'x'}, dimensions={0}, use_global_device_ids=true | all-gather | bytes 327680 | tf_op jit(solution)/shard_map/all_gather | solution.py:178
  24.4 0.0 all-gather.4.cloned.1.call-update
  24.4 0.1 collective-permute-start
  24.5 1.5 %collective-permute-done = bf16[4,2,128,128]{3,2,1,0:T(8,128)(2,1)S(1)} collective-permute-done((bf16[4,2,128,128]{3,2,1,0:T(8,128)(2,1)S(1)}, bf16[4,2,128,128]{3,2,1,0:T(8,128)(2,1)S(1)}, u32[]{:S(2)}, u32[]{:S(2)}) %collective-permute-start) | collective-permute-done | bytes 262176 | tf_op jit(solution)/shard_map/ppermute | solution.py:166
  26.0 0.3 fusion.1
  26.3 28.8 %all_to_all.10.refs_1_ = bf16[8,2,128,128]{3,2,1,0:T(8,128)(2,1)S(1)} all-to-all(bf16[8,2,128,128]{3,2,1,0:T(8,128)(2,1)S(1)} %fusion.1), channel_id=1, replica_groups=mesh['y'=4,'c'=2,'z'=8,'x'=4] {'z'}, dimensions={0} | all-to-all | bytes 1048576 | tf_op jit(solution)/shard_map/all_to_all | solution.py:185
  55.1 2.6 %collective-permute-start.2 = (bf16[8,2,128,128]{3,2,1,0:T(8,128)(2,1)S(1)}, bf16[8,2,128,128]{3,2,1,0:T(8,128)(2,1)S(1)}, u32[]{:S(2)}, u32[]{:S(2)}) collective-permute-start(bf16[8,2,128,128]{3,2,1,0:T(8,128)(2,1)S(1)} %all_to_all.10.refs_1_), channel_id=1, source_target_pairs={{0,3},{1,0},{2,1},{3,2},{4,7},{5,4},{6,5},{7,6},{8,11},{9,8},{10,9... | collective-permute-start | bytes 1572872 | tf_op jit(solution)/shard_map/ppermute | solution.py:162
  57.7 0.0 collective-permute-start.1
  57.7 8.4 %collective-permute-done.2.refs_3_ = bf16[8,2,128,128]{3,2,1,0:T(8,128)(2,1)S(1)} collective-permute-done((bf16[8,2,128,128]{3,2,1,0:T(8,128)(2,1)S(1)}, bf16[8,2,128,128]{3,2,1,0:T(8,128)(2,1)S(1)}, u32[]{:S(2)}, u32[]{:S(2)}) %collective-permute-start.2) | collective-permute-done | bytes 524320 | tf_op jit(solution)/shard_map/ppermute | solution.py:162
  66.1 0.7 slice.9
  66.8 2.8 %collective-permute-start.4 = (bf16[4,2,128,128]{3,2,1,0:T(8,128)(2,1)}, bf16[4,2,128,128]{3,2,1,0:T(8,128)(2,1)S(1)}, u32[]{:S(2)}, u32[]{:S(2)}) collective-permute-start(bf16[4,2,128,128]{3,2,1,0:T(8,128)(2,1)} %slice.9), channel_id=1, source_target_pairs={{0,3},{1,0},{2,1},{3,2},{4,7},{5,4},{6,5},{7,6},{8,11},{9,8},{10,9... | collective-permute-start | bytes 786440 | tf_op jit(solution)/shard_map/ppermute | solution.py:162
  69.6 0.0 collective-permute-done.1.refs_2_
  69.6 0.8 slice.8
  70.3 0.0 collective-permute-start.3
  70.4 0.1 collective-permute-start.5
  70.5 0.5 collective-permute-start.7
  71.0 0.1 collective-permute-start.6
  71.1 2.7 %collective-permute-done.4.refs_5_ = bf16[4,2,128,128]{3,2,1,0:T(8,128)(2,1)S(1)} collective-permute-done((bf16[4,2,128,128]{3,2,1,0:T(8,128)(2,1)}, bf16[4,2,128,128]{3,2,1,0:T(8,128)(2,1)S(1)}, u32[]{:S(2)}, u32[]{:S(2)}) %collective-permute-start.4) | collective-permute-done | bytes 262176 | tf_op jit(solution)/shard_map/ppermute | solution.py:162
  73.8 0.0 collective-permute-start.9
  73.8 4.4 %collective-permute-done.3.refs_4_ = bf16[4,2,128,128]{3,2,1,0:T(8,128)(2,1)} collective-permute-done((bf16[4,2,128,128]{3,2,1,0:T(8,128)(2,1)}, bf16[4,2,128,128]{3,2,1,0:T(8,128)(2,1)}, u32[]{:S(2)}, u32[]{:S(2)}) %collective-permute-start.3) | collective-permute-done | bytes 262176 | tf_op jit(solution)/shard_map/ppermute | solution.py:162
  78.2 0.0 collective-permute-start.8
  78.3 0.1 copy.19.occ_index
  78.4 0.1 copy.17.pair_tiles
  78.5 0.1 copy.18.pair_live
  78.6 0.0 collective-permute-done.5.refs_6_
  78.6 0.0 collective-permute-done.9.refs_10_
  78.6 1.6 %collective-permute-done.8.refs_9_ = bf16[4,2,128,128]{3,2,1,0:T(8,128)(2,1)} collective-permute-done((bf16[4,2,128,128]{3,2,1,0:T(8,128)(2,1)}, bf16[4,2,128,128]{3,2,1,0:T(8,128)(2,1)}, u32[]{:S(2)}, u32[]{:S(2)}) %collective-permute-start.8) | collective-permute-done | bytes 262176 | tf_op jit(solution)/shard_map/ppermute | solution.py:166
  80.1 0.0 collective-permute-done.7.refs_8_
  80.1 0.0 collective-permute-done.6.refs_7_
  80.1 0.0 all-gather.4.cloned.1.call-done
  80.2 1.6 %copy-done = bf16[32,4,64,128]{3,2,1,0:T(8,128)(2,1)S(1)} copy-done((bf16[32,4,64,128]{3,2,1,0:T(8,128)(2,1)S(1)}, bf16[32,4,64,128]{3,2,1,0:T(8,128)(2,1)}, u32[]{:S(2)}) %copy-start) | copy-done | bytes 2097176
  81.7 10.9 %exchange.1 = (f32[4,8,4,16,128]{4,3,2,1,0:T(8,128)S(1)}, f32[4,8,4,16,128]{4,3,2,1,0:T(8,128)S(1)}) custom-call(s32[4]{0:T(128)S(1)} %pad_add_fusion.pos, s32[32,4]{1,0:T(8,128)S(1)} %copy.17.pair_tiles, s32[32,4]{1,0:T(8,128)S(1)} %copy.18.pair_live, s32[32,4]{1,0:T(8,128)S(1)} %copy.19.occ_index, bf16[8,4,4,64,128]{4,3,2,1,0:T(8,128)(2,1)S(1)} %bitcast.10, ...), custom_call_target="tpu_custom_call" | custom-call | tf_op jit(solution)/shard_map/exchange/pallas_call | solution.py:145
  92.6 0.2 collective-permute-start.10
  92.8 2.5 %collective-permute-done.10 = f32[4,8,4,16,128]{4,3,2,1,0:T(8,128)S(1)} collective-permute-done((f32[4,8,4,16,128]{4,3,2,1,0:T(8,128)S(1)}, f32[4,8,4,16,128]{4,3,2,1,0:T(8,128)S(1)}, u32[]{:S(2)}, u32[]{:S(2)}) %collective-permute-start.10) | collective-permute-done | bytes 1048608 | tf_op jit(solution)/shard_map/ppermute | solution.py:166
  95.4 1.0 add_convert_fusion
  96.3 9.2 %all-to-all-start.1 = ((bf16[32,4,16,128]{3,2,1,0:T(8,128)(2,1)}), bf16[32,4,16,128]{3,2,1,0:T(8,128)(2,1)S(1)}, u32[]{:S(2)}, u32[]{:S(2)}) async-start(bf16[32,4,16,128]{3,2,1,0:T(8,128)(2,1)} %bitcast.7), calls=%async_computation.1 | async-start | bytes 1048576 | tf_op jit(solution)/shard_map/all_to_all | solution.py:197
  105.5 0.2 multiply_reduce_fusion
  105.7 17.7 %all-to-all-done.1 = bf16[32,4,16,128]{3,2,1,0:T(8,128)(2,1)S(1)} async-done(((bf16[32,4,16,128]{3,2,1,0:T(8,128)(2,1)}), bf16[32,4,16,128]{3,2,1,0:T(8,128)(2,1)S(1)}, u32[]{:S(2)}, u32[]{:S(2)}) %all-to-all-start.1) | async-done | bytes 524320 | tf_op jit(solution)/shard_map/all_to_all | solution.py:197
  123.5 0.1 convert_reduce_fusion
  123.5 0.7 bitcast_multiply_fusion
  (11 shorter events, 0.1 us)
Async XLA Ops:
  6.5 73.6 %all-gather.4.cloned.1.call-start = ((), (), s32[]{:S(2)}) async-start(), calls=%async_computation.2 | async-start | bytes 2359296 | tf_op jit(solution)/shard_map/all_gather | solution.py:179
  7.4 1.0 copy-start.1
  8.4 0.9 copy-start.2
  9.4 61.0 %copy-start.3 = (s32[32,8]{0,1:T(8,128)S(1)}, s32[32,8]{0,1:T(8,128)}, u32[]{:S(2)}) copy-start(s32[32,8]{0,1:T(8,128)} %param.9) | copy-start | bytes 3076
  11.0 67.4 %copy-start.5 = (s32[32,4]{0,1:T(4,128)S(1)}, s32[32,4]{0,1:T(4,128)}, u32[]{:S(2)}) copy-start(s32[32,4]{0,1:T(4,128)} %param.7) | copy-start | bytes 1540
  11.0 67.4 %copy-start.4 = (s32[32,4]{0,1:T(4,128)S(1)}, s32[32,4]{0,1:T(4,128)}, u32[]{:S(2)}) copy-start(s32[32,4]{0,1:T(4,128)} %param.8) | copy-start | bytes 1540
  24.4 1.6 %collective-permute-start = (bf16[4,2,128,128]{3,2,1,0:T(8,128)(2,1)S(1)}, bf16[4,2,128,128]{3,2,1,0:T(8,128)(2,1)S(1)}, u32[]{:S(2)}, u32[]{:S(2)}) collective-permute-start(bf16[4,2,128,128]{3,2,1,0:T(8,128)(2,1)S(1)} %get-tuple-element.12), channel_id=1, source_target_pairs={{0,32},{32,0},{1,33},{33,1},{2,34},{34,2},{3,35},{35,3},{4,36},{36... | collective-permute-start | bytes 786440 | tf_op jit(solution)/shard_map/ppermute | solution.py:166
  55.1 11.0 %collective-permute-start.2 = (bf16[8,2,128,128]{3,2,1,0:T(8,128)(2,1)S(1)}, bf16[8,2,128,128]{3,2,1,0:T(8,128)(2,1)S(1)}, u32[]{:S(2)}, u32[]{:S(2)}) collective-permute-start(bf16[8,2,128,128]{3,2,1,0:T(8,128)(2,1)S(1)} %all_to_all.10.refs_1_), channel_id=1, source_target_pairs={{0,3},{1,0},{2,1},{3,2},{4,7},{5,4},{6,5},{7,6},{8,11},{9,8},{10,9... | collective-permute-start | bytes 1572872 | tf_op jit(solution)/shard_map/ppermute | solution.py:162
  57.7 11.9 %collective-permute-start.1 = (bf16[8,2,128,128]{3,2,1,0:T(8,128)(2,1)S(1)}, bf16[8,2,128,128]{3,2,1,0:T(8,128)(2,1)S(1)}, u32[]{:S(2)}, u32[]{:S(2)}) collective-permute-start(bf16[8,2,128,128]{3,2,1,0:T(8,128)(2,1)S(1)} %all_to_all.10.refs_1_), channel_id=1, source_target_pairs={{0,1},{1,2},{2,3},{3,0},{4,5},{5,6},{6,7},{7,4},{8,9},{9,10},{10,1... | collective-permute-start | bytes 1572872 | tf_op jit(solution)/shard_map/ppermute | solution.py:162
  66.8 7.0 %collective-permute-start.4 = (bf16[4,2,128,128]{3,2,1,0:T(8,128)(2,1)}, bf16[4,2,128,128]{3,2,1,0:T(8,128)(2,1)S(1)}, u32[]{:S(2)}, u32[]{:S(2)}) collective-permute-start(bf16[4,2,128,128]{3,2,1,0:T(8,128)(2,1)} %slice.9), channel_id=1, source_target_pairs={{0,3},{1,0},{2,1},{3,2},{4,7},{5,4},{6,5},{7,6},{8,11},{9,8},{10,9... | collective-permute-start | bytes 786440 | tf_op jit(solution)/shard_map/ppermute | solution.py:162
  70.3 7.9 %collective-permute-start.3 = (bf16[4,2,128,128]{3,2,1,0:T(8,128)(2,1)}, bf16[4,2,128,128]{3,2,1,0:T(8,128)(2,1)}, u32[]{:S(2)}, u32[]{:S(2)}) collective-permute-start(bf16[4,2,128,128]{3,2,1,0:T(8,128)(2,1)} %slice.8), channel_id=1, source_target_pairs={{0,1},{1,2},{2,3},{3,0},{4,5},{5,6},{6,7},{7,4},{8,9},{9,10},{10,1... | collective-permute-start | bytes 786440 | tf_op jit(solution)/shard_map/ppermute | solution.py:162
  70.4 8.2 %collective-permute-start.5 = (bf16[8,2,128,128]{3,2,1,0:T(8,128)(2,1)S(1)}, bf16[8,2,128,128]{3,2,1,0:T(8,128)(2,1)S(1)}, u32[]{:S(2)}, u32[]{:S(2)}) collective-permute-start(bf16[8,2,128,128]{3,2,1,0:T(8,128)(2,1)S(1)} %all_to_all.10.refs_1_), channel_id=1, source_target_pairs={{0,32},{32,0},{1,33},{33,1},{2,34},{34,2},{3,35},{35,3},{4,36},{36... | collective-permute-start | bytes 1572872 | tf_op jit(solution)/shard_map/ppermute | solution.py:166
  70.5 9.7 %collective-permute-start.7 = (bf16[8,2,128,128]{3,2,1,0:T(8,128)(2,1)S(1)}, bf16[8,2,128,128]{3,2,1,0:T(8,128)(2,1)S(1)}, u32[]{:S(2)}, u32[]{:S(2)}) collective-permute-start(bf16[8,2,128,128]{3,2,1,0:T(8,128)(2,1)S(1)} %collective-permute-done.2.refs_3_), channel_id=1, source_target_pairs={{0,32},{32,0},{1,33},{33,1},{2,34},{34,2},{3,35},{35,3},{4,36},{36... | collective-permute-start | bytes 1572872 | tf_op jit(solution)/shard_map/ppermute | solution.py:166
  71.0 9.2 %collective-permute-start.6 = (bf16[8,2,128,128]{3,2,1,0:T(8,128)(2,1)S(1)}, bf16[8,2,128,128]{3,2,1,0:T(8,128)(2,1)S(1)}, u32[]{:S(2)}, u32[]{:S(2)}) collective-permute-start(bf16[8,2,128,128]{3,2,1,0:T(8,128)(2,1)S(1)} %collective-permute-done.1.refs_2_), channel_id=1, source_target_pairs={{0,32},{32,0},{1,33},{33,1},{2,34},{34,2},{3,35},{35,3},{4,36},{36... | collective-permute-start | bytes 1572872 | tf_op jit(solution)/shard_map/ppermute | solution.py:166
  73.8 4.8 %collective-permute-start.9 = (bf16[4,2,128,128]{3,2,1,0:T(8,128)(2,1)S(1)}, bf16[4,2,128,128]{3,2,1,0:T(8,128)(2,1)}, u32[]{:S(2)}, u32[]{:S(2)}) collective-permute-start(bf16[4,2,128,128]{3,2,1,0:T(8,128)(2,1)S(1)} %collective-permute-done.4.refs_5_), channel_id=1, source_target_pairs={{0,32},{32,0},{1,33},{33,1},{2,34},{34,2},{3,35},{35,3},{4,36},{36... | collective-permute-start | bytes 786440 | tf_op jit(solution)/shard_map/ppermute | solution.py:166
  78.2 1.9 %collective-permute-start.8 = (bf16[4,2,128,128]{3,2,1,0:T(8,128)(2,1)}, bf16[4,2,128,128]{3,2,1,0:T(8,128)(2,1)}, u32[]{:S(2)}, u32[]{:S(2)}) collective-permute-start(bf16[4,2,128,128]{3,2,1,0:T(8,128)(2,1)} %collective-permute-done.3.refs_4_), channel_id=1, source_target_pairs={{0,32},{32,0},{1,33},{33,1},{2,34},{34,2},{3,35},{35,3},{4,36},{36... | collective-permute-start | bytes 786440 | tf_op jit(solution)/shard_map/ppermute | solution.py:166
  80.2 1.6 %copy-start = (bf16[32,4,64,128]{3,2,1,0:T(8,128)(2,1)S(1)}, bf16[32,4,64,128]{3,2,1,0:T(8,128)(2,1)}, u32[]{:S(2)}) copy-start(bf16[32,4,64,128]{3,2,1,0:T(8,128)(2,1)} %all-gather.4.cloned.1.call-done) | copy-start | bytes 6291460
  92.6 2.7 %collective-permute-start.10 = (f32[4,8,4,16,128]{4,3,2,1,0:T(8,128)S(1)}, f32[4,8,4,16,128]{4,3,2,1,0:T(8,128)S(1)}, u32[]{:S(2)}, u32[]{:S(2)}) collective-permute-start(f32[4,8,4,16,128]{4,3,2,1,0:T(8,128)S(1)} %get-tuple-element.14), channel_id=1, source_target_pairs={{0,32},{32,0},{1,33},{33,1},{2,34},{34,2},{3,35},{35,3},{4,36},{36... | collective-permute-start | bytes 3145736 | tf_op jit(solution)/shard_map/ppermute | solution.py:166
  96.3 27.1 %all-to-all-start.1 = ((bf16[32,4,16,128]{3,2,1,0:T(8,128)(2,1)}), bf16[32,4,16,128]{3,2,1,0:T(8,128)(2,1)S(1)}, u32[]{:S(2)}, u32[]{:S(2)}) async-start(bf16[32,4,16,128]{3,2,1,0:T(8,128)(2,1)} %bitcast.7), calls=%async_computation.1 | async-start | bytes 1048576 | tf_op jit(solution)/shard_map/all_to_all | solution.py:197
Sparse Core Ops, SparseCore 0:
  24.5 49.1 all-gather.3

commit v3 on v2

--- a/solution.py
+++ b/solution.py
@@ -23,7 +23,7 @@
 
 
 def prep_kernel(pos, occ_live, eri, orb, keep, give, coeffs, rows, cols, sems):
-    core, tile = pos[1], pos[2] * NX + pos[3]
+    slab, core, tile = pos[0], pos[1], pos[2] * NX + pos[3]
     load_cols = pltpu.make_async_copy(orb, cols, sems.at[0])
     load_rows = pltpu.make_async_copy(eri, rows, sems.at[1])
     load_cols.start()
@@ -31,14 +31,14 @@
     load_cols.wait()
     count = jnp.int32(0)
     for occ in range(OCC):
-        live = occ_live[tile, occ]
-
-        @pl.when(live != 0)
+        live = occ_live[occ, tile] != 0
+
+        @pl.when(live & (count == slab))
         def _():
             flipped = cols[:, occ * TS:(occ + 1) * TS].astype(F32).T.astype(BF)
-            coeffs[jnp.minimum(count, LIVE - 1)] = jnp.where(core == 0, flipped[:HALF], flipped[HALF:])
-
-        count = count + jnp.where(live != 0, 1, 0)
+            coeffs[...] = jnp.where(core == 0, flipped[:HALF], flipped[HALF:])
+
+        count = count + jnp.where(live, 1, 0)
     row = lax.broadcasted_iota(jnp.int32, (TS, TS), 0)
     col = lax.broadcasted_iota(jnp.int32, (TS, TS), 1)
     block_nu = TS // AUXROWS
@@ -57,7 +57,7 @@
     piece = jax.ShapeDtypeStruct((AUXROWS, 2, TS, TS), BF)
     return pl.pallas_call(
         prep_kernel,
-        out_shape=(piece, piece, jax.ShapeDtypeStruct((LIVE, HALF, TS), BF)),
+        out_shape=(piece, piece, jax.ShapeDtypeStruct((HALF, TS), BF)),
         in_specs=[SMEM, SMEM, ANY, ANY],
         out_specs=(VMEM, VMEM, VMEM),
         scratch_shapes=[
@@ -65,34 +65,45 @@
             pltpu.VMEM(orb.shape, BF),
             pltpu.SemaphoreType.DMA((2,)),
         ],
-        compiler_params=pltpu.CompilerParams(vmem_limit_bytes=16 * 2**20),
+        compiler_params=pltpu.CompilerParams(vmem_limit_bytes=56 * 2**20),
         name="prep",
     )(pos, occ_live, eri, orb)
 
 
 def main_kernel(pos, pair_tiles, pair_live, occ_index, *refs):
-    inputs, (keep, send), scratch = refs[:11], refs[11:13], refs[13:]
-    held, (dense, field, block, sems) = scratch[:11], scratch[11:]
-    core, x = pos[1], pos[3]
+    inputs, (keep, send), scratch = refs[:15], refs[15:17], refs[17:]
+    held, (dense, field, block, sems) = scratch[:15], scratch[15:]
+    slab, core, x = pos[0], pos[1], pos[3]
     loads = [pltpu.make_async_copy(src, dst, sems.at[i]) for i, (src, dst) in enumerate(zip(inputs, held))]
     for load in loads:
         load.start()
-    coeffs, own0, own_r, own_l, own_r2, own_l2, oth0, oth_r, oth_l, oth_r2, oth_l2 = held
+    c0, c_u, c_d, c_u2, c_d2, own0, own_r, own_l, own_r2, own_l2, oth0, oth_r, oth_l, oth_r2, oth_l2 = held
 
     def clear(tile, carry):
         dense[tile] = jnp.zeros(dense.shape[1:], BF)
         return carry
 
     lax.fori_loop(0, TILES, clear, 0, unroll=4)
-    loads[0].wait()
-
-    def place(tile, carry):
-        for k in range(LIVE):
-            start = pl.multiple_of(occ_index[tile, k] * HALF, HALF)
-            dense[tile, pl.ds(start, HALF), :] = coeffs[tile // NX, tile % NX, k]
-        return carry
-
-    lax.fori_loop(0, TILES, place, 0, unroll=4)
+
+    def place(piece, k, lo, count):
+        def body(step, carry):
+            for entry in range(NX):
+                tile = (lo + step) * NX + (x - entry + NX) % NX
+                start = pl.multiple_of(occ_index[k, tile] * HALF, HALF)
+                dense[tile, pl.ds(start, HALF), :] = piece[step, entry]
+            return carry
+
+        lax.fori_loop(0, count, body, 0, unroll=True)
+
+    for index, (piece, k, lo, count) in enumerate((
+        (c0, slab, 0, 8),
+        (c_u, (slab + 3) % NY, 0, 8),
+        (c_d, (slab + 1) % NY, 0, 8),
+        (c_u2, (slab + 2) % NY, 0, 4),
+        (c_d2, (slab + 2) % NY, 4, 4),
+    )):
+        loads[index].wait()
+        place(piece, k, lo, count)
 
     def transform(xp, own, oth, lo, count):
         def body(step, carry):
@@ -102,8 +113,8 @@
                 for j in range(2):
                     slot = part * 2 + j
                     eri = ref[step, j]
-                    rhs.append(jnp.where(pair_live[tile, slot] != 0, eri, jnp.zeros_like(eri)))
-                    lhs.append(dense[pair_tiles[tile, slot]])
+                    rhs.append(jnp.where(pair_live[slot, tile] != 0, eri, jnp.zeros_like(eri)))
+                    lhs.append(dense[pair_tiles[slot, tile]])
             half = jnp.dot(
                 jnp.concatenate(lhs, axis=1), jnp.concatenate(rhs, axis=0), preferred_element_type=F32
             )
@@ -113,11 +124,11 @@
         lax.fori_loop(0, count, body, 0, unroll=4)
 
     for own, oth, xp, lo, count, first in (
-        (own0, oth0, x, 0, 8, 1),
-        (own_r, oth_r, (x + 3) % NX, 0, 8, 2),
-        (own_l, oth_l, (x + 1) % NX, 0, 8, 3),
-        (own_r2, oth_r2, (x + 2) % NX, 0, 4, 4),
-        (own_l2, oth_l2, (x + 2) % NX, 4, 4, 5),
+        (own0, oth0, x, 0, 8, 5),
+        (own_r, oth_r, (x + 3) % NX, 0, 8, 6),
+        (own_l, oth_l, (x + 1) % NX, 0, 8, 7),
+        (own_r2, oth_r2, (x + 2) % NX, 0, 4, 8),
+        (own_l2, oth_l2, (x + 2) % NX, 4, 4, 9),
     ):
         loads[first].wait()
         loads[first + 5].wait()
@@ -125,7 +136,7 @@
 
     def gram(zp, carry):
         tile = zp * NX + x
-        partners = jnp.concatenate([field[pair_tiles[tile, slot]] for slot in range(SLOTS)], axis=1)
+        partners = jnp.concatenate([field[pair_tiles[slot, tile]] for slot in range(SLOTS)], axis=1)
         block[...] = lax.dot_general(
             field[tile], partners, (((0,), (0,)), ((), ())), preferred_element_type=F32
         )
@@ -153,7 +164,7 @@
             pltpu.VMEM((TS, SLOTS * TS), F32),
             pltpu.SemaphoreType.DMA((len(pieces),)),
         ],
-        compiler_params=pltpu.CompilerParams(vmem_limit_bytes=40 * 2**20),
+        compiler_params=pltpu.CompilerParams(vmem_limit_bytes=56 * 2**20),
         name="exchange",
     )(pos, pair_tiles, pair_live, occ_index, *pieces)
 
@@ -170,28 +181,31 @@
     pos = jnp.stack([lax.axis_index(name).astype(jnp.int32) for name in ("y", "c", "z", "x")])
     tile = pos[2] * NX + pos[3]
     eri = integrals.reshape(SLOTS * TS * AUXROWS, TS)
-    keep_eri, give_eri, coeffs = prep(pos, occ_live, eri, orbitals)
+    keep_eri, give_eri, coeffs = prep(pos, occ_live.T, eri, orbitals)
     rank = jnp.cumsum(occ_live, axis=1) - 1
-    hits = (occ_live[:, :, None] != 0) & (rank[:, :, None] == jnp.arange(LIVE)[None, None, :])
-    occ_index = jnp.sum(jnp.where(hits, jnp.arange(OCC)[None, :, None], 0), axis=1).astype(jnp.int32)
-
-    row_coeffs = lax.all_gather(coeffs, "x", axis=0)
-    all_coeffs = lax.all_gather(row_coeffs, "z", axis=0)
+    hits = (occ_live[None] != 0) & (rank[None] == jnp.arange(LIVE)[:, None, None])
+    occ_index = jnp.sum(jnp.where(hits, jnp.arange(OCC)[None, None, :], 0), axis=2).astype(jnp.int32)
 
     got_eri = swap(give_eri)
+    row_coeffs = jnp.stack([coeffs] + [shift(coeffs, "x", NX, by) for by in (1, 2, 3)])
+    got_eri, row_coeffs = lax.optimization_barrier((got_eri, row_coeffs))
     by_aux = lax.dynamic_slice_in_dim(
         jnp.concatenate([keep_eri, got_eri, keep_eri]), pos[1] * AUXROWS, NZ, 0
     )
     own0 = lax.all_to_all(by_aux, "z", split_axis=0, concat_axis=0, tiled=True)
+    c0 = lax.all_gather(row_coeffs, "z", axis=0)
+    own0, c0 = lax.optimization_barrier((own0, c0))
     own_r, own_l = shift(own0, "x", NX, 1), shift(own0, "x", NX, -1)
+    c_u, c_d = shift(c0, "y", NY, 1), shift(c0, "y", NY, -1)
     oth0 = swap(own0)
     own_r2, own_l2 = shift(own_r[:4], "x", NX, 1), shift(own_l[4:], "x", NX, -1)
+    c_u2, c_d2 = shift(c_u[:4], "y", NY, 1), shift(c_d[4:], "y", NY, -1)
     oth_r, oth_l = swap(own_r), swap(own_l)
     oth_r2, oth_l2 = swap(own_r2), swap(own_l2)
 
     keep, send = exchange(
-        pos, pair_tiles, pair_live, occ_index,
-        all_coeffs, own0, own_r, own_l, own_r2, own_l2, oth0, oth_r, oth_l, oth_r2, oth_l2,
+        pos, pair_tiles.T, pair_live.T, occ_index,
+        c0, c_u, c_d, c_u2, c_d2, own0, own_r, own_l, own_r2, own_l2, oth0, oth_r, oth_l, oth_r2, oth_l2,
     )
     partial = (keep + swap(send)).astype(BF).reshape(NY * NZ, SLOTS, ROWS, TS)
     parts = lax.all_to_all(partial, ("y", "z"), split_axis=0, concat_axis=0, tiled=True).astype(F32)

time: 131 us -> 128 us (0.977)
  starting transfers between devices: 15.6 us -> 31.2 us
  between operations: 13.5 us -> 0.22 us
  blocking collectives: 42.1 us -> 33.3 us
  other arithmetic: 2.33 us -> 6.43 us
  Pallas kernels: 12.5 us -> 15.4 us
  local copies, waits for them, and re-layouts: 6.1 us -> 3.42 us
    all_to_all x1 -> x0, blocking collectives: 28.8 us -> none  [shards(): own0 = lax.all_to_all(by_aux, 'z', split_axis=0, concat_axis=0, tiled=True)]
    all_gather x1, blocking collectives: 13.3 us -> 33.3 us  [shards(): c0 = lax.all_gather(row_coeffs, 'z', axis=0)]
    ppermute x4 -> x11, starting transfers between devices: 5.44 us -> 16.2 us  [shift(): lax.ppermute(value, axis, [(i, (i + by) % size) for i in range(size)])]
    all_to_all x0 -> x1, starting transfers between devices: none -> 8.58 us  [shards(): own0 = lax.all_to_all(by_aux, 'z', split_axis=0, concat_axis=0, tiled=True)]
    all_to_all x1, starting transfers between devices: 9.16 us -> 5.58 us  [shards(): lax.all_to_all(partial, ('y', 'z'), split_axis=0, concat_axis=0, tiled=True)]
    ppermute x7, waiting for transfers between devices: 5.63 us -> 2.87 us  [swap(): return lax.ppermute(value, 'c', [(0, 1), (1, 0)])]
    unnamed x15 -> x28, local copies, waits for them, and re-layouts: 4.53 us -> 1.87 us
    ppermute x4 -> x11, waiting for transfers between devices: 15.6 us -> 17.8 us  [shift(): lax.ppermute(value, axis, [(i, (i + by) % size) for i in range(size)])]
  transfers between devices with their start and end apart: 13 -> 20, of which waited for: 7 -> 8; matrix products, arithmetic and copies ran while one was open for 2% -> 2% of each run, Pallas kernels for 0% -> 0%
where the time goes in v3:
time: 128 us
  waiting for transfers between devices  37.7 us (29%)
  blocking collectives  33.3 us (26%)
  starting transfers between devices  31.2 us (24%)
  Pallas kernels  15.4 us (12%)
  other arithmetic  6.43 us (5%)
  local copies, waits for them, and re-layouts  3.42 us (3%)
    all_gather x1, blocking collectives, shards(): c0 = lax.all_gather(row_coeffs, 'z', axis=0)  33.3 us
    ppermute x11, waiting for transfers between devices, shift(): lax.ppermute(value, axis, [(i, (i + by) % size) for i in range(size)])  17.8 us
    all_to_all x1, waiting for transfers between devices, shards(): lax.all_to_all(partial, ('y', 'z'), split_axis=0, concat_axis=0, tiled=True)  17.1 us
    ppermute x11, starting transfers between devices, shift(): lax.ppermute(value, axis, [(i, (i + by) % size) for i in range(size)])  16.2 us
    pallas_call x1, Pallas kernels, exchange(): pl.pallas_call(main_kernel, out_shape=(shape, shape), in_specs=[SMEM] * 4...  12.5 us
    all_to_all x1, starting transfers between devices, shards(): own0 = lax.all_to_all(by_aux, 'z', split_axis=0, concat_axis=0, tiled=True)  8.58 us
    all_to_all x1, starting transfers between devices, shards(): lax.all_to_all(partial, ('y', 'z'), split_axis=0, concat_axis=0, tiled=True)  5.58 us
    pallas_call x1, Pallas kernels, prep(): pl.pallas_call(prep_kernel, out_shape=(piece, piece, jax.ShapeDtypeStruct...  2.89 us
  transfers between devices with their start and end apart: 20, of which 8 were waited for; matrix products, arithmetic and copies ran while one was open for 2% of the time, Pallas kernels for 0%

profile of v3, /device:TPU:32, one launch (start us, length us, event | category | flops | bytes accessed | tf_op | source)
XLA Modules:
  0.0 127.6 jit_solution(693907350571281479)
XLA Ops:
  0.0 0.6 pad_add_fusion.pos
  0.6 2.9 %prep.1 = (bf16[4,2,128,128]{3,2,1,0:T(8,128)(2,1)}, bf16[4,2,128,128]{3,2,1,0:T(8,128)(2,1)}, bf16[64,128]{1,0:T(8,128)(2,1)}) custom-call(s32[4]{0:T(128)} %pad_add_fusion.pos, s32[8,32]{1,0:T(8,128)} %bitcast.20, bf16[2048,128]{1,0:T(8,128)(2,1)} %bitcast.19, bf16[128,1024]{1,0:T(8,128)(2,1)} %orb.1), custom_call_target="tpu_custom_call" | custom-call | tf_op jit(solution)/shard_map/prep/pallas_call | solution.py:58
  3.5 0.0 copy-start.12
  3.5 0.1 collective-permute-start
  3.6 2.8 %collective-permute-start.3 = (bf16[64,128]{1,0:T(8,128)(2,1)}, bf16[64,128]{1,0:T(8,128)(2,1)S(1)}, u32[]{:S(2)}, u32[]{:S(2)}) collective-permute-start(bf16[64,128]{1,0:T(8,128)(2,1)} %get-tuple-element.16), channel_id=1, source_target_pairs={{0,3},{1,0},{2,1},{3,2},{4,7},{5,4},{6,5},{7,6},{8,11},{9,8},{10,9... | collective-permute-start | bytes 49160 | tf_op jit(solution)/shard_map/ppermute | solution.py:173
  6.5 0.8 collective-permute-start.2
  7.3 0.9 collective-permute-start.1
  8.2 3.8 %collective-permute-done.2 = bf16[64,128]{1,0:T(8,128)(2,1)S(1)} collective-permute-done((bf16[64,128]{1,0:T(8,128)(2,1)}, bf16[64,128]{1,0:T(8,128)(2,1)S(1)}, u32[]{:S(2)}, u32[]{:S(2)}) %collective-permute-start.2) | collective-permute-done | bytes 16416 | tf_op jit(solution)/shard_map/ppermute | solution.py:173
  11.9 0.5 collective-permute-done.1
  12.4 2.0 %fusion.1 = bf16[8,2,128,128]{3,2,1,0:T(8,128)(2,1)} fusion(s32[]{:T(128)S(6)} %select_n.12, bf16[4,2,128,128]{3,2,1,0:T(8,128)(2,1)} %get-tuple-element.14, bf16[4,2,128,128]{3,2,1,0:T(8,128)(2,1)S(1)} %collective-permute-done), kind=kLoop, calls=%fused_computation.6 | loop fusion | flops 524288 | bytes 1048580 | tf_op jit(solution)/shard_map/concatenate | solution.py:193
  14.5 8.6 %all-to-all-start = ((bf16[8,2,128,128]{3,2,1,0:T(8,128)(2,1)}), bf16[8,2,128,128]{3,2,1,0:T(8,128)(2,1)S(1)}, u32[]{:S(2)}, u32[]{:S(2)}) async-start(bf16[8,2,128,128]{3,2,1,0:T(8,128)(2,1)} %fusion.1), calls=%async_computation | async-start | bytes 1048576 | tf_op jit(solution)/shard_map/all_to_all | solution.py:195
  23.0 33.3 %all-gather = bf16[32,64,128]{2,1,0:T(8,128)(2,1)S(1)} all-gather(bf16[4,64,128]{2,1,0:T(8,128)(2,1)S(1)} %pad_maximum_fusion), channel_id=2, replica_groups=mesh['y'=4,'c'=2,'z'=8,'x'=4] {'z'}, dimensions={0}, use_global_device_ids=true | all-gather | bytes 589824 | tf_op jit(solution)/shard_map/all_gather | solution.py:196
  56.3 3.1 %collective-permute-start.5 = (bf16[8,4,64,128]{3,2,1,0:T(8,128)(2,1)S(1)}, bf16[8,4,64,128]{3,2,1,0:T(8,128)(2,1)S(1)}, u32[]{:S(2)}, u32[]{:S(2)}) collective-permute-start(bf16[8,4,64,128]{3,2,1,0:T(8,128)(2,1)S(1)} %bitcast.16), channel_id=1, source_target_pairs={{0,192},{64,0},{128,64},{192,128},{1,193},{65,1},{129,65},{193,129... | collective-permute-start | bytes 1572872 | tf_op jit(solution)/shard_map/ppermute | solution.py:173
  59.4 0.9 collective-permute-start.9
  60.3 1.1 collective-permute-start.8
  61.4 0.0 collective-permute-start.4
  61.4 0.0 collective-permute-start.12
  61.4 5.3 %collective-permute-done.5.refs_2_ = bf16[8,4,64,128]{3,2,1,0:T(8,128)(2,1)S(1)} collective-permute-done((bf16[8,4,64,128]{3,2,1,0:T(8,128)(2,1)S(1)}, bf16[8,4,64,128]{3,2,1,0:T(8,128)(2,1)S(1)}, u32[]{:S(2)}, u32[]{:S(2)}) %collective-permute-start.5) | collective-permute-done | bytes 524320 | tf_op jit(solution)/shard_map/ppermute | solution.py:173
  66.8 3.8 %collective-permute-start.7 = (bf16[4,4,64,128]{3,2,1,0:T(8,128)(2,1)S(1)}, bf16[4,4,64,128]{3,2,1,0:T(8,128)(2,1)}, u32[]{:S(2)}, u32[]{:S(2)}) collective-permute-start(bf16[4,4,64,128]{3,2,1,0:T(8,128)(2,1)S(1)} %slice.17), channel_id=1, source_target_pairs={{0,192},{64,0},{128,64},{192,128},{1,193},{65,1},{129,65},{193,129... | collective-permute-start | bytes 786440 | tf_op jit(solution)/shard_map/ppermute | solution.py:173
  70.5 0.8 slice.19
  71.3 0.2 collective-permute-start.11
  71.5 0.0 collective-permute-done.8.refs_6_
  71.5 0.8 slice.18
  72.3 1.8 %collective-permute-start.10 = (bf16[4,2,128,128]{3,2,1,0:T(8,128)(2,1)}, bf16[4,2,128,128]{3,2,1,0:T(8,128)(2,1)}, u32[]{:S(2)}, u32[]{:S(2)}) collective-permute-start(bf16[4,2,128,128]{3,2,1,0:T(8,128)(2,1)} %slice.18), channel_id=1, source_target_pairs={{0,1},{1,2},{2,3},{3,0},{4,5},{5,6},{6,7},{7,4},{8,9},{9,10},{10,1... | collective-permute-start | bytes 786440 | tf_op jit(solution)/shard_map/ppermute | solution.py:173
  74.1 0.1 collective-permute-start.14
  74.2 0.5 collective-permute-start.13
  74.8 0.8 collective-permute-start.6
  75.6 2.4 %collective-permute-done.11.refs_9_ = bf16[4,2,128,128]{3,2,1,0:T(8,128)(2,1)} collective-permute-done((bf16[4,2,128,128]{3,2,1,0:T(8,128)(2,1)}, bf16[4,2,128,128]{3,2,1,0:T(8,128)(2,1)}, u32[]{:S(2)}, u32[]{:S(2)}) %collective-permute-start.11) | collective-permute-done | bytes 262176 | tf_op jit(solution)/shard_map/ppermute | solution.py:173
  78.0 0.0 collective-permute-start.16
  78.0 2.2 %collective-permute-done.10.refs_8_ = bf16[4,2,128,128]{3,2,1,0:T(8,128)(2,1)} collective-permute-done((bf16[4,2,128,128]{3,2,1,0:T(8,128)(2,1)}, bf16[4,2,128,128]{3,2,1,0:T(8,128)(2,1)}, u32[]{:S(2)}, u32[]{:S(2)}) %collective-permute-start.10) | collective-permute-done | bytes 262176 | tf_op jit(solution)/shard_map/ppermute | solution.py:173
  80.2 0.6 select_reduce_fusion.occ_index
  80.8 3.6 %collective-permute-done.6.refs_3_ = bf16[4,4,64,128]{3,2,1,0:T(8,128)(2,1)S(1)} collective-permute-done((bf16[4,4,64,128]{3,2,1,0:T(8,128)(2,1)S(1)}, bf16[4,4,64,128]{3,2,1,0:T(8,128)(2,1)S(1)}, u32[]{:S(2)}, u32[]{:S(2)}) %collective-permute-start.6) | collective-permute-done | bytes 262176 | tf_op jit(solution)/shard_map/ppermute | solution.py:173
  84.5 0.6 copy-done.8
  85.1 0.2 copy-done.9
  85.2 0.1 copy-done.10
  85.4 0.1 copy-done.6
  85.4 0.2 copy-done.7
  85.6 12.5 %exchange.1 = (f32[4,8,4,16,128]{4,3,2,1,0:T(8,128)}, f32[4,8,4,16,128]{4,3,2,1,0:T(8,128)}) custom-call(s32[4]{0:T(128)} %pad_add_fusion.pos, s32[4,32]{1,0:T(4,128)} %bitcast.26, s32[4,32]{1,0:T(4,128)} %bitcast.25, s32[4,32]{1,0:T(4,128)} %select_reduce_fusion.occ_index, bf16[8,4,64,128]{3,2,1,0:T(8,128)(2,1)} %bitcast.18, ...), custom_call_target="tpu_custom_call" | custom-call | tf_op jit(solution)/shard_map/exchange/pallas_call | solution.py:156
  98.1 0.1 collective-permute-start.17
  98.2 2.9 %collective-permute-done.17 = f32[4,8,4,16,128]{4,3,2,1,0:T(8,128)S(1)} collective-permute-done((f32[4,8,4,16,128]{4,3,2,1,0:T(8,128)}, f32[4,8,4,16,128]{4,3,2,1,0:T(8,128)S(1)}, u32[]{:S(2)}, u32[]{:S(2)}) %collective-permute-start.17) | collective-permute-done | bytes 1048608 | tf_op jit(solution)/shard_map/ppermute | solution.py:177
  101.1 2.2 %add_convert_fusion = bf16[4,8,4,16,128]{4,3,2,1,0:T(8,128)(2,1)} fusion(f32[4,8,4,16,128]{4,3,2,1,0:T(8,128)} %get-tuple-element.21, f32[4,8,4,16,128]{4,3,2,1,0:T(8,128)S(1)} %collective-permute-done.17), kind=kLoop, calls=%fused_computation.1 | loop fusion | flops 524288 | bytes 2621440 | tf_op jit(solution)/shard_map/convert_element_type | solution.py:210
  103.3 5.6 %all-to-all-start.1 = ((bf16[32,4,16,128]{3,2,1,0:T(8,128)(2,1)}), bf16[32,4,16,128]{3,2,1,0:T(8,128)(2,1)S(1)}, u32[]{:S(2)}, u32[]{:S(2)}) async-start(bf16[32,4,16,128]{3,2,1,0:T(8,128)(2,1)} %bitcast.13), calls=%async_computation.1 | async-start | bytes 1048576 | tf_op jit(solution)/shard_map/all_to_all | solution.py:211
  108.9 0.0 copy-start.13
  108.9 0.7 copy-done.13
  109.6 0.2 multiply_reduce_fusion
  109.7 17.1 %all-to-all-done.1 = bf16[32,4,16,128]{3,2,1,0:T(8,128)(2,1)S(1)} async-done(((bf16[32,4,16,128]{3,2,1,0:T(8,128)(2,1)}), bf16[32,4,16,128]{3,2,1,0:T(8,128)(2,1)S(1)}, u32[]{:S(2)}, u32[]{:S(2)}) %all-to-all-start.1) | async-done | bytes 524320 | tf_op jit(solution)/shard_map/all_to_all | solution.py:211
  126.8 0.1 convert_reduce_fusion
  126.9 0.7 bitcast_multiply_fusion
  (38 shorter events, 0.1 us)
Async XLA Ops:
  3.5 8.9 %copy-start.12 = (bf16[64,128]{1,0:T(8,128)(2,1)S(1)}, bf16[64,128]{1,0:T(8,128)(2,1)}, u32[]{:S(2)}) copy-start(bf16[64,128]{1,0:T(8,128)(2,1)} %get-tuple-element.16) | copy-start | bytes 49156
  3.5 8.9 %collective-permute-start = (bf16[4,2,128,128]{3,2,1,0:T(8,128)(2,1)}, bf16[4,2,128,128]{3,2,1,0:T(8,128)(2,1)S(1)}, u32[]{:S(2)}, u32[]{:S(2)}) collective-permute-start(bf16[4,2,128,128]{3,2,1,0:T(8,128)(2,1)} %get-tuple-element.15), channel_id=1, source_target_pairs={{0,32},{32,0},{1,33},{33,1},{2,34},{34,2},{3,35},{35,3},{4,36},{36... | collective-permute-start | bytes 786440 | tf_op jit(solution)/shard_map/ppermute | solution.py:177
  3.6 4.5 %collective-permute-start.3 = (bf16[64,128]{1,0:T(8,128)(2,1)}, bf16[64,128]{1,0:T(8,128)(2,1)S(1)}, u32[]{:S(2)}, u32[]{:S(2)}) collective-permute-start(bf16[64,128]{1,0:T(8,128)(2,1)} %get-tuple-element.16), channel_id=1, source_target_pairs={{0,3},{1,0},{2,1},{3,2},{4,7},{5,4},{6,5},{7,6},{8,11},{9,8},{10,9... | collective-permute-start | bytes 49160 | tf_op jit(solution)/shard_map/ppermute | solution.py:173
  6.5 5.5 %collective-permute-start.2 = (bf16[64,128]{1,0:T(8,128)(2,1)}, bf16[64,128]{1,0:T(8,128)(2,1)S(1)}, u32[]{:S(2)}, u32[]{:S(2)}) collective-permute-start(bf16[64,128]{1,0:T(8,128)(2,1)} %get-tuple-element.16), channel_id=1, source_target_pairs={{0,2},{1,3},{2,0},{3,1},{4,6},{5,7},{6,4},{7,5},{8,10},{9,11},{10,... | collective-permute-start | bytes 49160 | tf_op jit(solution)/shard_map/ppermute | solution.py:173
  7.3 5.2 %collective-permute-start.1 = (bf16[64,128]{1,0:T(8,128)(2,1)}, bf16[64,128]{1,0:T(8,128)(2,1)S(1)}, u32[]{:S(2)}, u32[]{:S(2)}) collective-permute-start(bf16[64,128]{1,0:T(8,128)(2,1)} %get-tuple-element.16), channel_id=1, source_target_pairs={{0,1},{1,2},{2,3},{3,0},{4,5},{5,6},{6,7},{7,4},{8,9},{9,10},{10,1... | collective-permute-start | bytes 49160 | tf_op jit(solution)/shard_map/ppermute | solution.py:173
  14.5 41.8 %all-to-all-start = ((bf16[8,2,128,128]{3,2,1,0:T(8,128)(2,1)}), bf16[8,2,128,128]{3,2,1,0:T(8,128)(2,1)S(1)}, u32[]{:S(2)}, u32[]{:S(2)}) async-start(bf16[8,2,128,128]{3,2,1,0:T(8,128)(2,1)} %fusion.1), calls=%async_computation | async-start | bytes 1048576 | tf_op jit(solution)/shard_map/all_to_all | solution.py:195
  56.3 15.0 %copy-start.1 = (bf16[32,64,128]{2,1,0:T(8,128)(2,1)}, bf16[32,64,128]{2,1,0:T(8,128)(2,1)S(1)}, u32[]{:S(2)}) copy-start(bf16[32,64,128]{2,1,0:T(8,128)(2,1)S(1)} %all-gather) | copy-start | bytes 1572868
  56.3 15.0 %copy-start = (bf16[8,2,128,128]{3,2,1,0:T(8,128)(2,1)}, bf16[8,2,128,128]{3,2,1,0:T(8,128)(2,1)S(1)}, u32[]{:S(2)}) copy-start(bf16[8,2,128,128]{3,2,1,0:T(8,128)(2,1)S(1)} %all-to-all-done.refs_5_) | copy-start | bytes 1572868
  56.3 10.4 %collective-permute-start.5 = (bf16[8,4,64,128]{3,2,1,0:T(8,128)(2,1)S(1)}, bf16[8,4,64,128]{3,2,1,0:T(8,128)(2,1)S(1)}, u32[]{:S(2)}, u32[]{:S(2)}) collective-permute-start(bf16[8,4,64,128]{3,2,1,0:T(8,128)(2,1)S(1)} %bitcast.16), channel_id=1, source_target_pairs={{0,192},{64,0},{128,64},{192,128},{1,193},{65,1},{129,65},{193,129... | collective-permute-start | bytes 1572872 | tf_op jit(solution)/shard_map/ppermute | solution.py:173
  59.4 11.1 %collective-permute-start.9 = (bf16[8,2,128,128]{3,2,1,0:T(8,128)(2,1)S(1)}, bf16[8,2,128,128]{3,2,1,0:T(8,128)(2,1)S(1)}, u32[]{:S(2)}, u32[]{:S(2)}) collective-permute-start(bf16[8,2,128,128]{3,2,1,0:T(8,128)(2,1)S(1)} %all-to-all-done.refs_5_), channel_id=1, source_target_pairs={{0,3},{1,0},{2,1},{3,2},{4,7},{5,4},{6,5},{7,6},{8,11},{9,8},{10,9... | collective-permute-start | bytes 1572872 | tf_op jit(solution)/shard_map/ppermute | solution.py:173
  60.3 11.3 %collective-permute-start.8 = (bf16[8,2,128,128]{3,2,1,0:T(8,128)(2,1)S(1)}, bf16[8,2,128,128]{3,2,1,0:T(8,128)(2,1)S(1)}, u32[]{:S(2)}, u32[]{:S(2)}) collective-permute-start(bf16[8,2,128,128]{3,2,1,0:T(8,128)(2,1)S(1)} %all-to-all-done.refs_5_), channel_id=1, source_target_pairs={{0,1},{1,2},{2,3},{3,0},{4,5},{5,6},{6,7},{7,4},{8,9},{9,10},{10,1... | collective-permute-start | bytes 1572872 | tf_op jit(solution)/shard_map/ppermute | solution.py:173
  61.4 12.7 %collective-permute-start.4 = (bf16[8,4,64,128]{3,2,1,0:T(8,128)(2,1)S(1)}, bf16[8,4,64,128]{3,2,1,0:T(8,128)(2,1)S(1)}, u32[]{:S(2)}, u32[]{:S(2)}) collective-permute-start(bf16[8,4,64,128]{3,2,1,0:T(8,128)(2,1)S(1)} %bitcast.17), channel_id=1, source_target_pairs={{0,64},{64,128},{128,192},{192,0},{1,65},{65,129},{129,193},{193,1... | collective-permute-start | bytes 1572872 | tf_op jit(solution)/shard_map/ppermute | solution.py:173
  61.4 12.8 %collective-permute-start.12 = (bf16[8,2,128,128]{3,2,1,0:T(8,128)(2,1)S(1)}, bf16[8,2,128,128]{3,2,1,0:T(8,128)(2,1)}, u32[]{:S(2)}, u32[]{:S(2)}) collective-permute-start(bf16[8,2,128,128]{3,2,1,0:T(8,128)(2,1)S(1)} %all-to-all-done.refs_5_), channel_id=1, source_target_pairs={{0,32},{32,0},{1,33},{33,1},{2,34},{34,2},{3,35},{35,3},{4,36},{36... | collective-permute-start | bytes 1572872 | tf_op jit(solution)/shard_map/ppermute | solution.py:177
  66.7 17.7 %copy-start.2 = (bf16[8,4,64,128]{3,2,1,0:T(8,128)(2,1)}, bf16[8,4,64,128]{3,2,1,0:T(8,128)(2,1)S(1)}, u32[]{:S(2)}) copy-start(bf16[8,4,64,128]{3,2,1,0:T(8,128)(2,1)S(1)} %collective-permute-done.5.refs_2_) | copy-start | bytes 1572868
  66.8 8.0 %collective-permute-start.7 = (bf16[4,4,64,128]{3,2,1,0:T(8,128)(2,1)S(1)}, bf16[4,4,64,128]{3,2,1,0:T(8,128)(2,1)}, u32[]{:S(2)}, u32[]{:S(2)}) collective-permute-start(bf16[4,4,64,128]{3,2,1,0:T(8,128)(2,1)S(1)} %slice.17), channel_id=1, source_target_pairs={{0,192},{64,0},{128,64},{192,128},{1,193},{65,1},{129,65},{193,129... | collective-permute-start | bytes 786440 | tf_op jit(solution)/shard_map/ppermute | solution.py:173
  70.5 13.9 %copy-start.3 = (bf16[8,2,128,128]{3,2,1,0:T(8,128)(2,1)}, bf16[8,2,128,128]{3,2,1,0:T(8,128)(2,1)S(1)}, u32[]{:S(2)}) copy-start(bf16[8,2,128,128]{3,2,1,0:T(8,128)(2,1)S(1)} %collective-permute-done.9.refs_7_) | copy-start | bytes 1572868
  71.3 2.8 %copy-start.11 = (s32[32,8]{0,1:T(8,128)S(1)}, s32[32,8]{0,1:T(8,128)}, u32[]{:S(2)}) copy-start(s32[32,8]{0,1:T(8,128)} %param.9) | copy-start | bytes 3076
  71.3 6.7 %collective-permute-start.11 = (bf16[4,2,128,128]{3,2,1,0:T(8,128)(2,1)}, bf16[4,2,128,128]{3,2,1,0:T(8,128)(2,1)}, u32[]{:S(2)}, u32[]{:S(2)}) collective-permute-start(bf16[4,2,128,128]{3,2,1,0:T(8,128)(2,1)} %slice.19), channel_id=1, source_target_pairs={{0,3},{1,0},{2,1},{3,2},{4,7},{5,4},{6,5},{7,6},{8,11},{9,8},{10,9... | collective-permute-start | bytes 786440 | tf_op jit(solution)/shard_map/ppermute | solution.py:173
  71.5 12.9 %copy-start.4 = (bf16[8,2,128,128]{3,2,1,0:T(8,128)(2,1)}, bf16[8,2,128,128]{3,2,1,0:T(8,128)(2,1)S(1)}, u32[]{:S(2)}) copy-start(bf16[8,2,128,128]{3,2,1,0:T(8,128)(2,1)S(1)} %collective-permute-done.8.refs_6_) | copy-start | bytes 1572868
  72.3 7.9 %collective-permute-start.10 = (bf16[4,2,128,128]{3,2,1,0:T(8,128)(2,1)}, bf16[4,2,128,128]{3,2,1,0:T(8,128)(2,1)}, u32[]{:S(2)}, u32[]{:S(2)}) collective-permute-start(bf16[4,2,128,128]{3,2,1,0:T(8,128)(2,1)} %slice.18), channel_id=1, source_target_pairs={{0,1},{1,2},{2,3},{3,0},{4,5},{5,6},{6,7},{7,4},{8,9},{9,10},{10,1... | collective-permute-start | bytes 786440 | tf_op jit(solution)/shard_map/ppermute | solution.py:173
  74.1 10.3 %copy-start.5 = (bf16[8,4,64,128]{3,2,1,0:T(8,128)(2,1)}, bf16[8,4,64,128]{3,2,1,0:T(8,128)(2,1)S(1)}, u32[]{:S(2)}) copy-start(bf16[8,4,64,128]{3,2,1,0:T(8,128)(2,1)S(1)} %collective-permute-done.4.refs_1_) | copy-start | bytes 1572868
  74.1 10.3 %collective-permute-start.14 = (bf16[8,2,128,128]{3,2,1,0:T(8,128)(2,1)S(1)}, bf16[8,2,128,128]{3,2,1,0:T(8,128)(2,1)S(1)}, u32[]{:S(2)}, u32[]{:S(2)}) collective-permute-start(bf16[8,2,128,128]{3,2,1,0:T(8,128)(2,1)S(1)} %collective-permute-done.9.refs_7_), channel_id=1, source_target_pairs={{0,32},{32,0},{1,33},{33,1},{2,34},{34,2},{3,35},{35,3},{4,36},{36... | collective-permute-start | bytes 1572872 | tf_op jit(solution)/shard_map/ppermute | solution.py:177
  74.2 10.2 %collective-permute-start.13 = (bf16[8,2,128,128]{3,2,1,0:T(8,128)(2,1)S(1)}, bf16[8,2,128,128]{3,2,1,0:T(8,128)(2,1)S(1)}, u32[]{:S(2)}, u32[]{:S(2)}) collective-permute-start(bf16[8,2,128,128]{3,2,1,0:T(8,128)(2,1)S(1)} %collective-permute-done.8.refs_6_), channel_id=1, source_target_pairs={{0,32},{32,0},{1,33},{33,1},{2,34},{34,2},{3,35},{35,3},{4,36},{36... | collective-permute-start | bytes 1572872 | tf_op jit(solution)/shard_map/ppermute | solution.py:177
  74.8 9.6 %collective-permute-start.6 = (bf16[4,4,64,128]{3,2,1,0:T(8,128)(2,1)S(1)}, bf16[4,4,64,128]{3,2,1,0:T(8,128)(2,1)S(1)}, u32[]{:S(2)}, u32[]{:S(2)}) collective-permute-start(bf16[4,4,64,128]{3,2,1,0:T(8,128)(2,1)S(1)} %slice.16), channel_id=1, source_target_pairs={{0,64},{64,128},{128,192},{192,0},{1,65},{65,129},{129,193},{193,1... | collective-permute-start | bytes 786440 | tf_op jit(solution)/shard_map/ppermute | solution.py:173
  78.0 6.4 %collective-permute-start.16 = (bf16[4,2,128,128]{3,2,1,0:T(8,128)(2,1)}, bf16[4,2,128,128]{3,2,1,0:T(8,128)(2,1)S(1)}, u32[]{:S(2)}, u32[]{:S(2)}) collective-permute-start(bf16[4,2,128,128]{3,2,1,0:T(8,128)(2,1)} %collective-permute-done.11.refs_9_), channel_id=1, source_target_pairs={{0,32},{32,0},{1,33},{33,1},{2,34},{34,2},{3,35},{35,3},{4,36},{36... | collective-permute-start | bytes 786440 | tf_op jit(solution)/shard_map/ppermute | solution.py:177
  80.2 4.2 %collective-permute-start.15 = (bf16[4,2,128,128]{3,2,1,0:T(8,128)(2,1)}, bf16[4,2,128,128]{3,2,1,0:T(8,128)(2,1)S(1)}, u32[]{:S(2)}, u32[]{:S(2)}) collective-permute-start(bf16[4,2,128,128]{3,2,1,0:T(8,128)(2,1)} %collective-permute-done.10.refs_8_), channel_id=1, source_target_pairs={{0,32},{32,0},{1,33},{33,1},{2,34},{34,2},{3,35},{35,3},{4,36},{36... | collective-permute-start | bytes 786440 | tf_op jit(solution)/shard_map/ppermute | solution.py:177
  84.4 0.7 copy-start.8
  84.4 0.9 copy-start.9
  84.4 1.0 copy-start.10
  84.4 1.1 copy-start.6
  84.4 1.2 copy-start.7
  98.1 3.0 %collective-permute-start.17 = (f32[4,8,4,16,128]{4,3,2,1,0:T(8,128)}, f32[4,8,4,16,128]{4,3,2,1,0:T(8,128)S(1)}, u32[]{:S(2)}, u32[]{:S(2)}) collective-permute-start(f32[4,8,4,16,128]{4,3,2,1,0:T(8,128)} %get-tuple-element.22), channel_id=1, source_target_pairs={{0,32},{32,0},{1,33},{33,1},{2,34},{34,2},{3,35},{35,3},{4,36},{36... | collective-permute-start | bytes 3145736 | tf_op jit(solution)/shard_map/ppermute | solution.py:177
  103.3 23.5 %all-to-all-start.1 = ((bf16[32,4,16,128]{3,2,1,0:T(8,128)(2,1)}), bf16[32,4,16,128]{3,2,1,0:T(8,128)(2,1)S(1)}, u32[]{:S(2)}, u32[]{:S(2)}) async-start(bf16[32,4,16,128]{3,2,1,0:T(8,128)(2,1)} %bitcast.13), calls=%async_computation.1 | async-start | bytes 1048576 | tf_op jit(solution)/shard_map/all_to_all | solution.py:211
  108.9 0.7 copy-start.13

commit v4 on v3

--- a/solution.py
+++ b/solution.py
@@ -20,14 +20,20 @@
 VMEM = pl.BlockSpec(memory_space=pltpu.VMEM)
 SMEM = pl.BlockSpec(memory_space=pltpu.SMEM)
 ANY = pl.BlockSpec(memory_space=pl.ANY)
+HBM = pl.BlockSpec(memory_space=pltpu.HBM)
 
 
 def prep_kernel(pos, occ_live, eri, orb, keep, give, coeffs, rows, cols, sems):
     slab, core, tile = pos[0], pos[1], pos[2] * NX + pos[3]
     load_cols = pltpu.make_async_copy(orb, cols, sems.at[0])
-    load_rows = pltpu.make_async_copy(eri, rows, sems.at[1])
+    size = 2 * AUXROWS * TS
+    loads = []
+    for index, part in enumerate((1 - core, core)):
+        span = pl.ds(pl.multiple_of(part * size, size), size)
+        loads.append(pltpu.make_async_copy(eri.at[span], rows.at[span], sems.at[index + 1]))
     load_cols.start()
-    load_rows.start()
+    for load in loads:
+        load.start()
     load_cols.wait()
     count = jnp.int32(0)
     for occ in range(OCC):
@@ -43,8 +49,8 @@
     col = lax.broadcasted_iota(jnp.int32, (TS, TS), 1)
     block_nu = TS // AUXROWS
     perm = (col == (row % block_nu) * AUXROWS + row // block_nu).astype(BF)
-    load_rows.wait()
-    for out, part in ((give, 1 - core), (keep, core)):
+    for out, part, load in ((give, 1 - core, loads[0]), (keep, core, loads[1])):
+        load.wait()
         for j in range(2):
             for quarter in range(AUXROWS):
                 start = pl.multiple_of(((part * 2 + j) * AUXROWS + quarter) * TS, TS)
@@ -58,14 +64,14 @@
     return pl.pallas_call(
         prep_kernel,
         out_shape=(piece, piece, jax.ShapeDtypeStruct((HALF, TS), BF)),
-        in_specs=[SMEM, SMEM, ANY, ANY],
+        in_specs=[SMEM, SMEM, HBM, HBM],
         out_specs=(VMEM, VMEM, VMEM),
         scratch_shapes=[
             pltpu.VMEM(eri.shape, BF),
             pltpu.VMEM(orb.shape, BF),
-            pltpu.SemaphoreType.DMA((2,)),
+            pltpu.SemaphoreType.DMA((3,)),
         ],
-        compiler_params=pltpu.CompilerParams(vmem_limit_bytes=56 * 2**20),
+        compiler_params=pltpu.CompilerParams(vmem_limit_bytes=8 * 2**20),
         name="prep",
     )(pos, occ_live, eri, orb)
 
@@ -164,7 +170,7 @@
             pltpu.VMEM((TS, SLOTS * TS), F32),
             pltpu.SemaphoreType.DMA((len(pieces),)),
         ],
-        compiler_params=pltpu.CompilerParams(vmem_limit_bytes=56 * 2**20),
+        compiler_params=pltpu.CompilerParams(vmem_limit_bytes=24 * 2**20),
         name="exchange",
     )(pos, pair_tiles, pair_live, occ_index, *pieces)
 
@@ -188,12 +194,16 @@
 
     got_eri = swap(give_eri)
     row_coeffs = jnp.stack([coeffs] + [shift(coeffs, "x", NX, by) for by in (1, 2, 3)])
-    got_eri, row_coeffs = lax.optimization_barrier((got_eri, row_coeffs))
     by_aux = lax.dynamic_slice_in_dim(
         jnp.concatenate([keep_eri, got_eri, keep_eri]), pos[1] * AUXROWS, NZ, 0
     )
-    own0 = lax.all_to_all(by_aux, "z", split_axis=0, concat_axis=0, tiled=True)
-    c0 = lax.all_gather(row_coeffs, "z", axis=0)
+    outgoing = jnp.concatenate([
+        by_aux.reshape(NZ, 2 * TS, TS),
+        jnp.broadcast_to(row_coeffs.reshape(1, NX * HALF, TS), (NZ, NX * HALF, TS)),
+    ], axis=1)
+    arrived = lax.all_to_all(outgoing, "z", split_axis=0, concat_axis=0, tiled=True)
+    own0 = arrived[:, :2 * TS].reshape(NZ, 2, TS, TS)
+    c0 = arrived[:, 2 * TS:].reshape(NZ, NX, HALF, TS)
     own0, c0 = lax.optimization_barrier((own0, c0))
     own_r, own_l = shift(own0, "x", NX, 1), shift(own0, "x", NX, -1)
     c_u, c_d = shift(c0, "y", NY, 1), shift(c0, "y", NY, -1)

time: 128 us -> 116 us (0.906)
  starting transfers between devices: 31.2 us -> 21.7 us
  other arithmetic: 6.43 us -> 2.41 us
  Pallas kernels: 15.4 us -> 11.5 us
  waiting for transfers between devices: 37.7 us -> 39.8 us
  local copies, waits for them, and re-layouts: 3.42 us -> 5.05 us
    all_to_all x0 -> x1, blocking collectives: none -> 34.5 us  [shards(): lax.all_to_all(outgoing, 'z', split_axis=0, concat_axis=0, tiled=True)]
    all_gather x1 -> x0, blocking collectives: 33.3 us -> none  [shards(): c0 = lax.all_gather(row_coeffs, 'z', axis=0)]
    all_to_all x1 -> x0, starting transfers between devices: 8.58 us -> none  [shards(): own0 = lax.all_to_all(by_aux, 'z', split_axis=0, concat_axis=0, tiled=True)]
    pallas_call x1, Pallas kernels: 12.5 us -> 10.2 us  [exchange(): pl.pallas_call(main_kernel, out_shape=(shape, shape), in_specs=[SMEM] * 4...]
    concatenate x1, other arithmetic: 2.02 us -> 0.27 us  [shards(): jnp.concatenate([keep_eri, got_eri, keep_eri])]
    ppermute x11, waiting for transfers between devices: 17.8 us -> 19.4 us  [shift(): lax.ppermute(value, axis, [(i, (i + by) % size) for i in range(size)])]
    pallas_call x1, Pallas kernels: 2.89 us -> 1.33 us  [prep(): pl.pallas_call(prep_kernel, out_shape=(piece, piece, jax.ShapeDtypeStruct...]
    unnamed x28 -> x12, local copies, waits for them, and re-layouts: 1.87 us -> 2.7 us
  transfers between devices with their start and end apart: 20 -> 19, of which waited for: 8 -> 9; matrix products, arithmetic and copies ran while one was open for 2% -> 2% of each run, Pallas kernels for 0% -> 0%
where the time goes in v4:
time: 116 us; the launch traced here: 115 us
  waiting for transfers between devices  39.8 us (34%)
  blocking collectives  34.5 us (30%)
  starting transfers between devices  21.7 us (19%)
  Pallas kernels  11.5 us (10%)
  local copies, waits for them, and re-layouts  5.05 us (4%)
  other arithmetic  2.41 us (2%)
    all_to_all x1, blocking collectives, shards(): lax.all_to_all(outgoing, 'z', split_axis=0, concat_axis=0, tiled=True)  34.5 us
    ppermute x11, waiting for transfers between devices, shift(): lax.ppermute(value, axis, [(i, (i + by) % size) for i in range(size)])  19.4 us
    all_to_all x1, waiting for transfers between devices, shards(): lax.all_to_all(partial, ('y', 'z'), split_axis=0, concat_axis=0, tiled=True)  17.7 us
    ppermute x11, starting transfers between devices, shift(): lax.ppermute(value, axis, [(i, (i + by) % size) for i in range(size)])  15.6 us
    pallas_call x1, Pallas kernels, exchange(): pl.pallas_call(main_kernel, out_shape=(shape, shape), in_specs=[SMEM] * 4...  10.2 us
    all_to_all x1, starting transfers between devices, shards(): lax.all_to_all(partial, ('y', 'z'), split_axis=0, concat_axis=0, tiled=True)  5.28 us
    unnamed x12, local copies, waits for them, and re-layouts  2.7 us
    ppermute x7, waiting for transfers between devices, swap(): return lax.ppermute(value, 'c', [(0, 1), (1, 0)])  2.66 us
  transfers between devices with their start and end apart: 19, of which 9 were waited for; matrix products, arithmetic and copies ran while one was open for 2% of the time, Pallas kernels for 0%

profile of v4, /device:TPU:32, one launch (start us, length us, event | category | flops | bytes accessed | tf_op | source)
XLA Modules:
  0.0 115.2 jit_solution(16409363623885057651)
XLA Ops:
  0.0 0.1 pad_add_fusion.pos
  0.1 1.0 copy-done
  1.1 0.9 copy-done.1
  2.1 0.7 copy-done.2
  2.8 1.3 %prep.1 = (bf16[4,2,128,128]{3,2,1,0:T(8,128)(2,1)S(1)}, bf16[4,2,128,128]{3,2,1,0:T(8,128)(2,1)S(1)}, bf16[64,128]{1,0:T(8,128)(2,1)S(1)}) custom-call(s32[4]{0:T(128)S(1)} %pad_add_fusion.pos, s32[8,32]{1,0:T(8,128)S(1)} %bitcast.27, bf16[2048,128]{1,0:T(8,128)(2,1)S(1)} %bitcast.26, bf16[128,1024]{1,0:T(8,128)(2,1)S(1)} %copy-done.1), custom_call_target="tpu_custom_call" | custom-call | tf_op jit(solution)/shard_map/prep/pallas_call | solution.py:64
  4.1 0.1 collective-permute-start
  4.2 2.8 %collective-permute-start.3 = (bf16[64,128]{1,0:T(8,128)(2,1)S(1)}, bf16[64,128]{1,0:T(8,128)(2,1)S(1)}, u32[]{:S(2)}, u32[]{:S(2)}) collective-permute-start(bf16[64,128]{1,0:T(8,128)(2,1)S(1)} %get-tuple-element.14), channel_id=1, source_target_pairs={{0,3},{1,0},{2,1},{3,2},{4,7},{5,4},{6,5},{7,6},{8,11},{9,8},{10,9... | collective-permute-start | bytes 49160 | tf_op jit(solution)/shard_map/ppermute | solution.py:179
  7.0 0.8 collective-permute-start.2
  7.8 0.9 collective-permute-start.1
  8.7 0.0 collective-permute-done.3
  8.7 3.6 %collective-permute-done.2 = bf16[64,128]{1,0:T(8,128)(2,1)S(1)} collective-permute-done((bf16[64,128]{1,0:T(8,128)(2,1)S(1)}, bf16[64,128]{1,0:T(8,128)(2,1)S(1)}, u32[]{:S(2)}, u32[]{:S(2)}) %collective-permute-start.2) | collective-permute-done | bytes 16416 | tf_op jit(solution)/shard_map/ppermute | solution.py:179
  12.3 0.5 collective-permute-done.1
  12.8 0.0 collective-permute-done
  12.8 0.3 fusion.1
  13.1 0.1 broadcast_in_dim.28
  13.2 0.1 pad_maximum_fusion
  13.2 34.5 %all_to_all.10 = bf16[8,512,128]{2,1,0:T(8,128)(2,1)S(1)} all-to-all(bf16[8,512,128]{2,1,0:T(8,128)(2,1)S(1)} %pad_maximum_fusion), channel_id=1, replica_groups=mesh['y'=4,'c'=2,'z'=8,'x'=4] {'z'}, dimensions={0} | all-to-all | bytes 2097152 | tf_op jit(solution)/shard_map/all_to_all | solution.py:204
  47.8 0.1 fusion.3
  47.9 0.0 copy-start.3
  47.9 0.0 copy-start.4
  47.9 0.0 copy-start.5
  47.9 3.1 %collective-permute-start.5 = (bf16[8,4,64,128]{3,2,1,0:T(8,128)(2,1)S(1)}, bf16[8,4,64,128]{3,2,1,0:T(8,128)(2,1)S(1)}, u32[]{:S(2)}, u32[]{:S(2)}) collective-permute-start(bf16[8,4,64,128]{3,2,1,0:T(8,128)(2,1)S(1)} %bitcast.19), channel_id=1, source_target_pairs={{0,192},{64,0},{128,64},{192,128},{1,193},{65,1},{129,65},{193,129... | collective-permute-start | bytes 1572872 | tf_op jit(solution)/shard_map/ppermute | solution.py:179
  51.0 0.8 collective-permute-start.9
  51.8 1.2 %collective-permute-start.8 = (bf16[8,2,128,128]{3,2,1,0:T(8,128)(2,1)S(1)}, bf16[8,2,128,128]{3,2,1,0:T(8,128)(2,1)S(1)}, u32[]{:S(2)}, u32[]{:S(2)}) collective-permute-start(bf16[8,2,128,128]{3,2,1,0:T(8,128)(2,1)S(1)} %bitcast.23), channel_id=1, source_target_pairs={{0,1},{1,2},{2,3},{3,0},{4,5},{5,6},{6,7},{7,4},{8,9},{9,10},{10,1... | collective-permute-start | bytes 1572872 | tf_op jit(solution)/shard_map/ppermute | solution.py:179
  53.0 6.1 %collective-permute-done.5.refs_2_ = bf16[8,4,64,128]{3,2,1,0:T(8,128)(2,1)S(1)} collective-permute-done((bf16[8,4,64,128]{3,2,1,0:T(8,128)(2,1)S(1)}, bf16[8,4,64,128]{3,2,1,0:T(8,128)(2,1)S(1)}, u32[]{:S(2)}, u32[]{:S(2)}) %collective-permute-start.5) | collective-permute-done | bytes 524320 | tf_op jit(solution)/shard_map/ppermute | solution.py:179
  59.1 0.7 slice.27
  59.8 3.7 %collective-permute-start.7 = (bf16[4,4,64,128]{3,2,1,0:T(8,128)(2,1)}, bf16[4,4,64,128]{3,2,1,0:T(8,128)(2,1)S(1)}, u32[]{:S(2)}, u32[]{:S(2)}) collective-permute-start(bf16[4,4,64,128]{3,2,1,0:T(8,128)(2,1)} %slice.27), channel_id=1, source_target_pairs={{0,192},{64,0},{128,64},{192,128},{1,193},{65,1},{129,65},{193,129... | collective-permute-start | bytes 786440 | tf_op jit(solution)/shard_map/ppermute | solution.py:179
  63.5 0.7 slice.29
  64.3 0.9 collective-permute-start.11
  65.2 0.7 slice.28
  65.9 1.1 collective-permute-start.10
  67.0 0.1 collective-permute-start.14
  67.1 0.5 collective-permute-start.13
  67.7 0.1 collective-permute-done.7.refs_4_
  67.7 0.3 collective-permute-start.6
  68.0 2.9 %collective-permute-done.11.refs_9_ = bf16[4,2,128,128]{3,2,1,0:T(8,128)(2,1)} collective-permute-done((bf16[4,2,128,128]{3,2,1,0:T(8,128)(2,1)}, bf16[4,2,128,128]{3,2,1,0:T(8,128)(2,1)}, u32[]{:S(2)}, u32[]{:S(2)}) %collective-permute-start.11) | collective-permute-done | bytes 262176 | tf_op jit(solution)/shard_map/ppermute | solution.py:179
  70.9 0.0 collective-permute-start.16
  70.9 2.9 %collective-permute-done.10.refs_8_ = bf16[4,2,128,128]{3,2,1,0:T(8,128)(2,1)} collective-permute-done((bf16[4,2,128,128]{3,2,1,0:T(8,128)(2,1)}, bf16[4,2,128,128]{3,2,1,0:T(8,128)(2,1)}, u32[]{:S(2)}, u32[]{:S(2)}) %collective-permute-start.10) | collective-permute-done | bytes 262176 | tf_op jit(solution)/shard_map/ppermute | solution.py:179
  73.8 3.4 %collective-permute-done.6.refs_3_ = bf16[4,4,64,128]{3,2,1,0:T(8,128)(2,1)S(1)} collective-permute-done((bf16[4,4,64,128]{3,2,1,0:T(8,128)(2,1)S(1)}, bf16[4,4,64,128]{3,2,1,0:T(8,128)(2,1)S(1)}, u32[]{:S(2)}, u32[]{:S(2)}) %collective-permute-start.6) | collective-permute-done | bytes 262176 | tf_op jit(solution)/shard_map/ppermute | solution.py:179
  77.3 10.2 %exchange.1 = (f32[4,8,4,16,128]{4,3,2,1,0:T(8,128)S(1)}, f32[4,8,4,16,128]{4,3,2,1,0:T(8,128)S(1)}) custom-call(s32[4]{0:T(128)S(1)} %pad_add_fusion.pos, s32[4,32]{1,0:T(4,128)S(1)} %bitcast.30, s32[4,32]{1,0:T(4,128)S(1)} %bitcast.29, s32[4,32]{1,0:T(4,128)S(1)} %select_reduce_fusion.occ_index, bf16[8,4,64,128]{3,2,1,0:T(8,128)(2,1)S(1)} %bitcast.21, ...), custom_call_target="tpu_custom_call" | custom-call | tf_op jit(solution)/shard_map/exchange/pallas_call | solution.py:162
  87.5 0.1 collective-permute-start.17
  87.6 2.6 %collective-permute-done.17 = f32[4,8,4,16,128]{4,3,2,1,0:T(8,128)S(1)} collective-permute-done((f32[4,8,4,16,128]{4,3,2,1,0:T(8,128)S(1)}, f32[4,8,4,16,128]{4,3,2,1,0:T(8,128)S(1)}, u32[]{:S(2)}, u32[]{:S(2)}) %collective-permute-start.17) | collective-permute-done | bytes 1048608 | tf_op jit(solution)/shard_map/ppermute | solution.py:183
  90.3 1.0 add_convert_fusion
  91.2 5.3 %all-to-all-start.1 = ((bf16[32,4,16,128]{3,2,1,0:T(8,128)(2,1)}), bf16[32,4,16,128]{3,2,1,0:T(8,128)(2,1)S(1)}, u32[]{:S(2)}, u32[]{:S(2)}) async-start(bf16[32,4,16,128]{3,2,1,0:T(8,128)(2,1)} %bitcast.16), calls=%async_computation.1 | async-start | bytes 1048576 | tf_op jit(solution)/shard_map/all_to_all | solution.py:221
  96.5 0.2 multiply_reduce_fusion
  96.7 17.7 %all-to-all-done.1 = bf16[32,4,16,128]{3,2,1,0:T(8,128)(2,1)S(1)} async-done(((bf16[32,4,16,128]{3,2,1,0:T(8,128)(2,1)}), bf16[32,4,16,128]{3,2,1,0:T(8,128)(2,1)S(1)}, u32[]{:S(2)}, u32[]{:S(2)}) %all-to-all-start.1) | async-done | bytes 524320 | tf_op jit(solution)/shard_map/all_to_all | solution.py:221
  114.5 0.1 convert_reduce_fusion
  114.5 0.7 bitcast_multiply_fusion
  (23 shorter events, 0.1 us)
Async XLA Ops:
  0.1 1.0 copy-start
  1.1 0.9 copy-start.1
  2.1 0.7 copy-start.2
  4.1 8.7 %collective-permute-start = (bf16[4,2,128,128]{3,2,1,0:T(8,128)(2,1)S(1)}, bf16[4,2,128,128]{3,2,1,0:T(8,128)(2,1)S(1)}, u32[]{:S(2)}, u32[]{:S(2)}) collective-permute-start(bf16[4,2,128,128]{3,2,1,0:T(8,128)(2,1)S(1)} %get-tuple-element.13), channel_id=1, source_target_pairs={{0,32},{32,0},{1,33},{33,1},{2,34},{34,2},{3,35},{35,3},{4,36},{36... | collective-permute-start | bytes 786440 | tf_op jit(solution)/shard_map/ppermute | solution.py:183
  4.2 4.5 %collective-permute-start.3 = (bf16[64,128]{1,0:T(8,128)(2,1)S(1)}, bf16[64,128]{1,0:T(8,128)(2,1)S(1)}, u32[]{:S(2)}, u32[]{:S(2)}) collective-permute-start(bf16[64,128]{1,0:T(8,128)(2,1)S(1)} %get-tuple-element.14), channel_id=1, source_target_pairs={{0,3},{1,0},{2,1},{3,2},{4,7},{5,4},{6,5},{7,6},{8,11},{9,8},{10,9... | collective-permute-start | bytes 49160 | tf_op jit(solution)/shard_map/ppermute | solution.py:179
  7.0 5.2 %collective-permute-start.2 = (bf16[64,128]{1,0:T(8,128)(2,1)S(1)}, bf16[64,128]{1,0:T(8,128)(2,1)S(1)}, u32[]{:S(2)}, u32[]{:S(2)}) collective-permute-start(bf16[64,128]{1,0:T(8,128)(2,1)S(1)} %get-tuple-element.14), channel_id=1, source_target_pairs={{0,2},{1,3},{2,0},{3,1},{4,6},{5,7},{6,4},{7,5},{8,10},{9,11},{10,... | collective-permute-start | bytes 49160 | tf_op jit(solution)/shard_map/ppermute | solution.py:179
  7.8 4.9 %collective-permute-start.1 = (bf16[64,128]{1,0:T(8,128)(2,1)S(1)}, bf16[64,128]{1,0:T(8,128)(2,1)S(1)}, u32[]{:S(2)}, u32[]{:S(2)}) collective-permute-start(bf16[64,128]{1,0:T(8,128)(2,1)S(1)} %get-tuple-element.14), channel_id=1, source_target_pairs={{0,1},{1,2},{2,3},{3,0},{4,5},{5,6},{6,7},{7,4},{8,9},{9,10},{10,1... | collective-permute-start | bytes 49160 | tf_op jit(solution)/shard_map/ppermute | solution.py:179
  47.9 19.1 %copy-start.3 = (s32[32,8]{0,1:T(8,128)S(1)}, s32[32,8]{0,1:T(8,128)}, u32[]{:S(2)}) copy-start(s32[32,8]{0,1:T(8,128)} %param.9) | copy-start | bytes 3076
  47.9 29.4 %copy-start.4 = (s32[32,4]{0,1:T(4,128)S(1)}, s32[32,4]{0,1:T(4,128)}, u32[]{:S(2)}) copy-start(s32[32,4]{0,1:T(4,128)} %param.8) | copy-start | bytes 1540
  47.9 29.4 %copy-start.5 = (s32[32,4]{0,1:T(4,128)S(1)}, s32[32,4]{0,1:T(4,128)}, u32[]{:S(2)}) copy-start(s32[32,4]{0,1:T(4,128)} %param.7) | copy-start | bytes 1540
  47.9 11.2 %collective-permute-start.5 = (bf16[8,4,64,128]{3,2,1,0:T(8,128)(2,1)S(1)}, bf16[8,4,64,128]{3,2,1,0:T(8,128)(2,1)S(1)}, u32[]{:S(2)}, u32[]{:S(2)}) collective-permute-start(bf16[8,4,64,128]{3,2,1,0:T(8,128)(2,1)S(1)} %bitcast.19), channel_id=1, source_target_pairs={{0,192},{64,0},{128,64},{192,128},{1,193},{65,1},{129,65},{193,129... | collective-permute-start | bytes 1572872 | tf_op jit(solution)/shard_map/ppermute | solution.py:179
  51.0 12.5 %collective-permute-start.9 = (bf16[8,2,128,128]{3,2,1,0:T(8,128)(2,1)S(1)}, bf16[8,2,128,128]{3,2,1,0:T(8,128)(2,1)S(1)}, u32[]{:S(2)}, u32[]{:S(2)}) collective-permute-start(bf16[8,2,128,128]{3,2,1,0:T(8,128)(2,1)S(1)} %bitcast.22), channel_id=1, source_target_pairs={{0,3},{1,0},{2,1},{3,2},{4,7},{5,4},{6,5},{7,6},{8,11},{9,8},{10,9... | collective-permute-start | bytes 1572872 | tf_op jit(solution)/shard_map/ppermute | solution.py:179
  51.8 13.4 %collective-permute-start.8 = (bf16[8,2,128,128]{3,2,1,0:T(8,128)(2,1)S(1)}, bf16[8,2,128,128]{3,2,1,0:T(8,128)(2,1)S(1)}, u32[]{:S(2)}, u32[]{:S(2)}) collective-permute-start(bf16[8,2,128,128]{3,2,1,0:T(8,128)(2,1)S(1)} %bitcast.23), channel_id=1, source_target_pairs={{0,1},{1,2},{2,3},{3,0},{4,5},{5,6},{6,7},{7,4},{8,9},{9,10},{10,1... | collective-permute-start | bytes 1572872 | tf_op jit(solution)/shard_map/ppermute | solution.py:179
  53.0 14.0 %collective-permute-start.4 = (bf16[8,4,64,128]{3,2,1,0:T(8,128)(2,1)S(1)}, bf16[8,4,64,128]{3,2,1,0:T(8,128)(2,1)S(1)}, u32[]{:S(2)}, u32[]{:S(2)}) collective-permute-start(bf16[8,4,64,128]{3,2,1,0:T(8,128)(2,1)S(1)} %bitcast.20), channel_id=1, source_target_pairs={{0,64},{64,128},{128,192},{192,0},{1,65},{65,129},{129,193},{193,1... | collective-permute-start | bytes 1572872 | tf_op jit(solution)/shard_map/ppermute | solution.py:179
  53.0 14.1 %collective-permute-start.12 = (bf16[8,2,128,128]{3,2,1,0:T(8,128)(2,1)S(1)}, bf16[8,2,128,128]{3,2,1,0:T(8,128)(2,1)}, u32[]{:S(2)}, u32[]{:S(2)}) collective-permute-start(bf16[8,2,128,128]{3,2,1,0:T(8,128)(2,1)S(1)} %bitcast.24), channel_id=1, source_target_pairs={{0,32},{32,0},{1,33},{33,1},{2,34},{34,2},{3,35},{35,3},{4,36},{36... | collective-permute-start | bytes 1572872 | tf_op jit(solution)/shard_map/ppermute | solution.py:183
  59.8 7.9 %collective-permute-start.7 = (bf16[4,4,64,128]{3,2,1,0:T(8,128)(2,1)}, bf16[4,4,64,128]{3,2,1,0:T(8,128)(2,1)S(1)}, u32[]{:S(2)}, u32[]{:S(2)}) collective-permute-start(bf16[4,4,64,128]{3,2,1,0:T(8,128)(2,1)} %slice.27), channel_id=1, source_target_pairs={{0,192},{64,0},{128,64},{192,128},{1,193},{65,1},{129,65},{193,129... | collective-permute-start | bytes 786440 | tf_op jit(solution)/shard_map/ppermute | solution.py:179
  64.3 6.7 %collective-permute-start.11 = (bf16[4,2,128,128]{3,2,1,0:T(8,128)(2,1)}, bf16[4,2,128,128]{3,2,1,0:T(8,128)(2,1)}, u32[]{:S(2)}, u32[]{:S(2)}) collective-permute-start(bf16[4,2,128,128]{3,2,1,0:T(8,128)(2,1)} %slice.29), channel_id=1, source_target_pairs={{0,3},{1,0},{2,1},{3,2},{4,7},{5,4},{6,5},{7,6},{8,11},{9,8},{10,9... | collective-permute-start | bytes 786440 | tf_op jit(solution)/shard_map/ppermute | solution.py:179
  65.9 7.9 %collective-permute-start.10 = (bf16[4,2,128,128]{3,2,1,0:T(8,128)(2,1)}, bf16[4,2,128,128]{3,2,1,0:T(8,128)(2,1)}, u32[]{:S(2)}, u32[]{:S(2)}) collective-permute-start(bf16[4,2,128,128]{3,2,1,0:T(8,128)(2,1)} %slice.28), channel_id=1, source_target_pairs={{0,1},{1,2},{2,3},{3,0},{4,5},{5,6},{6,7},{7,4},{8,9},{9,10},{10,1... | collective-permute-start | bytes 786440 | tf_op jit(solution)/shard_map/ppermute | solution.py:179
  67.0 10.2 %collective-permute-start.14 = (bf16[8,2,128,128]{3,2,1,0:T(8,128)(2,1)S(1)}, bf16[8,2,128,128]{3,2,1,0:T(8,128)(2,1)S(1)}, u32[]{:S(2)}, u32[]{:S(2)}) collective-permute-start(bf16[8,2,128,128]{3,2,1,0:T(8,128)(2,1)S(1)} %collective-permute-done.9.refs_7_), channel_id=1, source_target_pairs={{0,32},{32,0},{1,33},{33,1},{2,34},{34,2},{3,35},{35,3},{4,36},{36... | collective-permute-start | bytes 1572872 | tf_op jit(solution)/shard_map/ppermute | solution.py:183
  67.1 10.1 %collective-permute-start.13 = (bf16[8,2,128,128]{3,2,1,0:T(8,128)(2,1)S(1)}, bf16[8,2,128,128]{3,2,1,0:T(8,128)(2,1)S(1)}, u32[]{:S(2)}, u32[]{:S(2)}) collective-permute-start(bf16[8,2,128,128]{3,2,1,0:T(8,128)(2,1)S(1)} %collective-permute-done.8.refs_6_), channel_id=1, source_target_pairs={{0,32},{32,0},{1,33},{33,1},{2,34},{34,2},{3,35},{35,3},{4,36},{36... | collective-permute-start | bytes 1572872 | tf_op jit(solution)/shard_map/ppermute | solution.py:183
  67.7 9.5 %collective-permute-start.6 = (bf16[4,4,64,128]{3,2,1,0:T(8,128)(2,1)S(1)}, bf16[4,4,64,128]{3,2,1,0:T(8,128)(2,1)S(1)}, u32[]{:S(2)}, u32[]{:S(2)}) collective-permute-start(bf16[4,4,64,128]{3,2,1,0:T(8,128)(2,1)S(1)} %slice.26), channel_id=1, source_target_pairs={{0,64},{64,128},{128,192},{192,0},{1,65},{65,129},{129,193},{193,1... | collective-permute-start | bytes 786440 | tf_op jit(solution)/shard_map/ppermute | solution.py:179
  70.9 6.3 %collective-permute-start.16 = (bf16[4,2,128,128]{3,2,1,0:T(8,128)(2,1)}, bf16[4,2,128,128]{3,2,1,0:T(8,128)(2,1)S(1)}, u32[]{:S(2)}, u32[]{:S(2)}) collective-permute-start(bf16[4,2,128,128]{3,2,1,0:T(8,128)(2,1)} %collective-permute-done.11.refs_9_), channel_id=1, source_target_pairs={{0,32},{32,0},{1,33},{33,1},{2,34},{34,2},{3,35},{35,3},{4,36},{36... | collective-permute-start | bytes 786440 | tf_op jit(solution)/shard_map/ppermute | solution.py:183
  73.8 3.5 %collective-permute-start.15 = (bf16[4,2,128,128]{3,2,1,0:T(8,128)(2,1)}, bf16[4,2,128,128]{3,2,1,0:T(8,128)(2,1)S(1)}, u32[]{:S(2)}, u32[]{:S(2)}) collective-permute-start(bf16[4,2,128,128]{3,2,1,0:T(8,128)(2,1)} %collective-permute-done.10.refs_8_), channel_id=1, source_target_pairs={{0,32},{32,0},{1,33},{33,1},{2,34},{34,2},{3,35},{35,3},{4,36},{36... | collective-permute-start | bytes 786440 | tf_op jit(solution)/shard_map/ppermute | solution.py:183
  87.5 2.7 %collective-permute-start.17 = (f32[4,8,4,16,128]{4,3,2,1,0:T(8,128)S(1)}, f32[4,8,4,16,128]{4,3,2,1,0:T(8,128)S(1)}, u32[]{:S(2)}, u32[]{:S(2)}) collective-permute-start(f32[4,8,4,16,128]{4,3,2,1,0:T(8,128)S(1)} %get-tuple-element.18), channel_id=1, source_target_pairs={{0,32},{32,0},{1,33},{33,1},{2,34},{34,2},{3,35},{35,3},{4,36},{36... | collective-permute-start | bytes 3145736 | tf_op jit(solution)/shard_map/ppermute | solution.py:183
  91.2 23.2 %all-to-all-start.1 = ((bf16[32,4,16,128]{3,2,1,0:T(8,128)(2,1)}), bf16[32,4,16,128]{3,2,1,0:T(8,128)(2,1)S(1)}, u32[]{:S(2)}, u32[]{:S(2)}) async-start(bf16[32,4,16,128]{3,2,1,0:T(8,128)(2,1)} %bitcast.16), calls=%async_computation.1 | async-start | bytes 1048576 | tf_op jit(solution)/shard_map/all_to_all | solution.py:221

commit v5 on v4

--- a/solution.py
+++ b/solution.py
@@ -42,7 +42,9 @@
         @pl.when(live & (count == slab))
         def _():
             flipped = cols[:, occ * TS:(occ + 1) * TS].astype(F32).T.astype(BF)
-            coeffs[...] = jnp.where(core == 0, flipped[:HALF], flipped[HALF:])
+            mine = jnp.where(core == 0, flipped[:HALF], flipped[HALF:])
+            for target in range(NZ):
+                coeffs[target] = mine
 
         count = count + jnp.where(live, 1, 0)
     row = lax.broadcasted_iota(jnp.int32, (TS, TS), 0)
@@ -63,7 +65,7 @@
     piece = jax.ShapeDtypeStruct((AUXROWS, 2, TS, TS), BF)
     return pl.pallas_call(
         prep_kernel,
-        out_shape=(piece, piece, jax.ShapeDtypeStruct((HALF, TS), BF)),
+        out_shape=(piece, piece, jax.ShapeDtypeStruct((NZ, HALF, TS), BF)),
         in_specs=[SMEM, SMEM, HBM, HBM],
         out_specs=(VMEM, VMEM, VMEM),
         scratch_shapes=[
@@ -193,18 +195,13 @@
     occ_index = jnp.sum(jnp.where(hits, jnp.arange(OCC)[None, None, :], 0), axis=2).astype(jnp.int32)
 
     got_eri = swap(give_eri)
-    row_coeffs = jnp.stack([coeffs] + [shift(coeffs, "x", NX, by) for by in (1, 2, 3)])
+    column = lax.all_to_all(coeffs, "z", split_axis=0, concat_axis=0, tiled=True)
+    got_eri, column = lax.optimization_barrier((got_eri, column))
     by_aux = lax.dynamic_slice_in_dim(
         jnp.concatenate([keep_eri, got_eri, keep_eri]), pos[1] * AUXROWS, NZ, 0
     )
-    outgoing = jnp.concatenate([
-        by_aux.reshape(NZ, 2 * TS, TS),
-        jnp.broadcast_to(row_coeffs.reshape(1, NX * HALF, TS), (NZ, NX * HALF, TS)),
-    ], axis=1)
-    arrived = lax.all_to_all(outgoing, "z", split_axis=0, concat_axis=0, tiled=True)
-    own0 = arrived[:, :2 * TS].reshape(NZ, 2, TS, TS)
-    c0 = arrived[:, 2 * TS:].reshape(NZ, NX, HALF, TS)
-    own0, c0 = lax.optimization_barrier((own0, c0))
+    own0 = lax.all_to_all(by_aux, "z", split_axis=0, concat_axis=0, tiled=True)
+    c0 = jnp.stack([column] + [shift(column, "x", NX, by) for by in (1, 2, 3)], axis=1)
     own_r, own_l = shift(own0, "x", NX, 1), shift(own0, "x", NX, -1)
     c_u, c_d = shift(c0, "y", NY, 1), shift(c0, "y", NY, -1)
     oth0 = swap(own0)

time: 116 us -> 110 us (0.948)
  blocking collectives: 34.5 us -> 0 us
  starting transfers between devices: 21.7 us -> 40.7 us
  waiting for transfers between devices: 39.8 us -> 48.3 us
    all_to_all x1 -> x0, blocking collectives: 34.5 us -> none  [shards(): lax.all_to_all(outgoing, 'z', split_axis=0, concat_axis=0, tiled=True)]
    all_to_all x0 -> x2, starting transfers between devices: none -> 13.5 us  [the longest x1 8.58 us: shards(): lax.all_to_all(coeffs, 'z', split_axis=0, concat_axis=0, tiled=True)]
    all_to_all x0 -> x2, waiting for transfers between devices: none -> 9.6 us  [the longest x1 8.17 us: shards(): lax.all_to_all(coeffs, 'z', split_axis=0, concat_axis=0, tiled=True)]
    all_to_all x1, starting transfers between devices: 5.28 us -> 9.72 us  [shards(): lax.all_to_all(partial, ('y', 'z'), split_axis=0, concat_axis=0, tiled=True)]
    ppermute x11, waiting for transfers between devices: 19.4 us -> 16.7 us  [shift(): lax.ppermute(value, axis, [(i, (i + by) % size) for i in range(size)])]
    ppermute x7, waiting for transfers between devices: 2.66 us -> 4.2 us  [swap(): return lax.ppermute(value, 'c', [(0, 1), (1, 0)])]
    unnamed x12 -> x10, local copies, waits for them, and re-layouts: 2.7 us -> 2.61 us
  transfers between devices with their start and end apart: 19 -> 21, of which waited for: 9 -> 12; matrix products, arithmetic and copies ran while one was open for 2% -> 3% of each run, Pallas kernels for 0% -> 0%
where the time goes in v5:
time: 110 us
  waiting for transfers between devices  48.3 us (44%)
  starting transfers between devices  40.7 us (37%)
  Pallas kernels  11.9 us (11%)
  local copies, waits for them, and re-layouts  5.49 us (5%)
  other arithmetic  3.19 us (3%)
    all_to_all x1, waiting for transfers between devices, shards(): lax.all_to_all(partial, ('y', 'z'), split_axis=0, concat_axis=0, tiled=True)  17.7 us
    ppermute x11, waiting for transfers between devices, shift(): lax.ppermute(value, axis, [(i, (i + by) % size) for i in range(size)])  16.7 us
    ppermute x11, starting transfers between devices, shift(): lax.ppermute(value, axis, [(i, (i + by) % size) for i in range(size)])  16 us
    pallas_call x1, Pallas kernels, exchange(): pl.pallas_call(main_kernel, out_shape=(shape, shape), in_specs=[SMEM] * 4...  10.1 us
    all_to_all x1, starting transfers between devices, shards(): lax.all_to_all(partial, ('y', 'z'), split_axis=0, concat_axis=0, tiled=True)  9.72 us
    all_to_all x1, starting transfers between devices, shards(): lax.all_to_all(coeffs, 'z', split_axis=0, concat_axis=0, tiled=True)  8.58 us
    all_to_all x1, waiting for transfers between devices, shards(): lax.all_to_all(coeffs, 'z', split_axis=0, concat_axis=0, tiled=True)  8.17 us
    all_to_all x1, starting transfers between devices, shards(): own0 = lax.all_to_all(by_aux, 'z', split_axis=0, concat_axis=0, tiled=True)  4.95 us
  transfers between devices with their start and end apart: 21, of which 12 were waited for; matrix products, arithmetic and copies ran while one was open for 3% of the time, Pallas kernels for 0%

profile of v5, /device:TPU:32, one launch (start us, length us, event | category | flops | bytes accessed | tf_op | source)
XLA Modules:
  0.0 109.7 jit_solution(2182446509112614828)
XLA Ops:
  0.0 0.1 pad_add_fusion.pos
  0.1 0.6 copy-done.2
  0.7 1.0 copy-done
  1.7 0.9 copy-done.1
  2.7 1.8 %prep.1 = (bf16[4,2,128,128]{3,2,1,0:T(8,128)(2,1)S(1)}, bf16[4,2,128,128]{3,2,1,0:T(8,128)(2,1)S(1)}, bf16[8,64,128]{2,1,0:T(8,128)(2,1)}) custom-call(s32[4]{0:T(128)S(1)} %pad_add_fusion.pos, s32[8,32]{1,0:T(8,128)S(1)} %bitcast.22, bf16[2048,128]{1,0:T(8,128)(2,1)S(1)} %bitcast.21, bf16[128,1024]{1,0:T(8,128)(2,1)S(1)} %copy-done.1), custom_call_target="tpu_custom_call" | custom-call | tf_op jit(solution)/shard_map/prep/pallas_call | solution.py:66
  4.5 0.1 collective-permute-start
  4.6 8.6 %all-to-all-start = ((bf16[8,64,128]{2,1,0:T(8,128)(2,1)}), bf16[8,64,128]{2,1,0:T(8,128)(2,1)S(1)}, u32[]{:S(2)}, u32[]{:S(2)}) async-start(bf16[8,64,128]{2,1,0:T(8,128)(2,1)} %get-tuple-element.13), calls=%async_computation | async-start | bytes 262144 | tf_op jit(solution)/shard_map/all_to_all | solution.py:198
  13.1 8.2 %all-to-all-done = bf16[8,64,128]{2,1,0:T(8,128)(2,1)S(1)} async-done(((bf16[8,64,128]{2,1,0:T(8,128)(2,1)}), bf16[8,64,128]{2,1,0:T(8,128)(2,1)S(1)}, u32[]{:S(2)}, u32[]{:S(2)}) %all-to-all-start) | async-done | bytes 131104 | tf_op jit(solution)/shard_map/all_to_all | solution.py:198
  21.3 0.0 collective-permute-done
  21.3 1.1 fusion.1
  22.4 4.9 %all-to-all-start.1 = ((bf16[8,2,128,128]{3,2,1,0:T(8,128)(2,1)}), bf16[8,2,128,128]{3,2,1,0:T(8,128)(2,1)S(1)}, u32[]{:S(2)}, u32[]{:S(2)}) async-start(bf16[8,2,128,128]{3,2,1,0:T(8,128)(2,1)} %fusion.1), calls=%async_computation.1 | async-start | bytes 1048576 | tf_op jit(solution)/shard_map/all_to_all | solution.py:203
  27.3 2.8 %collective-permute-start.3 = (bf16[8,64,128]{2,1,0:T(8,128)(2,1)S(1)}, bf16[8,64,128]{2,1,0:T(8,128)(2,1)S(1)}, u32[]{:S(2)}, u32[]{:S(2)}) collective-permute-start(bf16[8,64,128]{2,1,0:T(8,128)(2,1)S(1)} %all-to-all-done), channel_id=1, source_target_pairs={{0,3},{1,0},{2,1},{3,2},{4,7},{5,4},{6,5},{7,6},{8,11},{9,8},{10,9... | collective-permute-start | bytes 393224 | tf_op jit(solution)/shard_map/ppermute | solution.py:181
  30.1 0.8 collective-permute-start.2
  30.9 0.9 collective-permute-start.1
  31.8 2.9 %collective-permute-done.3 = bf16[8,64,128]{2,1,0:T(8,128)(2,1)S(1)} collective-permute-done((bf16[8,64,128]{2,1,0:T(8,128)(2,1)S(1)}, bf16[8,64,128]{2,1,0:T(8,128)(2,1)S(1)}, u32[]{:S(2)}, u32[]{:S(2)}) %collective-permute-start.3) | collective-permute-done | bytes 131104 | tf_op jit(solution)/shard_map/ppermute | solution.py:181
  34.6 2.3 %collective-permute-done.2 = bf16[8,64,128]{2,1,0:T(8,128)(2,1)S(1)} collective-permute-done((bf16[8,64,128]{2,1,0:T(8,128)(2,1)S(1)}, bf16[8,64,128]{2,1,0:T(8,128)(2,1)S(1)}, u32[]{:S(2)}, u32[]{:S(2)}) %collective-permute-start.2) | collective-permute-done | bytes 131104 | tf_op jit(solution)/shard_map/ppermute | solution.py:181
  36.9 1.3 %collective-permute-done.1 = bf16[8,64,128]{2,1,0:T(8,128)(2,1)S(1)} collective-permute-done((bf16[8,64,128]{2,1,0:T(8,128)(2,1)S(1)}, bf16[8,64,128]{2,1,0:T(8,128)(2,1)S(1)}, u32[]{:S(2)}, u32[]{:S(2)}) %collective-permute-start.1) | collective-permute-done | bytes 131104 | tf_op jit(solution)/shard_map/ppermute | solution.py:181
  38.2 0.1 pad_maximum_fusion.refs_0_
  38.3 3.1 %collective-permute-start.5 = (bf16[8,4,64,128]{3,2,1,0:T(8,128)(2,1)S(1)}, bf16[8,4,64,128]{3,2,1,0:T(8,128)(2,1)S(1)}, u32[]{:S(2)}, u32[]{:S(2)}) collective-permute-start(bf16[8,4,64,128]{3,2,1,0:T(8,128)(2,1)S(1)} %pad_maximum_fusion.refs_0_), channel_id=1, source_target_pairs={{0,192},{64,0},{128,64},{192,128},{1,193},{65,1},{129,65},{193,129... | collective-permute-start | bytes 1572872 | tf_op jit(solution)/shard_map/ppermute | solution.py:181
  41.4 0.0 collective-permute-start.4
  41.4 1.4 %all-to-all-done.1.refs_5_ = bf16[8,2,128,128]{3,2,1,0:T(8,128)(2,1)S(1)} async-done(((bf16[8,2,128,128]{3,2,1,0:T(8,128)(2,1)}), bf16[8,2,128,128]{3,2,1,0:T(8,128)(2,1)S(1)}, u32[]{:S(2)}, u32[]{:S(2)}) %all-to-all-start.1) | async-done | bytes 524320 | tf_op jit(solution)/shard_map/all_to_all | solution.py:203
  42.8 2.8 %collective-permute-start.9 = (bf16[8,2,128,128]{3,2,1,0:T(8,128)(2,1)S(1)}, bf16[8,2,128,128]{3,2,1,0:T(8,128)(2,1)S(1)}, u32[]{:S(2)}, u32[]{:S(2)}) collective-permute-start(bf16[8,2,128,128]{3,2,1,0:T(8,128)(2,1)S(1)} %all-to-all-done.1.refs_5_), channel_id=1, source_target_pairs={{0,3},{1,0},{2,1},{3,2},{4,7},{5,4},{6,5},{7,6},{8,11},{9,8},{10,9... | collective-permute-start | bytes 1572872 | tf_op jit(solution)/shard_map/ppermute | solution.py:181
  45.6 4.7 %collective-permute-done.5.refs_2_ = bf16[8,4,64,128]{3,2,1,0:T(8,128)(2,1)S(1)} collective-permute-done((bf16[8,4,64,128]{3,2,1,0:T(8,128)(2,1)S(1)}, bf16[8,4,64,128]{3,2,1,0:T(8,128)(2,1)S(1)}, u32[]{:S(2)}, u32[]{:S(2)}) %collective-permute-start.5) | collective-permute-done | bytes 524320 | tf_op jit(solution)/shard_map/ppermute | solution.py:181
  50.2 0.7 slice.17
  50.9 3.7 %collective-permute-start.7 = (bf16[4,4,64,128]{3,2,1,0:T(8,128)(2,1)}, bf16[4,4,64,128]{3,2,1,0:T(8,128)(2,1)S(1)}, u32[]{:S(2)}, u32[]{:S(2)}) collective-permute-start(bf16[4,4,64,128]{3,2,1,0:T(8,128)(2,1)} %slice.17), channel_id=1, source_target_pairs={{0,192},{64,0},{128,64},{192,128},{1,193},{65,1},{129,65},{193,129... | collective-permute-start | bytes 786440 | tf_op jit(solution)/shard_map/ppermute | solution.py:181
  54.6 0.7 slice.16
  55.4 0.7 slice.19
  56.1 0.9 collective-permute-start.11
  57.0 0.7 slice.18
  57.7 1.1 %collective-permute-start.10 = (bf16[4,2,128,128]{3,2,1,0:T(8,128)(2,1)}, bf16[4,2,128,128]{3,2,1,0:T(8,128)(2,1)}, u32[]{:S(2)}, u32[]{:S(2)}) collective-permute-start(bf16[4,2,128,128]{3,2,1,0:T(8,128)(2,1)} %slice.18), channel_id=1, source_target_pairs={{0,1},{1,2},{2,3},{3,0},{4,5},{5,6},{6,7},{7,4},{8,9},{9,10},{10,1... | collective-permute-start | bytes 786440 | tf_op jit(solution)/shard_map/ppermute | solution.py:181
  58.9 0.1 collective-permute-start.12
  59.0 0.5 collective-permute-start.14
  59.5 3.8 %collective-permute-done.6.refs_3_ = bf16[4,4,64,128]{3,2,1,0:T(8,128)(2,1)} collective-permute-done((bf16[4,4,64,128]{3,2,1,0:T(8,128)(2,1)}, bf16[4,4,64,128]{3,2,1,0:T(8,128)(2,1)}, u32[]{:S(2)}, u32[]{:S(2)}) %collective-permute-start.6) | collective-permute-done | bytes 262176 | tf_op jit(solution)/shard_map/ppermute | solution.py:181
  63.3 0.5 collective-permute-start.16
  63.8 1.8 %collective-permute-done.10.refs_8_ = bf16[4,2,128,128]{3,2,1,0:T(8,128)(2,1)} collective-permute-done((bf16[4,2,128,128]{3,2,1,0:T(8,128)(2,1)}, bf16[4,2,128,128]{3,2,1,0:T(8,128)(2,1)}, u32[]{:S(2)}, u32[]{:S(2)}) %collective-permute-start.10) | collective-permute-done | bytes 262176 | tf_op jit(solution)/shard_map/ppermute | solution.py:181
  65.6 0.0 copy-start.4
  65.7 0.0 copy-start.3
  65.7 0.1 collective-permute-done.16.refs_14_
  65.7 1.6 %collective-permute-done.15.refs_13_ = bf16[4,2,128,128]{3,2,1,0:T(8,128)(2,1)S(1)} collective-permute-done((bf16[4,2,128,128]{3,2,1,0:T(8,128)(2,1)}, bf16[4,2,128,128]{3,2,1,0:T(8,128)(2,1)S(1)}, u32[]{:S(2)}, u32[]{:S(2)}) %collective-permute-start.15) | collective-permute-done | bytes 262176 | tf_op jit(solution)/shard_map/ppermute | solution.py:185
  67.4 10.1 %exchange.1 = (f32[4,8,4,16,128]{4,3,2,1,0:T(8,128)S(1)}, f32[4,8,4,16,128]{4,3,2,1,0:T(8,128)S(1)}) custom-call(s32[4]{0:T(128)S(1)} %pad_add_fusion.pos, s32[4,32]{1,0:T(4,128)S(1)} %bitcast.24, s32[4,32]{1,0:T(4,128)S(1)} %bitcast.23, s32[4,32]{1,0:T(4,128)S(1)} %select_reduce_fusion.occ_index, bf16[8,4,64,128]{3,2,1,0:T(8,128)(2,1)S(1)} %pad_maximum_fusion.refs_0_, ...), custom_call_target="tpu_custom_call" | custom-call | tf_op jit(solution)/shard_map/exchange/pallas_call | solution.py:164
  77.5 0.2 collective-permute-start.17
  77.7 2.5 %collective-permute-done.17 = f32[4,8,4,16,128]{4,3,2,1,0:T(8,128)S(1)} collective-permute-done((f32[4,8,4,16,128]{4,3,2,1,0:T(8,128)S(1)}, f32[4,8,4,16,128]{4,3,2,1,0:T(8,128)S(1)}, u32[]{:S(2)}, u32[]{:S(2)}) %collective-permute-start.17) | collective-permute-done | bytes 1048608 | tf_op jit(solution)/shard_map/ppermute | solution.py:185
  80.3 1.0 add_convert_fusion
  81.2 9.7 %all-to-all-start.2 = ((bf16[32,4,16,128]{3,2,1,0:T(8,128)(2,1)}), bf16[32,4,16,128]{3,2,1,0:T(8,128)(2,1)S(1)}, u32[]{:S(2)}, u32[]{:S(2)}) async-start(bf16[32,4,16,128]{3,2,1,0:T(8,128)(2,1)} %bitcast.15), calls=%async_computation.2 | async-start | bytes 1048576 | tf_op jit(solution)/shard_map/all_to_all | solution.py:218
  91.0 0.2 multiply_reduce_fusion
  91.2 17.7 %all-to-all-done.2 = bf16[32,4,16,128]{3,2,1,0:T(8,128)(2,1)S(1)} async-done(((bf16[32,4,16,128]{3,2,1,0:T(8,128)(2,1)}), bf16[32,4,16,128]{3,2,1,0:T(8,128)(2,1)S(1)}, u32[]{:S(2)}, u32[]{:S(2)}) %all-to-all-start.2) | async-done | bytes 524320 | tf_op jit(solution)/shard_map/all_to_all | solution.py:218
  108.9 0.1 convert_reduce_fusion
  109.0 0.7 bitcast_multiply_fusion
  (21 shorter events, 0.1 us)
Async XLA Ops:
  0.0 0.7 copy-start.2
  0.7 1.0 copy-start
  1.7 0.9 copy-start.1
  4.5 16.9 %collective-permute-start = (bf16[4,2,128,128]{3,2,1,0:T(8,128)(2,1)S(1)}, bf16[4,2,128,128]{3,2,1,0:T(8,128)(2,1)S(1)}, u32[]{:S(2)}, u32[]{:S(2)}) collective-permute-start(bf16[4,2,128,128]{3,2,1,0:T(8,128)(2,1)S(1)} %get-tuple-element.12), channel_id=1, source_target_pairs={{0,32},{32,0},{1,33},{33,1},{2,34},{34,2},{3,35},{35,3},{4,36},{36... | collective-permute-start | bytes 786440 | tf_op jit(solution)/shard_map/ppermute | solution.py:185
  4.6 16.8 %all-to-all-start = ((bf16[8,64,128]{2,1,0:T(8,128)(2,1)}), bf16[8,64,128]{2,1,0:T(8,128)(2,1)S(1)}, u32[]{:S(2)}, u32[]{:S(2)}) async-start(bf16[8,64,128]{2,1,0:T(8,128)(2,1)} %get-tuple-element.13), calls=%async_computation | async-start | bytes 262144 | tf_op jit(solution)/shard_map/all_to_all | solution.py:198
  22.4 20.4 %all-to-all-start.1 = ((bf16[8,2,128,128]{3,2,1,0:T(8,128)(2,1)}), bf16[8,2,128,128]{3,2,1,0:T(8,128)(2,1)S(1)}, u32[]{:S(2)}, u32[]{:S(2)}) async-start(bf16[8,2,128,128]{3,2,1,0:T(8,128)(2,1)} %fusion.1), calls=%async_computation.1 | async-start | bytes 1048576 | tf_op jit(solution)/shard_map/all_to_all | solution.py:203
  27.3 7.3 %collective-permute-start.3 = (bf16[8,64,128]{2,1,0:T(8,128)(2,1)S(1)}, bf16[8,64,128]{2,1,0:T(8,128)(2,1)S(1)}, u32[]{:S(2)}, u32[]{:S(2)}) collective-permute-start(bf16[8,64,128]{2,1,0:T(8,128)(2,1)S(1)} %all-to-all-done), channel_id=1, source_target_pairs={{0,3},{1,0},{2,1},{3,2},{4,7},{5,4},{6,5},{7,6},{8,11},{9,8},{10,9... | collective-permute-start | bytes 393224 | tf_op jit(solution)/shard_map/ppermute | solution.py:181
  30.1 6.8 %collective-permute-start.2 = (bf16[8,64,128]{2,1,0:T(8,128)(2,1)S(1)}, bf16[8,64,128]{2,1,0:T(8,128)(2,1)S(1)}, u32[]{:S(2)}, u32[]{:S(2)}) collective-permute-start(bf16[8,64,128]{2,1,0:T(8,128)(2,1)S(1)} %all-to-all-done), channel_id=1, source_target_pairs={{0,2},{1,3},{2,0},{3,1},{4,6},{5,7},{6,4},{7,5},{8,10},{9,11},{10,... | collective-permute-start | bytes 393224 | tf_op jit(solution)/shard_map/ppermute | solution.py:181
  30.9 7.3 %collective-permute-start.1 = (bf16[8,64,128]{2,1,0:T(8,128)(2,1)S(1)}, bf16[8,64,128]{2,1,0:T(8,128)(2,1)S(1)}, u32[]{:S(2)}, u32[]{:S(2)}) collective-permute-start(bf16[8,64,128]{2,1,0:T(8,128)(2,1)S(1)} %all-to-all-done), channel_id=1, source_target_pairs={{0,1},{1,2},{2,3},{3,0},{4,5},{5,6},{6,7},{7,4},{8,9},{9,10},{10,1... | collective-permute-start | bytes 393224 | tf_op jit(solution)/shard_map/ppermute | solution.py:181
  38.3 11.9 %collective-permute-start.5 = (bf16[8,4,64,128]{3,2,1,0:T(8,128)(2,1)S(1)}, bf16[8,4,64,128]{3,2,1,0:T(8,128)(2,1)S(1)}, u32[]{:S(2)}, u32[]{:S(2)}) collective-permute-start(bf16[8,4,64,128]{3,2,1,0:T(8,128)(2,1)S(1)} %pad_maximum_fusion.refs_0_), channel_id=1, source_target_pairs={{0,192},{64,0},{128,64},{192,128},{1,193},{65,1},{129,65},{193,129... | collective-permute-start | bytes 1572872 | tf_op jit(solution)/shard_map/ppermute | solution.py:181
  41.4 13.3 %collective-permute-start.4 = (bf16[8,4,64,128]{3,2,1,0:T(8,128)(2,1)S(1)}, bf16[8,4,64,128]{3,2,1,0:T(8,128)(2,1)S(1)}, u32[]{:S(2)}, u32[]{:S(2)}) collective-permute-start(bf16[8,4,64,128]{3,2,1,0:T(8,128)(2,1)S(1)} %pad_maximum_fusion.refs_0_), channel_id=1, source_target_pairs={{0,64},{64,128},{128,192},{192,0},{1,65},{65,129},{129,193},{193,1... | collective-permute-start | bytes 1572872 | tf_op jit(solution)/shard_map/ppermute | solution.py:181
  42.8 12.5 %collective-permute-start.9 = (bf16[8,2,128,128]{3,2,1,0:T(8,128)(2,1)S(1)}, bf16[8,2,128,128]{3,2,1,0:T(8,128)(2,1)S(1)}, u32[]{:S(2)}, u32[]{:S(2)}) collective-permute-start(bf16[8,2,128,128]{3,2,1,0:T(8,128)(2,1)S(1)} %all-to-all-done.1.refs_5_), channel_id=1, source_target_pairs={{0,3},{1,0},{2,1},{3,2},{4,7},{5,4},{6,5},{7,6},{8,11},{9,8},{10,9... | collective-permute-start | bytes 1572872 | tf_op jit(solution)/shard_map/ppermute | solution.py:181
  45.6 11.4 %collective-permute-start.8 = (bf16[8,2,128,128]{3,2,1,0:T(8,128)(2,1)S(1)}, bf16[8,2,128,128]{3,2,1,0:T(8,128)(2,1)S(1)}, u32[]{:S(2)}, u32[]{:S(2)}) collective-permute-start(bf16[8,2,128,128]{3,2,1,0:T(8,128)(2,1)S(1)} %all-to-all-done.1.refs_5_), channel_id=1, source_target_pairs={{0,1},{1,2},{2,3},{3,0},{4,5},{5,6},{6,7},{7,4},{8,9},{9,10},{10,1... | collective-permute-start | bytes 1572872 | tf_op jit(solution)/shard_map/ppermute | solution.py:181
  50.9 8.0 %collective-permute-start.7 = (bf16[4,4,64,128]{3,2,1,0:T(8,128)(2,1)}, bf16[4,4,64,128]{3,2,1,0:T(8,128)(2,1)S(1)}, u32[]{:S(2)}, u32[]{:S(2)}) collective-permute-start(bf16[4,4,64,128]{3,2,1,0:T(8,128)(2,1)} %slice.17), channel_id=1, source_target_pairs={{0,192},{64,0},{128,64},{192,128},{1,193},{65,1},{129,65},{193,129... | collective-permute-start | bytes 786440 | tf_op jit(solution)/shard_map/ppermute | solution.py:181
  55.4 7.9 %collective-permute-start.6 = (bf16[4,4,64,128]{3,2,1,0:T(8,128)(2,1)}, bf16[4,4,64,128]{3,2,1,0:T(8,128)(2,1)}, u32[]{:S(2)}, u32[]{:S(2)}) collective-permute-start(bf16[4,4,64,128]{3,2,1,0:T(8,128)(2,1)} %slice.16), channel_id=1, source_target_pairs={{0,64},{64,128},{128,192},{192,0},{1,65},{65,129},{129,193},{193,1... | collective-permute-start | bytes 786440 | tf_op jit(solution)/shard_map/ppermute | solution.py:181
  56.1 7.2 %collective-permute-start.11 = (bf16[4,2,128,128]{3,2,1,0:T(8,128)(2,1)}, bf16[4,2,128,128]{3,2,1,0:T(8,128)(2,1)}, u32[]{:S(2)}, u32[]{:S(2)}) collective-permute-start(bf16[4,2,128,128]{3,2,1,0:T(8,128)(2,1)} %slice.19), channel_id=1, source_target_pairs={{0,3},{1,0},{2,1},{3,2},{4,7},{5,4},{6,5},{7,6},{8,11},{9,8},{10,9... | collective-permute-start | bytes 786440 | tf_op jit(solution)/shard_map/ppermute | solution.py:181
  57.7 7.9 %collective-permute-start.10 = (bf16[4,2,128,128]{3,2,1,0:T(8,128)(2,1)}, bf16[4,2,128,128]{3,2,1,0:T(8,128)(2,1)}, u32[]{:S(2)}, u32[]{:S(2)}) collective-permute-start(bf16[4,2,128,128]{3,2,1,0:T(8,128)(2,1)} %slice.18), channel_id=1, source_target_pairs={{0,1},{1,2},{2,3},{3,0},{4,5},{5,6},{6,7},{7,4},{8,9},{9,10},{10,1... | collective-permute-start | bytes 786440 | tf_op jit(solution)/shard_map/ppermute | solution.py:181
  58.9 6.8 %collective-permute-start.12 = (bf16[8,2,128,128]{3,2,1,0:T(8,128)(2,1)S(1)}, bf16[8,2,128,128]{3,2,1,0:T(8,128)(2,1)S(1)}, u32[]{:S(2)}, u32[]{:S(2)}) collective-permute-start(bf16[8,2,128,128]{3,2,1,0:T(8,128)(2,1)S(1)} %all-to-all-done.1.refs_5_), channel_id=1, source_target_pairs={{0,32},{32,0},{1,33},{33,1},{2,34},{34,2},{3,35},{35,3},{4,36},{36... | collective-permute-start | bytes 1572872 | tf_op jit(solution)/shard_map/ppermute | solution.py:185
  59.0 8.4 %collective-permute-start.14 = (bf16[8,2,128,128]{3,2,1,0:T(8,128)(2,1)S(1)}, bf16[8,2,128,128]{3,2,1,0:T(8,128)(2,1)S(1)}, u32[]{:S(2)}, u32[]{:S(2)}) collective-permute-start(bf16[8,2,128,128]{3,2,1,0:T(8,128)(2,1)S(1)} %collective-permute-done.9.refs_7_), channel_id=1, source_target_pairs={{0,32},{32,0},{1,33},{33,1},{2,34},{34,2},{3,35},{35,3},{4,36},{36... | collective-permute-start | bytes 1572872 | tf_op jit(solution)/shard_map/ppermute | solution.py:185
  63.3 4.1 %collective-permute-start.13 = (bf16[8,2,128,128]{3,2,1,0:T(8,128)(2,1)S(1)}, bf16[8,2,128,128]{3,2,1,0:T(8,128)(2,1)S(1)}, u32[]{:S(2)}, u32[]{:S(2)}) collective-permute-start(bf16[8,2,128,128]{3,2,1,0:T(8,128)(2,1)S(1)} %collective-permute-done.8.refs_6_), channel_id=1, source_target_pairs={{0,32},{32,0},{1,33},{33,1},{2,34},{34,2},{3,35},{35,3},{4,36},{36... | collective-permute-start | bytes 1572872 | tf_op jit(solution)/shard_map/ppermute | solution.py:185
  63.3 2.5 %collective-permute-start.16 = (bf16[4,2,128,128]{3,2,1,0:T(8,128)(2,1)}, bf16[4,2,128,128]{3,2,1,0:T(8,128)(2,1)S(1)}, u32[]{:S(2)}, u32[]{:S(2)}) collective-permute-start(bf16[4,2,128,128]{3,2,1,0:T(8,128)(2,1)} %collective-permute-done.11.refs_9_), channel_id=1, source_target_pairs={{0,32},{32,0},{1,33},{33,1},{2,34},{34,2},{3,35},{35,3},{4,36},{36... | collective-permute-start | bytes 786440 | tf_op jit(solution)/shard_map/ppermute | solution.py:185
  65.6 1.7 %collective-permute-start.15 = (bf16[4,2,128,128]{3,2,1,0:T(8,128)(2,1)}, bf16[4,2,128,128]{3,2,1,0:T(8,128)(2,1)S(1)}, u32[]{:S(2)}, u32[]{:S(2)}) collective-permute-start(bf16[4,2,128,128]{3,2,1,0:T(8,128)(2,1)} %collective-permute-done.10.refs_8_), channel_id=1, source_target_pairs={{0,32},{32,0},{1,33},{33,1},{2,34},{34,2},{3,35},{35,3},{4,36},{36... | collective-permute-start | bytes 786440 | tf_op jit(solution)/shard_map/ppermute | solution.py:185
  65.6 1.7 %copy-start.4 = (s32[32,4]{0,1:T(4,128)S(1)}, s32[32,4]{0,1:T(4,128)}, u32[]{:S(2)}) copy-start(s32[32,4]{0,1:T(4,128)} %param.7) | copy-start | bytes 1540
  65.7 1.7 %copy-start.3 = (s32[32,4]{0,1:T(4,128)S(1)}, s32[32,4]{0,1:T(4,128)}, u32[]{:S(2)}) copy-start(s32[32,4]{0,1:T(4,128)} %param.8) | copy-start | bytes 1540
  77.5 2.7 %collective-permute-start.17 = (f32[4,8,4,16,128]{4,3,2,1,0:T(8,128)S(1)}, f32[4,8,4,16,128]{4,3,2,1,0:T(8,128)S(1)}, u32[]{:S(2)}, u32[]{:S(2)}) collective-permute-start(f32[4,8,4,16,128]{4,3,2,1,0:T(8,128)S(1)} %get-tuple-element.18), channel_id=1, source_target_pairs={{0,32},{32,0},{1,33},{33,1},{2,34},{34,2},{3,35},{35,3},{4,36},{36... | collective-permute-start | bytes 3145736 | tf_op jit(solution)/shard_map/ppermute | solution.py:185
  81.2 27.7 %all-to-all-start.2 = ((bf16[32,4,16,128]{3,2,1,0:T(8,128)(2,1)}), bf16[32,4,16,128]{3,2,1,0:T(8,128)(2,1)S(1)}, u32[]{:S(2)}, u32[]{:S(2)}) async-start(bf16[32,4,16,128]{3,2,1,0:T(8,128)(2,1)} %bitcast.15), calls=%async_computation.2 | async-start | bytes 1048576 | tf_op jit(solution)/shard_map/all_to_all | solution.py:218

commit v6 on v5

v6 whole, which is shorter than its diff:
```python
import functools
import math

import jax
import jax.numpy as jnp
from jax import lax
from jax.experimental import pallas as pl
from jax.experimental.pallas import tpu as pltpu
from jax.sharding import Mesh, PartitionSpec as P

NY, NC, NZ, NX = 4, 2, 8, 4
TILES, SLOTS, TS = 32, 4, 128
OCC, LIVE = 8, 4
AUXROWS = 4
HALF = TS // 2
ROWS = TS // (NY * NC)
SCALE = 1.0 / math.sqrt(32768.0)
BF = jnp.bfloat16
F32 = jnp.float32
VMEM = pl.BlockSpec(memory_space=pltpu.VMEM)
SMEM = pl.BlockSpec(memory_space=pltpu.SMEM)
ANY = pl.BlockSpec(memory_space=pl.ANY)


def slice_kernel(pos, occ_live, orb, coeffs, cols, sem):
    slab, core, tile = pos[0], pos[1], pos[2] * NX + pos[3]
    load = pltpu.make_async_copy(orb, cols, sem)
    load.start()
    load.wait()
    count = jnp.int32(0)
    for occ in range(OCC):
        live = occ_live[occ, tile] != 0

        @pl.when(live & (count == slab))
        def _():
            flipped = cols[:, occ * TS:(occ + 1) * TS].astype(F32).T.astype(BF)
            mine = jnp.where(core == 0, flipped[:HALF], flipped[HALF:])
            for target in range(NZ):
                coeffs[target] = mine

        count = count + jnp.where(live, 1, 0)


def slice_coeffs(pos, occ_live, orb):
    return pl.pallas_call(
        slice_kernel,
        out_shape=jax.ShapeDtypeStruct((NZ, HALF, TS), BF),
        in_specs=[SMEM, SMEM, ANY],
        out_specs=VMEM,
        scratch_shapes=[pltpu.VMEM(orb.shape, BF), pltpu.SemaphoreType.DMA],
        compiler_params=pltpu.CompilerParams(vmem_limit_bytes=60 * 2**20),
        cost_estimate=pl.CostEstimate(flops=0, bytes_accessed=2 * orb.size, transcendentals=0),
        name="slice_coeffs",
    )(pos, occ_live, orb)


def split_kernel(pos, eri, keep, give):
    core = pos[1]
    row = lax.broadcasted_iota(jnp.int32, (TS, TS), 0)
    col = lax.broadcasted_iota(jnp.int32, (TS, TS), 1)
    block_nu = TS // AUXROWS
    perm = (col == (row % block_nu) * AUXROWS + row // block_nu).astype(BF)
    for out, part in ((give, 1 - core), (keep, core)):
        for j in range(2):
            for quarter in range(AUXROWS):
                start = pl.multiple_of(((part * 2 + j) * AUXROWS + quarter) * TS, TS)
                mixed = jnp.dot(perm, eri[pl.ds(start, TS), :], preferred_element_type=F32).astype(BF)
                for aux in range(AUXROWS):
                    out[aux, j, pl.ds(quarter * block_nu, block_nu), :] = mixed[aux * block_nu:(aux + 1) * block_nu]


def split_aux(pos, eri):
    piece = jax.ShapeDtypeStruct((AUXROWS, 2, TS, TS), BF)
    return pl.pallas_call(
        split_kernel,
        out_shape=(piece, piece),
        in_specs=[SMEM, VMEM],
        out_specs=(VMEM, VMEM),
        compiler_params=pltpu.CompilerParams(vmem_limit_bytes=8 * 2**20),
        cost_estimate=pl.CostEstimate(flops=2 * TS * eri.size, bytes_accessed=4 * eri.size, transcendentals=0),
        name="split_aux",
    )(pos, eri)


def rebuild_kernel(pos, occ_index, c0, c_u, c_d, c_u2, c_d2, dense):
    slab, x = pos[0], pos[3]

    def clear(tile, carry):
        dense[tile] = jnp.zeros(dense.shape[1:], BF)
        return carry

    lax.fori_loop(0, TILES, clear, 0, unroll=4)

    def place(piece, k, lo, count):
        def body(step, carry):
            for entry in range(NX):
                tile = (lo + step) * NX + (x - entry + NX) % NX
                start = pl.multiple_of(occ_index[k, tile] * HALF, HALF)
                dense[tile, pl.ds(start, HALF), :] = piece[step, entry]
            return carry

        lax.fori_loop(0, count, body, 0, unroll=True)

    place(c0, slab, 0, 8)
    place(c_u, (slab + 3) % NY, 0, 8)
    place(c_d, (slab + 1) % NY, 0, 8)
    place(c_u2, (slab + 2) % NY, 0, 4)
    place(c_d2, (slab + 2) % NY, 4, 4)


def rebuild(pos, occ_index, *pieces):
    return pl.pallas_call(
        rebuild_kernel,
        out_shape=jax.ShapeDtypeStruct((TILES, OCC * HALF, TS), BF),
        in_specs=[SMEM] * 2 + [VMEM] * len(pieces),
        out_specs=VMEM,
        compiler_params=pltpu.CompilerParams(vmem_limit_bytes=16 * 2**20),
        cost_estimate=pl.CostEstimate(flops=0, bytes_accessed=6 * 2**20, transcendentals=0),
        name="rebuild",
    )(pos, occ_index, *pieces)


def main_kernel(pos, pair_tiles, pair_live, dense,
                own0, own_r, own_l, own_r2, own_l2, oth0, oth_r, oth_l, oth_r2, oth_l2,
                keep, send, field, block):
    core, x = pos[1], pos[3]

    def transform(xp, own, oth, lo, count):
        def body(step, carry):
            tile = (lo + step) * NX + xp
            lhs, rhs = [], []
            for part, ref in ((core, own), (1 - core, oth)):
                for j in range(2):
                    slot = part * 2 + j
                    eri = ref[step, j]
                    rhs.append(jnp.where(pair_live[slot, tile] != 0, eri, jnp.zeros_like(eri)))
                    lhs.append(dense[pair_tiles[slot, tile]])
            half = jnp.dot(
                jnp.concatenate(lhs, axis=1), jnp.concatenate(rhs, axis=0), preferred_element_type=F32
            )
            field[tile] = half.astype(BF)
            return carry

        lax.fori_loop(0, count, body, 0, unroll=4)

    transform(x, own0, oth0, 0, 8)
    transform((x + 3) % NX, own_r, oth_r, 0, 8)
    transform((x + 1) % NX, own_l, oth_l, 0, 8)
    transform((x + 2) % NX, own_r2, oth_r2, 0, 4)
    transform((x + 2) % NX, own_l2, oth_l2, 4, 4)

    def gram(zp, carry):
        tile = zp * NX + x
        partners = jnp.concatenate([field[pair_tiles[slot, tile]] for slot in range(SLOTS)], axis=1)
        block[...] = lax.dot_general(
            field[tile], partners, (((0,), (0,)), ((), ())), preferred_element_type=F32
        )
        for y in range(NY):
            near = pl.multiple_of(y * 2 * ROWS + core * ROWS, ROWS)
            far = pl.multiple_of(y * 2 * ROWS + (1 - core) * ROWS, ROWS)
            for slot in range(SLOTS):
                keep[y, zp, slot] = block[pl.ds(near, ROWS), slot * TS:(slot + 1) * TS]
                send[y, zp, slot] = block[pl.ds(far, ROWS), slot * TS:(slot + 1) * TS]
        return carry

    lax.fori_loop(0, NZ, gram, 0)


def exchange(pos, pair_tiles, pair_live, *pieces):
    shape = jax.ShapeDtypeStruct((NY, NZ, SLOTS, ROWS, TS), F32)
    return pl.pallas_call(
        main_kernel,
        out_shape=(shape, shape),
        in_specs=[SMEM] * 3 + [VMEM] * len(pieces),
        out_specs=(VMEM, VMEM),
        scratch_shapes=[
            pltpu.VMEM((TILES, OCC * HALF, TS), BF),
            pltpu.VMEM((TS, SLOTS * TS), F32),
        ],
        compiler_params=pltpu.CompilerParams(vmem_limit_bytes=24 * 2**20),
        cost_estimate=pl.CostEstimate(flops=2700000000, bytes_accessed=10 * 2**20, transcendentals=0),
        name="exchange",
    )(pos, pair_tiles, pair_live, *pieces)


def shift(value, axis, size, by):
    return lax.ppermute(value, axis, [(i, (i + by) % size) for i in range(size)])


def swap(value):
    return lax.ppermute(value, "c", [(0, 1), (1, 0)])


def shards(integrals, orbitals, pair_tiles, pair_live, occ_live):
    pos = jnp.stack([lax.axis_index(name).astype(jnp.int32) for name in ("y", "c", "z", "x")])
    tile = pos[2] * NX + pos[3]
    coeffs = slice_coeffs(pos, occ_live.T, orbitals)
    coeffs, eri = lax.optimization_barrier((coeffs, integrals.reshape(SLOTS * TS * AUXROWS, TS)))
    column = lax.all_to_all(coeffs, "z", split_axis=0, concat_axis=0, tiled=True)
    keep_eri, give_eri = split_aux(pos, eri)
    rank = jnp.cumsum(occ_live, axis=1) - 1
    hits = (occ_live[None] != 0) & (rank[None] == jnp.arange(LIVE)[:, None, None])
    occ_index = jnp.sum(jnp.where(hits, jnp.arange(OCC)[None, None, :], 0), axis=2).astype(jnp.int32)

    got_eri = swap(give_eri)
    c0 = jnp.stack([column] + [shift(column, "x", NX, by) for by in (1, 2, 3)], axis=1)
    got_eri, c0 = lax.optimization_barrier((got_eri, c0))
    by_aux = lax.dynamic_slice_in_dim(
        jnp.concatenate([keep_eri, got_eri, keep_eri]), pos[1] * AUXROWS, NZ, 0
    )
    own0 = lax.all_to_all(by_aux, "z", split_axis=0, concat_axis=0, tiled=True)
    own_r, own_l = shift(own0, "x", NX, 1), shift(own0, "x", NX, -1)
    c_u, c_d = shift(c0, "y", NY, 1), shift(c0, "y", NY, -1)
    oth0 = swap(own0)
    own_r2, own_l2 = shift(own_r[:4], "x", NX, 1), shift(own_l[4:], "x", NX, -1)
    c_u2, c_d2 = shift(c_u[:4], "y", NY, 1), shift(c_d[4:], "y", NY, -1)
    oth_r, oth_l = swap(own_r), swap(own_l)
    oth_r2, oth_l2 = swap(own_r2), swap(own_l2)

    dense = rebuild(pos, occ_index, c0, c_u, c_d, c_u2, c_d2)
    keep, send = exchange(
        pos, pair_tiles.T, pair_live.T, dense,
        own0, own_r, own_l, own_r2, own_l2, oth0, oth_r, oth_l, oth_r2, oth_l2,
    )
    partial = (keep + swap(send)).astype(BF).reshape(NY * NZ, SLOTS, ROWS, TS)
    parts = lax.all_to_all(partial, ("y", "z"), split_axis=0, concat_axis=0, tiled=True).astype(F32)
    flags = lax.dynamic_index_in_dim(pair_live, tile, 0, keepdims=False).astype(F32) * SCALE
    return (jnp.sum(parts, axis=0) * flags[:, None, None])[None]


def solution(mesh):
    grid = Mesh(mesh.devices.reshape(NY, NC, NZ, NX), ("y", "c", "z", "x"))
    return jax.shard_map(
        shards,
        mesh=grid,
        in_specs=(
            P(("z", "x"), None, None, ("y", "c"), None),
            P(("z", "x"), None),
            P(),
            P(),
            P(),
        ),
        out_specs=P(("z", "x"), None, ("y", "c"), None),
        check_vma=False,
    )
```

time: 110 us -> 113 us (1.027); the launches traced: 110 us -> 111 us
  Pallas kernels: 11.9 us -> 13.8 us
  waiting for transfers between devices: 48.3 us -> 47.1 us
    all_to_all x1, waiting for transfers between devices: 1.43 us -> 10.8 us  [shards(): own0 = lax.all_to_all(by_aux, 'z', split_axis=0, concat_axis=0, tiled=True)]
    ppermute x11, waiting for transfers between devices: 16.7 us -> 11.1 us  [shift(): lax.ppermute(value, axis, [(i, (i + by) % size) for i in range(size)])]
    all_to_all x1, waiting for transfers between devices: 8.17 us -> 4.8 us  [shards(): lax.all_to_all(coeffs, 'z', split_axis=0, concat_axis=0, tiled=True)]
    ppermute x11, starting transfers between devices: 16 us -> 18.6 us  [shift(): lax.ppermute(value, axis, [(i, (i + by) % size) for i in range(size)])]
    all_to_all x1, starting transfers between devices: 9.72 us -> 7.5 us  [shards(): lax.all_to_all(partial, ('y', 'z'), split_axis=0, concat_axis=0, tiled=True)]
    pallas_call x2 -> x4, Pallas kernels: 11.9 us -> 13.8 us  [the longest x1 8.77 us: exchange(): pl.pallas_call(main_kernel, out_shape=(shape, shape), in_specs=[SMEM] * 3...]
    ppermute x7, waiting for transfers between devices: 4.2 us -> 2.35 us  [swap(): return lax.ppermute(value, 'c', [(0, 1), (1, 0)])]
    unnamed x10 -> x16, local copies, waits for them, and re-layouts: 2.61 us -> 2.53 us
  transfers between devices with their start and end apart: 21 -> 21, of which waited for: 12 -> 10; matrix products, arithmetic and copies ran while one was open for 3% -> 3% of each run, Pallas kernels for 0% -> 2%
where the time goes in v6:
time: 113 us; the launch traced here: 111 us
  waiting for transfers between devices  47.1 us (42%)
  starting transfers between devices  41 us (36%)
  Pallas kernels  13.8 us (12%)
  local copies, waits for them, and re-layouts  5.4 us (5%)
  other arithmetic  3.78 us (3%)
    ppermute x11, starting transfers between devices, shift(): lax.ppermute(value, axis, [(i, (i + by) % size) for i in range(size)])  18.6 us
    all_to_all x1, waiting for transfers between devices, shards(): lax.all_to_all(partial, ('y', 'z'), split_axis=0, concat_axis=0, tiled=True)  18 us
    ppermute x11, waiting for transfers between devices, shift(): lax.ppermute(value, axis, [(i, (i + by) % size) for i in range(size)])  11.1 us
    all_to_all x1, waiting for transfers between devices, shards(): own0 = lax.all_to_all(by_aux, 'z', split_axis=0, concat_axis=0, tiled=True)  10.8 us
    pallas_call x1, Pallas kernels, exchange(): pl.pallas_call(main_kernel, out_shape=(shape, shape), in_specs=[SMEM] * 3...  8.77 us
    all_to_all x1, starting transfers between devices, shards(): lax.all_to_all(coeffs, 'z', split_axis=0, concat_axis=0, tiled=True)  8.58 us
    all_to_all x1, starting transfers between devices, shards(): lax.all_to_all(partial, ('y', 'z'), split_axis=0, concat_axis=0, tiled=True)  7.5 us
    all_to_all x1, starting transfers between devices, shards(): own0 = lax.all_to_all(by_aux, 'z', split_axis=0, concat_axis=0, tiled=True)  5.05 us
  transfers between devices with their start and end apart: 21, of which 10 were waited for; matrix products, arithmetic and copies ran while one was open for 3% of the time, Pallas kernels for 2%

profile of v6, /device:TPU:32, one launch (start us, length us, event | category | flops | bytes accessed | tf_op | source)
XLA Modules:
  0.0 111.3 jit_solution(11565278334098045388)
XLA Ops:
  0.0 0.7 pad_add_fusion.pos
  0.7 2.6 %slice_coeffs.1 = bf16[8,64,128]{2,1,0:T(8,128)(2,1)} custom-call(s32[4]{0:T(128)} %pad_add_fusion.pos, s32[8,32]{1,0:T(8,128)} %bitcast.28, bf16[128,1024]{1,0:T(8,128)(2,1)} %orb.1), custom_call_target="tpu_custom_call" | custom-call | bytes 262144 | tf_op jit(solution)/shard_map/slice_coeffs/pallas_call | solution.py:45
  3.2 8.6 %all-to-all-start = ((bf16[8,64,128]{2,1,0:T(8,128)(2,1)}), bf16[8,64,128]{2,1,0:T(8,128)(2,1)S(1)}, u32[]{:S(2)}, u32[]{:S(2)}) async-start(bf16[8,64,128]{2,1,0:T(8,128)(2,1)} %slice_coeffs.1), calls=%async_computation | async-start | bytes 262144 | tf_op jit(solution)/shard_map/all_to_all | solution.py:199
  11.8 1.0 copy-done
  12.9 0.7 copy-done.3
  13.5 0.8 split_aux.1
  14.4 0.1 collective-permute-start
  14.5 4.8 %all-to-all-done = bf16[8,64,128]{2,1,0:T(8,128)(2,1)S(1)} async-done(((bf16[8,64,128]{2,1,0:T(8,128)(2,1)}), bf16[8,64,128]{2,1,0:T(8,128)(2,1)S(1)}, u32[]{:S(2)}, u32[]{:S(2)}) %all-to-all-start) | async-done | bytes 131104 | tf_op jit(solution)/shard_map/all_to_all | solution.py:199
  19.3 1.5 %collective-permute-start.1 = (bf16[8,64,128]{2,1,0:T(8,128)(2,1)S(1)}, bf16[8,64,128]{2,1,0:T(8,128)(2,1)S(1)}, u32[]{:S(2)}, u32[]{:S(2)}) collective-permute-start(bf16[8,64,128]{2,1,0:T(8,128)(2,1)S(1)} %all-to-all-done), channel_id=1, source_target_pairs={{0,1},{1,2},{2,3},{3,0},{4,5},{5,6},{6,7},{7,4},{8,9},{9,10},{10,1... | collective-permute-start | bytes 393224 | tf_op jit(solution)/shard_map/ppermute | solution.py:187
  20.8 2.7 %collective-permute-start.2 = (bf16[8,64,128]{2,1,0:T(8,128)(2,1)S(1)}, bf16[8,64,128]{2,1,0:T(8,128)(2,1)S(1)}, u32[]{:S(2)}, u32[]{:S(2)}) collective-permute-start(bf16[8,64,128]{2,1,0:T(8,128)(2,1)S(1)} %all-to-all-done), channel_id=1, source_target_pairs={{0,2},{1,3},{2,0},{3,1},{4,6},{5,7},{6,4},{7,5},{8,10},{9,11},{10,... | collective-permute-start | bytes 393224 | tf_op jit(solution)/shard_map/ppermute | solution.py:187
  23.5 1.4 %collective-permute-start.3 = (bf16[8,64,128]{2,1,0:T(8,128)(2,1)S(1)}, bf16[8,64,128]{2,1,0:T(8,128)(2,1)S(1)}, u32[]{:S(2)}, u32[]{:S(2)}) collective-permute-start(bf16[8,64,128]{2,1,0:T(8,128)(2,1)S(1)} %all-to-all-done), channel_id=1, source_target_pairs={{0,3},{1,0},{2,1},{3,2},{4,7},{5,4},{6,5},{7,6},{8,11},{9,8},{10,9... | collective-permute-start | bytes 393224 | tf_op jit(solution)/shard_map/ppermute | solution.py:187
  24.9 1.9 %collective-permute-done.1 = bf16[8,64,128]{2,1,0:T(8,128)(2,1)S(1)} collective-permute-done((bf16[8,64,128]{2,1,0:T(8,128)(2,1)S(1)}, bf16[8,64,128]{2,1,0:T(8,128)(2,1)S(1)}, u32[]{:S(2)}, u32[]{:S(2)}) %collective-permute-start.1) | collective-permute-done | bytes 131104 | tf_op jit(solution)/shard_map/ppermute | solution.py:187
  26.8 1.4 %collective-permute-done.2 = bf16[8,64,128]{2,1,0:T(8,128)(2,1)S(1)} collective-permute-done((bf16[8,64,128]{2,1,0:T(8,128)(2,1)S(1)}, bf16[8,64,128]{2,1,0:T(8,128)(2,1)S(1)}, u32[]{:S(2)}, u32[]{:S(2)}) %collective-permute-start.2) | collective-permute-done | bytes 131104 | tf_op jit(solution)/shard_map/ppermute | solution.py:187
  28.3 0.2 collective-permute-done.3
  28.5 0.1 pad_maximum_fusion.c0
  28.5 1.1 fusion.1
  29.6 5.0 %all-to-all-start.1 = ((bf16[8,2,128,128]{3,2,1,0:T(8,128)(2,1)}), bf16[8,2,128,128]{3,2,1,0:T(8,128)(2,1)S(1)}, u32[]{:S(2)}, u32[]{:S(2)}) async-start(bf16[8,2,128,128]{3,2,1,0:T(8,128)(2,1)} %fusion.1), calls=%async_computation.1 | async-start | bytes 1048576 | tf_op jit(solution)/shard_map/all_to_all | solution.py:211
  34.7 1.5 %collective-permute-start.4 = (bf16[8,4,64,128]{3,2,1,0:T(8,128)(2,1)S(1)}, bf16[8,4,64,128]{3,2,1,0:T(8,128)(2,1)S(1)}, u32[]{:S(2)}, u32[]{:S(2)}) collective-permute-start(bf16[8,4,64,128]{3,2,1,0:T(8,128)(2,1)S(1)} %pad_maximum_fusion.c0), channel_id=1, source_target_pairs={{0,64},{64,128},{128,192},{192,0},{1,65},{65,129},{129,193},{193,1... | collective-permute-start | bytes 1572872 | tf_op jit(solution)/shard_map/ppermute | solution.py:187
  36.2 1.7 %collective-permute-start.5 = (bf16[8,4,64,128]{3,2,1,0:T(8,128)(2,1)S(1)}, bf16[8,4,64,128]{3,2,1,0:T(8,128)(2,1)S(1)}, u32[]{:S(2)}, u32[]{:S(2)}) collective-permute-start(bf16[8,4,64,128]{3,2,1,0:T(8,128)(2,1)S(1)} %pad_maximum_fusion.c0), channel_id=1, source_target_pairs={{0,192},{64,0},{128,64},{192,128},{1,193},{65,1},{129,65},{193,129... | collective-permute-start | bytes 1572872 | tf_op jit(solution)/shard_map/ppermute | solution.py:187
  37.9 10.8 %all-to-all-done.1.own0 = bf16[8,2,128,128]{3,2,1,0:T(8,128)(2,1)S(1)} async-done(((bf16[8,2,128,128]{3,2,1,0:T(8,128)(2,1)}), bf16[8,2,128,128]{3,2,1,0:T(8,128)(2,1)S(1)}, u32[]{:S(2)}, u32[]{:S(2)}) %all-to-all-start.1) | async-done | bytes 524320 | tf_op jit(solution)/shard_map/all_to_all | solution.py:211
  48.7 1.4 %collective-permute-start.8 = (bf16[8,2,128,128]{3,2,1,0:T(8,128)(2,1)S(1)}, bf16[8,2,128,128]{3,2,1,0:T(8,128)(2,1)S(1)}, u32[]{:S(2)}, u32[]{:S(2)}) collective-permute-start(bf16[8,2,128,128]{3,2,1,0:T(8,128)(2,1)S(1)} %all-to-all-done.1.own0), channel_id=1, source_target_pairs={{0,1},{1,2},{2,3},{3,0},{4,5},{5,6},{6,7},{7,4},{8,9},{9,10},{10,1... | collective-permute-start | bytes 1572872 | tf_op jit(solution)/shard_map/ppermute | solution.py:187
  50.1 1.9 %collective-permute-start.9 = (bf16[8,2,128,128]{3,2,1,0:T(8,128)(2,1)S(1)}, bf16[8,2,128,128]{3,2,1,0:T(8,128)(2,1)S(1)}, u32[]{:S(2)}, u32[]{:S(2)}) collective-permute-start(bf16[8,2,128,128]{3,2,1,0:T(8,128)(2,1)S(1)} %all-to-all-done.1.own0), channel_id=1, source_target_pairs={{0,3},{1,0},{2,1},{3,2},{4,7},{5,4},{6,5},{7,6},{8,11},{9,8},{10,9... | collective-permute-start | bytes 1572872 | tf_op jit(solution)/shard_map/ppermute | solution.py:187
  52.0 0.7 slice.16
  52.7 1.5 %collective-permute-start.6 = (bf16[4,4,64,128]{3,2,1,0:T(8,128)(2,1)}, bf16[4,4,64,128]{3,2,1,0:T(8,128)(2,1)S(1)}, u32[]{:S(2)}, u32[]{:S(2)}) collective-permute-start(bf16[4,4,64,128]{3,2,1,0:T(8,128)(2,1)} %slice.16), channel_id=1, source_target_pairs={{0,64},{64,128},{128,192},{192,0},{1,65},{65,129},{129,193},{193,1... | collective-permute-start | bytes 786440 | tf_op jit(solution)/shard_map/ppermute | solution.py:187
  54.2 0.7 slice.17
  54.9 1.7 %collective-permute-start.7 = (bf16[4,4,64,128]{3,2,1,0:T(8,128)(2,1)}, bf16[4,4,64,128]{3,2,1,0:T(8,128)(2,1)S(1)}, u32[]{:S(2)}, u32[]{:S(2)}) collective-permute-start(bf16[4,4,64,128]{3,2,1,0:T(8,128)(2,1)} %slice.17), channel_id=1, source_target_pairs={{0,192},{64,0},{128,64},{192,128},{1,193},{65,1},{129,65},{193,129... | collective-permute-start | bytes 786440 | tf_op jit(solution)/shard_map/ppermute | solution.py:187
  56.6 3.6 %collective-permute-done.8.own_r = bf16[8,2,128,128]{3,2,1,0:T(8,128)(2,1)S(1)} collective-permute-done((bf16[8,2,128,128]{3,2,1,0:T(8,128)(2,1)S(1)}, bf16[8,2,128,128]{3,2,1,0:T(8,128)(2,1)S(1)}, u32[]{:S(2)}, u32[]{:S(2)}) %collective-permute-start.8) | collective-permute-done | bytes 524320 | tf_op jit(solution)/shard_map/ppermute | solution.py:187
  60.2 0.7 slice.18
  60.9 1.3 %collective-permute-start.10 = (bf16[4,2,128,128]{3,2,1,0:T(8,128)(2,1)}, bf16[4,2,128,128]{3,2,1,0:T(8,128)(2,1)S(1)}, u32[]{:S(2)}, u32[]{:S(2)}) collective-permute-start(bf16[4,2,128,128]{3,2,1,0:T(8,128)(2,1)} %slice.18), channel_id=1, source_target_pairs={{0,1},{1,2},{2,3},{3,0},{4,5},{5,6},{6,7},{7,4},{8,9},{9,10},{10,1... | collective-permute-start | bytes 786440 | tf_op jit(solution)/shard_map/ppermute | solution.py:187
  62.2 0.8 copy-done.1
  63.0 0.7 slice.19
  63.7 2.0 %collective-permute-start.11 = (bf16[4,2,128,128]{3,2,1,0:T(8,128)(2,1)}, bf16[4,2,128,128]{3,2,1,0:T(8,128)(2,1)}, u32[]{:S(2)}, u32[]{:S(2)}) collective-permute-start(bf16[4,2,128,128]{3,2,1,0:T(8,128)(2,1)} %slice.19), channel_id=1, source_target_pairs={{0,3},{1,0},{2,1},{3,2},{4,7},{5,4},{6,5},{7,6},{8,11},{9,8},{10,9... | collective-permute-start | bytes 786440 | tf_op jit(solution)/shard_map/ppermute | solution.py:187
  65.7 0.1 collective-permute-start.12
  65.8 0.5 collective-permute-start.13
  66.3 0.1 collective-permute-start.14
  66.5 2.3 %collective-permute-done.10.own_r2 = bf16[4,2,128,128]{3,2,1,0:T(8,128)(2,1)S(1)} collective-permute-done((bf16[4,2,128,128]{3,2,1,0:T(8,128)(2,1)}, bf16[4,2,128,128]{3,2,1,0:T(8,128)(2,1)S(1)}, u32[]{:S(2)}, u32[]{:S(2)}) %collective-permute-start.10) | collective-permute-done | bytes 262176 | tf_op jit(solution)/shard_map/ppermute | solution.py:187
  68.7 1.7 %collective-permute-done.11.own_l2 = bf16[4,2,128,128]{3,2,1,0:T(8,128)(2,1)} collective-permute-done((bf16[4,2,128,128]{3,2,1,0:T(8,128)(2,1)}, bf16[4,2,128,128]{3,2,1,0:T(8,128)(2,1)}, u32[]{:S(2)}, u32[]{:S(2)}) %collective-permute-start.11) | collective-permute-done | bytes 262176 | tf_op jit(solution)/shard_map/ppermute | solution.py:187
  70.5 1.6 %rebuild.1.dense = bf16[32,512,128]{2,1,0:T(8,128)(2,1)S(1)} custom-call(s32[4]{0:T(128)S(1)} %copy-done.4, s32[4,32]{1,0:T(4,128)S(1)} %select_reduce_fusion.occ_index, bf16[8,4,64,128]{3,2,1,0:T(8,128)(2,1)S(1)} %pad_maximum_fusion.c0, bf16[8,4,64,128]{3,2,1,0:T(8,128)(2,1)S(1)} %collective-permute-done.4.c_u, ...), custom_call_target="tpu_custom_call" | custom-call | bytes 6291456 | tf_op jit(solution)/shard_map/rebuild/pallas_call | solution.py:112
  72.1 0.0 collective-permute-done.16.oth_l2
  72.2 8.8 %exchange.1 = (f32[4,8,4,16,128]{4,3,2,1,0:T(8,128)S(1)}, f32[4,8,4,16,128]{4,3,2,1,0:T(8,128)S(1)}) custom-call(s32[4]{0:T(128)S(1)} %copy-done.4, s32[4,32]{1,0:T(4,128)S(1)} %bitcast.23, s32[4,32]{1,0:T(4,128)S(1)} %bitcast.22, bf16[32,512,128]{2,1,0:T(8,128)(2,1)S(1)} %rebuild.1.dense, bf16[8,2,128,128]{3,2,1,0:T(8,128)(2,1)S(1)} %all-to-all-done.1.own0, ...), custom_call_target="tpu_custom_call" | custom-call | flops 2700000000 | bytes 10485760 | tf_op jit(solution)/shard_map/exchange/pallas_call | solution.py:171
  81.0 0.6 collective-permute-start.17
  81.5 2.3 %collective-permute-done.17 = f32[4,8,4,16,128]{4,3,2,1,0:T(8,128)S(1)} collective-permute-done((f32[4,8,4,16,128]{4,3,2,1,0:T(8,128)S(1)}, f32[4,8,4,16,128]{4,3,2,1,0:T(8,128)S(1)}, u32[]{:S(2)}, u32[]{:S(2)}) %collective-permute-start.17) | collective-permute-done | bytes 1048608 | tf_op jit(solution)/shard_map/ppermute | solution.py:191
  83.8 1.0 add_convert_fusion
  84.8 7.5 %all-to-all-start.2 = ((bf16[32,4,16,128]{3,2,1,0:T(8,128)(2,1)}), bf16[32,4,16,128]{3,2,1,0:T(8,128)(2,1)S(1)}, u32[]{:S(2)}, u32[]{:S(2)}) async-start(bf16[32,4,16,128]{3,2,1,0:T(8,128)(2,1)} %bitcast.15), calls=%async_computation.2 | async-start | bytes 1048576 | tf_op jit(solution)/shard_map/all_to_all | solution.py:226
  92.3 0.2 multiply_reduce_fusion
  92.5 18.0 %all-to-all-done.2 = bf16[32,4,16,128]{3,2,1,0:T(8,128)(2,1)S(1)} async-done(((bf16[32,4,16,128]{3,2,1,0:T(8,128)(2,1)}), bf16[32,4,16,128]{3,2,1,0:T(8,128)(2,1)S(1)}, u32[]{:S(2)}, u32[]{:S(2)}) %all-to-all-start.2) | async-done | bytes 524320 | tf_op jit(solution)/shard_map/all_to_all | solution.py:226
  110.5 0.1 convert_reduce_fusion
  110.6 0.7 bitcast_multiply_fusion
  (29 shorter events, 0.1 us)
Async XLA Ops:
  0.0 65.7 %copy-start.7 = (s32[32,8]{0,1:T(8,128)S(1)}, s32[32,8]{0,1:T(8,128)}, u32[]{:S(2)}) copy-start(s32[32,8]{0,1:T(8,128)} %param.9) | copy-start | bytes 3076
  0.7 69.8 %copy-start.4 = (s32[4]{0:T(128)S(1)}, s32[4]{0:T(128)}, u32[]{:S(2)}) copy-start(s32[4]{0:T(128)} %pad_add_fusion.pos) | copy-start | bytes 52
  3.2 16.0 %all-to-all-start = ((bf16[8,64,128]{2,1,0:T(8,128)(2,1)}), bf16[8,64,128]{2,1,0:T(8,128)(2,1)S(1)}, u32[]{:S(2)}, u32[]{:S(2)}) async-start(bf16[8,64,128]{2,1,0:T(8,128)(2,1)} %slice_coeffs.1), calls=%async_computation | async-start | bytes 262144 | tf_op jit(solution)/shard_map/all_to_all | solution.py:199
  11.8 1.0 copy-start
  12.9 0.7 copy-start.3
  14.4 14.2 %collective-permute-start = (bf16[4,2,128,128]{3,2,1,0:T(8,128)(2,1)S(1)}, bf16[4,2,128,128]{3,2,1,0:T(8,128)(2,1)S(1)}, u32[]{:S(2)}, u32[]{:S(2)}) collective-permute-start(bf16[4,2,128,128]{3,2,1,0:T(8,128)(2,1)S(1)} %get-tuple-element.14), channel_id=1, source_target_pairs={{0,32},{32,0},{1,33},{33,1},{2,34},{34,2},{3,35},{35,3},{4,36},{36... | collective-permute-start | bytes 786440 | tf_op jit(solution)/shard_map/ppermute | solution.py:191
  19.3 7.6 %collective-permute-start.1 = (bf16[8,64,128]{2,1,0:T(8,128)(2,1)S(1)}, bf16[8,64,128]{2,1,0:T(8,128)(2,1)S(1)}, u32[]{:S(2)}, u32[]{:S(2)}) collective-permute-start(bf16[8,64,128]{2,1,0:T(8,128)(2,1)S(1)} %all-to-all-done), channel_id=1, source_target_pairs={{0,1},{1,2},{2,3},{3,0},{4,5},{5,6},{6,7},{7,4},{8,9},{9,10},{10,1... | collective-permute-start | bytes 393224 | tf_op jit(solution)/shard_map/ppermute | solution.py:187
  20.8 7.5 %collective-permute-start.2 = (bf16[8,64,128]{2,1,0:T(8,128)(2,1)S(1)}, bf16[8,64,128]{2,1,0:T(8,128)(2,1)S(1)}, u32[]{:S(2)}, u32[]{:S(2)}) collective-permute-start(bf16[8,64,128]{2,1,0:T(8,128)(2,1)S(1)} %all-to-all-done), channel_id=1, source_target_pairs={{0,2},{1,3},{2,0},{3,1},{4,6},{5,7},{6,4},{7,5},{8,10},{9,11},{10,... | collective-permute-start | bytes 393224 | tf_op jit(solution)/shard_map/ppermute | solution.py:187
  23.5 5.0 %collective-permute-start.3 = (bf16[8,64,128]{2,1,0:T(8,128)(2,1)S(1)}, bf16[8,64,128]{2,1,0:T(8,128)(2,1)S(1)}, u32[]{:S(2)}, u32[]{:S(2)}) collective-permute-start(bf16[8,64,128]{2,1,0:T(8,128)(2,1)S(1)} %all-to-all-done), channel_id=1, source_target_pairs={{0,3},{1,0},{2,1},{3,2},{4,7},{5,4},{6,5},{7,6},{8,11},{9,8},{10,9... | collective-permute-start | bytes 393224 | tf_op jit(solution)/shard_map/ppermute | solution.py:187
  29.6 19.1 %all-to-all-start.1 = ((bf16[8,2,128,128]{3,2,1,0:T(8,128)(2,1)}), bf16[8,2,128,128]{3,2,1,0:T(8,128)(2,1)S(1)}, u32[]{:S(2)}, u32[]{:S(2)}) async-start(bf16[8,2,128,128]{3,2,1,0:T(8,128)(2,1)} %fusion.1), calls=%async_computation.1 | async-start | bytes 1048576 | tf_op jit(solution)/shard_map/all_to_all | solution.py:211
  34.7 37.5 %copy-start.5 = (s32[32,4]{0,1:T(4,128)S(1)}, s32[32,4]{0,1:T(4,128)}, u32[]{:S(2)}) copy-start(s32[32,4]{0,1:T(4,128)} %param.8) | copy-start | bytes 1540
  34.7 37.5 %copy-start.6 = (s32[32,4]{0,1:T(4,128)S(1)}, s32[32,4]{0,1:T(4,128)}, u32[]{:S(2)}) copy-start(s32[32,4]{0,1:T(4,128)} %param.7) | copy-start | bytes 1540
  34.7 17.3 %collective-permute-start.4 = (bf16[8,4,64,128]{3,2,1,0:T(8,128)(2,1)S(1)}, bf16[8,4,64,128]{3,2,1,0:T(8,128)(2,1)S(1)}, u32[]{:S(2)}, u32[]{:S(2)}) collective-permute-start(bf16[8,4,64,128]{3,2,1,0:T(8,128)(2,1)S(1)} %pad_maximum_fusion.c0), channel_id=1, source_target_pairs={{0,64},{64,128},{128,192},{192,0},{1,65},{65,129},{129,193},{193,1... | collective-permute-start | bytes 1572872 | tf_op jit(solution)/shard_map/ppermute | solution.py:187
  36.2 18.0 %collective-permute-start.5 = (bf16[8,4,64,128]{3,2,1,0:T(8,128)(2,1)S(1)}, bf16[8,4,64,128]{3,2,1,0:T(8,128)(2,1)S(1)}, u32[]{:S(2)}, u32[]{:S(2)}) collective-permute-start(bf16[8,4,64,128]{3,2,1,0:T(8,128)(2,1)S(1)} %pad_maximum_fusion.c0), channel_id=1, source_target_pairs={{0,192},{64,0},{128,64},{192,128},{1,193},{65,1},{129,65},{193,129... | collective-permute-start | bytes 1572872 | tf_op jit(solution)/shard_map/ppermute | solution.py:187
  48.7 11.5 %collective-permute-start.8 = (bf16[8,2,128,128]{3,2,1,0:T(8,128)(2,1)S(1)}, bf16[8,2,128,128]{3,2,1,0:T(8,128)(2,1)S(1)}, u32[]{:S(2)}, u32[]{:S(2)}) collective-permute-start(bf16[8,2,128,128]{3,2,1,0:T(8,128)(2,1)S(1)} %all-to-all-done.1.own0), channel_id=1, source_target_pairs={{0,1},{1,2},{2,3},{3,0},{4,5},{5,6},{6,7},{7,4},{8,9},{9,10},{10,1... | collective-permute-start | bytes 1572872 | tf_op jit(solution)/shard_map/ppermute | solution.py:187
  50.1 12.1 %collective-permute-start.9 = (bf16[8,2,128,128]{3,2,1,0:T(8,128)(2,1)S(1)}, bf16[8,2,128,128]{3,2,1,0:T(8,128)(2,1)S(1)}, u32[]{:S(2)}, u32[]{:S(2)}) collective-permute-start(bf16[8,2,128,128]{3,2,1,0:T(8,128)(2,1)S(1)} %all-to-all-done.1.own0), channel_id=1, source_target_pairs={{0,3},{1,0},{2,1},{3,2},{4,7},{5,4},{6,5},{7,6},{8,11},{9,8},{10,9... | collective-permute-start | bytes 1572872 | tf_op jit(solution)/shard_map/ppermute | solution.py:187
  52.7 13.2 %collective-permute-start.6 = (bf16[4,4,64,128]{3,2,1,0:T(8,128)(2,1)}, bf16[4,4,64,128]{3,2,1,0:T(8,128)(2,1)S(1)}, u32[]{:S(2)}, u32[]{:S(2)}) collective-permute-start(bf16[4,4,64,128]{3,2,1,0:T(8,128)(2,1)} %slice.16), channel_id=1, source_target_pairs={{0,64},{64,128},{128,192},{192,0},{1,65},{65,129},{129,193},{193,1... | collective-permute-start | bytes 786440 | tf_op jit(solution)/shard_map/ppermute | solution.py:187
  54.9 11.4 %collective-permute-start.7 = (bf16[4,4,64,128]{3,2,1,0:T(8,128)(2,1)}, bf16[4,4,64,128]{3,2,1,0:T(8,128)(2,1)S(1)}, u32[]{:S(2)}, u32[]{:S(2)}) collective-permute-start(bf16[4,4,64,128]{3,2,1,0:T(8,128)(2,1)} %slice.17), channel_id=1, source_target_pairs={{0,192},{64,0},{128,64},{192,128},{1,193},{65,1},{129,65},{193,129... | collective-permute-start | bytes 786440 | tf_op jit(solution)/shard_map/ppermute | solution.py:187
  60.9 7.8 %collective-permute-start.10 = (bf16[4,2,128,128]{3,2,1,0:T(8,128)(2,1)}, bf16[4,2,128,128]{3,2,1,0:T(8,128)(2,1)S(1)}, u32[]{:S(2)}, u32[]{:S(2)}) collective-permute-start(bf16[4,2,128,128]{3,2,1,0:T(8,128)(2,1)} %slice.18), channel_id=1, source_target_pairs={{0,1},{1,2},{2,3},{3,0},{4,5},{5,6},{6,7},{7,4},{8,9},{9,10},{10,1... | collective-permute-start | bytes 786440 | tf_op jit(solution)/shard_map/ppermute | solution.py:187
  62.2 0.8 copy-start.1
  63.7 6.7 %collective-permute-start.11 = (bf16[4,2,128,128]{3,2,1,0:T(8,128)(2,1)}, bf16[4,2,128,128]{3,2,1,0:T(8,128)(2,1)}, u32[]{:S(2)}, u32[]{:S(2)}) collective-permute-start(bf16[4,2,128,128]{3,2,1,0:T(8,128)(2,1)} %slice.19), channel_id=1, source_target_pairs={{0,3},{1,0},{2,1},{3,2},{4,7},{5,4},{6,5},{7,6},{8,11},{9,8},{10,9... | collective-permute-start | bytes 786440 | tf_op jit(solution)/shard_map/ppermute | solution.py:187
  65.7 6.5 %copy-start.2 = (bf16[8,2,128,128]{3,2,1,0:T(8,128)(2,1)S(1)}, bf16[8,2,128,128]{3,2,1,0:T(8,128)(2,1)}, u32[]{:S(2)}) copy-start(bf16[8,2,128,128]{3,2,1,0:T(8,128)(2,1)} %copy-done.1) | copy-start | bytes 1572868
  65.7 6.4 %collective-permute-start.12 = (bf16[8,2,128,128]{3,2,1,0:T(8,128)(2,1)S(1)}, bf16[8,2,128,128]{3,2,1,0:T(8,128)(2,1)S(1)}, u32[]{:S(2)}, u32[]{:S(2)}) collective-permute-start(bf16[8,2,128,128]{3,2,1,0:T(8,128)(2,1)S(1)} %all-to-all-done.1.own0), channel_id=1, source_target_pairs={{0,32},{32,0},{1,33},{33,1},{2,34},{34,2},{3,35},{35,3},{4,36},{36... | collective-permute-start | bytes 1572872 | tf_op jit(solution)/shard_map/ppermute | solution.py:191
  65.8 6.3 %collective-permute-start.13 = (bf16[8,2,128,128]{3,2,1,0:T(8,128)(2,1)S(1)}, bf16[8,2,128,128]{3,2,1,0:T(8,128)(2,1)S(1)}, u32[]{:S(2)}, u32[]{:S(2)}) collective-permute-start(bf16[8,2,128,128]{3,2,1,0:T(8,128)(2,1)S(1)} %collective-permute-done.8.own_r), channel_id=1, source_target_pairs={{0,32},{32,0},{1,33},{33,1},{2,34},{34,2},{3,35},{35,3},{4,36},{36... | collective-permute-start | bytes 1572872 | tf_op jit(solution)/shard_map/ppermute | solution.py:191
  66.3 5.8 %collective-permute-start.14 = (bf16[8,2,128,128]{3,2,1,0:T(8,128)(2,1)}, bf16[8,2,128,128]{3,2,1,0:T(8,128)(2,1)S(1)}, u32[]{:S(2)}, u32[]{:S(2)}) collective-permute-start(bf16[8,2,128,128]{3,2,1,0:T(8,128)(2,1)} %copy-done.1), channel_id=1, source_target_pairs={{0,32},{32,0},{1,33},{33,1},{2,34},{34,2},{3,35},{35,3},{4,36},{36... | collective-permute-start | bytes 1572872 | tf_op jit(solution)/shard_map/ppermute | solution.py:191
  68.7 3.4 %collective-permute-start.15 = (bf16[4,2,128,128]{3,2,1,0:T(8,128)(2,1)S(1)}, bf16[4,2,128,128]{3,2,1,0:T(8,128)(2,1)S(1)}, u32[]{:S(2)}, u32[]{:S(2)}) collective-permute-start(bf16[4,2,128,128]{3,2,1,0:T(8,128)(2,1)S(1)} %collective-permute-done.10.own_r2), channel_id=1, source_target_pairs={{0,32},{32,0},{1,33},{33,1},{2,34},{34,2},{3,35},{35,3},{4,36},{36... | collective-permute-start | bytes 786440 | tf_op jit(solution)/shard_map/ppermute | solution.py:191
  70.4 1.7 %collective-permute-start.16 = (bf16[4,2,128,128]{3,2,1,0:T(8,128)(2,1)}, bf16[4,2,128,128]{3,2,1,0:T(8,128)(2,1)S(1)}, u32[]{:S(2)}, u32[]{:S(2)}) collective-permute-start(bf16[4,2,128,128]{3,2,1,0:T(8,128)(2,1)} %collective-permute-done.11.own_l2), channel_id=1, source_target_pairs={{0,32},{32,0},{1,33},{33,1},{2,34},{34,2},{3,35},{35,3},{4,36},{36... | collective-permute-start | bytes 786440 | tf_op jit(solution)/shard_map/ppermute | solution.py:191
  81.0 2.8 %collective-permute-start.17 = (f32[4,8,4,16,128]{4,3,2,1,0:T(8,128)S(1)}, f32[4,8,4,16,128]{4,3,2,1,0:T(8,128)S(1)}, u32[]{:S(2)}, u32[]{:S(2)}) collective-permute-start(f32[4,8,4,16,128]{4,3,2,1,0:T(8,128)S(1)} %get-tuple-element.20), channel_id=1, source_target_pairs={{0,32},{32,0},{1,33},{33,1},{2,34},{34,2},{3,35},{35,3},{4,36},{36... | collective-permute-start | bytes 3145736 | tf_op jit(solution)/shard_map/ppermute | solution.py:191
  84.8 25.7 %all-to-all-start.2 = ((bf16[32,4,16,128]{3,2,1,0:T(8,128)(2,1)}), bf16[32,4,16,128]{3,2,1,0:T(8,128)(2,1)S(1)}, u32[]{:S(2)}, u32[]{:S(2)}) async-start(bf16[32,4,16,128]{3,2,1,0:T(8,128)(2,1)} %bitcast.15), calls=%async_computation.2 | async-start | bytes 1048576 | tf_op jit(solution)/shard_map/all_to_all | solution.py:226

commit v7 on v6

--- a/solution.py
+++ b/solution.py
@@ -120,67 +120,90 @@
     )(pos, occ_index, *pieces)
 
 
-def main_kernel(pos, pair_tiles, pair_live, dense,
-                own0, own_r, own_l, own_r2, own_l2, oth0, oth_r, oth_l, oth_r2, oth_l2,
-                keep, send, field, block):
+def transform(pos, pair_tiles, pair_live, dense, field, first, xp, own, oth, lo, count):
+    core = pos[1]
+
+    def body(step, carry):
+        tile = (lo + step) * NX + xp
+        lhs, rhs = [], []
+        for part, ref in ((core, own), (1 - core, oth)):
+            for j in range(2):
+                slot = part * 2 + j
+                eri = ref[step, j]
+                rhs.append(jnp.where(pair_live[slot, tile] != 0, eri, jnp.zeros_like(eri)))
+                lhs.append(dense[pair_tiles[slot, tile]])
+        half = jnp.dot(jnp.concatenate(lhs, axis=1), jnp.concatenate(rhs, axis=0), preferred_element_type=F32)
+        field[first + lo + step] = half.astype(BF)
+        return carry
+
+    lax.fori_loop(0, count, body, 0, unroll=4)
+
+
+def near_kernel(pos, pair_tiles, pair_live, dense, own0, own_r, own_l, oth0, oth_rl, field):
+    x = pos[3]
+    run = functools.partial(transform, pos, pair_tiles, pair_live, dense, field)
+    run(0, x, own0, oth0, 0, NZ)
+    run(NZ, (x + 3) % NX, own_r, oth_rl.at[0], 0, NZ)
+    run(2 * NZ, (x + 1) % NX, own_l, oth_rl.at[1], 0, NZ)
+
+
+def near_columns(pos, pair_tiles, pair_live, dense, *pieces):
+    return pl.pallas_call(
+        near_kernel,
+        out_shape=jax.ShapeDtypeStruct((3 * NZ, OCC * HALF, TS), BF),
+        in_specs=[SMEM] * 3 + [VMEM] * (1 + len(pieces)),
+        out_specs=VMEM,
+        compiler_params=pltpu.CompilerParams(vmem_limit_bytes=16 * 2**20),
+        cost_estimate=pl.CostEstimate(flops=1600000000, bytes_accessed=10 * 2**20, transcendentals=0),
+        name="near_columns",
+    )(pos, pair_tiles, pair_live, dense, *pieces)
+
+
+def far_kernel(pos, pair_tiles, pair_live, dense, near, own_r2, own_l2, oth_r2, oth_l2, keep, send, far, block):
     core, x = pos[1], pos[3]
-
-    def transform(xp, own, oth, lo, count):
-        def body(step, carry):
-            tile = (lo + step) * NX + xp
-            lhs, rhs = [], []
-            for part, ref in ((core, own), (1 - core, oth)):
-                for j in range(2):
-                    slot = part * 2 + j
-                    eri = ref[step, j]
-                    rhs.append(jnp.where(pair_live[slot, tile] != 0, eri, jnp.zeros_like(eri)))
-                    lhs.append(dense[pair_tiles[slot, tile]])
-            half = jnp.dot(
-                jnp.concatenate(lhs, axis=1), jnp.concatenate(rhs, axis=0), preferred_element_type=F32
-            )
-            field[tile] = half.astype(BF)
-            return carry
-
-        lax.fori_loop(0, count, body, 0, unroll=4)
-
-    transform(x, own0, oth0, 0, 8)
-    transform((x + 3) % NX, own_r, oth_r, 0, 8)
-    transform((x + 1) % NX, own_l, oth_l, 0, 8)
-    transform((x + 2) % NX, own_r2, oth_r2, 0, 4)
-    transform((x + 2) % NX, own_l2, oth_l2, 4, 4)
+    run = functools.partial(transform, pos, pair_tiles, pair_live, dense, far)
+    run(0, (x + 2) % NX, own_r2, oth_r2, 0, 4)
+    run(0, (x + 2) % NX, own_l2, oth_l2, 4, 4)
+
+    def partner(slot, tile):
+        other = pair_tiles[slot, tile]
+        offset = (other % NX - x + NX) % NX
+        row = other // NX
+        column = jnp.where(offset == 0, 0, jnp.where(offset == 3, 1, 2))
+        return jnp.where(offset == 2, far[row], near[column * NZ + row])
 
     def gram(zp, carry):
         tile = zp * NX + x
-        partners = jnp.concatenate([field[pair_tiles[slot, tile]] for slot in range(SLOTS)], axis=1)
+        partners = jnp.concatenate([partner(slot, tile) for slot in range(SLOTS)], axis=1)
         block[...] = lax.dot_general(
-            field[tile], partners, (((0,), (0,)), ((), ())), preferred_element_type=F32
+            near[zp], partners, (((0,), (0,)), ((), ())), preferred_element_type=F32
         )
         for y in range(NY):
-            near = pl.multiple_of(y * 2 * ROWS + core * ROWS, ROWS)
-            far = pl.multiple_of(y * 2 * ROWS + (1 - core) * ROWS, ROWS)
+            mine = pl.multiple_of(y * 2 * ROWS + core * ROWS, ROWS)
+            other = pl.multiple_of(y * 2 * ROWS + (1 - core) * ROWS, ROWS)
             for slot in range(SLOTS):
-                keep[y, zp, slot] = block[pl.ds(near, ROWS), slot * TS:(slot + 1) * TS]
-                send[y, zp, slot] = block[pl.ds(far, ROWS), slot * TS:(slot + 1) * TS]
+                keep[y, zp, slot] = block[pl.ds(mine, ROWS), slot * TS:(slot + 1) * TS]
+                send[y, zp, slot] = block[pl.ds(other, ROWS), slot * TS:(slot + 1) * TS]
         return carry
 
     lax.fori_loop(0, NZ, gram, 0)
 
 
-def exchange(pos, pair_tiles, pair_live, *pieces):
+def far_column(pos, pair_tiles, pair_live, dense, near, *pieces):
     shape = jax.ShapeDtypeStruct((NY, NZ, SLOTS, ROWS, TS), F32)
     return pl.pallas_call(
-        main_kernel,
+        far_kernel,
         out_shape=(shape, shape),
-        in_specs=[SMEM] * 3 + [VMEM] * len(pieces),
+        in_specs=[SMEM] * 3 + [VMEM] * (2 + len(pieces)),
         out_specs=(VMEM, VMEM),
         scratch_shapes=[
-            pltpu.VMEM((TILES, OCC * HALF, TS), BF),
+            pltpu.VMEM((NZ, OCC * HALF, TS), BF),
             pltpu.VMEM((TS, SLOTS * TS), F32),
         ],
-        compiler_params=pltpu.CompilerParams(vmem_limit_bytes=24 * 2**20),
-        cost_estimate=pl.CostEstimate(flops=2700000000, bytes_accessed=10 * 2**20, transcendentals=0),
-        name="exchange",
-    )(pos, pair_tiles, pair_live, *pieces)
+        compiler_params=pltpu.CompilerParams(vmem_limit_bytes=16 * 2**20),
+        cost_estimate=pl.CostEstimate(flops=1100000000, bytes_accessed=10 * 2**20, transcendentals=0),
+        name="far_column",
+    )(pos, pair_tiles, pair_live, dense, near, *pieces)
 
 
 def shift(value, axis, size, by):
@@ -203,25 +226,26 @@
     occ_index = jnp.sum(jnp.where(hits, jnp.arange(OCC)[None, None, :], 0), axis=2).astype(jnp.int32)
 
     got_eri = swap(give_eri)
-    c0 = jnp.stack([column] + [shift(column, "x", NX, by) for by in (1, 2, 3)], axis=1)
-    got_eri, c0 = lax.optimization_barrier((got_eri, c0))
+    got_eri, column = lax.optimization_barrier((got_eri, column))
     by_aux = lax.dynamic_slice_in_dim(
         jnp.concatenate([keep_eri, got_eri, keep_eri]), pos[1] * AUXROWS, NZ, 0
     )
     own0 = lax.all_to_all(by_aux, "z", split_axis=0, concat_axis=0, tiled=True)
+    c0 = jnp.stack([column] + [shift(column, "x", NX, by) for by in (1, 2, 3)], axis=1)
+    own0, c0 = lax.optimization_barrier((own0, c0))
     own_r, own_l = shift(own0, "x", NX, 1), shift(own0, "x", NX, -1)
     c_u, c_d = shift(c0, "y", NY, 1), shift(c0, "y", NY, -1)
     oth0 = swap(own0)
+    own_r, own_l, c_u, c_d, oth0 = lax.optimization_barrier((own_r, own_l, c_u, c_d, oth0))
     own_r2, own_l2 = shift(own_r[:4], "x", NX, 1), shift(own_l[4:], "x", NX, -1)
     c_u2, c_d2 = shift(c_u[:4], "y", NY, 1), shift(c_d[4:], "y", NY, -1)
-    oth_r, oth_l = swap(own_r), swap(own_l)
+    oth_rl = swap(jnp.stack([own_r, own_l]))
+    tables = (pos, pair_tiles.T, pair_live.T)
+    dense = rebuild(pos, occ_index, c0, c_u, c_d, c_u2, c_d2)
+    near = near_columns(*tables, dense, own0, own_r, own_l, oth0, oth_rl)
+    near, own_r2, own_l2 = lax.optimization_barrier((near, own_r2, own_l2))
     oth_r2, oth_l2 = swap(own_r2), swap(own_l2)
-
-    dense = rebuild(pos, occ_index, c0, c_u, c_d, c_u2, c_d2)
-    keep, send = exchange(
-        pos, pair_tiles.T, pair_live.T, dense,
-        own0, own_r, own_l, own_r2, own_l2, oth0, oth_r, oth_l, oth_r2, oth_l2,
-    )
+    keep, send = far_column(*tables, dense, near, own_r2, own_l2, oth_r2, oth_l2)
     partial = (keep + swap(send)).astype(BF).reshape(NY * NZ, SLOTS, ROWS, TS)
     parts = lax.all_to_all(partial, ("y", "z"), split_axis=0, concat_axis=0, tiled=True).astype(F32)
     flags = lax.dynamic_index_in_dim(pair_live, tile, 0, keepdims=False).astype(F32) * SCALE

time: 113 us -> 117 us (1.035); the launches traced: 111 us -> 116 us
  waiting for transfers between devices: 47.1 us -> 53.7 us
  local copies, waits for them, and re-layouts: 5.4 us -> 2.53 us
  Pallas kernels: 13.8 us -> 15.1 us
    ppermute x11, waiting for transfers between devices: 11.1 us -> 17.3 us  [shift(): lax.ppermute(value, axis, [(i, (i + by) % size) for i in range(size)])]
    all_to_all x1, waiting for transfers between devices: 10.8 us -> 6.25 us  [shards(): own0 = lax.all_to_all(by_aux, 'z', split_axis=0, concat_axis=0, tiled=True)]
    all_to_all x1, waiting for transfers between devices: 4.8 us -> 8.17 us  [shards(): lax.all_to_all(coeffs, 'z', split_axis=0, concat_axis=0, tiled=True)]
    ppermute x7 -> x6, waiting for transfers between devices: 2.35 us -> 3.93 us  [swap(): return lax.ppermute(value, 'c', [(0, 1), (1, 0)])]
    slice x2, local copies, waits for them, and re-layouts: 1.44 us -> 0.04 us  [shards(): c_u2, c_d2 = (shift(c_u[:4], 'y', NY, 1), shift(c_d[4:], 'y', NY, -1))]
    pallas_call x1 -> x2, Pallas kernels: 8.77 us -> 10 us  [the longest x1 5.59 us: near_columns(): pl.pallas_call(near_kernel, out_shape=jax.ShapeDtypeStruct((3 * NZ, OCC *...]
  transfers between devices with their start and end apart: 21 -> 20, of which waited for: 10 -> 14; matrix products, arithmetic and copies ran while one was open for 3% -> 0% of each run, Pallas kernels for 2% -> 6%
where the time goes in v7:
time: 117 us; the launch traced here: 116 us
  waiting for transfers between devices  53.7 us (46%)
  starting transfers between devices  40.2 us (34%)
  Pallas kernels  15.1 us (13%)
  other arithmetic  4.77 us (4%)
  local copies, waits for them, and re-layouts  2.53 us (2%)
    ppermute x11, starting transfers between devices, shift(): lax.ppermute(value, axis, [(i, (i + by) % size) for i in range(size)])  18.5 us
    all_to_all x1, waiting for transfers between devices, shards(): lax.all_to_all(partial, ('y', 'z'), split_axis=0, concat_axis=0, tiled=True)  18.1 us
    ppermute x11, waiting for transfers between devices, shift(): lax.ppermute(value, axis, [(i, (i + by) % size) for i in range(size)])  17.3 us
    all_to_all x1, starting transfers between devices, shards(): lax.all_to_all(coeffs, 'z', split_axis=0, concat_axis=0, tiled=True)  8.59 us
    all_to_all x1, waiting for transfers between devices, shards(): lax.all_to_all(coeffs, 'z', split_axis=0, concat_axis=0, tiled=True)  8.17 us
    all_to_all x1, starting transfers between devices, shards(): lax.all_to_all(partial, ('y', 'z'), split_axis=0, concat_axis=0, tiled=True)  7.25 us
    all_to_all x1, waiting for transfers between devices, shards(): own0 = lax.all_to_all(by_aux, 'z', split_axis=0, concat_axis=0, tiled=True)  6.25 us
    pallas_call x1, Pallas kernels, near_columns(): pl.pallas_call(near_kernel, out_shape=jax.ShapeDtypeStruct((3 * NZ, OCC *...  5.59 us
  transfers between devices with their start and end apart: 20, of which 14 were waited for; matrix products, arithmetic and copies ran while one was open for 0% of the time, Pallas kernels for 6%

profile of v7, /device:TPU:32, one launch (start us, length us, event | category | flops | bytes accessed | tf_op | source)
XLA Modules:
  0.0 116.5 jit_solution(9247047165101440166)
XLA Ops:
  0.0 0.6 pad_add_fusion.pos
  0.6 2.6 %slice_coeffs.1 = bf16[8,64,128]{2,1,0:T(8,128)(2,1)} custom-call(s32[4]{0:T(128)} %pad_add_fusion.pos, s32[8,32]{1,0:T(8,128)} %bitcast.34, bf16[128,1024]{1,0:T(8,128)(2,1)} %orb.1), custom_call_target="tpu_custom_call" | custom-call | bytes 262144 | tf_op jit(solution)/shard_map/slice_coeffs/pallas_call | solution.py:45
  3.2 1.0 copy-done.2
  4.2 0.6 copy-done.3
  4.8 0.8 split_aux.1
  5.7 0.1 collective-permute-start
  5.8 8.6 %all-to-all-start = ((bf16[8,64,128]{2,1,0:T(8,128)(2,1)}), bf16[8,64,128]{2,1,0:T(8,128)(2,1)S(1)}, u32[]{:S(2)}, u32[]{:S(2)}) async-start(bf16[8,64,128]{2,1,0:T(8,128)(2,1)} %slice_coeffs.1), calls=%async_computation | async-start | bytes 262144 | tf_op jit(solution)/shard_map/all_to_all | solution.py:222
  14.4 8.2 %all-to-all-done = bf16[8,64,128]{2,1,0:T(8,128)(2,1)S(1)} async-done(((bf16[8,64,128]{2,1,0:T(8,128)(2,1)}), bf16[8,64,128]{2,1,0:T(8,128)(2,1)S(1)}, u32[]{:S(2)}, u32[]{:S(2)}) %all-to-all-start) | async-done | bytes 131104 | tf_op jit(solution)/shard_map/all_to_all | solution.py:222
  22.5 1.1 fusion.1
  23.6 4.9 %all-to-all-start.1 = ((bf16[8,2,128,128]{3,2,1,0:T(8,128)(2,1)}), bf16[8,2,128,128]{3,2,1,0:T(8,128)(2,1)S(1)}, u32[]{:S(2)}, u32[]{:S(2)}) async-start(bf16[8,2,128,128]{3,2,1,0:T(8,128)(2,1)} %fusion.1), calls=%async_computation.1 | async-start | bytes 1048576 | tf_op jit(solution)/shard_map/all_to_all | solution.py:233
  28.6 1.5 %collective-permute-start.1 = (bf16[8,64,128]{2,1,0:T(8,128)(2,1)S(1)}, bf16[8,64,128]{2,1,0:T(8,128)(2,1)S(1)}, u32[]{:S(2)}, u32[]{:S(2)}) collective-permute-start(bf16[8,64,128]{2,1,0:T(8,128)(2,1)S(1)} %all-to-all-done), channel_id=1, source_target_pairs={{0,1},{1,2},{2,3},{3,0},{4,5},{5,6},{6,7},{7,4},{8,9},{9,10},{10,1... | collective-permute-start | bytes 393224 | tf_op jit(solution)/shard_map/ppermute | solution.py:210
  30.0 2.7 %collective-permute-start.2 = (bf16[8,64,128]{2,1,0:T(8,128)(2,1)S(1)}, bf16[8,64,128]{2,1,0:T(8,128)(2,1)S(1)}, u32[]{:S(2)}, u32[]{:S(2)}) collective-permute-start(bf16[8,64,128]{2,1,0:T(8,128)(2,1)S(1)} %all-to-all-done), channel_id=1, source_target_pairs={{0,2},{1,3},{2,0},{3,1},{4,6},{5,7},{6,4},{7,5},{8,10},{9,11},{10,... | collective-permute-start | bytes 393224 | tf_op jit(solution)/shard_map/ppermute | solution.py:210
  32.7 1.4 %collective-permute-start.3 = (bf16[8,64,128]{2,1,0:T(8,128)(2,1)S(1)}, bf16[8,64,128]{2,1,0:T(8,128)(2,1)S(1)}, u32[]{:S(2)}, u32[]{:S(2)}) collective-permute-start(bf16[8,64,128]{2,1,0:T(8,128)(2,1)S(1)} %all-to-all-done), channel_id=1, source_target_pairs={{0,3},{1,0},{2,1},{3,2},{4,7},{5,4},{6,5},{7,6},{8,11},{9,8},{10,9... | collective-permute-start | bytes 393224 | tf_op jit(solution)/shard_map/ppermute | solution.py:210
  34.2 1.9 %collective-permute-done.1 = bf16[8,64,128]{2,1,0:T(8,128)(2,1)S(1)} collective-permute-done((bf16[8,64,128]{2,1,0:T(8,128)(2,1)S(1)}, bf16[8,64,128]{2,1,0:T(8,128)(2,1)S(1)}, u32[]{:S(2)}, u32[]{:S(2)}) %collective-permute-start.1) | collective-permute-done | bytes 131104 | tf_op jit(solution)/shard_map/ppermute | solution.py:210
  36.1 1.5 %collective-permute-done.2 = bf16[8,64,128]{2,1,0:T(8,128)(2,1)S(1)} collective-permute-done((bf16[8,64,128]{2,1,0:T(8,128)(2,1)S(1)}, bf16[8,64,128]{2,1,0:T(8,128)(2,1)S(1)}, u32[]{:S(2)}, u32[]{:S(2)}) %collective-permute-start.2) | collective-permute-done | bytes 131104 | tf_op jit(solution)/shard_map/ppermute | solution.py:210
  37.6 0.1 collective-permute-done.3
  37.7 0.1 pad_maximum_fusion.1.c0
  37.8 6.3 %all-to-all-done.1.own0 = bf16[8,2,128,128]{3,2,1,0:T(8,128)(2,1)S(1)} async-done(((bf16[8,2,128,128]{3,2,1,0:T(8,128)(2,1)}), bf16[8,2,128,128]{3,2,1,0:T(8,128)(2,1)S(1)}, u32[]{:S(2)}, u32[]{:S(2)}) %all-to-all-start.1) | async-done | bytes 524320 | tf_op jit(solution)/shard_map/all_to_all | solution.py:233
  44.0 1.5 %collective-permute-start.4 = (bf16[8,2,128,128]{3,2,1,0:T(8,128)(2,1)S(1)}, bf16[8,2,128,128]{3,2,1,0:T(8,128)(2,1)S(1)}, u32[]{:S(2)}, u32[]{:S(2)}) collective-permute-start(bf16[8,2,128,128]{3,2,1,0:T(8,128)(2,1)S(1)} %all-to-all-done.1.own0), channel_id=1, source_target_pairs={{0,1},{1,2},{2,3},{3,0},{4,5},{5,6},{6,7},{7,4},{8,9},{9,10},{10,1... | collective-permute-start | bytes 1572872 | tf_op jit(solution)/shard_map/ppermute | solution.py:210
  45.5 1.8 %collective-permute-start.5 = (bf16[8,2,128,128]{3,2,1,0:T(8,128)(2,1)S(1)}, bf16[8,2,128,128]{3,2,1,0:T(8,128)(2,1)S(1)}, u32[]{:S(2)}, u32[]{:S(2)}) collective-permute-start(bf16[8,2,128,128]{3,2,1,0:T(8,128)(2,1)S(1)} %all-to-all-done.1.own0), channel_id=1, source_target_pairs={{0,3},{1,0},{2,1},{3,2},{4,7},{5,4},{6,5},{7,6},{8,11},{9,8},{10,9... | collective-permute-start | bytes 1572872 | tf_op jit(solution)/shard_map/ppermute | solution.py:210
  47.3 1.6 %collective-permute-start.6 = (bf16[8,4,64,128]{3,2,1,0:T(8,128)(2,1)S(1)}, bf16[8,4,64,128]{3,2,1,0:T(8,128)(2,1)S(1)}, u32[]{:S(2)}, u32[]{:S(2)}) collective-permute-start(bf16[8,4,64,128]{3,2,1,0:T(8,128)(2,1)S(1)} %pad_maximum_fusion.1.c0), channel_id=1, source_target_pairs={{0,64},{64,128},{128,192},{192,0},{1,65},{65,129},{129,193},{193,1... | collective-permute-start | bytes 1572872 | tf_op jit(solution)/shard_map/ppermute | solution.py:210
  48.8 1.7 %collective-permute-start.7 = (bf16[8,4,64,128]{3,2,1,0:T(8,128)(2,1)S(1)}, bf16[8,4,64,128]{3,2,1,0:T(8,128)(2,1)S(1)}, u32[]{:S(2)}, u32[]{:S(2)}) collective-permute-start(bf16[8,4,64,128]{3,2,1,0:T(8,128)(2,1)S(1)} %pad_maximum_fusion.1.c0), channel_id=1, source_target_pairs={{0,192},{64,0},{128,64},{192,128},{1,193},{65,1},{129,65},{193,129... | collective-permute-start | bytes 1572872 | tf_op jit(solution)/shard_map/ppermute | solution.py:210
  50.5 4.2 %collective-permute-done.4.own_r = bf16[8,2,128,128]{3,2,1,0:T(8,128)(2,1)S(1)} collective-permute-done((bf16[8,2,128,128]{3,2,1,0:T(8,128)(2,1)S(1)}, bf16[8,2,128,128]{3,2,1,0:T(8,128)(2,1)S(1)}, u32[]{:S(2)}, u32[]{:S(2)}) %collective-permute-start.4) | collective-permute-done | bytes 524320 | tf_op jit(solution)/shard_map/ppermute | solution.py:210
  54.7 2.9 %collective-permute-done.6.c_u = bf16[8,4,64,128]{3,2,1,0:T(8,128)(2,1)S(1)} collective-permute-done((bf16[8,4,64,128]{3,2,1,0:T(8,128)(2,1)S(1)}, bf16[8,4,64,128]{3,2,1,0:T(8,128)(2,1)S(1)}, u32[]{:S(2)}, u32[]{:S(2)}) %collective-permute-start.6) | collective-permute-done | bytes 524320 | tf_op jit(solution)/shard_map/ppermute | solution.py:210
  57.7 0.3 collective-permute-done.7.c_d
  58.0 0.8 copy-done
  58.8 1.1 pad_maximum_fusion
  60.0 3.0 %collective-permute-start.10 = (bf16[4,4,64,128]{3,2,1,0:T(8,128)(2,1)S(1)}, bf16[4,4,64,128]{3,2,1,0:T(8,128)(2,1)S(1)}, u32[]{:S(2)}, u32[]{:S(2)}) collective-permute-start(bf16[4,4,64,128]{3,2,1,0:T(8,128)(2,1)S(1)} %slice.13), channel_id=1, source_target_pairs={{0,192},{64,0},{128,64},{192,128},{1,193},{65,1},{129,65},{193,129... | collective-permute-start | bytes 786440 | tf_op jit(solution)/shard_map/ppermute | solution.py:210
  63.0 0.1 collective-permute-start.9
  63.1 0.3 collective-permute-start.12
  63.5 3.0 %collective-permute-start.13 = (bf16[4,2,128,128]{3,2,1,0:T(8,128)(2,1)S(1)}, bf16[4,2,128,128]{3,2,1,0:T(8,128)(2,1)S(1)}, u32[]{:S(2)}, u32[]{:S(2)}) collective-permute-start(bf16[4,2,128,128]{3,2,1,0:T(8,128)(2,1)S(1)} %slice.15), channel_id=1, source_target_pairs={{0,3},{1,0},{2,1},{3,2},{4,7},{5,4},{6,5},{7,6},{8,11},{9,8},{10,9... | collective-permute-start | bytes 786440 | tf_op jit(solution)/shard_map/ppermute | solution.py:210
  66.5 2.7 %collective-permute-done.10.c_d2 = bf16[4,4,64,128]{3,2,1,0:T(8,128)(2,1)S(1)} collective-permute-done((bf16[4,4,64,128]{3,2,1,0:T(8,128)(2,1)S(1)}, bf16[4,4,64,128]{3,2,1,0:T(8,128)(2,1)S(1)}, u32[]{:S(2)}, u32[]{:S(2)}) %collective-permute-start.10) | collective-permute-done | bytes 262176 | tf_op jit(solution)/shard_map/ppermute | solution.py:210
  69.2 3.5 %collective-permute-done.9.c_u2 = bf16[4,4,64,128]{3,2,1,0:T(8,128)(2,1)S(1)} collective-permute-done((bf16[4,4,64,128]{3,2,1,0:T(8,128)(2,1)S(1)}, bf16[4,4,64,128]{3,2,1,0:T(8,128)(2,1)S(1)}, u32[]{:S(2)}, u32[]{:S(2)}) %collective-permute-start.9) | collective-permute-done | bytes 262176 | tf_op jit(solution)/shard_map/ppermute | solution.py:210
  72.7 1.6 %rebuild.1.dense = bf16[32,512,128]{2,1,0:T(8,128)(2,1)S(1)} custom-call(s32[4]{0:T(128)S(1)} %copy-done.4, s32[4,32]{1,0:T(4,128)S(1)} %select_reduce_fusion.occ_index, bf16[8,4,64,128]{3,2,1,0:T(8,128)(2,1)S(1)} %pad_maximum_fusion.1.c0, bf16[8,4,64,128]{3,2,1,0:T(8,128)(2,1)S(1)} %collective-permute-done.6.c_u, ...), custom_call_target="tpu_custom_call" | custom-call | bytes 6291456 | tf_op jit(solution)/shard_map/rebuild/pallas_call | solution.py:112
  74.4 5.6 %near_columns.1.near = bf16[24,512,128]{2,1,0:T(8,128)(2,1)S(1)} custom-call(s32[4]{0:T(128)S(1)} %copy-done.4, s32[4,32]{1,0:T(4,128)S(1)} %bitcast.28, s32[4,32]{1,0:T(4,128)S(1)} %bitcast.26, bf16[32,512,128]{2,1,0:T(8,128)(2,1)S(1)} %rebuild.1.dense, bf16[8,2,128,128]{3,2,1,0:T(8,128)(2,1)S(1)} %all-to-all-done.1.own0, ...), custom_call_target="tpu_custom_call" | custom-call | flops 1600000000 | bytes 10485760 | tf_op jit(solution)/shard_map/near_columns/pallas_call | solution.py:151
  80.0 0.1 collective-permute-start.14
  80.1 0.5 collective-permute-start.15
  80.6 1.0 collective-permute-done.14.oth_r2
  81.6 0.4 collective-permute-done.15.oth_l2
  82.0 4.4 %far_column.1 = (f32[4,8,4,16,128]{4,3,2,1,0:T(8,128)S(1)}, f32[4,8,4,16,128]{4,3,2,1,0:T(8,128)S(1)}) custom-call(s32[4]{0:T(128)S(1)} %copy-done.4, s32[4,32]{1,0:T(4,128)S(1)} %bitcast.29, s32[4,32]{1,0:T(4,128)S(1)} %bitcast.27, bf16[32,512,128]{2,1,0:T(8,128)(2,1)S(1)} %rebuild.1.dense, bf16[24,512,128]{2,1,0:T(8,128)(2,1)S(1)} %near_columns.1.near, ...), custom_call_target="tpu_custom_call" | custom-call | flops 1100000000 | bytes 10485760 | tf_op jit(solution)/shard_map/far_column/pallas_call | solution.py:194
  86.4 0.2 collective-permute-start.16
  86.6 2.5 %collective-permute-done.16 = f32[4,8,4,16,128]{4,3,2,1,0:T(8,128)S(1)} collective-permute-done((f32[4,8,4,16,128]{4,3,2,1,0:T(8,128)S(1)}, f32[4,8,4,16,128]{4,3,2,1,0:T(8,128)S(1)}, u32[]{:S(2)}, u32[]{:S(2)}) %collective-permute-start.16) | collective-permute-done | bytes 1048608 | tf_op jit(solution)/shard_map/ppermute | solution.py:214
  89.2 1.0 add_convert_fusion
  90.1 7.3 %all-to-all-start.2 = ((bf16[32,4,16,128]{3,2,1,0:T(8,128)(2,1)}), bf16[32,4,16,128]{3,2,1,0:T(8,128)(2,1)S(1)}, u32[]{:S(2)}, u32[]{:S(2)}) async-start(bf16[32,4,16,128]{3,2,1,0:T(8,128)(2,1)} %bitcast.17), calls=%async_computation.2 | async-start | bytes 1048576 | tf_op jit(solution)/shard_map/all_to_all | solution.py:250
  97.4 0.2 multiply_reduce_fusion
  97.6 18.1 %all-to-all-done.2 = bf16[32,4,16,128]{3,2,1,0:T(8,128)(2,1)S(1)} async-done(((bf16[32,4,16,128]{3,2,1,0:T(8,128)(2,1)}), bf16[32,4,16,128]{3,2,1,0:T(8,128)(2,1)S(1)}, u32[]{:S(2)}, u32[]{:S(2)}) %all-to-all-start.2) | async-done | bytes 524320 | tf_op jit(solution)/shard_map/all_to_all | solution.py:250
  115.7 0.1 convert_reduce_fusion
  115.8 0.7 bitcast_multiply_fusion
  (29 shorter events, 0.2 us)
Async XLA Ops:
  0.0 59.9 %copy-start.7 = (s32[32,8]{0,1:T(8,128)S(1)}, s32[32,8]{0,1:T(8,128)}, u32[]{:S(2)}) copy-start(s32[32,8]{0,1:T(8,128)} %param.9) | copy-start | bytes 3076
  0.6 72.1 %copy-start.4 = (s32[4]{0:T(128)S(1)}, s32[4]{0:T(128)}, u32[]{:S(2)}) copy-start(s32[4]{0:T(128)} %pad_add_fusion.pos) | copy-start | bytes 52
  3.2 1.0 copy-start.2
  4.2 0.6 copy-start.3
  5.7 16.9 %collective-permute-start = (bf16[4,2,128,128]{3,2,1,0:T(8,128)(2,1)S(1)}, bf16[4,2,128,128]{3,2,1,0:T(8,128)(2,1)S(1)}, u32[]{:S(2)}, u32[]{:S(2)}) collective-permute-start(bf16[4,2,128,128]{3,2,1,0:T(8,128)(2,1)S(1)} %get-tuple-element.25), channel_id=1, source_target_pairs={{0,32},{32,0},{1,33},{33,1},{2,34},{34,2},{3,35},{35,3},{4,36},{36... | collective-permute-start | bytes 786440 | tf_op jit(solution)/shard_map/ppermute | solution.py:214
  5.8 16.8 %all-to-all-start = ((bf16[8,64,128]{2,1,0:T(8,128)(2,1)}), bf16[8,64,128]{2,1,0:T(8,128)(2,1)S(1)}, u32[]{:S(2)}, u32[]{:S(2)}) async-start(bf16[8,64,128]{2,1,0:T(8,128)(2,1)} %slice_coeffs.1), calls=%async_computation | async-start | bytes 262144 | tf_op jit(solution)/shard_map/all_to_all | solution.py:222
  23.6 20.4 %all-to-all-start.1 = ((bf16[8,2,128,128]{3,2,1,0:T(8,128)(2,1)}), bf16[8,2,128,128]{3,2,1,0:T(8,128)(2,1)S(1)}, u32[]{:S(2)}, u32[]{:S(2)}) async-start(bf16[8,2,128,128]{3,2,1,0:T(8,128)(2,1)} %fusion.1), calls=%async_computation.1 | async-start | bytes 1048576 | tf_op jit(solution)/shard_map/all_to_all | solution.py:233
  28.6 7.6 %collective-permute-start.1 = (bf16[8,64,128]{2,1,0:T(8,128)(2,1)S(1)}, bf16[8,64,128]{2,1,0:T(8,128)(2,1)S(1)}, u32[]{:S(2)}, u32[]{:S(2)}) collective-permute-start(bf16[8,64,128]{2,1,0:T(8,128)(2,1)S(1)} %all-to-all-done), channel_id=1, source_target_pairs={{0,1},{1,2},{2,3},{3,0},{4,5},{5,6},{6,7},{7,4},{8,9},{9,10},{10,1... | collective-permute-start | bytes 393224 | tf_op jit(solution)/shard_map/ppermute | solution.py:210
  30.0 7.6 %collective-permute-start.2 = (bf16[8,64,128]{2,1,0:T(8,128)(2,1)S(1)}, bf16[8,64,128]{2,1,0:T(8,128)(2,1)S(1)}, u32[]{:S(2)}, u32[]{:S(2)}) collective-permute-start(bf16[8,64,128]{2,1,0:T(8,128)(2,1)S(1)} %all-to-all-done), channel_id=1, source_target_pairs={{0,2},{1,3},{2,0},{3,1},{4,6},{5,7},{6,4},{7,5},{8,10},{9,11},{10,... | collective-permute-start | bytes 393224 | tf_op jit(solution)/shard_map/ppermute | solution.py:210
  32.7 5.0 %collective-permute-start.3 = (bf16[8,64,128]{2,1,0:T(8,128)(2,1)S(1)}, bf16[8,64,128]{2,1,0:T(8,128)(2,1)S(1)}, u32[]{:S(2)}, u32[]{:S(2)}) collective-permute-start(bf16[8,64,128]{2,1,0:T(8,128)(2,1)S(1)} %all-to-all-done), channel_id=1, source_target_pairs={{0,3},{1,0},{2,1},{3,2},{4,7},{5,4},{6,5},{7,6},{8,11},{9,8},{10,9... | collective-permute-start | bytes 393224 | tf_op jit(solution)/shard_map/ppermute | solution.py:210
  44.0 10.7 %collective-permute-start.4 = (bf16[8,2,128,128]{3,2,1,0:T(8,128)(2,1)S(1)}, bf16[8,2,128,128]{3,2,1,0:T(8,128)(2,1)S(1)}, u32[]{:S(2)}, u32[]{:S(2)}) collective-permute-start(bf16[8,2,128,128]{3,2,1,0:T(8,128)(2,1)S(1)} %all-to-all-done.1.own0), channel_id=1, source_target_pairs={{0,1},{1,2},{2,3},{3,0},{4,5},{5,6},{6,7},{7,4},{8,9},{9,10},{10,1... | collective-permute-start | bytes 1572872 | tf_op jit(solution)/shard_map/ppermute | solution.py:210
  45.5 9.2 %collective-permute-start.5 = (bf16[8,2,128,128]{3,2,1,0:T(8,128)(2,1)S(1)}, bf16[8,2,128,128]{3,2,1,0:T(8,128)(2,1)S(1)}, u32[]{:S(2)}, u32[]{:S(2)}) collective-permute-start(bf16[8,2,128,128]{3,2,1,0:T(8,128)(2,1)S(1)} %all-to-all-done.1.own0), channel_id=1, source_target_pairs={{0,3},{1,0},{2,1},{3,2},{4,7},{5,4},{6,5},{7,6},{8,11},{9,8},{10,9... | collective-permute-start | bytes 1572872 | tf_op jit(solution)/shard_map/ppermute | solution.py:210
  47.3 10.4 %collective-permute-start.6 = (bf16[8,4,64,128]{3,2,1,0:T(8,128)(2,1)S(1)}, bf16[8,4,64,128]{3,2,1,0:T(8,128)(2,1)S(1)}, u32[]{:S(2)}, u32[]{:S(2)}) collective-permute-start(bf16[8,4,64,128]{3,2,1,0:T(8,128)(2,1)S(1)} %pad_maximum_fusion.1.c0), channel_id=1, source_target_pairs={{0,64},{64,128},{128,192},{192,0},{1,65},{65,129},{129,193},{193,1... | collective-permute-start | bytes 1572872 | tf_op jit(solution)/shard_map/ppermute | solution.py:210
  48.8 9.2 %collective-permute-start.7 = (bf16[8,4,64,128]{3,2,1,0:T(8,128)(2,1)S(1)}, bf16[8,4,64,128]{3,2,1,0:T(8,128)(2,1)S(1)}, u32[]{:S(2)}, u32[]{:S(2)}) collective-permute-start(bf16[8,4,64,128]{3,2,1,0:T(8,128)(2,1)S(1)} %pad_maximum_fusion.1.c0), channel_id=1, source_target_pairs={{0,192},{64,0},{128,64},{192,128},{1,193},{65,1},{129,65},{193,129... | collective-permute-start | bytes 1572872 | tf_op jit(solution)/shard_map/ppermute | solution.py:210
  50.5 7.5 %collective-permute-start.8 = (bf16[8,2,128,128]{3,2,1,0:T(8,128)(2,1)S(1)}, bf16[8,2,128,128]{3,2,1,0:T(8,128)(2,1)S(1)}, u32[]{:S(2)}, u32[]{:S(2)}) collective-permute-start(bf16[8,2,128,128]{3,2,1,0:T(8,128)(2,1)S(1)} %all-to-all-done.1.own0), channel_id=1, source_target_pairs={{0,32},{32,0},{1,33},{33,1},{2,34},{34,2},{3,35},{35,3},{4,36},{36... | collective-permute-start | bytes 1572872 | tf_op jit(solution)/shard_map/ppermute | solution.py:214
  58.0 0.8 copy-start
  59.9 14.4 %collective-permute-start.11 = (bf16[2,8,2,128,128]{4,3,2,1,0:T(8,128)(2,1)}, bf16[2,8,2,128,128]{4,3,2,1,0:T(8,128)(2,1)}, u32[]{:S(2)}, u32[]{:S(2)}) collective-permute-start(bf16[2,8,2,128,128]{4,3,2,1,0:T(8,128)(2,1)} %pad_maximum_fusion), channel_id=1, source_target_pairs={{0,32},{32,0},{1,33},{33,1},{2,34},{34,2},{3,35},{35,3},{4,36},{36... | collective-permute-start | bytes 3145736 | tf_op jit(solution)/shard_map/ppermute | solution.py:214
  59.9 14.4 %copy-start.1 = (bf16[8,2,128,128]{3,2,1,0:T(8,128)(2,1)S(1)}, bf16[8,2,128,128]{3,2,1,0:T(8,128)(2,1)}, u32[]{:S(2)}) copy-start(bf16[8,2,128,128]{3,2,1,0:T(8,128)(2,1)} %copy-done) | copy-start | bytes 1572868
  59.9 14.4 %copy-start.5 = (s32[32,4]{0,1:T(4,128)S(1)}, s32[32,4]{0,1:T(4,128)}, u32[]{:S(2)}) copy-start(s32[32,4]{0,1:T(4,128)} %param.8) | copy-start | bytes 1540
  59.9 14.4 %copy-start.6 = (s32[32,4]{0,1:T(4,128)S(1)}, s32[32,4]{0,1:T(4,128)}, u32[]{:S(2)}) copy-start(s32[32,4]{0,1:T(4,128)} %param.7) | copy-start | bytes 1540
  60.0 9.2 %collective-permute-start.10 = (bf16[4,4,64,128]{3,2,1,0:T(8,128)(2,1)S(1)}, bf16[4,4,64,128]{3,2,1,0:T(8,128)(2,1)S(1)}, u32[]{:S(2)}, u32[]{:S(2)}) collective-permute-start(bf16[4,4,64,128]{3,2,1,0:T(8,128)(2,1)S(1)} %slice.13), channel_id=1, source_target_pairs={{0,192},{64,0},{128,64},{192,128},{1,193},{65,1},{129,65},{193,129... | collective-permute-start | bytes 786440 | tf_op jit(solution)/shard_map/ppermute | solution.py:210
  63.0 9.7 %collective-permute-start.9 = (bf16[4,4,64,128]{3,2,1,0:T(8,128)(2,1)S(1)}, bf16[4,4,64,128]{3,2,1,0:T(8,128)(2,1)S(1)}, u32[]{:S(2)}, u32[]{:S(2)}) collective-permute-start(bf16[4,4,64,128]{3,2,1,0:T(8,128)(2,1)S(1)} %slice.12), channel_id=1, source_target_pairs={{0,64},{64,128},{128,192},{192,0},{1,65},{65,129},{129,193},{193,1... | collective-permute-start | bytes 786440 | tf_op jit(solution)/shard_map/ppermute | solution.py:210
  63.1 16.8 %collective-permute-start.12 = (bf16[4,2,128,128]{3,2,1,0:T(8,128)(2,1)S(1)}, bf16[4,2,128,128]{3,2,1,0:T(8,128)(2,1)S(1)}, u32[]{:S(2)}, u32[]{:S(2)}) collective-permute-start(bf16[4,2,128,128]{3,2,1,0:T(8,128)(2,1)S(1)} %slice.14), channel_id=1, source_target_pairs={{0,1},{1,2},{2,3},{3,0},{4,5},{5,6},{6,7},{7,4},{8,9},{9,10},{10,1... | collective-permute-start | bytes 786440 | tf_op jit(solution)/shard_map/ppermute | solution.py:210
  63.5 16.5 %collective-permute-start.13 = (bf16[4,2,128,128]{3,2,1,0:T(8,128)(2,1)S(1)}, bf16[4,2,128,128]{3,2,1,0:T(8,128)(2,1)S(1)}, u32[]{:S(2)}, u32[]{:S(2)}) collective-permute-start(bf16[4,2,128,128]{3,2,1,0:T(8,128)(2,1)S(1)} %slice.15), channel_id=1, source_target_pairs={{0,3},{1,0},{2,1},{3,2},{4,7},{5,4},{6,5},{7,6},{8,11},{9,8},{10,9... | collective-permute-start | bytes 786440 | tf_op jit(solution)/shard_map/ppermute | solution.py:210
  80.0 1.6 %collective-permute-start.14 = (bf16[4,2,128,128]{3,2,1,0:T(8,128)(2,1)S(1)}, bf16[4,2,128,128]{3,2,1,0:T(8,128)(2,1)S(1)}, u32[]{:S(2)}, u32[]{:S(2)}) collective-permute-start(bf16[4,2,128,128]{3,2,1,0:T(8,128)(2,1)S(1)} %collective-permute-done.12.own_r2), channel_id=1, source_target_pairs={{0,32},{32,0},{1,33},{33,1},{2,34},{34,2},{3,35},{35,3},{4,36},{36... | collective-permute-start | bytes 786440 | tf_op jit(solution)/shard_map/ppermute | solution.py:214
  80.1 1.9 %collective-permute-start.15 = (bf16[4,2,128,128]{3,2,1,0:T(8,128)(2,1)S(1)}, bf16[4,2,128,128]{3,2,1,0:T(8,128)(2,1)S(1)}, u32[]{:S(2)}, u32[]{:S(2)}) collective-permute-start(bf16[4,2,128,128]{3,2,1,0:T(8,128)(2,1)S(1)} %collective-permute-done.13.own_l2), channel_id=1, source_target_pairs={{0,32},{32,0},{1,33},{33,1},{2,34},{34,2},{3,35},{35,3},{4,36},{36... | collective-permute-start | bytes 786440 | tf_op jit(solution)/shard_map/ppermute | solution.py:214
  86.4 2.7 %collective-permute-start.16 = (f32[4,8,4,16,128]{4,3,2,1,0:T(8,128)S(1)}, f32[4,8,4,16,128]{4,3,2,1,0:T(8,128)S(1)}, u32[]{:S(2)}, u32[]{:S(2)}) collective-permute-start(f32[4,8,4,16,128]{4,3,2,1,0:T(8,128)S(1)} %get-tuple-element.40), channel_id=1, source_target_pairs={{0,32},{32,0},{1,33},{33,1},{2,34},{34,2},{3,35},{35,3},{4,36},{36... | collective-permute-start | bytes 3145736 | tf_op jit(solution)/shard_map/ppermute | solution.py:214
  90.1 25.6 %all-to-all-start.2 = ((bf16[32,4,16,128]{3,2,1,0:T(8,128)(2,1)}), bf16[32,4,16,128]{3,2,1,0:T(8,128)(2,1)S(1)}, u32[]{:S(2)}, u32[]{:S(2)}) async-start(bf16[32,4,16,128]{3,2,1,0:T(8,128)(2,1)} %bitcast.17), calls=%async_computation.2 | async-start | bytes 1048576 | tf_op jit(solution)/shard_map/all_to_all | solution.py:250

commit v8 on v6

--- a/solution.py
+++ b/solution.py
@@ -22,40 +22,44 @@
 ANY = pl.BlockSpec(memory_space=pl.ANY)
 
 
-def slice_kernel(pos, occ_live, orb, coeffs, cols, sem):
-    slab, core, tile = pos[0], pos[1], pos[2] * NX + pos[3]
-    load = pltpu.make_async_copy(orb, cols, sem)
-    load.start()
-    load.wait()
+def position():
+    return tuple(lax.axis_index(name).astype(jnp.int32) for name in ("y", "c", "z", "x"))
+
+
+def slice_kernel(occ_live, orb, coeffs, cols, sem):
+    slab, core, z, x = position()
+    tile = z * NX + x
+    chosen = jnp.int32(0)
     count = jnp.int32(0)
     for occ in range(OCC):
         live = occ_live[occ, tile] != 0
-
-        @pl.when(live & (count == slab))
-        def _():
-            flipped = cols[:, occ * TS:(occ + 1) * TS].astype(F32).T.astype(BF)
-            mine = jnp.where(core == 0, flipped[:HALF], flipped[HALF:])
-            for target in range(NZ):
-                coeffs[target] = mine
-
+        chosen = jnp.where(live & (count == slab), occ, chosen)
         count = count + jnp.where(live, 1, 0)
-
-
-def slice_coeffs(pos, occ_live, orb):
+    span = pl.ds(pl.multiple_of(chosen * TS, TS), TS)
+    load = pltpu.make_async_copy(orb.at[:, span], cols, sem)
+    load.start()
+    load.wait()
+    flipped = cols[...].astype(F32).T.astype(BF)
+    mine = jnp.where(core == 0, flipped[:HALF], flipped[HALF:])
+    for target in range(NZ):
+        coeffs[target] = mine
+
+
+def slice_coeffs(occ_live, orb):
     return pl.pallas_call(
         slice_kernel,
         out_shape=jax.ShapeDtypeStruct((NZ, HALF, TS), BF),
-        in_specs=[SMEM, SMEM, ANY],
+        in_specs=[SMEM, ANY],
         out_specs=VMEM,
-        scratch_shapes=[pltpu.VMEM(orb.shape, BF), pltpu.SemaphoreType.DMA],
+        scratch_shapes=[pltpu.VMEM((TS, TS), BF), pltpu.SemaphoreType.DMA],
         compiler_params=pltpu.CompilerParams(vmem_limit_bytes=60 * 2**20),
         cost_estimate=pl.CostEstimate(flops=0, bytes_accessed=2 * orb.size, transcendentals=0),
         name="slice_coeffs",
-    )(pos, occ_live, orb)
-
-
-def split_kernel(pos, eri, keep, give):
-    core = pos[1]
+    )(occ_live, orb)
+
+
+def split_kernel(eri, keep, give):
+    core = position()[1]
     row = lax.broadcasted_iota(jnp.int32, (TS, TS), 0)
     col = lax.broadcasted_iota(jnp.int32, (TS, TS), 1)
     block_nu = TS // AUXROWS
@@ -69,21 +73,21 @@
                     out[aux, j, pl.ds(quarter * block_nu, block_nu), :] = mixed[aux * block_nu:(aux + 1) * block_nu]
 
 
-def split_aux(pos, eri):
+def split_aux(eri):
     piece = jax.ShapeDtypeStruct((AUXROWS, 2, TS, TS), BF)
     return pl.pallas_call(
         split_kernel,
         out_shape=(piece, piece),
-        in_specs=[SMEM, VMEM],
+        in_specs=[VMEM],
         out_specs=(VMEM, VMEM),
         compiler_params=pltpu.CompilerParams(vmem_limit_bytes=8 * 2**20),
         cost_estimate=pl.CostEstimate(flops=2 * TS * eri.size, bytes_accessed=4 * eri.size, transcendentals=0),
         name="split_aux",
-    )(pos, eri)
-
-
-def rebuild_kernel(pos, occ_index, c0, c_u, c_d, c_u2, c_d2, dense):
-    slab, x = pos[0], pos[3]
+    )(eri)
+
+
+def rebuild_kernel(occ_index, c0, c_u, c_d, c_u2, c_d2, dense):
+    slab, _, _, x = position()
 
     def clear(tile, carry):
         dense[tile] = jnp.zeros(dense.shape[1:], BF)
@@ -108,22 +112,22 @@
     place(c_d2, (slab + 2) % NY, 4, 4)
 
 
-def rebuild(pos, occ_index, *pieces):
+def rebuild(occ_index, *pieces):
     return pl.pallas_call(
         rebuild_kernel,
         out_shape=jax.ShapeDtypeStruct((TILES, OCC * HALF, TS), BF),
-        in_specs=[SMEM] * 2 + [VMEM] * len(pieces),
+        in_specs=[SMEM] + [VMEM] * len(pieces),
         out_specs=VMEM,
         compiler_params=pltpu.CompilerParams(vmem_limit_bytes=16 * 2**20),
         cost_estimate=pl.CostEstimate(flops=0, bytes_accessed=6 * 2**20, transcendentals=0),
         name="rebuild",
-    )(pos, occ_index, *pieces)
-
-
-def main_kernel(pos, pair_tiles, pair_live, dense,
+    )(occ_index, *pieces)
+
+
+def main_kernel(pair_tiles, pair_live, dense,
                 own0, own_r, own_l, own_r2, own_l2, oth0, oth_r, oth_l, oth_r2, oth_l2,
                 keep, send, field, block):
-    core, x = pos[1], pos[3]
+    _, core, _, x = position()
 
     def transform(xp, own, oth, lo, count):
         def body(step, carry):
@@ -141,7 +145,7 @@
             field[tile] = half.astype(BF)
             return carry
 
-        lax.fori_loop(0, count, body, 0, unroll=4)
+        lax.fori_loop(0, count, body, 0, unroll=True)
 
     transform(x, own0, oth0, 0, 8)
     transform((x + 3) % NX, own_r, oth_r, 0, 8)
@@ -166,12 +170,12 @@
     lax.fori_loop(0, NZ, gram, 0)
 
 
-def exchange(pos, pair_tiles, pair_live, *pieces):
+def exchange(pair_tiles, pair_live, *pieces):
     shape = jax.ShapeDtypeStruct((NY, NZ, SLOTS, ROWS, TS), F32)
     return pl.pallas_call(
         main_kernel,
         out_shape=(shape, shape),
-        in_specs=[SMEM] * 3 + [VMEM] * len(pieces),
+        in_specs=[SMEM] * 2 + [VMEM] * len(pieces),
         out_specs=(VMEM, VMEM),
         scratch_shapes=[
             pltpu.VMEM((TILES, OCC * HALF, TS), BF),
@@ -180,7 +184,7 @@
         compiler_params=pltpu.CompilerParams(vmem_limit_bytes=24 * 2**20),
         cost_estimate=pl.CostEstimate(flops=2700000000, bytes_accessed=10 * 2**20, transcendentals=0),
         name="exchange",
-    )(pos, pair_tiles, pair_live, *pieces)
+    )(pair_tiles, pair_live, *pieces)
 
 
 def shift(value, axis, size, by):
@@ -192,23 +196,23 @@
 
 
 def shards(integrals, orbitals, pair_tiles, pair_live, occ_live):
-    pos = jnp.stack([lax.axis_index(name).astype(jnp.int32) for name in ("y", "c", "z", "x")])
-    tile = pos[2] * NX + pos[3]
-    coeffs = slice_coeffs(pos, occ_live.T, orbitals)
-    coeffs, eri = lax.optimization_barrier((coeffs, integrals.reshape(SLOTS * TS * AUXROWS, TS)))
+    _, core, z, x = position()
+    tile = z * NX + x
+    coeffs = slice_coeffs(occ_live.T, orbitals)
+    eri = integrals.reshape(SLOTS * TS * AUXROWS, TS)
     column = lax.all_to_all(coeffs, "z", split_axis=0, concat_axis=0, tiled=True)
-    keep_eri, give_eri = split_aux(pos, eri)
+    keep_eri, give_eri = split_aux(eri)
     rank = jnp.cumsum(occ_live, axis=1) - 1
     hits = (occ_live[None] != 0) & (rank[None] == jnp.arange(LIVE)[:, None, None])
     occ_index = jnp.sum(jnp.where(hits, jnp.arange(OCC)[None, None, :], 0), axis=2).astype(jnp.int32)
 
     got_eri = swap(give_eri)
+    by_aux = lax.dynamic_slice_in_dim(
+        jnp.concatenate([keep_eri, got_eri, keep_eri]), core * AUXROWS, NZ, 0
+    )
+    by_aux, column = lax.optimization_barrier((by_aux, column))
+    own0 = lax.all_to_all(by_aux, "z", split_axis=0, concat_axis=0, tiled=True)
     c0 = jnp.stack([column] + [shift(column, "x", NX, by) for by in (1, 2, 3)], axis=1)
-    got_eri, c0 = lax.optimization_barrier((got_eri, c0))
-    by_aux = lax.dynamic_slice_in_dim(
-        jnp.concatenate([keep_eri, got_eri, keep_eri]), pos[1] * AUXROWS, NZ, 0
-    )
-    own0 = lax.all_to_all(by_aux, "z", split_axis=0, concat_axis=0, tiled=True)
     own_r, own_l = shift(own0, "x", NX, 1), shift(own0, "x", NX, -1)
     c_u, c_d = shift(c0, "y", NY, 1), shift(c0, "y", NY, -1)
     oth0 = swap(own0)
@@ -217,9 +221,9 @@
     oth_r, oth_l = swap(own_r), swap(own_l)
     oth_r2, oth_l2 = swap(own_r2), swap(own_l2)
 
-    dense = rebuild(pos, occ_index, c0, c_u, c_d, c_u2, c_d2)
+    dense = rebuild(occ_index, c0, c_u, c_d, c_u2, c_d2)
     keep, send = exchange(
-        pos, pair_tiles.T, pair_live.T, dense,
+        pair_tiles.T, pair_live.T, dense,
         own0, own_r, own_l, own_r2, own_l2, oth0, oth_r, oth_l, oth_r2, oth_l2,
     )
     partial = (keep + swap(send)).astype(BF).reshape(NY * NZ, SLOTS, ROWS, TS)

time: 113 us -> 105 us (0.929)
  waiting for transfers between devices: 47.1 us -> 42.7 us
  Pallas kernels: 13.8 us -> 12 us
    all_to_all x1, waiting for transfers between devices: 10.8 us -> 1.48 us  [shards(): own0 = lax.all_to_all(by_aux, 'z', split_axis=0, concat_axis=0, tiled=True)]
    ppermute x11, waiting for transfers between devices: 11.1 us -> 13.7 us  [shift(): lax.ppermute(value, axis, [(i, (i + by) % size) for i in range(size)])]
    all_to_all x1, waiting for transfers between devices: 4.8 us -> 7.12 us  [shards(): lax.all_to_all(coeffs, 'z', split_axis=0, concat_axis=0, tiled=True)]
    pallas_call x2, Pallas kernels: 9.6 us -> 8.1 us  [the longest x1 7.8 us: exchange(): pl.pallas_call(main_kernel, out_shape=(shape, shape), in_specs=[SMEM] * 2...]
    unnamed x16 -> x12, local copies, waits for them, and re-layouts: 2.53 us -> 1.85 us
  transfers between devices with their start and end apart: 21 -> 21, of which waited for: 10 -> 10; matrix products, arithmetic and copies ran while one was open for 3% -> 4% of each run, Pallas kernels for 2% -> 4%
where the time goes in v8:
time: 105 us; the launch traced here: 103 us
  waiting for transfers between devices  42.7 us (41%)
  starting transfers between devices  40.5 us (39%)
  Pallas kernels  12 us (11%)
  local copies, waits for them, and re-layouts  4.75 us (5%)
  other arithmetic  3.08 us (3%)
    ppermute x11, starting transfers between devices, shift(): lax.ppermute(value, axis, [(i, (i + by) % size) for i in range(size)])  18.1 us
    all_to_all x1, waiting for transfers between devices, shards(): lax.all_to_all(partial, ('y', 'z'), split_axis=0, concat_axis=0, tiled=True)  18 us
    ppermute x11, waiting for transfers between devices, shift(): lax.ppermute(value, axis, [(i, (i + by) % size) for i in range(size)])  13.7 us
    all_to_all x1, starting transfers between devices, shards(): lax.all_to_all(coeffs, 'z', split_axis=0, concat_axis=0, tiled=True)  8.58 us
    pallas_call x1, Pallas kernels, exchange(): pl.pallas_call(main_kernel, out_shape=(shape, shape), in_specs=[SMEM] * 2...  7.8 us
    all_to_all x1, starting transfers between devices, shards(): lax.all_to_all(partial, ('y', 'z'), split_axis=0, concat_axis=0, tiled=True)  7.54 us
    all_to_all x1, waiting for transfers between devices, shards(): lax.all_to_all(coeffs, 'z', split_axis=0, concat_axis=0, tiled=True)  7.12 us
    all_to_all x1, starting transfers between devices, shards(): own0 = lax.all_to_all(by_aux, 'z', split_axis=0, concat_axis=0, tiled=True)  4.95 us
  transfers between devices with their start and end apart: 21, of which 10 were waited for; matrix products, arithmetic and copies ran while one was open for 4% of the time, Pallas kernels for 4%

profile of v8, /device:TPU:32, one launch (start us, length us, event | category | flops | bytes accessed | tf_op | source)
XLA Modules:
  0.0 103.2 jit_solution(2631964583844525237)
XLA Ops:
  0.0 1.0 %copy-done = bf16[1,4,128,4,128]{4,3,2,1,0:T(4,128)(2,1)S(1)} copy-done((bf16[1,4,128,4,128]{4,3,2,1,0:T(4,128)(2,1)S(1)}, bf16[1,4,128,4,128]{4,3,2,1,0:T(4,128)(2,1)}, u32[]{:S(2)}) %copy-start) | copy-done | bytes 524312
  1.0 0.3 split_aux.1
  1.4 0.1 collective-permute-start
  1.5 2.3 %slice_coeffs.1 = bf16[8,64,128]{2,1,0:T(8,128)(2,1)} custom-call(s32[8,32]{1,0:T(8,128)} %bitcast.24, bf16[128,1024]{1,0:T(8,128)(2,1)} %orb.1), custom_call_target="tpu_custom_call" | custom-call | bytes 262144 | tf_op jit(solution)/shard_map/slice_coeffs/pallas_call | solution.py:49
  3.7 8.6 %all-to-all-start = ((bf16[8,64,128]{2,1,0:T(8,128)(2,1)}), bf16[8,64,128]{2,1,0:T(8,128)(2,1)S(1)}, u32[]{:S(2)}, u32[]{:S(2)}) async-start(bf16[8,64,128]{2,1,0:T(8,128)(2,1)} %slice_coeffs.1), calls=%async_computation | async-start | bytes 262144 | tf_op jit(solution)/shard_map/all_to_all | solution.py:203
  12.3 0.0 collective-permute-done
  12.3 1.1 %fusion.1 = bf16[8,2,128,128]{3,2,1,0:T(8,128)(2,1)} fusion(s32[]{:T(128)S(6)} %select_n.12, bf16[4,2,128,128]{3,2,1,0:T(8,128)(2,1)S(1)} %get-tuple-element.11, bf16[4,2,128,128]{3,2,1,0:T(8,128)(2,1)S(1)} %collective-permute-done), kind=kLoop, calls=%fused_computation.6 | loop fusion | flops 524288 | bytes 1048580 | tf_op jit(solution)/shard_map/concatenate | solution.py:211
  13.4 7.1 %all-to-all-done = bf16[8,64,128]{2,1,0:T(8,128)(2,1)S(1)} async-done(((bf16[8,64,128]{2,1,0:T(8,128)(2,1)}), bf16[8,64,128]{2,1,0:T(8,128)(2,1)S(1)}, u32[]{:S(2)}, u32[]{:S(2)}) %all-to-all-start) | async-done | bytes 131104 | tf_op jit(solution)/shard_map/all_to_all | solution.py:203
  20.5 5.0 %all-to-all-start.1 = ((bf16[8,2,128,128]{3,2,1,0:T(8,128)(2,1)}), bf16[8,2,128,128]{3,2,1,0:T(8,128)(2,1)S(1)}, u32[]{:S(2)}, u32[]{:S(2)}) async-start(bf16[8,2,128,128]{3,2,1,0:T(8,128)(2,1)} %fusion.1), calls=%async_computation.1 | async-start | bytes 1048576 | tf_op jit(solution)/shard_map/all_to_all | solution.py:214
  25.5 2.8 %collective-permute-start.3 = (bf16[8,64,128]{2,1,0:T(8,128)(2,1)S(1)}, bf16[8,64,128]{2,1,0:T(8,128)(2,1)S(1)}, u32[]{:S(2)}, u32[]{:S(2)}) collective-permute-start(bf16[8,64,128]{2,1,0:T(8,128)(2,1)S(1)} %all-to-all-done), channel_id=1, source_target_pairs={{0,3},{1,0},{2,1},{3,2},{4,7},{5,4},{6,5},{7,6},{8,11},{9,8},{10,9... | collective-permute-start | bytes 393224 | tf_op jit(solution)/shard_map/ppermute | solution.py:191
  28.2 2.3 %collective-permute-start.2 = (bf16[8,64,128]{2,1,0:T(8,128)(2,1)S(1)}, bf16[8,64,128]{2,1,0:T(8,128)(2,1)S(1)}, u32[]{:S(2)}, u32[]{:S(2)}) collective-permute-start(bf16[8,64,128]{2,1,0:T(8,128)(2,1)S(1)} %all-to-all-done), channel_id=1, source_target_pairs={{0,2},{1,3},{2,0},{3,1},{4,6},{5,7},{6,4},{7,5},{8,10},{9,11},{10,... | collective-permute-start | bytes 393224 | tf_op jit(solution)/shard_map/ppermute | solution.py:191
  30.5 1.6 %collective-permute-done.3 = bf16[8,64,128]{2,1,0:T(8,128)(2,1)S(1)} collective-permute-done((bf16[8,64,128]{2,1,0:T(8,128)(2,1)S(1)}, bf16[8,64,128]{2,1,0:T(8,128)(2,1)S(1)}, u32[]{:S(2)}, u32[]{:S(2)}) %collective-permute-start.3) | collective-permute-done | bytes 131104 | tf_op jit(solution)/shard_map/ppermute | solution.py:191
  32.1 3.9 %collective-permute-done.1 = bf16[8,64,128]{2,1,0:T(8,128)(2,1)S(1)} collective-permute-done((bf16[8,64,128]{2,1,0:T(8,128)(2,1)S(1)}, bf16[8,64,128]{2,1,0:T(8,128)(2,1)S(1)}, u32[]{:S(2)}, u32[]{:S(2)}) %collective-permute-start.1) | collective-permute-done | bytes 131104 | tf_op jit(solution)/shard_map/ppermute | solution.py:191
  36.1 0.1 pad_maximum_fusion.c0
  36.1 0.0 copy-start.3
  36.2 0.0 copy-start.4
  36.2 1.7 %collective-permute-start.4 = (bf16[8,4,64,128]{3,2,1,0:T(8,128)(2,1)S(1)}, bf16[8,4,64,128]{3,2,1,0:T(8,128)(2,1)S(1)}, u32[]{:S(2)}, u32[]{:S(2)}) collective-permute-start(bf16[8,4,64,128]{3,2,1,0:T(8,128)(2,1)S(1)} %pad_maximum_fusion.c0), channel_id=1, source_target_pairs={{0,64},{64,128},{128,192},{192,0},{1,65},{65,129},{129,193},{193,1... | collective-permute-start | bytes 1572872 | tf_op jit(solution)/shard_map/ppermute | solution.py:191
  37.8 1.7 %collective-permute-start.5 = (bf16[8,4,64,128]{3,2,1,0:T(8,128)(2,1)S(1)}, bf16[8,4,64,128]{3,2,1,0:T(8,128)(2,1)S(1)}, u32[]{:S(2)}, u32[]{:S(2)}) collective-permute-start(bf16[8,4,64,128]{3,2,1,0:T(8,128)(2,1)S(1)} %pad_maximum_fusion.c0), channel_id=1, source_target_pairs={{0,192},{64,0},{128,64},{192,128},{1,193},{65,1},{129,65},{193,129... | collective-permute-start | bytes 1572872 | tf_op jit(solution)/shard_map/ppermute | solution.py:191
  39.5 1.5 %all-to-all-done.1.own0 = bf16[8,2,128,128]{3,2,1,0:T(8,128)(2,1)S(1)} async-done(((bf16[8,2,128,128]{3,2,1,0:T(8,128)(2,1)}), bf16[8,2,128,128]{3,2,1,0:T(8,128)(2,1)S(1)}, u32[]{:S(2)}, u32[]{:S(2)}) %all-to-all-start.1) | async-done | bytes 524320 | tf_op jit(solution)/shard_map/all_to_all | solution.py:214
  41.0 1.5 %collective-permute-start.8 = (bf16[8,2,128,128]{3,2,1,0:T(8,128)(2,1)S(1)}, bf16[8,2,128,128]{3,2,1,0:T(8,128)(2,1)S(1)}, u32[]{:S(2)}, u32[]{:S(2)}) collective-permute-start(bf16[8,2,128,128]{3,2,1,0:T(8,128)(2,1)S(1)} %all-to-all-done.1.own0), channel_id=1, source_target_pairs={{0,1},{1,2},{2,3},{3,0},{4,5},{5,6},{6,7},{7,4},{8,9},{9,10},{10,1... | collective-permute-start | bytes 1572872 | tf_op jit(solution)/shard_map/ppermute | solution.py:191
  42.5 1.7 %collective-permute-start.9 = (bf16[8,2,128,128]{3,2,1,0:T(8,128)(2,1)S(1)}, bf16[8,2,128,128]{3,2,1,0:T(8,128)(2,1)S(1)}, u32[]{:S(2)}, u32[]{:S(2)}) collective-permute-start(bf16[8,2,128,128]{3,2,1,0:T(8,128)(2,1)S(1)} %all-to-all-done.1.own0), channel_id=1, source_target_pairs={{0,3},{1,0},{2,1},{3,2},{4,7},{5,4},{6,5},{7,6},{8,11},{9,8},{10,9... | collective-permute-start | bytes 1572872 | tf_op jit(solution)/shard_map/ppermute | solution.py:191
  44.2 4.7 %collective-permute-done.4.c_u = bf16[8,4,64,128]{3,2,1,0:T(8,128)(2,1)S(1)} collective-permute-done((bf16[8,4,64,128]{3,2,1,0:T(8,128)(2,1)S(1)}, bf16[8,4,64,128]{3,2,1,0:T(8,128)(2,1)S(1)}, u32[]{:S(2)}, u32[]{:S(2)}) %collective-permute-start.4) | collective-permute-done | bytes 524320 | tf_op jit(solution)/shard_map/ppermute | solution.py:191
  48.9 0.7 slice.16
  49.6 0.3 collective-permute-start.6
  49.9 0.7 slice.17
  50.6 2.9 %collective-permute-start.7 = (bf16[4,4,64,128]{3,2,1,0:T(8,128)(2,1)}, bf16[4,4,64,128]{3,2,1,0:T(8,128)(2,1)S(1)}, u32[]{:S(2)}, u32[]{:S(2)}) collective-permute-start(bf16[4,4,64,128]{3,2,1,0:T(8,128)(2,1)} %slice.17), channel_id=1, source_target_pairs={{0,192},{64,0},{128,64},{192,128},{1,193},{65,1},{129,65},{193,129... | collective-permute-start | bytes 786440 | tf_op jit(solution)/shard_map/ppermute | solution.py:191
  53.5 0.7 slice.18
  54.3 0.5 collective-permute-start.10
  54.8 0.8 copy-done.1
  55.6 0.7 slice.19
  56.3 2.7 %collective-permute-start.11 = (bf16[4,2,128,128]{3,2,1,0:T(8,128)(2,1)}, bf16[4,2,128,128]{3,2,1,0:T(8,128)(2,1)}, u32[]{:S(2)}, u32[]{:S(2)}) collective-permute-start(bf16[4,2,128,128]{3,2,1,0:T(8,128)(2,1)} %slice.19), channel_id=1, source_target_pairs={{0,3},{1,0},{2,1},{3,2},{4,7},{5,4},{6,5},{7,6},{8,11},{9,8},{10,9... | collective-permute-start | bytes 786440 | tf_op jit(solution)/shard_map/ppermute | solution.py:191
  59.1 0.1 collective-permute-start.12
  59.2 0.5 collective-permute-start.13
  59.7 0.1 collective-permute-start.14
  59.8 2.3 %collective-permute-done.10.own_r2 = bf16[4,2,128,128]{3,2,1,0:T(8,128)(2,1)S(1)} collective-permute-done((bf16[4,2,128,128]{3,2,1,0:T(8,128)(2,1)}, bf16[4,2,128,128]{3,2,1,0:T(8,128)(2,1)S(1)}, u32[]{:S(2)}, u32[]{:S(2)}) %collective-permute-start.10) | collective-permute-done | bytes 262176 | tf_op jit(solution)/shard_map/ppermute | solution.py:191
  62.1 0.0 collective-permute-start.15
  62.1 1.2 %collective-permute-done.11.own_l2 = bf16[4,2,128,128]{3,2,1,0:T(8,128)(2,1)} collective-permute-done((bf16[4,2,128,128]{3,2,1,0:T(8,128)(2,1)}, bf16[4,2,128,128]{3,2,1,0:T(8,128)(2,1)}, u32[]{:S(2)}, u32[]{:S(2)}) %collective-permute-start.11) | collective-permute-done | bytes 262176 | tf_op jit(solution)/shard_map/ppermute | solution.py:191
  63.3 1.6 %rebuild.1.dense = bf16[32,512,128]{2,1,0:T(8,128)(2,1)S(1)} custom-call(s32[4,32]{1,0:T(4,128)S(1)} %select_reduce_fusion.occ_index, bf16[8,4,64,128]{3,2,1,0:T(8,128)(2,1)S(1)} %pad_maximum_fusion.c0, bf16[8,4,64,128]{3,2,1,0:T(8,128)(2,1)S(1)} %collective-permute-done.4.c_u, bf16[8,4,64,128]{3,2,1,0:T(8,128)(2,1)S(1)} %collective-permute-done.5.c_d, ...), custom_call_target="tpu_custom_call" | custom-call | bytes 6291456 | tf_op jit(solution)/shard_map/rebuild/pallas_call | solution.py:116
  64.9 0.1 collective-permute-done.16.oth_l2
  65.0 7.8 %exchange.1 = (f32[4,8,4,16,128]{4,3,2,1,0:T(8,128)S(1)}, f32[4,8,4,16,128]{4,3,2,1,0:T(8,128)S(1)}) custom-call(s32[4,32]{1,0:T(4,128)S(1)} %bitcast.19, s32[4,32]{1,0:T(4,128)S(1)} %bitcast.18, bf16[32,512,128]{2,1,0:T(8,128)(2,1)S(1)} %rebuild.1.dense, bf16[8,2,128,128]{3,2,1,0:T(8,128)(2,1)S(1)} %all-to-all-done.1.own0, ...), custom_call_target="tpu_custom_call" | custom-call | flops 2700000000 | bytes 10485760 | tf_op jit(solution)/shard_map/exchange/pallas_call | solution.py:175
  72.8 0.6 collective-permute-start.17
  73.4 2.3 %collective-permute-done.17 = f32[4,8,4,16,128]{4,3,2,1,0:T(8,128)S(1)} collective-permute-done((f32[4,8,4,16,128]{4,3,2,1,0:T(8,128)S(1)}, f32[4,8,4,16,128]{4,3,2,1,0:T(8,128)S(1)}, u32[]{:S(2)}, u32[]{:S(2)}) %collective-permute-start.17) | collective-permute-done | bytes 1048608 | tf_op jit(solution)/shard_map/ppermute | solution.py:195
  75.7 1.0 add_convert_fusion
  76.7 7.5 %all-to-all-start.2 = ((bf16[32,4,16,128]{3,2,1,0:T(8,128)(2,1)}), bf16[32,4,16,128]{3,2,1,0:T(8,128)(2,1)S(1)}, u32[]{:S(2)}, u32[]{:S(2)}) async-start(bf16[32,4,16,128]{3,2,1,0:T(8,128)(2,1)} %bitcast.11), calls=%async_computation.2 | async-start | bytes 1048576 | tf_op jit(solution)/shard_map/all_to_all | solution.py:230
  84.2 0.2 multiply_reduce_fusion
  84.4 18.0 %all-to-all-done.2 = bf16[32,4,16,128]{3,2,1,0:T(8,128)(2,1)S(1)} async-done(((bf16[32,4,16,128]{3,2,1,0:T(8,128)(2,1)}), bf16[32,4,16,128]{3,2,1,0:T(8,128)(2,1)S(1)}, u32[]{:S(2)}, u32[]{:S(2)}) %all-to-all-start.2) | async-done | bytes 524320 | tf_op jit(solution)/shard_map/all_to_all | solution.py:230
  102.4 0.1 convert_reduce_fusion
  102.5 0.7 bitcast_multiply_fusion
  (24 shorter events, 0.1 us)
Async XLA Ops:
  0.0 1.0 %copy-start = (bf16[1,4,128,4,128]{4,3,2,1,0:T(4,128)(2,1)S(1)}, bf16[1,4,128,4,128]{4,3,2,1,0:T(4,128)(2,1)}, u32[]{:S(2)}) copy-start(bf16[1,4,128,4,128]{4,3,2,1,0:T(4,128)(2,1)} %param.5) | copy-start | bytes 1572868
  1.0 58.0 %copy-start.5 = (s32[32,8]{0,1:T(8,128)S(1)}, s32[32,8]{0,1:T(8,128)}, u32[]{:S(2)}) copy-start(s32[32,8]{0,1:T(8,128)} %param.9) | copy-start | bytes 3076
  1.4 11.0 %collective-permute-start = (bf16[4,2,128,128]{3,2,1,0:T(8,128)(2,1)S(1)}, bf16[4,2,128,128]{3,2,1,0:T(8,128)(2,1)S(1)}, u32[]{:S(2)}, u32[]{:S(2)}) collective-permute-start(bf16[4,2,128,128]{3,2,1,0:T(8,128)(2,1)S(1)} %get-tuple-element.12), channel_id=1, source_target_pairs={{0,32},{32,0},{1,33},{33,1},{2,34},{34,2},{3,35},{35,3},{4,36},{36... | collective-permute-start | bytes 786440 | tf_op jit(solution)/shard_map/ppermute | solution.py:195
  3.7 16.8 %all-to-all-start = ((bf16[8,64,128]{2,1,0:T(8,128)(2,1)}), bf16[8,64,128]{2,1,0:T(8,128)(2,1)S(1)}, u32[]{:S(2)}, u32[]{:S(2)}) async-start(bf16[8,64,128]{2,1,0:T(8,128)(2,1)} %slice_coeffs.1), calls=%async_computation | async-start | bytes 262144 | tf_op jit(solution)/shard_map/all_to_all | solution.py:203
  20.5 20.5 %all-to-all-start.1 = ((bf16[8,2,128,128]{3,2,1,0:T(8,128)(2,1)}), bf16[8,2,128,128]{3,2,1,0:T(8,128)(2,1)S(1)}, u32[]{:S(2)}, u32[]{:S(2)}) async-start(bf16[8,2,128,128]{3,2,1,0:T(8,128)(2,1)} %fusion.1), calls=%async_computation.1 | async-start | bytes 1048576 | tf_op jit(solution)/shard_map/all_to_all | solution.py:214
  25.5 6.7 %collective-permute-start.3 = (bf16[8,64,128]{2,1,0:T(8,128)(2,1)S(1)}, bf16[8,64,128]{2,1,0:T(8,128)(2,1)S(1)}, u32[]{:S(2)}, u32[]{:S(2)}) collective-permute-start(bf16[8,64,128]{2,1,0:T(8,128)(2,1)S(1)} %all-to-all-done), channel_id=1, source_target_pairs={{0,3},{1,0},{2,1},{3,2},{4,7},{5,4},{6,5},{7,6},{8,11},{9,8},{10,9... | collective-permute-start | bytes 393224 | tf_op jit(solution)/shard_map/ppermute | solution.py:191
  28.2 7.9 %collective-permute-start.1 = (bf16[8,64,128]{2,1,0:T(8,128)(2,1)S(1)}, bf16[8,64,128]{2,1,0:T(8,128)(2,1)S(1)}, u32[]{:S(2)}, u32[]{:S(2)}) collective-permute-start(bf16[8,64,128]{2,1,0:T(8,128)(2,1)S(1)} %all-to-all-done), channel_id=1, source_target_pairs={{0,1},{1,2},{2,3},{3,0},{4,5},{5,6},{6,7},{7,4},{8,9},{9,10},{10,1... | collective-permute-start | bytes 393224 | tf_op jit(solution)/shard_map/ppermute | solution.py:191
  28.2 7.9 %collective-permute-start.2 = (bf16[8,64,128]{2,1,0:T(8,128)(2,1)S(1)}, bf16[8,64,128]{2,1,0:T(8,128)(2,1)S(1)}, u32[]{:S(2)}, u32[]{:S(2)}) collective-permute-start(bf16[8,64,128]{2,1,0:T(8,128)(2,1)S(1)} %all-to-all-done), channel_id=1, source_target_pairs={{0,2},{1,3},{2,0},{3,1},{4,6},{5,7},{6,4},{7,5},{8,10},{9,11},{10,... | collective-permute-start | bytes 393224 | tf_op jit(solution)/shard_map/ppermute | solution.py:191
  36.1 28.9 %copy-start.3 = (s32[32,4]{0,1:T(4,128)S(1)}, s32[32,4]{0,1:T(4,128)}, u32[]{:S(2)}) copy-start(s32[32,4]{0,1:T(4,128)} %param.8) | copy-start | bytes 1540
  36.2 28.8 %copy-start.4 = (s32[32,4]{0,1:T(4,128)S(1)}, s32[32,4]{0,1:T(4,128)}, u32[]{:S(2)}) copy-start(s32[32,4]{0,1:T(4,128)} %param.7) | copy-start | bytes 1540
  36.2 12.7 %collective-permute-start.4 = (bf16[8,4,64,128]{3,2,1,0:T(8,128)(2,1)S(1)}, bf16[8,4,64,128]{3,2,1,0:T(8,128)(2,1)S(1)}, u32[]{:S(2)}, u32[]{:S(2)}) collective-permute-start(bf16[8,4,64,128]{3,2,1,0:T(8,128)(2,1)S(1)} %pad_maximum_fusion.c0), channel_id=1, source_target_pairs={{0,64},{64,128},{128,192},{192,0},{1,65},{65,129},{129,193},{193,1... | collective-permute-start | bytes 1572872 | tf_op jit(solution)/shard_map/ppermute | solution.py:191
  37.8 12.1 %collective-permute-start.5 = (bf16[8,4,64,128]{3,2,1,0:T(8,128)(2,1)S(1)}, bf16[8,4,64,128]{3,2,1,0:T(8,128)(2,1)S(1)}, u32[]{:S(2)}, u32[]{:S(2)}) collective-permute-start(bf16[8,4,64,128]{3,2,1,0:T(8,128)(2,1)S(1)} %pad_maximum_fusion.c0), channel_id=1, source_target_pairs={{0,192},{64,0},{128,64},{192,128},{1,193},{65,1},{129,65},{193,129... | collective-permute-start | bytes 1572872 | tf_op jit(solution)/shard_map/ppermute | solution.py:191
  41.0 12.6 %collective-permute-start.8 = (bf16[8,2,128,128]{3,2,1,0:T(8,128)(2,1)S(1)}, bf16[8,2,128,128]{3,2,1,0:T(8,128)(2,1)S(1)}, u32[]{:S(2)}, u32[]{:S(2)}) collective-permute-start(bf16[8,2,128,128]{3,2,1,0:T(8,128)(2,1)S(1)} %all-to-all-done.1.own0), channel_id=1, source_target_pairs={{0,1},{1,2},{2,3},{3,0},{4,5},{5,6},{6,7},{7,4},{8,9},{9,10},{10,1... | collective-permute-start | bytes 1572872 | tf_op jit(solution)/shard_map/ppermute | solution.py:191
  42.5 12.4 %collective-permute-start.9 = (bf16[8,2,128,128]{3,2,1,0:T(8,128)(2,1)S(1)}, bf16[8,2,128,128]{3,2,1,0:T(8,128)(2,1)S(1)}, u32[]{:S(2)}, u32[]{:S(2)}) collective-permute-start(bf16[8,2,128,128]{3,2,1,0:T(8,128)(2,1)S(1)} %all-to-all-done.1.own0), channel_id=1, source_target_pairs={{0,3},{1,0},{2,1},{3,2},{4,7},{5,4},{6,5},{7,6},{8,11},{9,8},{10,9... | collective-permute-start | bytes 1572872 | tf_op jit(solution)/shard_map/ppermute | solution.py:191
  49.6 9.6 %collective-permute-start.6 = (bf16[4,4,64,128]{3,2,1,0:T(8,128)(2,1)}, bf16[4,4,64,128]{3,2,1,0:T(8,128)(2,1)S(1)}, u32[]{:S(2)}, u32[]{:S(2)}) collective-permute-start(bf16[4,4,64,128]{3,2,1,0:T(8,128)(2,1)} %slice.16), channel_id=1, source_target_pairs={{0,64},{64,128},{128,192},{192,0},{1,65},{65,129},{129,193},{193,1... | collective-permute-start | bytes 786440 | tf_op jit(solution)/shard_map/ppermute | solution.py:191
  50.6 9.1 %collective-permute-start.7 = (bf16[4,4,64,128]{3,2,1,0:T(8,128)(2,1)}, bf16[4,4,64,128]{3,2,1,0:T(8,128)(2,1)S(1)}, u32[]{:S(2)}, u32[]{:S(2)}) collective-permute-start(bf16[4,4,64,128]{3,2,1,0:T(8,128)(2,1)} %slice.17), channel_id=1, source_target_pairs={{0,192},{64,0},{128,64},{192,128},{1,193},{65,1},{129,65},{193,129... | collective-permute-start | bytes 786440 | tf_op jit(solution)/shard_map/ppermute | solution.py:191
  54.3 7.8 %collective-permute-start.10 = (bf16[4,2,128,128]{3,2,1,0:T(8,128)(2,1)}, bf16[4,2,128,128]{3,2,1,0:T(8,128)(2,1)S(1)}, u32[]{:S(2)}, u32[]{:S(2)}) collective-permute-start(bf16[4,2,128,128]{3,2,1,0:T(8,128)(2,1)} %slice.18), channel_id=1, source_target_pairs={{0,1},{1,2},{2,3},{3,0},{4,5},{5,6},{6,7},{7,4},{8,9},{9,10},{10,1... | collective-permute-start | bytes 786440 | tf_op jit(solution)/shard_map/ppermute | solution.py:191
  54.8 0.8 copy-start.1
  56.3 6.9 %collective-permute-start.11 = (bf16[4,2,128,128]{3,2,1,0:T(8,128)(2,1)}, bf16[4,2,128,128]{3,2,1,0:T(8,128)(2,1)}, u32[]{:S(2)}, u32[]{:S(2)}) collective-permute-start(bf16[4,2,128,128]{3,2,1,0:T(8,128)(2,1)} %slice.19), channel_id=1, source_target_pairs={{0,3},{1,0},{2,1},{3,2},{4,7},{5,4},{6,5},{7,6},{8,11},{9,8},{10,9... | collective-permute-start | bytes 786440 | tf_op jit(solution)/shard_map/ppermute | solution.py:191
  59.1 6.0 %copy-start.2 = (bf16[8,2,128,128]{3,2,1,0:T(8,128)(2,1)S(1)}, bf16[8,2,128,128]{3,2,1,0:T(8,128)(2,1)}, u32[]{:S(2)}) copy-start(bf16[8,2,128,128]{3,2,1,0:T(8,128)(2,1)} %copy-done.1) | copy-start | bytes 1572868
  59.1 5.8 %collective-permute-start.12 = (bf16[8,2,128,128]{3,2,1,0:T(8,128)(2,1)S(1)}, bf16[8,2,128,128]{3,2,1,0:T(8,128)(2,1)S(1)}, u32[]{:S(2)}, u32[]{:S(2)}) collective-permute-start(bf16[8,2,128,128]{3,2,1,0:T(8,128)(2,1)S(1)} %all-to-all-done.1.own0), channel_id=1, source_target_pairs={{0,32},{32,0},{1,33},{33,1},{2,34},{34,2},{3,35},{35,3},{4,36},{36... | collective-permute-start | bytes 1572872 | tf_op jit(solution)/shard_map/ppermute | solution.py:195
  59.2 5.8 %collective-permute-start.13 = (bf16[8,2,128,128]{3,2,1,0:T(8,128)(2,1)S(1)}, bf16[8,2,128,128]{3,2,1,0:T(8,128)(2,1)S(1)}, u32[]{:S(2)}, u32[]{:S(2)}) collective-permute-start(bf16[8,2,128,128]{3,2,1,0:T(8,128)(2,1)S(1)} %collective-permute-done.8.own_r), channel_id=1, source_target_pairs={{0,32},{32,0},{1,33},{33,1},{2,34},{34,2},{3,35},{35,3},{4,36},{36... | collective-permute-start | bytes 1572872 | tf_op jit(solution)/shard_map/ppermute | solution.py:195
  59.7 5.3 %collective-permute-start.14 = (bf16[8,2,128,128]{3,2,1,0:T(8,128)(2,1)}, bf16[8,2,128,128]{3,2,1,0:T(8,128)(2,1)S(1)}, u32[]{:S(2)}, u32[]{:S(2)}) collective-permute-start(bf16[8,2,128,128]{3,2,1,0:T(8,128)(2,1)} %copy-done.1), channel_id=1, source_target_pairs={{0,32},{32,0},{1,33},{33,1},{2,34},{34,2},{3,35},{35,3},{4,36},{36... | collective-permute-start | bytes 1572872 | tf_op jit(solution)/shard_map/ppermute | solution.py:195
  62.1 2.8 %collective-permute-start.15 = (bf16[4,2,128,128]{3,2,1,0:T(8,128)(2,1)S(1)}, bf16[4,2,128,128]{3,2,1,0:T(8,128)(2,1)S(1)}, u32[]{:S(2)}, u32[]{:S(2)}) collective-permute-start(bf16[4,2,128,128]{3,2,1,0:T(8,128)(2,1)S(1)} %collective-permute-done.10.own_r2), channel_id=1, source_target_pairs={{0,32},{32,0},{1,33},{33,1},{2,34},{34,2},{3,35},{35,3},{4,36},{36... | collective-permute-start | bytes 786440 | tf_op jit(solution)/shard_map/ppermute | solution.py:195
  63.2 1.7 %collective-permute-start.16 = (bf16[4,2,128,128]{3,2,1,0:T(8,128)(2,1)}, bf16[4,2,128,128]{3,2,1,0:T(8,128)(2,1)S(1)}, u32[]{:S(2)}, u32[]{:S(2)}) collective-permute-start(bf16[4,2,128,128]{3,2,1,0:T(8,128)(2,1)} %collective-permute-done.11.own_l2), channel_id=1, source_target_pairs={{0,32},{32,0},{1,33},{33,1},{2,34},{34,2},{3,35},{35,3},{4,36},{36... | collective-permute-start | bytes 786440 | tf_op jit(solution)/shard_map/ppermute | solution.py:195
  72.8 2.9 %collective-permute-start.17 = (f32[4,8,4,16,128]{4,3,2,1,0:T(8,128)S(1)}, f32[4,8,4,16,128]{4,3,2,1,0:T(8,128)S(1)}, u32[]{:S(2)}, u32[]{:S(2)}) collective-permute-start(f32[4,8,4,16,128]{4,3,2,1,0:T(8,128)S(1)} %get-tuple-element.16), channel_id=1, source_target_pairs={{0,32},{32,0},{1,33},{33,1},{2,34},{34,2},{3,35},{35,3},{4,36},{36... | collective-permute-start | bytes 3145736 | tf_op jit(solution)/shard_map/ppermute | solution.py:195
  76.7 25.7 %all-to-all-start.2 = ((bf16[32,4,16,128]{3,2,1,0:T(8,128)(2,1)}), bf16[32,4,16,128]{3,2,1,0:T(8,128)(2,1)S(1)}, u32[]{:S(2)}, u32[]{:S(2)}) async-start(bf16[32,4,16,128]{3,2,1,0:T(8,128)(2,1)} %bitcast.11), calls=%async_computation.2 | async-start | bytes 1048576 | tf_op jit(solution)/shard_map/all_to_all | solution.py:230

commit v9 on v8

--- a/solution.py
+++ b/solution.py
@@ -167,7 +167,7 @@
                 send[y, zp, slot] = block[pl.ds(far, ROWS), slot * TS:(slot + 1) * TS]
         return carry
 
-    lax.fori_loop(0, NZ, gram, 0)
+    lax.fori_loop(0, NZ, gram, 0, unroll=True)
 
 
 def exchange(pair_tiles, pair_live, *pieces):
@@ -199,7 +199,7 @@
     _, core, z, x = position()
     tile = z * NX + x
     coeffs = slice_coeffs(occ_live.T, orbitals)
-    eri = integrals.reshape(SLOTS * TS * AUXROWS, TS)
+    coeffs, eri = lax.optimization_barrier((coeffs, integrals.reshape(SLOTS * TS * AUXROWS, TS)))
     column = lax.all_to_all(coeffs, "z", split_axis=0, concat_axis=0, tiled=True)
     keep_eri, give_eri = split_aux(eri)
     rank = jnp.cumsum(occ_live, axis=1) - 1
@@ -210,7 +210,7 @@
     by_aux = lax.dynamic_slice_in_dim(
         jnp.concatenate([keep_eri, got_eri, keep_eri]), core * AUXROWS, NZ, 0
     )
-    by_aux, column = lax.optimization_barrier((by_aux, column))
+    by_aux, column, occ_index = lax.optimization_barrier((by_aux, column, occ_index))
     own0 = lax.all_to_all(by_aux, "z", split_axis=0, concat_axis=0, tiled=True)
     c0 = jnp.stack([column] + [shift(column, "x", NX, by) for by in (1, 2, 3)], axis=1)
     own_r, own_l = shift(own0, "x", NX, 1), shift(own0, "x", NX, -1)

time: 105 us -> 102 us (0.971); the launches traced: 103 us -> 101 us
  local copies, waits for them, and re-layouts: 4.75 us -> 1.12 us
  Pallas kernels: 12 us -> 10.5 us
  other arithmetic: 3.08 us -> 4.47 us
  waiting for transfers between devices: 42.7 us -> 43.8 us
    ppermute x11, waiting for transfers between devices: 13.7 us -> 16.3 us  [shift(): lax.ppermute(value, axis, [(i, (i + by) % size) for i in range(size)])]
    pallas_call x1, Pallas kernels: 7.8 us -> 6.29 us  [exchange(): pl.pallas_call(main_kernel, out_shape=(shape, shape), in_specs=[SMEM] * 2...]
    all_to_all x1, waiting for transfers between devices: 7.12 us -> 5.67 us  [shards(): lax.all_to_all(coeffs, 'z', split_axis=0, concat_axis=0, tiled=True)]
    slice x2, local copies, waits for them, and re-layouts: 1.44 us -> 0.04 us  [shards(): c_u2, c_d2 = (shift(c_u[:4], 'y', NY, 1), shift(c_d[4:], 'y', NY, -1))]
  transfers between devices with their start and end apart: 21 -> 21, of which waited for: 10 -> 9; matrix products, arithmetic and copies ran while one was open for 4% -> 3% of each run, Pallas kernels for 4% -> 2%
where the time goes in v9:
time: 102 us; the launch traced here: 101 us
  waiting for transfers between devices  43.8 us (43%)
  starting transfers between devices  41.3 us (40%)
  Pallas kernels  10.5 us (10%)
  other arithmetic  4.47 us (4%)
  local copies, waits for them, and re-layouts  1.12 us (1%)
    ppermute x11, starting transfers between devices, shift(): lax.ppermute(value, axis, [(i, (i + by) % size) for i in range(size)])  18.4 us
    all_to_all x1, waiting for transfers between devices, shards(): lax.all_to_all(partial, ('y', 'z'), split_axis=0, concat_axis=0, tiled=True)  17.7 us
    ppermute x11, waiting for transfers between devices, shift(): lax.ppermute(value, axis, [(i, (i + by) % size) for i in range(size)])  16.3 us
    all_to_all x1, starting transfers between devices, shards(): lax.all_to_all(coeffs, 'z', split_axis=0, concat_axis=0, tiled=True)  8.58 us
    all_to_all x1, starting transfers between devices, shards(): lax.all_to_all(partial, ('y', 'z'), split_axis=0, concat_axis=0, tiled=True)  8.2 us
    pallas_call x1, Pallas kernels, exchange(): pl.pallas_call(main_kernel, out_shape=(shape, shape), in_specs=[SMEM] * 2...  6.29 us
    all_to_all x1, waiting for transfers between devices, shards(): lax.all_to_all(coeffs, 'z', split_axis=0, concat_axis=0, tiled=True)  5.67 us
    all_to_all x1, starting transfers between devices, shards(): own0 = lax.all_to_all(by_aux, 'z', split_axis=0, concat_axis=0, tiled=True)  4.95 us
  transfers between devices with their start and end apart: 21, of which 9 were waited for; matrix products, arithmetic and copies ran while one was open for 3% of the time, Pallas kernels for 2%

profile of v9, /device:TPU:32, one launch (start us, length us, event | category | flops | bytes accessed | tf_op | source)
XLA Modules:
  0.0 101.4 jit_solution(15657155031958614607)
XLA Ops:
  0.0 2.3 %slice_coeffs.1 = bf16[8,64,128]{2,1,0:T(8,128)(2,1)} custom-call(s32[8,32]{1,0:T(8,128)} %bitcast.24, bf16[128,1024]{1,0:T(8,128)(2,1)} %orb.1), custom_call_target="tpu_custom_call" | custom-call | bytes 262144 | tf_op jit(solution)/shard_map/slice_coeffs/pallas_call | solution.py:49
  2.3 0.0 copy-start
  2.3 1.0 %copy-done = bf16[1,4,128,4,128]{4,3,2,1,0:T(4,128)(2,1)S(1)} copy-done((bf16[1,4,128,4,128]{4,3,2,1,0:T(4,128)(2,1)S(1)}, bf16[1,4,128,4,128]{4,3,2,1,0:T(4,128)(2,1)}, u32[]{:S(2)}) %copy-start) | copy-done | bytes 524312
  3.3 0.3 split_aux.1
  3.6 0.1 collective-permute-start
  3.7 8.6 %all-to-all-start = ((bf16[8,64,128]{2,1,0:T(8,128)(2,1)}), bf16[8,64,128]{2,1,0:T(8,128)(2,1)S(1)}, u32[]{:S(2)}, u32[]{:S(2)}) async-start(bf16[8,64,128]{2,1,0:T(8,128)(2,1)} %slice_coeffs.1), calls=%async_computation | async-start | bytes 262144 | tf_op jit(solution)/shard_map/all_to_all | solution.py:203
  12.3 0.7 reduce_window_sum.11
  13.0 0.7 broadcast_compare_fusion
  13.8 0.0 collective-permute-done
  13.8 1.1 %fusion.1 = bf16[8,2,128,128]{3,2,1,0:T(8,128)(2,1)} fusion(s32[]{:T(128)S(6)} %select_n.11, bf16[4,2,128,128]{3,2,1,0:T(8,128)(2,1)S(1)} %get-tuple-element.15, bf16[4,2,128,128]{3,2,1,0:T(8,128)(2,1)S(1)} %collective-permute-done), kind=kLoop, calls=%fused_computation.6 | loop fusion | flops 524288 | bytes 1048580 | tf_op jit(solution)/shard_map/concatenate | solution.py:211
  14.8 5.7 %all-to-all-done = bf16[8,64,128]{2,1,0:T(8,128)(2,1)S(1)} async-done(((bf16[8,64,128]{2,1,0:T(8,128)(2,1)}), bf16[8,64,128]{2,1,0:T(8,128)(2,1)S(1)}, u32[]{:S(2)}, u32[]{:S(2)}) %all-to-all-start) | async-done | bytes 131104 | tf_op jit(solution)/shard_map/all_to_all | solution.py:203
  20.5 4.9 %all-to-all-start.1 = ((bf16[8,2,128,128]{3,2,1,0:T(8,128)(2,1)}), bf16[8,2,128,128]{3,2,1,0:T(8,128)(2,1)S(1)}, u32[]{:S(2)}, u32[]{:S(2)}) async-start(bf16[8,2,128,128]{3,2,1,0:T(8,128)(2,1)} %fusion.1), calls=%async_computation.1 | async-start | bytes 1048576 | tf_op jit(solution)/shard_map/all_to_all | solution.py:214
  25.4 2.8 %collective-permute-start.3 = (bf16[8,64,128]{2,1,0:T(8,128)(2,1)S(1)}, bf16[8,64,128]{2,1,0:T(8,128)(2,1)S(1)}, u32[]{:S(2)}, u32[]{:S(2)}) collective-permute-start(bf16[8,64,128]{2,1,0:T(8,128)(2,1)S(1)} %all-to-all-done), channel_id=1, source_target_pairs={{0,3},{1,0},{2,1},{3,2},{4,7},{5,4},{6,5},{7,6},{8,11},{9,8},{10,9... | collective-permute-start | bytes 393224 | tf_op jit(solution)/shard_map/ppermute | solution.py:191
  28.2 2.3 %collective-permute-start.2 = (bf16[8,64,128]{2,1,0:T(8,128)(2,1)S(1)}, bf16[8,64,128]{2,1,0:T(8,128)(2,1)S(1)}, u32[]{:S(2)}, u32[]{:S(2)}) collective-permute-start(bf16[8,64,128]{2,1,0:T(8,128)(2,1)S(1)} %all-to-all-done), channel_id=1, source_target_pairs={{0,2},{1,3},{2,0},{3,1},{4,6},{5,7},{6,4},{7,5},{8,10},{9,11},{10,... | collective-permute-start | bytes 393224 | tf_op jit(solution)/shard_map/ppermute | solution.py:191
  30.5 1.6 %collective-permute-done.3 = bf16[8,64,128]{2,1,0:T(8,128)(2,1)S(1)} collective-permute-done((bf16[8,64,128]{2,1,0:T(8,128)(2,1)S(1)}, bf16[8,64,128]{2,1,0:T(8,128)(2,1)S(1)}, u32[]{:S(2)}, u32[]{:S(2)}) %collective-permute-start.3) | collective-permute-done | bytes 131104 | tf_op jit(solution)/shard_map/ppermute | solution.py:191
  32.1 3.9 %collective-permute-done.1 = bf16[8,64,128]{2,1,0:T(8,128)(2,1)S(1)} collective-permute-done((bf16[8,64,128]{2,1,0:T(8,128)(2,1)S(1)}, bf16[8,64,128]{2,1,0:T(8,128)(2,1)S(1)}, u32[]{:S(2)}, u32[]{:S(2)}) %collective-permute-start.1) | collective-permute-done | bytes 131104 | tf_op jit(solution)/shard_map/ppermute | solution.py:191
  36.0 0.0 collective-permute-done.2
  36.0 0.1 pad_maximum_fusion.c0
  36.1 0.0 copy-start.1
  36.1 0.0 copy-start.2
  36.1 1.7 %collective-permute-start.4 = (bf16[8,4,64,128]{3,2,1,0:T(8,128)(2,1)S(1)}, bf16[8,4,64,128]{3,2,1,0:T(8,128)(2,1)S(1)}, u32[]{:S(2)}, u32[]{:S(2)}) collective-permute-start(bf16[8,4,64,128]{3,2,1,0:T(8,128)(2,1)S(1)} %pad_maximum_fusion.c0), channel_id=1, source_target_pairs={{0,64},{64,128},{128,192},{192,0},{1,65},{65,129},{129,193},{193,1... | collective-permute-start | bytes 1572872 | tf_op jit(solution)/shard_map/ppermute | solution.py:191
  37.8 1.7 %collective-permute-start.5 = (bf16[8,4,64,128]{3,2,1,0:T(8,128)(2,1)S(1)}, bf16[8,4,64,128]{3,2,1,0:T(8,128)(2,1)S(1)}, u32[]{:S(2)}, u32[]{:S(2)}) collective-permute-start(bf16[8,4,64,128]{3,2,1,0:T(8,128)(2,1)S(1)} %pad_maximum_fusion.c0), channel_id=1, source_target_pairs={{0,192},{64,0},{128,64},{192,128},{1,193},{65,1},{129,65},{193,129... | collective-permute-start | bytes 1572872 | tf_op jit(solution)/shard_map/ppermute | solution.py:191
  39.5 1.5 %all-to-all-done.1.own0 = bf16[8,2,128,128]{3,2,1,0:T(8,128)(2,1)S(1)} async-done(((bf16[8,2,128,128]{3,2,1,0:T(8,128)(2,1)}), bf16[8,2,128,128]{3,2,1,0:T(8,128)(2,1)S(1)}, u32[]{:S(2)}, u32[]{:S(2)}) %all-to-all-start.1) | async-done | bytes 524320 | tf_op jit(solution)/shard_map/all_to_all | solution.py:214
  40.9 1.5 %collective-permute-start.8 = (bf16[8,2,128,128]{3,2,1,0:T(8,128)(2,1)S(1)}, bf16[8,2,128,128]{3,2,1,0:T(8,128)(2,1)S(1)}, u32[]{:S(2)}, u32[]{:S(2)}) collective-permute-start(bf16[8,2,128,128]{3,2,1,0:T(8,128)(2,1)S(1)} %all-to-all-done.1.own0), channel_id=1, source_target_pairs={{0,1},{1,2},{2,3},{3,0},{4,5},{5,6},{6,7},{7,4},{8,9},{9,10},{10,1... | collective-permute-start | bytes 1572872 | tf_op jit(solution)/shard_map/ppermute | solution.py:191
  42.4 1.7 %collective-permute-start.9 = (bf16[8,2,128,128]{3,2,1,0:T(8,128)(2,1)S(1)}, bf16[8,2,128,128]{3,2,1,0:T(8,128)(2,1)S(1)}, u32[]{:S(2)}, u32[]{:S(2)}) collective-permute-start(bf16[8,2,128,128]{3,2,1,0:T(8,128)(2,1)S(1)} %all-to-all-done.1.own0), channel_id=1, source_target_pairs={{0,3},{1,0},{2,1},{3,2},{4,7},{5,4},{6,5},{7,6},{8,11},{9,8},{10,9... | collective-permute-start | bytes 1572872 | tf_op jit(solution)/shard_map/ppermute | solution.py:191
  44.2 4.6 %collective-permute-done.4.c_u = bf16[8,4,64,128]{3,2,1,0:T(8,128)(2,1)S(1)} collective-permute-done((bf16[8,4,64,128]{3,2,1,0:T(8,128)(2,1)S(1)}, bf16[8,4,64,128]{3,2,1,0:T(8,128)(2,1)S(1)}, u32[]{:S(2)}, u32[]{:S(2)}) %collective-permute-start.4) | collective-permute-done | bytes 524320 | tf_op jit(solution)/shard_map/ppermute | solution.py:191
  48.8 1.0 collective-permute-start.6
  49.9 2.4 %collective-permute-start.7 = (bf16[4,4,64,128]{3,2,1,0:T(8,128)(2,1)S(1)}, bf16[4,4,64,128]{3,2,1,0:T(8,128)(2,1)S(1)}, u32[]{:S(2)}, u32[]{:S(2)}) collective-permute-start(bf16[4,4,64,128]{3,2,1,0:T(8,128)(2,1)S(1)} %slice.17), channel_id=1, source_target_pairs={{0,192},{64,0},{128,64},{192,128},{1,193},{65,1},{129,65},{193,129... | collective-permute-start | bytes 786440 | tf_op jit(solution)/shard_map/ppermute | solution.py:191
  52.3 0.0 collective-permute-done.8.own_r
  52.3 0.6 collective-permute-start.10
  52.9 2.8 %collective-permute-start.11 = (bf16[4,2,128,128]{3,2,1,0:T(8,128)(2,1)S(1)}, bf16[4,2,128,128]{3,2,1,0:T(8,128)(2,1)S(1)}, u32[]{:S(2)}, u32[]{:S(2)}) collective-permute-start(bf16[4,2,128,128]{3,2,1,0:T(8,128)(2,1)S(1)} %slice.19), channel_id=1, source_target_pairs={{0,3},{1,0},{2,1},{3,2},{4,7},{5,4},{6,5},{7,6},{8,11},{9,8},{10,9... | collective-permute-start | bytes 786440 | tf_op jit(solution)/shard_map/ppermute | solution.py:191
  55.7 0.8 collective-permute-done.6.c_u2
  56.5 0.5 collective-permute-start.14
  57.0 5.3 %collective-permute-done.10.own_r2 = bf16[4,2,128,128]{3,2,1,0:T(8,128)(2,1)S(1)} collective-permute-done((bf16[4,2,128,128]{3,2,1,0:T(8,128)(2,1)S(1)}, bf16[4,2,128,128]{3,2,1,0:T(8,128)(2,1)S(1)}, u32[]{:S(2)}, u32[]{:S(2)}) %collective-permute-start.10) | collective-permute-done | bytes 262176 | tf_op jit(solution)/shard_map/ppermute | solution.py:191
  62.3 0.0 collective-permute-start.15
  62.3 0.0 collective-permute-done.11.own_l2
  62.3 0.5 collective-permute-start.16
  62.8 1.6 %rebuild.1.dense = bf16[32,512,128]{2,1,0:T(8,128)(2,1)S(1)} custom-call(s32[4,32]{1,0:T(4,128)S(1)} %select_reduce_fusion.occ_index, bf16[8,4,64,128]{3,2,1,0:T(8,128)(2,1)S(1)} %pad_maximum_fusion.c0, bf16[8,4,64,128]{3,2,1,0:T(8,128)(2,1)S(1)} %collective-permute-done.4.c_u, bf16[8,4,64,128]{3,2,1,0:T(8,128)(2,1)S(1)} %collective-permute-done.5.c_d, ...), custom_call_target="tpu_custom_call" | custom-call | bytes 6291456 | tf_op jit(solution)/shard_map/rebuild/pallas_call | solution.py:116
  64.4 0.0 collective-permute-done.15.oth_r2
  64.5 6.3 %exchange.1 = (f32[4,8,4,16,128]{4,3,2,1,0:T(8,128)S(1)}, f32[4,8,4,16,128]{4,3,2,1,0:T(8,128)S(1)}) custom-call(s32[4,32]{1,0:T(4,128)S(1)} %bitcast.19, s32[4,32]{1,0:T(4,128)S(1)} %bitcast.18, bf16[32,512,128]{2,1,0:T(8,128)(2,1)S(1)} %rebuild.1.dense, bf16[8,2,128,128]{3,2,1,0:T(8,128)(2,1)S(1)} %all-to-all-done.1.own0, ...), custom_call_target="tpu_custom_call" | custom-call | flops 2700000000 | bytes 10485760 | tf_op jit(solution)/shard_map/exchange/pallas_call | solution.py:175
  70.8 0.1 collective-permute-start.17
  70.9 2.6 %collective-permute-done.17 = f32[4,8,4,16,128]{4,3,2,1,0:T(8,128)S(1)} collective-permute-done((f32[4,8,4,16,128]{4,3,2,1,0:T(8,128)S(1)}, f32[4,8,4,16,128]{4,3,2,1,0:T(8,128)S(1)}, u32[]{:S(2)}, u32[]{:S(2)}) %collective-permute-start.17) | collective-permute-done | bytes 1048608 | tf_op jit(solution)/shard_map/ppermute | solution.py:195
  73.6 1.0 add_convert_fusion
  74.5 8.2 %all-to-all-start.2 = ((bf16[32,4,16,128]{3,2,1,0:T(8,128)(2,1)}), bf16[32,4,16,128]{3,2,1,0:T(8,128)(2,1)S(1)}, u32[]{:S(2)}, u32[]{:S(2)}) async-start(bf16[32,4,16,128]{3,2,1,0:T(8,128)(2,1)} %bitcast.11), calls=%async_computation.2 | async-start | bytes 1048576 | tf_op jit(solution)/shard_map/all_to_all | solution.py:230
  82.7 0.2 multiply_reduce_fusion
  82.9 17.7 %all-to-all-done.2 = bf16[32,4,16,128]{3,2,1,0:T(8,128)(2,1)S(1)} async-done(((bf16[32,4,16,128]{3,2,1,0:T(8,128)(2,1)}), bf16[32,4,16,128]{3,2,1,0:T(8,128)(2,1)S(1)}, u32[]{:S(2)}, u32[]{:S(2)}) %all-to-all-start.2) | async-done | bytes 524320 | tf_op jit(solution)/shard_map/all_to_all | solution.py:230
  100.6 0.1 convert_reduce_fusion
  100.7 0.7 bitcast_multiply_fusion
  (18 shorter events, 0.1 us)
Async XLA Ops:
  2.3 1.0 %copy-start = (bf16[1,4,128,4,128]{4,3,2,1,0:T(4,128)(2,1)S(1)}, bf16[1,4,128,4,128]{4,3,2,1,0:T(4,128)(2,1)}, u32[]{:S(2)}) copy-start(bf16[1,4,128,4,128]{4,3,2,1,0:T(4,128)(2,1)} %param.5) | copy-start | bytes 1572868
  3.6 10.1 %collective-permute-start = (bf16[4,2,128,128]{3,2,1,0:T(8,128)(2,1)S(1)}, bf16[4,2,128,128]{3,2,1,0:T(8,128)(2,1)S(1)}, u32[]{:S(2)}, u32[]{:S(2)}) collective-permute-start(bf16[4,2,128,128]{3,2,1,0:T(8,128)(2,1)S(1)} %get-tuple-element.16), channel_id=1, source_target_pairs={{0,32},{32,0},{1,33},{33,1},{2,34},{34,2},{3,35},{35,3},{4,36},{36... | collective-permute-start | bytes 786440 | tf_op jit(solution)/shard_map/ppermute | solution.py:195
  3.7 16.8 %all-to-all-start = ((bf16[8,64,128]{2,1,0:T(8,128)(2,1)}), bf16[8,64,128]{2,1,0:T(8,128)(2,1)S(1)}, u32[]{:S(2)}, u32[]{:S(2)}) async-start(bf16[8,64,128]{2,1,0:T(8,128)(2,1)} %slice_coeffs.1), calls=%async_computation | async-start | bytes 262144 | tf_op jit(solution)/shard_map/all_to_all | solution.py:203
  20.5 20.4 %all-to-all-start.1 = ((bf16[8,2,128,128]{3,2,1,0:T(8,128)(2,1)}), bf16[8,2,128,128]{3,2,1,0:T(8,128)(2,1)S(1)}, u32[]{:S(2)}, u32[]{:S(2)}) async-start(bf16[8,2,128,128]{3,2,1,0:T(8,128)(2,1)} %fusion.1), calls=%async_computation.1 | async-start | bytes 1048576 | tf_op jit(solution)/shard_map/all_to_all | solution.py:214
  25.4 6.7 %collective-permute-start.3 = (bf16[8,64,128]{2,1,0:T(8,128)(2,1)S(1)}, bf16[8,64,128]{2,1,0:T(8,128)(2,1)S(1)}, u32[]{:S(2)}, u32[]{:S(2)}) collective-permute-start(bf16[8,64,128]{2,1,0:T(8,128)(2,1)S(1)} %all-to-all-done), channel_id=1, source_target_pairs={{0,3},{1,0},{2,1},{3,2},{4,7},{5,4},{6,5},{7,6},{8,11},{9,8},{10,9... | collective-permute-start | bytes 393224 | tf_op jit(solution)/shard_map/ppermute | solution.py:191
  28.2 7.8 %collective-permute-start.1 = (bf16[8,64,128]{2,1,0:T(8,128)(2,1)S(1)}, bf16[8,64,128]{2,1,0:T(8,128)(2,1)S(1)}, u32[]{:S(2)}, u32[]{:S(2)}) collective-permute-start(bf16[8,64,128]{2,1,0:T(8,128)(2,1)S(1)} %all-to-all-done), channel_id=1, source_target_pairs={{0,1},{1,2},{2,3},{3,0},{4,5},{5,6},{6,7},{7,4},{8,9},{9,10},{10,1... | collective-permute-start | bytes 393224 | tf_op jit(solution)/shard_map/ppermute | solution.py:191
  28.2 7.8 %collective-permute-start.2 = (bf16[8,64,128]{2,1,0:T(8,128)(2,1)S(1)}, bf16[8,64,128]{2,1,0:T(8,128)(2,1)S(1)}, u32[]{:S(2)}, u32[]{:S(2)}) collective-permute-start(bf16[8,64,128]{2,1,0:T(8,128)(2,1)S(1)} %all-to-all-done), channel_id=1, source_target_pairs={{0,2},{1,3},{2,0},{3,1},{4,6},{5,7},{6,4},{7,5},{8,10},{9,11},{10,... | collective-permute-start | bytes 393224 | tf_op jit(solution)/shard_map/ppermute | solution.py:191
  36.1 28.4 %copy-start.1 = (s32[32,4]{0,1:T(4,128)S(1)}, s32[32,4]{0,1:T(4,128)}, u32[]{:S(2)}) copy-start(s32[32,4]{0,1:T(4,128)} %param.8) | copy-start | bytes 1540
  36.1 28.4 %copy-start.2 = (s32[32,4]{0,1:T(4,128)S(1)}, s32[32,4]{0,1:T(4,128)}, u32[]{:S(2)}) copy-start(s32[32,4]{0,1:T(4,128)} %param.7) | copy-start | bytes 1540
  36.1 12.7 %collective-permute-start.4 = (bf16[8,4,64,128]{3,2,1,0:T(8,128)(2,1)S(1)}, bf16[8,4,64,128]{3,2,1,0:T(8,128)(2,1)S(1)}, u32[]{:S(2)}, u32[]{:S(2)}) collective-permute-start(bf16[8,4,64,128]{3,2,1,0:T(8,128)(2,1)S(1)} %pad_maximum_fusion.c0), channel_id=1, source_target_pairs={{0,64},{64,128},{128,192},{192,0},{1,65},{65,129},{129,193},{193,1... | collective-permute-start | bytes 1572872 | tf_op jit(solution)/shard_map/ppermute | solution.py:191
  37.8 12.0 %collective-permute-start.5 = (bf16[8,4,64,128]{3,2,1,0:T(8,128)(2,1)S(1)}, bf16[8,4,64,128]{3,2,1,0:T(8,128)(2,1)S(1)}, u32[]{:S(2)}, u32[]{:S(2)}) collective-permute-start(bf16[8,4,64,128]{3,2,1,0:T(8,128)(2,1)S(1)} %pad_maximum_fusion.c0), channel_id=1, source_target_pairs={{0,192},{64,0},{128,64},{192,128},{1,193},{65,1},{129,65},{193,129... | collective-permute-start | bytes 1572872 | tf_op jit(solution)/shard_map/ppermute | solution.py:191
  40.9 11.3 %collective-permute-start.8 = (bf16[8,2,128,128]{3,2,1,0:T(8,128)(2,1)S(1)}, bf16[8,2,128,128]{3,2,1,0:T(8,128)(2,1)S(1)}, u32[]{:S(2)}, u32[]{:S(2)}) collective-permute-start(bf16[8,2,128,128]{3,2,1,0:T(8,128)(2,1)S(1)} %all-to-all-done.1.own0), channel_id=1, source_target_pairs={{0,1},{1,2},{2,3},{3,0},{4,5},{5,6},{6,7},{7,4},{8,9},{9,10},{10,1... | collective-permute-start | bytes 1572872 | tf_op jit(solution)/shard_map/ppermute | solution.py:191
  42.4 10.5 %collective-permute-start.9 = (bf16[8,2,128,128]{3,2,1,0:T(8,128)(2,1)S(1)}, bf16[8,2,128,128]{3,2,1,0:T(8,128)(2,1)S(1)}, u32[]{:S(2)}, u32[]{:S(2)}) collective-permute-start(bf16[8,2,128,128]{3,2,1,0:T(8,128)(2,1)S(1)} %all-to-all-done.1.own0), channel_id=1, source_target_pairs={{0,3},{1,0},{2,1},{3,2},{4,7},{5,4},{6,5},{7,6},{8,11},{9,8},{10,9... | collective-permute-start | bytes 1572872 | tf_op jit(solution)/shard_map/ppermute | solution.py:191
  48.8 7.7 %collective-permute-start.6 = (bf16[4,4,64,128]{3,2,1,0:T(8,128)(2,1)S(1)}, bf16[4,4,64,128]{3,2,1,0:T(8,128)(2,1)S(1)}, u32[]{:S(2)}, u32[]{:S(2)}) collective-permute-start(bf16[4,4,64,128]{3,2,1,0:T(8,128)(2,1)S(1)} %slice.16), channel_id=1, source_target_pairs={{0,64},{64,128},{128,192},{192,0},{1,65},{65,129},{129,193},{193,1... | collective-permute-start | bytes 786440 | tf_op jit(solution)/shard_map/ppermute | solution.py:191
  49.9 6.6 %collective-permute-start.7 = (bf16[4,4,64,128]{3,2,1,0:T(8,128)(2,1)S(1)}, bf16[4,4,64,128]{3,2,1,0:T(8,128)(2,1)S(1)}, u32[]{:S(2)}, u32[]{:S(2)}) collective-permute-start(bf16[4,4,64,128]{3,2,1,0:T(8,128)(2,1)S(1)} %slice.17), channel_id=1, source_target_pairs={{0,192},{64,0},{128,64},{192,128},{1,193},{65,1},{129,65},{193,129... | collective-permute-start | bytes 786440 | tf_op jit(solution)/shard_map/ppermute | solution.py:191
  52.3 12.2 %collective-permute-start.12 = (bf16[8,2,128,128]{3,2,1,0:T(8,128)(2,1)S(1)}, bf16[8,2,128,128]{3,2,1,0:T(8,128)(2,1)S(1)}, u32[]{:S(2)}, u32[]{:S(2)}) collective-permute-start(bf16[8,2,128,128]{3,2,1,0:T(8,128)(2,1)S(1)} %all-to-all-done.1.own0), channel_id=1, source_target_pairs={{0,32},{32,0},{1,33},{33,1},{2,34},{34,2},{3,35},{35,3},{4,36},{36... | collective-permute-start | bytes 1572872 | tf_op jit(solution)/shard_map/ppermute | solution.py:195
  52.3 10.0 %collective-permute-start.10 = (bf16[4,2,128,128]{3,2,1,0:T(8,128)(2,1)S(1)}, bf16[4,2,128,128]{3,2,1,0:T(8,128)(2,1)S(1)}, u32[]{:S(2)}, u32[]{:S(2)}) collective-permute-start(bf16[4,2,128,128]{3,2,1,0:T(8,128)(2,1)S(1)} %slice.18), channel_id=1, source_target_pairs={{0,1},{1,2},{2,3},{3,0},{4,5},{5,6},{6,7},{7,4},{8,9},{9,10},{10,1... | collective-permute-start | bytes 786440 | tf_op jit(solution)/shard_map/ppermute | solution.py:191
  52.9 9.4 %collective-permute-start.11 = (bf16[4,2,128,128]{3,2,1,0:T(8,128)(2,1)S(1)}, bf16[4,2,128,128]{3,2,1,0:T(8,128)(2,1)S(1)}, u32[]{:S(2)}, u32[]{:S(2)}) collective-permute-start(bf16[4,2,128,128]{3,2,1,0:T(8,128)(2,1)S(1)} %slice.19), channel_id=1, source_target_pairs={{0,3},{1,0},{2,1},{3,2},{4,7},{5,4},{6,5},{7,6},{8,11},{9,8},{10,9... | collective-permute-start | bytes 786440 | tf_op jit(solution)/shard_map/ppermute | solution.py:191
  56.5 8.0 %collective-permute-start.13 = (bf16[8,2,128,128]{3,2,1,0:T(8,128)(2,1)S(1)}, bf16[8,2,128,128]{3,2,1,0:T(8,128)(2,1)S(1)}, u32[]{:S(2)}, u32[]{:S(2)}) collective-permute-start(bf16[8,2,128,128]{3,2,1,0:T(8,128)(2,1)S(1)} %collective-permute-done.8.own_r), channel_id=1, source_target_pairs={{0,32},{32,0},{1,33},{33,1},{2,34},{34,2},{3,35},{35,3},{4,36},{36... | collective-permute-start | bytes 1572872 | tf_op jit(solution)/shard_map/ppermute | solution.py:195
  56.5 8.0 %collective-permute-start.14 = (bf16[8,2,128,128]{3,2,1,0:T(8,128)(2,1)S(1)}, bf16[8,2,128,128]{3,2,1,0:T(8,128)(2,1)S(1)}, u32[]{:S(2)}, u32[]{:S(2)}) collective-permute-start(bf16[8,2,128,128]{3,2,1,0:T(8,128)(2,1)S(1)} %collective-permute-done.9.own_l), channel_id=1, source_target_pairs={{0,32},{32,0},{1,33},{33,1},{2,34},{34,2},{3,35},{35,3},{4,36},{36... | collective-permute-start | bytes 1572872 | tf_op jit(solution)/shard_map/ppermute | solution.py:195
  62.3 2.2 %collective-permute-start.15 = (bf16[4,2,128,128]{3,2,1,0:T(8,128)(2,1)S(1)}, bf16[4,2,128,128]{3,2,1,0:T(8,128)(2,1)S(1)}, u32[]{:S(2)}, u32[]{:S(2)}) collective-permute-start(bf16[4,2,128,128]{3,2,1,0:T(8,128)(2,1)S(1)} %collective-permute-done.10.own_r2), channel_id=1, source_target_pairs={{0,32},{32,0},{1,33},{33,1},{2,34},{34,2},{3,35},{35,3},{4,36},{36... | collective-permute-start | bytes 786440 | tf_op jit(solution)/shard_map/ppermute | solution.py:195
  62.3 2.2 %collective-permute-start.16 = (bf16[4,2,128,128]{3,2,1,0:T(8,128)(2,1)S(1)}, bf16[4,2,128,128]{3,2,1,0:T(8,128)(2,1)S(1)}, u32[]{:S(2)}, u32[]{:S(2)}) collective-permute-start(bf16[4,2,128,128]{3,2,1,0:T(8,128)(2,1)S(1)} %collective-permute-done.11.own_l2), channel_id=1, source_target_pairs={{0,32},{32,0},{1,33},{33,1},{2,34},{34,2},{3,35},{35,3},{4,36},{36... | collective-permute-start | bytes 786440 | tf_op jit(solution)/shard_map/ppermute | solution.py:195
  70.8 2.7 %collective-permute-start.17 = (f32[4,8,4,16,128]{4,3,2,1,0:T(8,128)S(1)}, f32[4,8,4,16,128]{4,3,2,1,0:T(8,128)S(1)}, u32[]{:S(2)}, u32[]{:S(2)}) collective-permute-start(f32[4,8,4,16,128]{4,3,2,1,0:T(8,128)S(1)} %get-tuple-element.22), channel_id=1, source_target_pairs={{0,32},{32,0},{1,33},{33,1},{2,34},{34,2},{3,35},{35,3},{4,36},{36... | collective-permute-start | bytes 3145736 | tf_op jit(solution)/shard_map/ppermute | solution.py:195
  74.5 26.1 %all-to-all-start.2 = ((bf16[32,4,16,128]{3,2,1,0:T(8,128)(2,1)}), bf16[32,4,16,128]{3,2,1,0:T(8,128)(2,1)S(1)}, u32[]{:S(2)}, u32[]{:S(2)}) async-start(bf16[32,4,16,128]{3,2,1,0:T(8,128)(2,1)} %bitcast.11), calls=%async_computation.2 | async-start | bytes 1048576 | tf_op jit(solution)/shard_map/all_to_all | solution.py:230

commit v10 on v9

--- a/solution.py
+++ b/solution.py
@@ -26,9 +26,14 @@
     return tuple(lax.axis_index(name).astype(jnp.int32) for name in ("y", "c", "z", "x"))
 
 
-def slice_kernel(occ_live, orb, coeffs, cols, sem):
+def prep_kernel(occ_live, orb, eri, coeffs, keep, give, cols, rows, sems):
     slab, core, z, x = position()
     tile = z * NX + x
+    size = 2 * AUXROWS * TS
+    loads = []
+    for index, part in enumerate((1 - core, core)):
+        span = pl.ds(pl.multiple_of(part * size, size), size)
+        loads.append(pltpu.make_async_copy(eri.at[span], rows.at[span], sems.at[index + 1]))
     chosen = jnp.int32(0)
     count = jnp.int32(0)
     for occ in range(OCC):
@@ -36,54 +41,40 @@
         chosen = jnp.where(live & (count == slab), occ, chosen)
         count = count + jnp.where(live, 1, 0)
     span = pl.ds(pl.multiple_of(chosen * TS, TS), TS)
-    load = pltpu.make_async_copy(orb.at[:, span], cols, sem)
+    load = pltpu.make_async_copy(orb.at[:, span], cols, sems.at[0])
     load.start()
+    for part in loads:
+        part.start()
     load.wait()
     flipped = cols[...].astype(F32).T.astype(BF)
     mine = jnp.where(core == 0, flipped[:HALF], flipped[HALF:])
     for target in range(NZ):
         coeffs[target] = mine
-
-
-def slice_coeffs(occ_live, orb):
-    return pl.pallas_call(
-        slice_kernel,
-        out_shape=jax.ShapeDtypeStruct((NZ, HALF, TS), BF),
-        in_specs=[SMEM, ANY],
-        out_specs=VMEM,
-        scratch_shapes=[pltpu.VMEM((TS, TS), BF), pltpu.SemaphoreType.DMA],
-        compiler_params=pltpu.CompilerParams(vmem_limit_bytes=60 * 2**20),
-        cost_estimate=pl.CostEstimate(flops=0, bytes_accessed=2 * orb.size, transcendentals=0),
-        name="slice_coeffs",
-    )(occ_live, orb)
-
-
-def split_kernel(eri, keep, give):
-    core = position()[1]
     row = lax.broadcasted_iota(jnp.int32, (TS, TS), 0)
     col = lax.broadcasted_iota(jnp.int32, (TS, TS), 1)
     block_nu = TS // AUXROWS
     perm = (col == (row % block_nu) * AUXROWS + row // block_nu).astype(BF)
-    for out, part in ((give, 1 - core), (keep, core)):
+    for out, part, load in ((give, 1 - core, loads[0]), (keep, core, loads[1])):
+        load.wait()
         for j in range(2):
             for quarter in range(AUXROWS):
                 start = pl.multiple_of(((part * 2 + j) * AUXROWS + quarter) * TS, TS)
-                mixed = jnp.dot(perm, eri[pl.ds(start, TS), :], preferred_element_type=F32).astype(BF)
+                mixed = jnp.dot(perm, rows[pl.ds(start, TS), :], preferred_element_type=F32).astype(BF)
                 for aux in range(AUXROWS):
                     out[aux, j, pl.ds(quarter * block_nu, block_nu), :] = mixed[aux * block_nu:(aux + 1) * block_nu]
 
 
-def split_aux(eri):
+def prep(occ_live, orb, eri):
     piece = jax.ShapeDtypeStruct((AUXROWS, 2, TS, TS), BF)
     return pl.pallas_call(
-        split_kernel,
-        out_shape=(piece, piece),
-        in_specs=[VMEM],
-        out_specs=(VMEM, VMEM),
-        compiler_params=pltpu.CompilerParams(vmem_limit_bytes=8 * 2**20),
-        cost_estimate=pl.CostEstimate(flops=2 * TS * eri.size, bytes_accessed=4 * eri.size, transcendentals=0),
-        name="split_aux",
-    )(eri)
+        prep_kernel,
+        out_shape=(jax.ShapeDtypeStruct((NZ, HALF, TS), BF), piece, piece),
+        in_specs=[SMEM, ANY, ANY],
+        out_specs=(VMEM, VMEM, VMEM),
+        scratch_shapes=[pltpu.VMEM((TS, TS), BF), pltpu.VMEM(eri.shape, BF), pltpu.SemaphoreType.DMA((3,))],
+        compiler_params=pltpu.CompilerParams(vmem_limit_bytes=60 * 2**20),
+        name="prep",
+    )(occ_live, orb, eri)
 
 
 def rebuild_kernel(occ_index, c0, c_u, c_d, c_u2, c_d2, dense):
@@ -124,34 +115,55 @@
     )(occ_index, *pieces)
 
 
+def transform(pair_tiles, pair_live, dense, core, own, oth, first, row, xp, count):
+    def body(step, carry):
+        tile = (row + step) * NX + xp
+        lhs, rhs = [], []
+        for part, ref in ((core, own), (1 - core, oth)):
+            for j in range(2):
+                slot = part * 2 + j
+                eri = ref[step, j]
+                rhs.append(jnp.where(pair_live[slot, tile] != 0, eri, jnp.zeros_like(eri)))
+                lhs.append(dense[pair_tiles[slot, tile]])
+        half = jnp.dot(jnp.concatenate(lhs, axis=1), jnp.concatenate(rhs, axis=0), preferred_element_type=F32)
+        first(step, tile)[...] = half.astype(BF)
+        return carry
+
+    lax.fori_loop(0, count, body, 0, unroll=True)
+
+
+def own_kernel(pair_tiles, pair_live, dense, own0, oth0, column):
+    _, core, _, x = position()
+    transform(pair_tiles, pair_live, dense, core, own0, oth0, lambda step, tile: column.at[step], 0, x, NZ)
+
+
+def own_column(pair_tiles, pair_live, *pieces):
+    return pl.pallas_call(
+        own_kernel,
+        out_shape=jax.ShapeDtypeStruct((NZ, OCC * HALF, TS), BF),
+        in_specs=[SMEM] * 2 + [VMEM] * len(pieces),
+        out_specs=VMEM,
+        compiler_params=pltpu.CompilerParams(vmem_limit_bytes=16 * 2**20),
+        cost_estimate=pl.CostEstimate(flops=0, bytes_accessed=0, transcendentals=0),
+        name="own_column",
+    )(pair_tiles, pair_live, *pieces)
+
+
 def main_kernel(pair_tiles, pair_live, dense,
-                own0, own_r, own_l, own_r2, own_l2, oth0, oth_r, oth_l, oth_r2, oth_l2,
+                column, own_r, own_l, own_r2, own_l2, oth_r, oth_l, oth_r2, oth_l2,
                 keep, send, field, block):
     _, core, _, x = position()
 
-    def transform(xp, own, oth, lo, count):
-        def body(step, carry):
-            tile = (lo + step) * NX + xp
-            lhs, rhs = [], []
-            for part, ref in ((core, own), (1 - core, oth)):
-                for j in range(2):
-                    slot = part * 2 + j
-                    eri = ref[step, j]
-                    rhs.append(jnp.where(pair_live[slot, tile] != 0, eri, jnp.zeros_like(eri)))
-                    lhs.append(dense[pair_tiles[slot, tile]])
-            half = jnp.dot(
-                jnp.concatenate(lhs, axis=1), jnp.concatenate(rhs, axis=0), preferred_element_type=F32
-            )
-            field[tile] = half.astype(BF)
-            return carry
-
-        lax.fori_loop(0, count, body, 0, unroll=True)
-
-    transform(x, own0, oth0, 0, 8)
-    transform((x + 3) % NX, own_r, oth_r, 0, 8)
-    transform((x + 1) % NX, own_l, oth_l, 0, 8)
-    transform((x + 2) % NX, own_r2, oth_r2, 0, 4)
-    transform((x + 2) % NX, own_l2, oth_l2, 4, 4)
+    for row in range(NZ):
+        field[row * NX + x] = column[row]
+
+    def run(own, oth, row, xp, count):
+        transform(pair_tiles, pair_live, dense, core, own, oth, lambda step, tile: field.at[tile], row, xp, count)
+
+    run(own_r, oth_r, 0, (x + 3) % NX, NZ)
+    run(own_l, oth_l, 0, (x + 1) % NX, NZ)
+    run(own_r2, oth_r2, 0, (x + 2) % NX, 4)
+    run(own_l2, oth_l2, 4, (x + 2) % NX, 4)
 
     def gram(zp, carry):
         tile = zp * NX + x
@@ -198,10 +210,8 @@
 def shards(integrals, orbitals, pair_tiles, pair_live, occ_live):
     _, core, z, x = position()
     tile = z * NX + x
-    coeffs = slice_coeffs(occ_live.T, orbitals)
-    coeffs, eri = lax.optimization_barrier((coeffs, integrals.reshape(SLOTS * TS * AUXROWS, TS)))
+    coeffs, keep_eri, give_eri = prep(occ_live.T, orbitals, integrals.reshape(SLOTS * TS * AUXROWS, TS))
     column = lax.all_to_all(coeffs, "z", split_axis=0, concat_axis=0, tiled=True)
-    keep_eri, give_eri = split_aux(eri)
     rank = jnp.cumsum(occ_live, axis=1) - 1
     hits = (occ_live[None] != 0) & (rank[None] == jnp.arange(LIVE)[:, None, None])
     occ_index = jnp.sum(jnp.where(hits, jnp.arange(OCC)[None, None, :], 0), axis=2).astype(jnp.int32)
@@ -219,12 +229,14 @@
     own_r2, own_l2 = shift(own_r[:4], "x", NX, 1), shift(own_l[4:], "x", NX, -1)
     c_u2, c_d2 = shift(c_u[:4], "y", NY, 1), shift(c_d[4:], "y", NY, -1)
     oth_r, oth_l = swap(own_r), swap(own_l)
+    dense = rebuild(occ_index, c0, c_u, c_d, c_u2, c_d2)
+    column = own_column(pair_tiles.T, pair_live.T, dense, own0, oth0)
+    column, own_r2, own_l2 = lax.optimization_barrier((column, own_r2, own_l2))
     oth_r2, oth_l2 = swap(own_r2), swap(own_l2)
 
-    dense = rebuild(occ_index, c0, c_u, c_d, c_u2, c_d2)
     keep, send = exchange(
         pair_tiles.T, pair_live.T, dense,
-        own0, own_r, own_l, own_r2, own_l2, oth0, oth_r, oth_l, oth_r2, oth_l2,
+        column, own_r, own_l, own_r2, own_l2, oth_r, oth_l, oth_r2, oth_l2,
     )
     partial = (keep + swap(send)).astype(BF).reshape(NY * NZ, SLOTS, ROWS, TS)
     parts = lax.all_to_all(partial, ("y", "z"), split_axis=0, concat_axis=0, tiled=True).astype(F32)

time: 102 us -> 99.2 us (0.973)
  starting transfers between devices: 41.3 us -> 38.6 us
  Pallas kernels: 10.5 us -> 11.7 us
  waiting for transfers between devices: 43.8 us -> 42.7 us
  local copies, waits for them, and re-layouts: 1.12 us -> 0.09 us
    pallas_call x2, Pallas kernels: 2.58 us -> 4.87 us  [the longest x1 2.99 us: prep(): pl.pallas_call(prep_kernel, out_shape=(jax.ShapeDtypeStruct((NZ, HALF, TS...]
    ppermute x11, starting transfers between devices: 18.4 us -> 16.2 us  [shift(): lax.ppermute(value, axis, [(i, (i + by) % size) for i in range(size)])]
    all_to_all x1, waiting for transfers between devices: 5.67 us -> 3.7 us  [shards(): lax.all_to_all(coeffs, 'z', split_axis=0, concat_axis=0, tiled=True)]
    ppermute x7, waiting for transfers between devices: 2.66 us -> 4.04 us  [swap(): return lax.ppermute(value, 'c', [(0, 1), (1, 0)])]
    pallas_call x1, Pallas kernels: 6.29 us -> 5.2 us  [exchange(): pl.pallas_call(main_kernel, out_shape=(shape, shape), in_specs=[SMEM] * 2...]
    unnamed x6 -> x4, local copies, waits for them, and re-layouts: 1.05 us -> 0.01 us
  transfers between devices with their start and end apart: 21 -> 21, of which waited for: 9 -> 13; matrix products, arithmetic and copies ran while one was open for 3% -> 4% of each run, Pallas kernels for 2% -> 4%
where the time goes in v10:
time: 99.2 us; the launch traced here: 98.7 us
  waiting for transfers between devices  42.7 us (43%)
  starting transfers between devices  38.6 us (39%)
  Pallas kernels  11.7 us (12%)
  other arithmetic  5.41 us (5%)
    all_to_all x1, waiting for transfers between devices, shards(): lax.all_to_all(partial, ('y', 'z'), split_axis=0, concat_axis=0, tiled=True)  17.7 us
    ppermute x11, starting transfers between devices, shift(): lax.ppermute(value, axis, [(i, (i + by) % size) for i in range(size)])  16.2 us
    ppermute x11, waiting for transfers between devices, shift(): lax.ppermute(value, axis, [(i, (i + by) % size) for i in range(size)])  16.1 us
    all_to_all x1, starting transfers between devices, shards(): lax.all_to_all(coeffs, 'z', split_axis=0, concat_axis=0, tiled=True)  8.58 us
    all_to_all x1, starting transfers between devices, shards(): lax.all_to_all(partial, ('y', 'z'), split_axis=0, concat_axis=0, tiled=True)  7.63 us
    pallas_call x1, Pallas kernels, exchange(): pl.pallas_call(main_kernel, out_shape=(shape, shape), in_specs=[SMEM] * 2...  5.2 us
    all_to_all x1, starting transfers between devices, shards(): own0 = lax.all_to_all(by_aux, 'z', split_axis=0, concat_axis=0, tiled=True)  5.05 us
    ppermute x7, waiting for transfers between devices, swap(): return lax.ppermute(value, 'c', [(0, 1), (1, 0)])  4.04 us
  transfers between devices with their start and end apart: 21, of which 13 were waited for; matrix products, arithmetic and copies ran while one was open for 4% of the time, Pallas kernels for 4%

profile of v10, /device:TPU:32, one launch (start us, length us, event | category | flops | bytes accessed | tf_op | source)
XLA Modules:
  0.0 98.7 jit_solution(11917377608975202837)
XLA Ops:
  0.0 3.0 %prep.1 = (bf16[8,64,128]{2,1,0:T(8,128)(2,1)}, bf16[4,2,128,128]{3,2,1,0:T(8,128)(2,1)}, bf16[4,2,128,128]{3,2,1,0:T(8,128)(2,1)}) custom-call(s32[8,32]{1,0:T(8,128)} %bitcast.26, bf16[128,1024]{1,0:T(8,128)(2,1)} %orb.1, bf16[2048,128]{1,0:T(8,128)(2,1)} %bitcast.21), custom_call_target="tpu_custom_call" | custom-call | tf_op jit(solution)/shard_map/prep/pallas_call | solution.py:69
  3.0 8.6 %all-to-all-start = ((bf16[8,64,128]{2,1,0:T(8,128)(2,1)}), bf16[8,64,128]{2,1,0:T(8,128)(2,1)S(1)}, u32[]{:S(2)}, u32[]{:S(2)}) async-start(bf16[8,64,128]{2,1,0:T(8,128)(2,1)} %get-tuple-element.18), calls=%async_computation | async-start | bytes 262144 | tf_op jit(solution)/shard_map/all_to_all | solution.py:214
  11.6 0.0 collective-permute-start
  11.6 0.7 reduce_window_sum.11
  12.3 0.7 broadcast_compare_fusion
  13.0 0.3 collective-permute-done
  13.3 2.0 %fusion.1 = bf16[8,2,128,128]{3,2,1,0:T(8,128)(2,1)} fusion(s32[]{:T(128)S(6)} %select_n.11, bf16[4,2,128,128]{3,2,1,0:T(8,128)(2,1)} %get-tuple-element.16, bf16[4,2,128,128]{3,2,1,0:T(8,128)(2,1)S(1)} %collective-permute-done), kind=kLoop, calls=%fused_computation.6 | loop fusion | flops 524288 | bytes 1048580 | tf_op jit(solution)/shard_map/concatenate | solution.py:221
  15.3 3.7 %all-to-all-done = bf16[8,64,128]{2,1,0:T(8,128)(2,1)S(1)} async-done(((bf16[8,64,128]{2,1,0:T(8,128)(2,1)}), bf16[8,64,128]{2,1,0:T(8,128)(2,1)S(1)}, u32[]{:S(2)}, u32[]{:S(2)}) %all-to-all-start) | async-done | bytes 131104 | tf_op jit(solution)/shard_map/all_to_all | solution.py:214
  19.0 5.0 %all-to-all-start.1 = ((bf16[8,2,128,128]{3,2,1,0:T(8,128)(2,1)}), bf16[8,2,128,128]{3,2,1,0:T(8,128)(2,1)S(1)}, u32[]{:S(2)}, u32[]{:S(2)}) async-start(bf16[8,2,128,128]{3,2,1,0:T(8,128)(2,1)} %fusion.1), calls=%async_computation.1 | async-start | bytes 1048576 | tf_op jit(solution)/shard_map/all_to_all | solution.py:224
  24.1 2.8 %collective-permute-start.3 = (bf16[8,64,128]{2,1,0:T(8,128)(2,1)S(1)}, bf16[8,64,128]{2,1,0:T(8,128)(2,1)S(1)}, u32[]{:S(2)}, u32[]{:S(2)}) collective-permute-start(bf16[8,64,128]{2,1,0:T(8,128)(2,1)S(1)} %all-to-all-done), channel_id=1, source_target_pairs={{0,3},{1,0},{2,1},{3,2},{4,7},{5,4},{6,5},{7,6},{8,11},{9,8},{10,9... | collective-permute-start | bytes 393224 | tf_op jit(solution)/shard_map/ppermute | solution.py:203
  26.8 0.8 collective-permute-start.2
  27.6 0.9 collective-permute-start.1
  28.5 2.3 %collective-permute-done.3 = bf16[8,64,128]{2,1,0:T(8,128)(2,1)S(1)} collective-permute-done((bf16[8,64,128]{2,1,0:T(8,128)(2,1)S(1)}, bf16[8,64,128]{2,1,0:T(8,128)(2,1)S(1)}, u32[]{:S(2)}, u32[]{:S(2)}) %collective-permute-start.3) | collective-permute-done | bytes 131104 | tf_op jit(solution)/shard_map/ppermute | solution.py:203
  30.8 2.6 %collective-permute-done.2 = bf16[8,64,128]{2,1,0:T(8,128)(2,1)S(1)} collective-permute-done((bf16[8,64,128]{2,1,0:T(8,128)(2,1)S(1)}, bf16[8,64,128]{2,1,0:T(8,128)(2,1)S(1)}, u32[]{:S(2)}, u32[]{:S(2)}) %collective-permute-start.2) | collective-permute-done | bytes 131104 | tf_op jit(solution)/shard_map/ppermute | solution.py:203
  33.4 1.3 %collective-permute-done.1 = bf16[8,64,128]{2,1,0:T(8,128)(2,1)S(1)} collective-permute-done((bf16[8,64,128]{2,1,0:T(8,128)(2,1)S(1)}, bf16[8,64,128]{2,1,0:T(8,128)(2,1)S(1)}, u32[]{:S(2)}, u32[]{:S(2)}) %collective-permute-start.1) | collective-permute-done | bytes 131104 | tf_op jit(solution)/shard_map/ppermute | solution.py:203
  34.7 0.1 pad_maximum_fusion.c0
  34.8 0.0 copy-start
  34.8 0.0 copy-start.1
  34.8 3.1 %collective-permute-start.5 = (bf16[8,4,64,128]{3,2,1,0:T(8,128)(2,1)S(1)}, bf16[8,4,64,128]{3,2,1,0:T(8,128)(2,1)S(1)}, u32[]{:S(2)}, u32[]{:S(2)}) collective-permute-start(bf16[8,4,64,128]{3,2,1,0:T(8,128)(2,1)S(1)} %pad_maximum_fusion.c0), channel_id=1, source_target_pairs={{0,192},{64,0},{128,64},{192,128},{1,193},{65,1},{129,65},{193,129... | collective-permute-start | bytes 1572872 | tf_op jit(solution)/shard_map/ppermute | solution.py:203
  37.9 1.1 %all-to-all-done.1.own0 = bf16[8,2,128,128]{3,2,1,0:T(8,128)(2,1)S(1)} async-done(((bf16[8,2,128,128]{3,2,1,0:T(8,128)(2,1)}), bf16[8,2,128,128]{3,2,1,0:T(8,128)(2,1)S(1)}, u32[]{:S(2)}, u32[]{:S(2)}) %all-to-all-start.1) | async-done | bytes 524320 | tf_op jit(solution)/shard_map/all_to_all | solution.py:224
  39.0 2.8 %collective-permute-start.11 = (bf16[8,2,128,128]{3,2,1,0:T(8,128)(2,1)S(1)}, bf16[8,2,128,128]{3,2,1,0:T(8,128)(2,1)S(1)}, u32[]{:S(2)}, u32[]{:S(2)}) collective-permute-start(bf16[8,2,128,128]{3,2,1,0:T(8,128)(2,1)S(1)} %all-to-all-done.1.own0), channel_id=1, source_target_pairs={{0,3},{1,0},{2,1},{3,2},{4,7},{5,4},{6,5},{7,6},{8,11},{9,8},{10,9... | collective-permute-start | bytes 1572872 | tf_op jit(solution)/shard_map/ppermute | solution.py:203
  41.7 0.0 collective-permute-start.8
  41.7 4.6 %collective-permute-done.5.c_d = bf16[8,4,64,128]{3,2,1,0:T(8,128)(2,1)S(1)} collective-permute-done((bf16[8,4,64,128]{3,2,1,0:T(8,128)(2,1)S(1)}, bf16[8,4,64,128]{3,2,1,0:T(8,128)(2,1)S(1)}, u32[]{:S(2)}, u32[]{:S(2)}) %collective-permute-start.5) | collective-permute-done | bytes 524320 | tf_op jit(solution)/shard_map/ppermute | solution.py:203
  46.4 3.6 %collective-permute-start.7 = (bf16[4,4,64,128]{3,2,1,0:T(8,128)(2,1)S(1)}, bf16[4,4,64,128]{3,2,1,0:T(8,128)(2,1)S(1)}, u32[]{:S(2)}, u32[]{:S(2)}) collective-permute-start(bf16[4,4,64,128]{3,2,1,0:T(8,128)(2,1)S(1)} %slice.17), channel_id=1, source_target_pairs={{0,192},{64,0},{128,64},{192,128},{1,193},{65,1},{129,65},{193,129... | collective-permute-start | bytes 786440 | tf_op jit(solution)/shard_map/ppermute | solution.py:203
  50.0 0.0 collective-permute-done.4.c_u
  50.0 0.1 collective-permute-start.6
  50.1 0.0 collective-permute-done.11.own_l
  50.2 2.0 %collective-permute-start.12 = (bf16[4,2,128,128]{3,2,1,0:T(8,128)(2,1)S(1)}, bf16[4,2,128,128]{3,2,1,0:T(8,128)(2,1)S(1)}, u32[]{:S(2)}, u32[]{:S(2)}) collective-permute-start(bf16[4,2,128,128]{3,2,1,0:T(8,128)(2,1)S(1)} %slice.19), channel_id=1, source_target_pairs={{0,3},{1,0},{2,1},{3,2},{4,7},{5,4},{6,5},{7,6},{8,11},{9,8},{10,9... | collective-permute-start | bytes 786440 | tf_op jit(solution)/shard_map/ppermute | solution.py:203
  52.2 0.0 collective-permute-done.9.own_r
  52.2 0.1 collective-permute-start.10
  52.4 1.5 %collective-permute-done.7.c_d2 = bf16[4,4,64,128]{3,2,1,0:T(8,128)(2,1)S(1)} collective-permute-done((bf16[4,4,64,128]{3,2,1,0:T(8,128)(2,1)S(1)}, bf16[4,4,64,128]{3,2,1,0:T(8,128)(2,1)S(1)}, u32[]{:S(2)}, u32[]{:S(2)}) %collective-permute-start.7) | collective-permute-done | bytes 262176 | tf_op jit(solution)/shard_map/ppermute | solution.py:203
  53.9 3.8 %collective-permute-done.6.c_u2 = bf16[4,4,64,128]{3,2,1,0:T(8,128)(2,1)S(1)} collective-permute-done((bf16[4,4,64,128]{3,2,1,0:T(8,128)(2,1)S(1)}, bf16[4,4,64,128]{3,2,1,0:T(8,128)(2,1)S(1)}, u32[]{:S(2)}, u32[]{:S(2)}) %collective-permute-start.6) | collective-permute-done | bytes 262176 | tf_op jit(solution)/shard_map/ppermute | solution.py:203
  57.7 0.0 collective-permute-start.13
  57.7 1.6 %rebuild.1.dense = bf16[32,512,128]{2,1,0:T(8,128)(2,1)S(1)} custom-call(s32[4,32]{1,0:T(4,128)S(1)} %select_reduce_fusion.occ_index, bf16[8,4,64,128]{3,2,1,0:T(8,128)(2,1)S(1)} %pad_maximum_fusion.c0, bf16[8,4,64,128]{3,2,1,0:T(8,128)(2,1)S(1)} %collective-permute-done.4.c_u, bf16[8,4,64,128]{3,2,1,0:T(8,128)(2,1)S(1)} %collective-permute-done.5.c_d, ...), custom_call_target="tpu_custom_call" | custom-call | bytes 6291456 | tf_op jit(solution)/shard_map/rebuild/pallas_call | solution.py:107
  59.4 1.9 %own_column.1.column = bf16[8,512,128]{2,1,0:T(8,128)(2,1)S(1)} custom-call(s32[4,32]{1,0:T(4,128)S(1)} %bitcast.19, s32[4,32]{1,0:T(4,128)S(1)} %bitcast.17, bf16[32,512,128]{2,1,0:T(8,128)(2,1)S(1)} %rebuild.1.dense, bf16[8,2,128,128]{3,2,1,0:T(8,128)(2,1)S(1)} %all-to-all-done.1.own0, bf16[8,2,128,128]{3,2,1,0:T(8,128)(2,1)S(1)} %collective-permute-done.8.oth0), custom_call_target="tpu_custom_call" | custom-call | tf_op jit(solution)/shard_map/own_column/pallas_call | solution.py:141
  61.3 0.6 collective-permute-start.15
  61.9 0.1 collective-permute-start.16
  62.0 1.1 %collective-permute-done.15.oth_r2 = bf16[4,2,128,128]{3,2,1,0:T(8,128)(2,1)S(1)} collective-permute-done((bf16[4,2,128,128]{3,2,1,0:T(8,128)(2,1)S(1)}, bf16[4,2,128,128]{3,2,1,0:T(8,128)(2,1)S(1)}, u32[]{:S(2)}, u32[]{:S(2)}) %collective-permute-start.15) | collective-permute-done | bytes 262176 | tf_op jit(solution)/shard_map/ppermute | solution.py:207
  63.0 0.4 collective-permute-done.16.oth_l2
  63.4 5.2 %exchange.1 = (f32[4,8,4,16,128]{4,3,2,1,0:T(8,128)S(1)}, f32[4,8,4,16,128]{4,3,2,1,0:T(8,128)S(1)}) custom-call(s32[4,32]{1,0:T(4,128)S(1)} %bitcast.20, s32[4,32]{1,0:T(4,128)S(1)} %bitcast.18, bf16[32,512,128]{2,1,0:T(8,128)(2,1)S(1)} %rebuild.1.dense, bf16[8,512,128]{2,1,0:T(8,128)(2,1)S(1)} %own_column.1.column, ...), custom_call_target="tpu_custom_call" | custom-call | flops 2700000000 | bytes 10485760 | tf_op jit(solution)/shard_map/exchange/pallas_call | solution.py:187
  68.6 0.5 collective-permute-start.17
  69.1 2.3 %collective-permute-done.17 = f32[4,8,4,16,128]{4,3,2,1,0:T(8,128)S(1)} collective-permute-done((f32[4,8,4,16,128]{4,3,2,1,0:T(8,128)S(1)}, f32[4,8,4,16,128]{4,3,2,1,0:T(8,128)S(1)}, u32[]{:S(2)}, u32[]{:S(2)}) %collective-permute-start.17) | collective-permute-done | bytes 1048608 | tf_op jit(solution)/shard_map/ppermute | solution.py:207
  71.4 1.0 add_convert_fusion
  72.3 7.6 %all-to-all-start.2 = ((bf16[32,4,16,128]{3,2,1,0:T(8,128)(2,1)}), bf16[32,4,16,128]{3,2,1,0:T(8,128)(2,1)S(1)}, u32[]{:S(2)}, u32[]{:S(2)}) async-start(bf16[32,4,16,128]{3,2,1,0:T(8,128)(2,1)} %bitcast.11), calls=%async_computation.2 | async-start | bytes 1048576 | tf_op jit(solution)/shard_map/all_to_all | solution.py:242
  80.0 0.2 multiply_reduce_fusion
  80.2 17.7 %all-to-all-done.2 = bf16[32,4,16,128]{3,2,1,0:T(8,128)(2,1)S(1)} async-done(((bf16[32,4,16,128]{3,2,1,0:T(8,128)(2,1)}), bf16[32,4,16,128]{3,2,1,0:T(8,128)(2,1)S(1)}, u32[]{:S(2)}, u32[]{:S(2)}) %all-to-all-start.2) | async-done | bytes 524320 | tf_op jit(solution)/shard_map/all_to_all | solution.py:242
  97.9 0.1 convert_reduce_fusion
  98.0 0.7 bitcast_multiply_fusion
  (16 shorter events, 0.1 us)
Async XLA Ops:
  3.0 16.0 %all-to-all-start = ((bf16[8,64,128]{2,1,0:T(8,128)(2,1)}), bf16[8,64,128]{2,1,0:T(8,128)(2,1)S(1)}, u32[]{:S(2)}, u32[]{:S(2)}) async-start(bf16[8,64,128]{2,1,0:T(8,128)(2,1)} %get-tuple-element.18), calls=%async_computation | async-start | bytes 262144 | tf_op jit(solution)/shard_map/all_to_all | solution.py:214
  11.6 1.7 %collective-permute-start = (bf16[4,2,128,128]{3,2,1,0:T(8,128)(2,1)}, bf16[4,2,128,128]{3,2,1,0:T(8,128)(2,1)S(1)}, u32[]{:S(2)}, u32[]{:S(2)}) collective-permute-start(bf16[4,2,128,128]{3,2,1,0:T(8,128)(2,1)} %get-tuple-element.17), channel_id=1, source_target_pairs={{0,32},{32,0},{1,33},{33,1},{2,34},{34,2},{3,35},{35,3},{4,36},{36... | collective-permute-start | bytes 786440 | tf_op jit(solution)/shard_map/ppermute | solution.py:207
  19.0 19.9 %all-to-all-start.1 = ((bf16[8,2,128,128]{3,2,1,0:T(8,128)(2,1)}), bf16[8,2,128,128]{3,2,1,0:T(8,128)(2,1)S(1)}, u32[]{:S(2)}, u32[]{:S(2)}) async-start(bf16[8,2,128,128]{3,2,1,0:T(8,128)(2,1)} %fusion.1), calls=%async_computation.1 | async-start | bytes 1048576 | tf_op jit(solution)/shard_map/all_to_all | solution.py:224
  24.1 6.7 %collective-permute-start.3 = (bf16[8,64,128]{2,1,0:T(8,128)(2,1)S(1)}, bf16[8,64,128]{2,1,0:T(8,128)(2,1)S(1)}, u32[]{:S(2)}, u32[]{:S(2)}) collective-permute-start(bf16[8,64,128]{2,1,0:T(8,128)(2,1)S(1)} %all-to-all-done), channel_id=1, source_target_pairs={{0,3},{1,0},{2,1},{3,2},{4,7},{5,4},{6,5},{7,6},{8,11},{9,8},{10,9... | collective-permute-start | bytes 393224 | tf_op jit(solution)/shard_map/ppermute | solution.py:203
  26.8 6.6 %collective-permute-start.2 = (bf16[8,64,128]{2,1,0:T(8,128)(2,1)S(1)}, bf16[8,64,128]{2,1,0:T(8,128)(2,1)S(1)}, u32[]{:S(2)}, u32[]{:S(2)}) collective-permute-start(bf16[8,64,128]{2,1,0:T(8,128)(2,1)S(1)} %all-to-all-done), channel_id=1, source_target_pairs={{0,2},{1,3},{2,0},{3,1},{4,6},{5,7},{6,4},{7,5},{8,10},{9,11},{10,... | collective-permute-start | bytes 393224 | tf_op jit(solution)/shard_map/ppermute | solution.py:203
  27.6 7.1 %collective-permute-start.1 = (bf16[8,64,128]{2,1,0:T(8,128)(2,1)S(1)}, bf16[8,64,128]{2,1,0:T(8,128)(2,1)S(1)}, u32[]{:S(2)}, u32[]{:S(2)}) collective-permute-start(bf16[8,64,128]{2,1,0:T(8,128)(2,1)S(1)} %all-to-all-done), channel_id=1, source_target_pairs={{0,1},{1,2},{2,3},{3,0},{4,5},{5,6},{6,7},{7,4},{8,9},{9,10},{10,1... | collective-permute-start | bytes 393224 | tf_op jit(solution)/shard_map/ppermute | solution.py:203
  34.8 24.6 %copy-start = (s32[32,4]{0,1:T(4,128)S(1)}, s32[32,4]{0,1:T(4,128)}, u32[]{:S(2)}) copy-start(s32[32,4]{0,1:T(4,128)} %param.8) | copy-start | bytes 1540
  34.8 24.6 %copy-start.1 = (s32[32,4]{0,1:T(4,128)S(1)}, s32[32,4]{0,1:T(4,128)}, u32[]{:S(2)}) copy-start(s32[32,4]{0,1:T(4,128)} %param.7) | copy-start | bytes 1540
  34.8 11.6 %collective-permute-start.5 = (bf16[8,4,64,128]{3,2,1,0:T(8,128)(2,1)S(1)}, bf16[8,4,64,128]{3,2,1,0:T(8,128)(2,1)S(1)}, u32[]{:S(2)}, u32[]{:S(2)}) collective-permute-start(bf16[8,4,64,128]{3,2,1,0:T(8,128)(2,1)S(1)} %pad_maximum_fusion.c0), channel_id=1, source_target_pairs={{0,192},{64,0},{128,64},{192,128},{1,193},{65,1},{129,65},{193,129... | collective-permute-start | bytes 1572872 | tf_op jit(solution)/shard_map/ppermute | solution.py:203
  37.9 12.1 %collective-permute-start.4 = (bf16[8,4,64,128]{3,2,1,0:T(8,128)(2,1)S(1)}, bf16[8,4,64,128]{3,2,1,0:T(8,128)(2,1)S(1)}, u32[]{:S(2)}, u32[]{:S(2)}) collective-permute-start(bf16[8,4,64,128]{3,2,1,0:T(8,128)(2,1)S(1)} %pad_maximum_fusion.c0), channel_id=1, source_target_pairs={{0,64},{64,128},{128,192},{192,0},{1,65},{65,129},{129,193},{193,1... | collective-permute-start | bytes 1572872 | tf_op jit(solution)/shard_map/ppermute | solution.py:203
  39.0 11.2 %collective-permute-start.11 = (bf16[8,2,128,128]{3,2,1,0:T(8,128)(2,1)S(1)}, bf16[8,2,128,128]{3,2,1,0:T(8,128)(2,1)S(1)}, u32[]{:S(2)}, u32[]{:S(2)}) collective-permute-start(bf16[8,2,128,128]{3,2,1,0:T(8,128)(2,1)S(1)} %all-to-all-done.1.own0), channel_id=1, source_target_pairs={{0,3},{1,0},{2,1},{3,2},{4,7},{5,4},{6,5},{7,6},{8,11},{9,8},{10,9... | collective-permute-start | bytes 1572872 | tf_op jit(solution)/shard_map/ppermute | solution.py:203
  41.7 10.5 %collective-permute-start.9 = (bf16[8,2,128,128]{3,2,1,0:T(8,128)(2,1)S(1)}, bf16[8,2,128,128]{3,2,1,0:T(8,128)(2,1)S(1)}, u32[]{:S(2)}, u32[]{:S(2)}) collective-permute-start(bf16[8,2,128,128]{3,2,1,0:T(8,128)(2,1)S(1)} %all-to-all-done.1.own0), channel_id=1, source_target_pairs={{0,1},{1,2},{2,3},{3,0},{4,5},{5,6},{6,7},{7,4},{8,9},{9,10},{10,1... | collective-permute-start | bytes 1572872 | tf_op jit(solution)/shard_map/ppermute | solution.py:203
  41.7 17.6 %collective-permute-start.8 = (bf16[8,2,128,128]{3,2,1,0:T(8,128)(2,1)S(1)}, bf16[8,2,128,128]{3,2,1,0:T(8,128)(2,1)S(1)}, u32[]{:S(2)}, u32[]{:S(2)}) collective-permute-start(bf16[8,2,128,128]{3,2,1,0:T(8,128)(2,1)S(1)} %all-to-all-done.1.own0), channel_id=1, source_target_pairs={{0,32},{32,0},{1,33},{33,1},{2,34},{34,2},{3,35},{35,3},{4,36},{36... | collective-permute-start | bytes 1572872 | tf_op jit(solution)/shard_map/ppermute | solution.py:207
  46.4 7.5 %collective-permute-start.7 = (bf16[4,4,64,128]{3,2,1,0:T(8,128)(2,1)S(1)}, bf16[4,4,64,128]{3,2,1,0:T(8,128)(2,1)S(1)}, u32[]{:S(2)}, u32[]{:S(2)}) collective-permute-start(bf16[4,4,64,128]{3,2,1,0:T(8,128)(2,1)S(1)} %slice.17), channel_id=1, source_target_pairs={{0,192},{64,0},{128,64},{192,128},{1,193},{65,1},{129,65},{193,129... | collective-permute-start | bytes 786440 | tf_op jit(solution)/shard_map/ppermute | solution.py:203
  50.0 7.7 %collective-permute-start.6 = (bf16[4,4,64,128]{3,2,1,0:T(8,128)(2,1)S(1)}, bf16[4,4,64,128]{3,2,1,0:T(8,128)(2,1)S(1)}, u32[]{:S(2)}, u32[]{:S(2)}) collective-permute-start(bf16[4,4,64,128]{3,2,1,0:T(8,128)(2,1)S(1)} %slice.16), channel_id=1, source_target_pairs={{0,64},{64,128},{128,192},{192,0},{1,65},{65,129},{129,193},{193,1... | collective-permute-start | bytes 786440 | tf_op jit(solution)/shard_map/ppermute | solution.py:203
  50.2 11.1 %collective-permute-start.12 = (bf16[4,2,128,128]{3,2,1,0:T(8,128)(2,1)S(1)}, bf16[4,2,128,128]{3,2,1,0:T(8,128)(2,1)S(1)}, u32[]{:S(2)}, u32[]{:S(2)}) collective-permute-start(bf16[4,2,128,128]{3,2,1,0:T(8,128)(2,1)S(1)} %slice.19), channel_id=1, source_target_pairs={{0,3},{1,0},{2,1},{3,2},{4,7},{5,4},{6,5},{7,6},{8,11},{9,8},{10,9... | collective-permute-start | bytes 786440 | tf_op jit(solution)/shard_map/ppermute | solution.py:203
  52.2 9.0 %collective-permute-start.10 = (bf16[4,2,128,128]{3,2,1,0:T(8,128)(2,1)S(1)}, bf16[4,2,128,128]{3,2,1,0:T(8,128)(2,1)S(1)}, u32[]{:S(2)}, u32[]{:S(2)}) collective-permute-start(bf16[4,2,128,128]{3,2,1,0:T(8,128)(2,1)S(1)} %slice.18), channel_id=1, source_target_pairs={{0,1},{1,2},{2,3},{3,0},{4,5},{5,6},{6,7},{7,4},{8,9},{9,10},{10,1... | collective-permute-start | bytes 786440 | tf_op jit(solution)/shard_map/ppermute | solution.py:203
  53.9 9.5 %collective-permute-start.14 = (bf16[8,2,128,128]{3,2,1,0:T(8,128)(2,1)S(1)}, bf16[8,2,128,128]{3,2,1,0:T(8,128)(2,1)S(1)}, u32[]{:S(2)}, u32[]{:S(2)}) collective-permute-start(bf16[8,2,128,128]{3,2,1,0:T(8,128)(2,1)S(1)} %collective-permute-done.11.own_l), channel_id=1, source_target_pairs={{0,32},{32,0},{1,33},{33,1},{2,34},{34,2},{3,35},{35,3},{4,36},{36... | collective-permute-start | bytes 1572872 | tf_op jit(solution)/shard_map/ppermute | solution.py:207
  57.7 5.7 %collective-permute-start.13 = (bf16[8,2,128,128]{3,2,1,0:T(8,128)(2,1)S(1)}, bf16[8,2,128,128]{3,2,1,0:T(8,128)(2,1)S(1)}, u32[]{:S(2)}, u32[]{:S(2)}) collective-permute-start(bf16[8,2,128,128]{3,2,1,0:T(8,128)(2,1)S(1)} %collective-permute-done.9.own_r), channel_id=1, source_target_pairs={{0,32},{32,0},{1,33},{33,1},{2,34},{34,2},{3,35},{35,3},{4,36},{36... | collective-permute-start | bytes 1572872 | tf_op jit(solution)/shard_map/ppermute | solution.py:207
  61.3 1.8 %collective-permute-start.15 = (bf16[4,2,128,128]{3,2,1,0:T(8,128)(2,1)S(1)}, bf16[4,2,128,128]{3,2,1,0:T(8,128)(2,1)S(1)}, u32[]{:S(2)}, u32[]{:S(2)}) collective-permute-start(bf16[4,2,128,128]{3,2,1,0:T(8,128)(2,1)S(1)} %collective-permute-done.10.own_r2), channel_id=1, source_target_pairs={{0,32},{32,0},{1,33},{33,1},{2,34},{34,2},{3,35},{35,3},{4,36},{36... | collective-permute-start | bytes 786440 | tf_op jit(solution)/shard_map/ppermute | solution.py:207
  61.9 1.5 %collective-permute-start.16 = (bf16[4,2,128,128]{3,2,1,0:T(8,128)(2,1)S(1)}, bf16[4,2,128,128]{3,2,1,0:T(8,128)(2,1)S(1)}, u32[]{:S(2)}, u32[]{:S(2)}) collective-permute-start(bf16[4,2,128,128]{3,2,1,0:T(8,128)(2,1)S(1)} %collective-permute-done.12.own_l2), channel_id=1, source_target_pairs={{0,32},{32,0},{1,33},{33,1},{2,34},{34,2},{3,35},{35,3},{4,36},{36... | collective-permute-start | bytes 786440 | tf_op jit(solution)/shard_map/ppermute | solution.py:207
  68.6 2.8 %collective-permute-start.17 = (f32[4,8,4,16,128]{4,3,2,1,0:T(8,128)S(1)}, f32[4,8,4,16,128]{4,3,2,1,0:T(8,128)S(1)}, u32[]{:S(2)}, u32[]{:S(2)}) collective-permute-start(f32[4,8,4,16,128]{4,3,2,1,0:T(8,128)S(1)} %get-tuple-element.26), channel_id=1, source_target_pairs={{0,32},{32,0},{1,33},{33,1},{2,34},{34,2},{3,35},{35,3},{4,36},{36... | collective-permute-start | bytes 3145736 | tf_op jit(solution)/shard_map/ppermute | solution.py:207
  72.3 25.6 %all-to-all-start.2 = ((bf16[32,4,16,128]{3,2,1,0:T(8,128)(2,1)}), bf16[32,4,16,128]{3,2,1,0:T(8,128)(2,1)S(1)}, u32[]{:S(2)}, u32[]{:S(2)}) async-start(bf16[32,4,16,128]{3,2,1,0:T(8,128)(2,1)} %bitcast.11), calls=%async_computation.2 | async-start | bytes 1048576 | tf_op jit(solution)/shard_map/all_to_all | solution.py:242

commit v11 on v10

--- a/solution.py
+++ b/solution.py
@@ -176,17 +176,17 @@
             far = pl.multiple_of(y * 2 * ROWS + (1 - core) * ROWS, ROWS)
             for slot in range(SLOTS):
                 keep[y, zp, slot] = block[pl.ds(near, ROWS), slot * TS:(slot + 1) * TS]
-                send[y, zp, slot] = block[pl.ds(far, ROWS), slot * TS:(slot + 1) * TS]
+                send[y, zp, slot] = block[pl.ds(far, ROWS), slot * TS:(slot + 1) * TS].astype(BF)
         return carry
 
     lax.fori_loop(0, NZ, gram, 0, unroll=True)
 
 
 def exchange(pair_tiles, pair_live, *pieces):
-    shape = jax.ShapeDtypeStruct((NY, NZ, SLOTS, ROWS, TS), F32)
+    shape = (NY, NZ, SLOTS, ROWS, TS)
     return pl.pallas_call(
         main_kernel,
-        out_shape=(shape, shape),
+        out_shape=(jax.ShapeDtypeStruct(shape, F32), jax.ShapeDtypeStruct(shape, BF)),
         in_specs=[SMEM] * 2 + [VMEM] * len(pieces),
         out_specs=(VMEM, VMEM),
         scratch_shapes=[
@@ -238,7 +238,7 @@
         pair_tiles.T, pair_live.T, dense,
         column, own_r, own_l, own_r2, own_l2, oth_r, oth_l, oth_r2, oth_l2,
     )
-    partial = (keep + swap(send)).astype(BF).reshape(NY * NZ, SLOTS, ROWS, TS)
+    partial = (keep + swap(send).astype(F32)).astype(BF).reshape(NY * NZ, SLOTS, ROWS, TS)
     parts = lax.all_to_all(partial, ("y", "z"), split_axis=0, concat_axis=0, tiled=True).astype(F32)
     flags = lax.dynamic_index_in_dim(pair_live, tile, 0, keepdims=False).astype(F32) * SCALE
     return (jnp.sum(parts, axis=0) * flags[:, None, None])[None]

time: 99.2 us -> 99.3 us (level)
  starting transfers between devices: 38.6 us -> 43.1 us
  waiting for transfers between devices: 42.7 us -> 38.4 us
    ppermute x11, waiting for transfers between devices: 16.1 us -> 11 us  [shift(): lax.ppermute(value, axis, [(i, (i + by) % size) for i in range(size)])]
    all_to_all x1, starting transfers between devices: 7.63 us -> 9.8 us  [shards(): lax.all_to_all(partial, ('y', 'z'), split_axis=0, concat_axis=0, tiled=True)]
    ppermute x11, starting transfers between devices: 16.2 us -> 18.4 us  [shift(): lax.ppermute(value, axis, [(i, (i + by) % size) for i in range(size)])]
    all_to_all x1, waiting for transfers between devices: 3.7 us -> 4.72 us  [shards(): lax.all_to_all(coeffs, 'z', split_axis=0, concat_axis=0, tiled=True)]
  transfers between devices with their start and end apart: 21 -> 21, of which waited for: 13 -> 10; matrix products, arithmetic and copies ran while one was open for 4% -> 4% of each run, Pallas kernels for 4% -> 4%
where the time goes in v11:
time: 99.3 us; the launch traced here: 98.8 us
  starting transfers between devices  43.1 us (43%)
  waiting for transfers between devices  38.4 us (39%)
  Pallas kernels  11.7 us (12%)
  other arithmetic  5.43 us (5%)
    ppermute x11, starting transfers between devices, shift(): lax.ppermute(value, axis, [(i, (i + by) % size) for i in range(size)])  18.4 us
    all_to_all x1, waiting for transfers between devices, shards(): lax.all_to_all(partial, ('y', 'z'), split_axis=0, concat_axis=0, tiled=True)  18 us
    ppermute x11, waiting for transfers between devices, shift(): lax.ppermute(value, axis, [(i, (i + by) % size) for i in range(size)])  11 us
    all_to_all x1, starting transfers between devices, shards(): lax.all_to_all(partial, ('y', 'z'), split_axis=0, concat_axis=0, tiled=True)  9.8 us
    all_to_all x1, starting transfers between devices, shards(): lax.all_to_all(coeffs, 'z', split_axis=0, concat_axis=0, tiled=True)  8.58 us
    pallas_call x1, Pallas kernels, exchange(): pl.pallas_call(main_kernel, out_shape=(jax.ShapeDtypeStruct(shape, F32),...  5.18 us
    all_to_all x1, starting transfers between devices, shards(): own0 = lax.all_to_all(by_aux, 'z', split_axis=0, concat_axis=0, tiled=True)  4.95 us
    all_to_all x1, waiting for transfers between devices, shards(): lax.all_to_all(coeffs, 'z', split_axis=0, concat_axis=0, tiled=True)  4.72 us
  transfers between devices with their start and end apart: 21, of which 10 were waited for; matrix products, arithmetic and copies ran while one was open for 4% of the time, Pallas kernels for 4%

profile of v11, /device:TPU:32, one launch (start us, length us, event | category | flops | bytes accessed | tf_op | source)
XLA Modules:
  0.0 98.8 jit_solution(4841386997517728718)
XLA Ops:
  0.0 3.0 %prep.1 = (bf16[8,64,128]{2,1,0:T(8,128)(2,1)}, bf16[4,2,128,128]{3,2,1,0:T(8,128)(2,1)}, bf16[4,2,128,128]{3,2,1,0:T(8,128)(2,1)}) custom-call(s32[8,32]{1,0:T(8,128)} %bitcast.26, bf16[128,1024]{1,0:T(8,128)(2,1)} %orb.1, bf16[2048,128]{1,0:T(8,128)(2,1)} %bitcast.21), custom_call_target="tpu_custom_call" | custom-call | tf_op jit(solution)/shard_map/prep/pallas_call | solution.py:69
  3.0 0.1 collective-permute-start
  3.1 8.6 %all-to-all-start = ((bf16[8,64,128]{2,1,0:T(8,128)(2,1)}), bf16[8,64,128]{2,1,0:T(8,128)(2,1)S(1)}, u32[]{:S(2)}, u32[]{:S(2)}) async-start(bf16[8,64,128]{2,1,0:T(8,128)(2,1)} %get-tuple-element.18), calls=%async_computation | async-start | bytes 262144 | tf_op jit(solution)/shard_map/all_to_all | solution.py:214
  11.7 0.7 reduce_window_sum.11
  12.4 0.7 broadcast_compare_fusion
  13.1 2.0 %fusion.1 = bf16[8,2,128,128]{3,2,1,0:T(8,128)(2,1)} fusion(s32[]{:T(128)S(6)} %select_n.11, bf16[4,2,128,128]{3,2,1,0:T(8,128)(2,1)} %get-tuple-element.16, bf16[4,2,128,128]{3,2,1,0:T(8,128)(2,1)S(1)} %collective-permute-done), kind=kLoop, calls=%fused_computation.6 | loop fusion | flops 524288 | bytes 1048580 | tf_op jit(solution)/shard_map/concatenate | solution.py:221
  15.1 4.7 %all-to-all-done = bf16[8,64,128]{2,1,0:T(8,128)(2,1)S(1)} async-done(((bf16[8,64,128]{2,1,0:T(8,128)(2,1)}), bf16[8,64,128]{2,1,0:T(8,128)(2,1)S(1)}, u32[]{:S(2)}, u32[]{:S(2)}) %all-to-all-start) | async-done | bytes 131104 | tf_op jit(solution)/shard_map/all_to_all | solution.py:214
  19.9 4.9 %all-to-all-start.1 = ((bf16[8,2,128,128]{3,2,1,0:T(8,128)(2,1)}), bf16[8,2,128,128]{3,2,1,0:T(8,128)(2,1)S(1)}, u32[]{:S(2)}, u32[]{:S(2)}) async-start(bf16[8,2,128,128]{3,2,1,0:T(8,128)(2,1)} %fusion.1), calls=%async_computation.1 | async-start | bytes 1048576 | tf_op jit(solution)/shard_map/all_to_all | solution.py:224
  24.8 2.8 %collective-permute-start.3 = (bf16[8,64,128]{2,1,0:T(8,128)(2,1)S(1)}, bf16[8,64,128]{2,1,0:T(8,128)(2,1)S(1)}, u32[]{:S(2)}, u32[]{:S(2)}) collective-permute-start(bf16[8,64,128]{2,1,0:T(8,128)(2,1)S(1)} %all-to-all-done), channel_id=1, source_target_pairs={{0,3},{1,0},{2,1},{3,2},{4,7},{5,4},{6,5},{7,6},{8,11},{9,8},{10,9... | collective-permute-start | bytes 393224 | tf_op jit(solution)/shard_map/ppermute | solution.py:203
  27.6 0.0 collective-permute-start.1
  27.6 2.3 %collective-permute-start.2 = (bf16[8,64,128]{2,1,0:T(8,128)(2,1)S(1)}, bf16[8,64,128]{2,1,0:T(8,128)(2,1)S(1)}, u32[]{:S(2)}, u32[]{:S(2)}) collective-permute-start(bf16[8,64,128]{2,1,0:T(8,128)(2,1)S(1)} %all-to-all-done), channel_id=1, source_target_pairs={{0,2},{1,3},{2,0},{3,1},{4,6},{5,7},{6,4},{7,5},{8,10},{9,11},{10,... | collective-permute-start | bytes 393224 | tf_op jit(solution)/shard_map/ppermute | solution.py:203
  29.8 1.6 %collective-permute-done.3 = bf16[8,64,128]{2,1,0:T(8,128)(2,1)S(1)} collective-permute-done((bf16[8,64,128]{2,1,0:T(8,128)(2,1)S(1)}, bf16[8,64,128]{2,1,0:T(8,128)(2,1)S(1)}, u32[]{:S(2)}, u32[]{:S(2)}) %collective-permute-start.3) | collective-permute-done | bytes 131104 | tf_op jit(solution)/shard_map/ppermute | solution.py:203
  31.5 3.9 %collective-permute-done.1 = bf16[8,64,128]{2,1,0:T(8,128)(2,1)S(1)} collective-permute-done((bf16[8,64,128]{2,1,0:T(8,128)(2,1)S(1)}, bf16[8,64,128]{2,1,0:T(8,128)(2,1)S(1)}, u32[]{:S(2)}, u32[]{:S(2)}) %collective-permute-start.1) | collective-permute-done | bytes 131104 | tf_op jit(solution)/shard_map/ppermute | solution.py:203
  35.4 0.0 collective-permute-done.2
  35.4 0.1 pad_maximum_fusion.c0
  35.5 0.0 copy-start
  35.5 0.0 copy-start.1
  35.5 1.6 %collective-permute-start.4 = (bf16[8,4,64,128]{3,2,1,0:T(8,128)(2,1)S(1)}, bf16[8,4,64,128]{3,2,1,0:T(8,128)(2,1)S(1)}, u32[]{:S(2)}, u32[]{:S(2)}) collective-permute-start(bf16[8,4,64,128]{3,2,1,0:T(8,128)(2,1)S(1)} %pad_maximum_fusion.c0), channel_id=1, source_target_pairs={{0,64},{64,128},{128,192},{192,0},{1,65},{65,129},{129,193},{193,1... | collective-permute-start | bytes 1572872 | tf_op jit(solution)/shard_map/ppermute | solution.py:203
  37.2 1.7 %collective-permute-start.5 = (bf16[8,4,64,128]{3,2,1,0:T(8,128)(2,1)S(1)}, bf16[8,4,64,128]{3,2,1,0:T(8,128)(2,1)S(1)}, u32[]{:S(2)}, u32[]{:S(2)}) collective-permute-start(bf16[8,4,64,128]{3,2,1,0:T(8,128)(2,1)S(1)} %pad_maximum_fusion.c0), channel_id=1, source_target_pairs={{0,192},{64,0},{128,64},{192,128},{1,193},{65,1},{129,65},{193,129... | collective-permute-start | bytes 1572872 | tf_op jit(solution)/shard_map/ppermute | solution.py:203
  38.8 1.5 %all-to-all-done.1.own0 = bf16[8,2,128,128]{3,2,1,0:T(8,128)(2,1)S(1)} async-done(((bf16[8,2,128,128]{3,2,1,0:T(8,128)(2,1)}), bf16[8,2,128,128]{3,2,1,0:T(8,128)(2,1)S(1)}, u32[]{:S(2)}, u32[]{:S(2)}) %all-to-all-start.1) | async-done | bytes 524320 | tf_op jit(solution)/shard_map/all_to_all | solution.py:224
  40.3 1.5 %collective-permute-start.9 = (bf16[8,2,128,128]{3,2,1,0:T(8,128)(2,1)S(1)}, bf16[8,2,128,128]{3,2,1,0:T(8,128)(2,1)S(1)}, u32[]{:S(2)}, u32[]{:S(2)}) collective-permute-start(bf16[8,2,128,128]{3,2,1,0:T(8,128)(2,1)S(1)} %all-to-all-done.1.own0), channel_id=1, source_target_pairs={{0,1},{1,2},{2,3},{3,0},{4,5},{5,6},{6,7},{7,4},{8,9},{9,10},{10,1... | collective-permute-start | bytes 1572872 | tf_op jit(solution)/shard_map/ppermute | solution.py:203
  41.8 1.8 %collective-permute-start.11 = (bf16[8,2,128,128]{3,2,1,0:T(8,128)(2,1)S(1)}, bf16[8,2,128,128]{3,2,1,0:T(8,128)(2,1)S(1)}, u32[]{:S(2)}, u32[]{:S(2)}) collective-permute-start(bf16[8,2,128,128]{3,2,1,0:T(8,128)(2,1)S(1)} %all-to-all-done.1.own0), channel_id=1, source_target_pairs={{0,3},{1,0},{2,1},{3,2},{4,7},{5,4},{6,5},{7,6},{8,11},{9,8},{10,9... | collective-permute-start | bytes 1572872 | tf_op jit(solution)/shard_map/ppermute | solution.py:203
  43.5 4.6 %collective-permute-done.4.c_u = bf16[8,4,64,128]{3,2,1,0:T(8,128)(2,1)S(1)} collective-permute-done((bf16[8,4,64,128]{3,2,1,0:T(8,128)(2,1)S(1)}, bf16[8,4,64,128]{3,2,1,0:T(8,128)(2,1)S(1)}, u32[]{:S(2)}, u32[]{:S(2)}) %collective-permute-start.4) | collective-permute-done | bytes 524320 | tf_op jit(solution)/shard_map/ppermute | solution.py:203
  48.2 0.5 collective-permute-start.6
  48.7 0.0 collective-permute-done.5.c_d
  48.7 2.9 %collective-permute-start.7 = (bf16[4,4,64,128]{3,2,1,0:T(8,128)(2,1)S(1)}, bf16[4,4,64,128]{3,2,1,0:T(8,128)(2,1)S(1)}, u32[]{:S(2)}, u32[]{:S(2)}) collective-permute-start(bf16[4,4,64,128]{3,2,1,0:T(8,128)(2,1)S(1)} %slice.17), channel_id=1, source_target_pairs={{0,192},{64,0},{128,64},{192,128},{1,193},{65,1},{129,65},{193,129... | collective-permute-start | bytes 786440 | tf_op jit(solution)/shard_map/ppermute | solution.py:203
  51.6 0.0 collective-permute-done.9.own_r
  51.6 0.6 collective-permute-start.10
  52.3 2.8 %collective-permute-start.12 = (bf16[4,2,128,128]{3,2,1,0:T(8,128)(2,1)S(1)}, bf16[4,2,128,128]{3,2,1,0:T(8,128)(2,1)S(1)}, u32[]{:S(2)}, u32[]{:S(2)}) collective-permute-start(bf16[4,2,128,128]{3,2,1,0:T(8,128)(2,1)S(1)} %slice.19), channel_id=1, source_target_pairs={{0,3},{1,0},{2,1},{3,2},{4,7},{5,4},{6,5},{7,6},{8,11},{9,8},{10,9... | collective-permute-start | bytes 786440 | tf_op jit(solution)/shard_map/ppermute | solution.py:203
  55.1 0.8 collective-permute-done.6.c_u2
  55.9 0.0 collective-permute-start.13
  55.9 0.0 collective-permute-done.7.c_d2
  55.9 0.5 collective-permute-start.14
  56.4 1.6 %rebuild.1.dense = bf16[32,512,128]{2,1,0:T(8,128)(2,1)S(1)} custom-call(s32[4,32]{1,0:T(4,128)S(1)} %select_reduce_fusion.occ_index, bf16[8,4,64,128]{3,2,1,0:T(8,128)(2,1)S(1)} %pad_maximum_fusion.c0, bf16[8,4,64,128]{3,2,1,0:T(8,128)(2,1)S(1)} %collective-permute-done.4.c_u, bf16[8,4,64,128]{3,2,1,0:T(8,128)(2,1)S(1)} %collective-permute-done.5.c_d, ...), custom_call_target="tpu_custom_call" | custom-call | bytes 6291456 | tf_op jit(solution)/shard_map/rebuild/pallas_call | solution.py:107
  58.0 1.9 %own_column.1.column = bf16[8,512,128]{2,1,0:T(8,128)(2,1)S(1)} custom-call(s32[4,32]{1,0:T(4,128)S(1)} %bitcast.19, s32[4,32]{1,0:T(4,128)S(1)} %bitcast.17, bf16[32,512,128]{2,1,0:T(8,128)(2,1)S(1)} %rebuild.1.dense, bf16[8,2,128,128]{3,2,1,0:T(8,128)(2,1)S(1)} %all-to-all-done.1.own0, bf16[8,2,128,128]{3,2,1,0:T(8,128)(2,1)S(1)} %collective-permute-done.8.oth0), custom_call_target="tpu_custom_call" | custom-call | tf_op jit(solution)/shard_map/own_column/pallas_call | solution.py:141
  59.9 0.1 collective-permute-start.15
  60.0 0.5 collective-permute-start.16
  60.5 1.0 %collective-permute-done.15.oth_r2 = bf16[4,2,128,128]{3,2,1,0:T(8,128)(2,1)S(1)} collective-permute-done((bf16[4,2,128,128]{3,2,1,0:T(8,128)(2,1)S(1)}, bf16[4,2,128,128]{3,2,1,0:T(8,128)(2,1)S(1)}, u32[]{:S(2)}, u32[]{:S(2)}) %collective-permute-start.15) | collective-permute-done | bytes 262176 | tf_op jit(solution)/shard_map/ppermute | solution.py:207
  61.6 0.4 collective-permute-done.16.oth_l2
  61.9 5.2 %exchange.1 = (f32[4,8,4,16,128]{4,3,2,1,0:T(8,128)S(1)}, bf16[4,8,4,16,128]{4,3,2,1,0:T(8,128)(2,1)S(1)}) custom-call(s32[4,32]{1,0:T(4,128)S(1)} %bitcast.20, s32[4,32]{1,0:T(4,128)S(1)} %bitcast.18, bf16[32,512,128]{2,1,0:T(8,128)(2,1)S(1)} %rebuild.1.dense, bf16[8,512,128]{2,1,0:T(8,128)(2,1)S(1)} %own_column.1.column, ...), custom_call_target="tpu_custom_call" | custom-call | flops 2700000000 | bytes 10485760 | tf_op jit(solution)/shard_map/exchange/pallas_call | solution.py:187
  67.1 0.2 collective-permute-start.17
  67.3 1.8 %collective-permute-done.17 = bf16[4,8,4,16,128]{4,3,2,1,0:T(8,128)(2,1)S(1)} collective-permute-done((bf16[4,8,4,16,128]{4,3,2,1,0:T(8,128)(2,1)S(1)}, bf16[4,8,4,16,128]{4,3,2,1,0:T(8,128)(2,1)S(1)}, u32[]{:S(2)}, u32[]{:S(2)}) %collective-permute-start.17) | collective-permute-done | bytes 524320 | tf_op jit(solution)/shard_map/ppermute | solution.py:207
  69.1 1.0 add_convert_fusion
  70.1 9.8 %all-to-all-start.2 = ((bf16[32,4,16,128]{3,2,1,0:T(8,128)(2,1)}), bf16[32,4,16,128]{3,2,1,0:T(8,128)(2,1)S(1)}, u32[]{:S(2)}, u32[]{:S(2)}) async-start(bf16[32,4,16,128]{3,2,1,0:T(8,128)(2,1)} %bitcast.11), calls=%async_computation.2 | async-start | bytes 1048576 | tf_op jit(solution)/shard_map/all_to_all | solution.py:242
  79.9 0.2 multiply_reduce_fusion
  80.1 18.0 %all-to-all-done.2 = bf16[32,4,16,128]{3,2,1,0:T(8,128)(2,1)S(1)} async-done(((bf16[32,4,16,128]{3,2,1,0:T(8,128)(2,1)}), bf16[32,4,16,128]{3,2,1,0:T(8,128)(2,1)S(1)}, u32[]{:S(2)}, u32[]{:S(2)}) %all-to-all-start.2) | async-done | bytes 524320 | tf_op jit(solution)/shard_map/all_to_all | solution.py:242
  98.1 0.1 convert_reduce_fusion
  98.1 0.7 bitcast_multiply_fusion
  (16 shorter events, 0.1 us)
Async XLA Ops:
  3.0 10.1 %collective-permute-start = (bf16[4,2,128,128]{3,2,1,0:T(8,128)(2,1)}, bf16[4,2,128,128]{3,2,1,0:T(8,128)(2,1)S(1)}, u32[]{:S(2)}, u32[]{:S(2)}) collective-permute-start(bf16[4,2,128,128]{3,2,1,0:T(8,128)(2,1)} %get-tuple-element.17), channel_id=1, source_target_pairs={{0,32},{32,0},{1,33},{33,1},{2,34},{34,2},{3,35},{35,3},{4,36},{36... | collective-permute-start | bytes 786440 | tf_op jit(solution)/shard_map/ppermute | solution.py:207
  3.1 16.8 %all-to-all-start = ((bf16[8,64,128]{2,1,0:T(8,128)(2,1)}), bf16[8,64,128]{2,1,0:T(8,128)(2,1)S(1)}, u32[]{:S(2)}, u32[]{:S(2)}) async-start(bf16[8,64,128]{2,1,0:T(8,128)(2,1)} %get-tuple-element.18), calls=%async_computation | async-start | bytes 262144 | tf_op jit(solution)/shard_map/all_to_all | solution.py:214
  19.9 20.4 %all-to-all-start.1 = ((bf16[8,2,128,128]{3,2,1,0:T(8,128)(2,1)}), bf16[8,2,128,128]{3,2,1,0:T(8,128)(2,1)S(1)}, u32[]{:S(2)}, u32[]{:S(2)}) async-start(bf16[8,2,128,128]{3,2,1,0:T(8,128)(2,1)} %fusion.1), calls=%async_computation.1 | async-start | bytes 1048576 | tf_op jit(solution)/shard_map/all_to_all | solution.py:224
  24.8 6.7 %collective-permute-start.3 = (bf16[8,64,128]{2,1,0:T(8,128)(2,1)S(1)}, bf16[8,64,128]{2,1,0:T(8,128)(2,1)S(1)}, u32[]{:S(2)}, u32[]{:S(2)}) collective-permute-start(bf16[8,64,128]{2,1,0:T(8,128)(2,1)S(1)} %all-to-all-done), channel_id=1, source_target_pairs={{0,3},{1,0},{2,1},{3,2},{4,7},{5,4},{6,5},{7,6},{8,11},{9,8},{10,9... | collective-permute-start | bytes 393224 | tf_op jit(solution)/shard_map/ppermute | solution.py:203
  27.6 7.8 %collective-permute-start.1 = (bf16[8,64,128]{2,1,0:T(8,128)(2,1)S(1)}, bf16[8,64,128]{2,1,0:T(8,128)(2,1)S(1)}, u32[]{:S(2)}, u32[]{:S(2)}) collective-permute-start(bf16[8,64,128]{2,1,0:T(8,128)(2,1)S(1)} %all-to-all-done), channel_id=1, source_target_pairs={{0,1},{1,2},{2,3},{3,0},{4,5},{5,6},{6,7},{7,4},{8,9},{9,10},{10,1... | collective-permute-start | bytes 393224 | tf_op jit(solution)/shard_map/ppermute | solution.py:203
  27.6 7.8 %collective-permute-start.2 = (bf16[8,64,128]{2,1,0:T(8,128)(2,1)S(1)}, bf16[8,64,128]{2,1,0:T(8,128)(2,1)S(1)}, u32[]{:S(2)}, u32[]{:S(2)}) collective-permute-start(bf16[8,64,128]{2,1,0:T(8,128)(2,1)S(1)} %all-to-all-done), channel_id=1, source_target_pairs={{0,2},{1,3},{2,0},{3,1},{4,6},{5,7},{6,4},{7,5},{8,10},{9,11},{10,... | collective-permute-start | bytes 393224 | tf_op jit(solution)/shard_map/ppermute | solution.py:203
  35.5 22.5 %copy-start = (s32[32,4]{0,1:T(4,128)S(1)}, s32[32,4]{0,1:T(4,128)}, u32[]{:S(2)}) copy-start(s32[32,4]{0,1:T(4,128)} %param.8) | copy-start | bytes 1540
  35.5 22.5 %copy-start.1 = (s32[32,4]{0,1:T(4,128)S(1)}, s32[32,4]{0,1:T(4,128)}, u32[]{:S(2)}) copy-start(s32[32,4]{0,1:T(4,128)} %param.7) | copy-start | bytes 1540
  35.5 12.7 %collective-permute-start.4 = (bf16[8,4,64,128]{3,2,1,0:T(8,128)(2,1)S(1)}, bf16[8,4,64,128]{3,2,1,0:T(8,128)(2,1)S(1)}, u32[]{:S(2)}, u32[]{:S(2)}) collective-permute-start(bf16[8,4,64,128]{3,2,1,0:T(8,128)(2,1)S(1)} %pad_maximum_fusion.c0), channel_id=1, source_target_pairs={{0,64},{64,128},{128,192},{192,0},{1,65},{65,129},{129,193},{193,1... | collective-permute-start | bytes 1572872 | tf_op jit(solution)/shard_map/ppermute | solution.py:203
  37.2 11.5 %collective-permute-start.5 = (bf16[8,4,64,128]{3,2,1,0:T(8,128)(2,1)S(1)}, bf16[8,4,64,128]{3,2,1,0:T(8,128)(2,1)S(1)}, u32[]{:S(2)}, u32[]{:S(2)}) collective-permute-start(bf16[8,4,64,128]{3,2,1,0:T(8,128)(2,1)S(1)} %pad_maximum_fusion.c0), channel_id=1, source_target_pairs={{0,192},{64,0},{128,64},{192,128},{1,193},{65,1},{129,65},{193,129... | collective-permute-start | bytes 1572872 | tf_op jit(solution)/shard_map/ppermute | solution.py:203
  40.3 11.3 %collective-permute-start.9 = (bf16[8,2,128,128]{3,2,1,0:T(8,128)(2,1)S(1)}, bf16[8,2,128,128]{3,2,1,0:T(8,128)(2,1)S(1)}, u32[]{:S(2)}, u32[]{:S(2)}) collective-permute-start(bf16[8,2,128,128]{3,2,1,0:T(8,128)(2,1)S(1)} %all-to-all-done.1.own0), channel_id=1, source_target_pairs={{0,1},{1,2},{2,3},{3,0},{4,5},{5,6},{6,7},{7,4},{8,9},{9,10},{10,1... | collective-permute-start | bytes 1572872 | tf_op jit(solution)/shard_map/ppermute | solution.py:203
  41.8 10.5 %collective-permute-start.11 = (bf16[8,2,128,128]{3,2,1,0:T(8,128)(2,1)S(1)}, bf16[8,2,128,128]{3,2,1,0:T(8,128)(2,1)S(1)}, u32[]{:S(2)}, u32[]{:S(2)}) collective-permute-start(bf16[8,2,128,128]{3,2,1,0:T(8,128)(2,1)S(1)} %all-to-all-done.1.own0), channel_id=1, source_target_pairs={{0,3},{1,0},{2,1},{3,2},{4,7},{5,4},{6,5},{7,6},{8,11},{9,8},{10,9... | collective-permute-start | bytes 1572872 | tf_op jit(solution)/shard_map/ppermute | solution.py:203
  43.5 14.5 %collective-permute-start.8 = (bf16[8,2,128,128]{3,2,1,0:T(8,128)(2,1)S(1)}, bf16[8,2,128,128]{3,2,1,0:T(8,128)(2,1)S(1)}, u32[]{:S(2)}, u32[]{:S(2)}) collective-permute-start(bf16[8,2,128,128]{3,2,1,0:T(8,128)(2,1)S(1)} %all-to-all-done.1.own0), channel_id=1, source_target_pairs={{0,32},{32,0},{1,33},{33,1},{2,34},{34,2},{3,35},{35,3},{4,36},{36... | collective-permute-start | bytes 1572872 | tf_op jit(solution)/shard_map/ppermute | solution.py:207
  48.2 7.7 %collective-permute-start.6 = (bf16[4,4,64,128]{3,2,1,0:T(8,128)(2,1)S(1)}, bf16[4,4,64,128]{3,2,1,0:T(8,128)(2,1)S(1)}, u32[]{:S(2)}, u32[]{:S(2)}) collective-permute-start(bf16[4,4,64,128]{3,2,1,0:T(8,128)(2,1)S(1)} %slice.16), channel_id=1, source_target_pairs={{0,64},{64,128},{128,192},{192,0},{1,65},{65,129},{129,193},{193,1... | collective-permute-start | bytes 786440 | tf_op jit(solution)/shard_map/ppermute | solution.py:203
  48.7 7.2 %collective-permute-start.7 = (bf16[4,4,64,128]{3,2,1,0:T(8,128)(2,1)S(1)}, bf16[4,4,64,128]{3,2,1,0:T(8,128)(2,1)S(1)}, u32[]{:S(2)}, u32[]{:S(2)}) collective-permute-start(bf16[4,4,64,128]{3,2,1,0:T(8,128)(2,1)S(1)} %slice.17), channel_id=1, source_target_pairs={{0,192},{64,0},{128,64},{192,128},{1,193},{65,1},{129,65},{193,129... | collective-permute-start | bytes 786440 | tf_op jit(solution)/shard_map/ppermute | solution.py:203
  51.6 8.3 %collective-permute-start.10 = (bf16[4,2,128,128]{3,2,1,0:T(8,128)(2,1)S(1)}, bf16[4,2,128,128]{3,2,1,0:T(8,128)(2,1)S(1)}, u32[]{:S(2)}, u32[]{:S(2)}) collective-permute-start(bf16[4,2,128,128]{3,2,1,0:T(8,128)(2,1)S(1)} %slice.18), channel_id=1, source_target_pairs={{0,1},{1,2},{2,3},{3,0},{4,5},{5,6},{6,7},{7,4},{8,9},{9,10},{10,1... | collective-permute-start | bytes 786440 | tf_op jit(solution)/shard_map/ppermute | solution.py:203
  52.3 7.7 %collective-permute-start.12 = (bf16[4,2,128,128]{3,2,1,0:T(8,128)(2,1)S(1)}, bf16[4,2,128,128]{3,2,1,0:T(8,128)(2,1)S(1)}, u32[]{:S(2)}, u32[]{:S(2)}) collective-permute-start(bf16[4,2,128,128]{3,2,1,0:T(8,128)(2,1)S(1)} %slice.19), channel_id=1, source_target_pairs={{0,3},{1,0},{2,1},{3,2},{4,7},{5,4},{6,5},{7,6},{8,11},{9,8},{10,9... | collective-permute-start | bytes 786440 | tf_op jit(solution)/shard_map/ppermute | solution.py:203
  55.9 6.1 %collective-permute-start.13 = (bf16[8,2,128,128]{3,2,1,0:T(8,128)(2,1)S(1)}, bf16[8,2,128,128]{3,2,1,0:T(8,128)(2,1)S(1)}, u32[]{:S(2)}, u32[]{:S(2)}) collective-permute-start(bf16[8,2,128,128]{3,2,1,0:T(8,128)(2,1)S(1)} %collective-permute-done.9.own_r), channel_id=1, source_target_pairs={{0,32},{32,0},{1,33},{33,1},{2,34},{34,2},{3,35},{35,3},{4,36},{36... | collective-permute-start | bytes 1572872 | tf_op jit(solution)/shard_map/ppermute | solution.py:207
  55.9 6.1 %collective-permute-start.14 = (bf16[8,2,128,128]{3,2,1,0:T(8,128)(2,1)S(1)}, bf16[8,2,128,128]{3,2,1,0:T(8,128)(2,1)S(1)}, u32[]{:S(2)}, u32[]{:S(2)}) collective-permute-start(bf16[8,2,128,128]{3,2,1,0:T(8,128)(2,1)S(1)} %collective-permute-done.11.own_l), channel_id=1, source_target_pairs={{0,32},{32,0},{1,33},{33,1},{2,34},{34,2},{3,35},{35,3},{4,36},{36... | collective-permute-start | bytes 1572872 | tf_op jit(solution)/shard_map/ppermute | solution.py:207
  59.9 1.6 %collective-permute-start.15 = (bf16[4,2,128,128]{3,2,1,0:T(8,128)(2,1)S(1)}, bf16[4,2,128,128]{3,2,1,0:T(8,128)(2,1)S(1)}, u32[]{:S(2)}, u32[]{:S(2)}) collective-permute-start(bf16[4,2,128,128]{3,2,1,0:T(8,128)(2,1)S(1)} %collective-permute-done.10.own_r2), channel_id=1, source_target_pairs={{0,32},{32,0},{1,33},{33,1},{2,34},{34,2},{3,35},{35,3},{4,36},{36... | collective-permute-start | bytes 786440 | tf_op jit(solution)/shard_map/ppermute | solution.py:207
  60.0 1.9 %collective-permute-start.16 = (bf16[4,2,128,128]{3,2,1,0:T(8,128)(2,1)S(1)}, bf16[4,2,128,128]{3,2,1,0:T(8,128)(2,1)S(1)}, u32[]{:S(2)}, u32[]{:S(2)}) collective-permute-start(bf16[4,2,128,128]{3,2,1,0:T(8,128)(2,1)S(1)} %collective-permute-done.12.own_l2), channel_id=1, source_target_pairs={{0,32},{32,0},{1,33},{33,1},{2,34},{34,2},{3,35},{35,3},{4,36},{36... | collective-permute-start | bytes 786440 | tf_op jit(solution)/shard_map/ppermute | solution.py:207
  67.1 2.0 %collective-permute-start.17 = (bf16[4,8,4,16,128]{4,3,2,1,0:T(8,128)(2,1)S(1)}, bf16[4,8,4,16,128]{4,3,2,1,0:T(8,128)(2,1)S(1)}, u32[]{:S(2)}, u32[]{:S(2)}) collective-permute-start(bf16[4,8,4,16,128]{4,3,2,1,0:T(8,128)(2,1)S(1)} %get-tuple-element.26), channel_id=1, source_target_pairs={{0,32},{32,0},{1,33},{33,1},{2,34},{34,2},{3,35},{35,3},{4,36},{36... | collective-permute-start | bytes 1572872 | tf_op jit(solution)/shard_map/ppermute | solution.py:207
  70.1 28.0 %all-to-all-start.2 = ((bf16[32,4,16,128]{3,2,1,0:T(8,128)(2,1)}), bf16[32,4,16,128]{3,2,1,0:T(8,128)(2,1)S(1)}, u32[]{:S(2)}, u32[]{:S(2)}) async-start(bf16[32,4,16,128]{3,2,1,0:T(8,128)(2,1)} %bitcast.11), calls=%async_computation.2 | async-start | bytes 1048576 | tf_op jit(solution)/shard_map/all_to_all | solution.py:242
